TPU v7x, 256 devices: a whole 4x4x8 slice. The times are simulated.
256 devices in a mesh: dp: 16 (over y, x), pass: 8 (over z), tensor: 2 (over core).
Axes of the slice: x: 4, y: 4, z: 8, core: 2. Of those that a mesh axis runs over, the one named last changes fastest.
Arguments:
- question_q: bfloat16 [512, 32, 4096], P(('dp', 'pass'), None, 'tensor'), may hold values from -4.5 to 4.5
- question_grad: bfloat16 [512, 32, 4096], P(('dp', 'pass'), None, 'tensor'), may hold values from -6 to 6
- question_kv: bfloat16 [512, 32, 2, 512], P(('dp', 'pass'), None, None, 'tensor'), may hold values from -4.5 to 4.5
- passage_kv: bfloat16 [256, 256, 2, 512], P(('dp', 'pass'), None, None, 'tensor'), may hold values from -6 to 6
- question_hidden: bfloat16 [512, 32, 4096], P(('dp', 'pass'), 'tensor'), may hold values from -24 to 24
- passage_hidden: bfloat16 [256, 256, 4096], P(('dp', 'pass'), 'tensor'), may hold values from -24 to 24
- reuse: int32 [16, 8, 16], P(None, 'pass'), may hold values from 0 to 31, as said below
- passage_blocks: int32 [16, 8, 2], P(None, 'pass'), may hold values from 1 to 2
Outputs:
- question_dq: bfloat16 [512, 32, 4096], P(('dp', 'pass'), None, 'tensor')
- question_dkv: bfloat16 [512, 32, 2, 512], P(('dp', 'pass'), None, None, 'tensor')
- passage_dkv: bfloat16 [256, 256, 2, 512], P(('dp', 'pass'), None, None, 'tensor')
- weight_grad: float32 [4096, 2, 512], P(('dp', 'pass', 'tensor'))
Inputs may be any that keep to these rules, and one draw needn't show every extreme that they name: `reuse`: an entry is owner * 2 + slot, owner being the dp index of the owning device within the same pass group. The 16 entries of one reading device name every owner of its pass group exactly once; entry j belongs to that device's sample j // 4.
All inputs are finite; a program needn't handle non-finite values.
Results may differ from a plain program's by a relative error of at most 0.0068.
Values may be sent and summed in bfloat16 or wider, within the bound.
No kernel may reach another device: no remote copies, remote signals or barrier semaphores. Data moves between devices by JAX's collectives and lax.ppermute only.
A program may use at most 128 MiB of HBM per device.

v0:
```python
import jax
import jax.numpy as jnp
from jax import lax
from jax.sharding import PartitionSpec as P

HD = 128
BLOCK = 128


NEG_FILL = -1e30


def key_valid(block_counts, query_len, slot_len):
    position = jnp.arange(slot_len, dtype=jnp.int32)
    passage_ok = (position[None, :] < block_counts[:, None] * BLOCK).reshape(-1)
    query_rows = jnp.arange(query_len, dtype=jnp.int32)
    own_ok = jnp.arange(BLOCK, dtype=jnp.int32)[None, :] <= query_rows[:, None]
    spread = jnp.broadcast_to(passage_ok[None, :], (query_len, passage_ok.shape[0]))
    return jnp.concatenate([spread, own_ok], axis=1)


def attend(queries, out_grad, key_rows, key_ok):
    query_len = queries.shape[0]
    key_count = key_rows.shape[0]
    kv_heads = key_rows.shape[2] // HD
    group_size = queries.shape[1] // HD // kv_heads
    score_scale = HD ** (-0.5)
    query_heads = queries.reshape(query_len, kv_heads, group_size, HD)
    grad_heads = out_grad.reshape(query_len, kv_heads, group_size, HD)
    key_heads = key_rows[:, 0].reshape(key_count, kv_heads, HD)
    value_heads = key_rows[:, 1].reshape(key_count, kv_heads, HD)
    scores = (
        jnp.einsum("qgrd,kgd->grqk", query_heads, key_heads, preferred_element_type=jnp.float32)
        * score_scale
    )
    scores = jnp.where(key_ok[None, None], scores, NEG_FILL)
    row_top = jnp.max(scores, axis=-1, keepdims=True)
    shifted_exp = jnp.exp(scores - row_top)
    attn_prob = shifted_exp / jnp.sum(shifted_exp, axis=-1, keepdims=True)
    prob_low = attn_prob.astype(jnp.bfloat16)
    prob_grad = jnp.einsum(
        "qgrd,kgd->grqk", grad_heads, value_heads, preferred_element_type=jnp.float32
    )
    row_delta = jnp.sum(attn_prob * prob_grad, axis=-1, keepdims=True)
    dscore = (attn_prob * (prob_grad - row_delta) * score_scale).astype(jnp.bfloat16)
    query_grad = jnp.einsum("grqk,kgd->qgrd", dscore, key_heads, preferred_element_type=jnp.float32)
    key_grad = jnp.einsum("grqk,qgrd->kgd", dscore, query_heads, preferred_element_type=jnp.float32)
    value_grad = jnp.einsum(
        "grqk,qgrd->kgd", prob_low, grad_heads, preferred_element_type=jnp.float32
    )
    stacked = jnp.stack(
        [key_grad.reshape(key_count, kv_heads * HD), value_grad.reshape(key_count, kv_heads * HD)],
        axis=1,
    )
    return (query_grad.reshape(query_len, -1).astype(jnp.bfloat16), stacked.astype(jnp.bfloat16))


def weight_terms(hidden_pass, grads_pass, hidden_query, grads_query, count):
    contract = (((0,), (0,)), ((), ()))
    summed = lax.dot_general(hidden_pass, grads_pass, contract, preferred_element_type=jnp.float32)
    summed = summed + lax.dot_general(
        hidden_query, grads_query, contract, preferred_element_type=jnp.float32
    )
    return summed.reshape(count, 2, -1)


def local(
    question_q,
    question_grad,
    question_kv,
    passage_kv,
    question_hidden,
    passage_hidden,
    reuse,
    passage_blocks,
):
    dp_index = lax.axis_index("dp")
    slot_count = passage_kv.shape[0]
    slot_len = passage_kv.shape[1]
    channels = passage_kv.shape[3]
    samples = question_q.shape[0]
    query_len = question_q.shape[1]
    reuse_table = reuse[:, 0, :]
    peer_count = reuse_table.shape[0]
    ref_count = reuse_table.shape[1] // samples
    owner_table = reuse_table // slot_count
    owner_hit = owner_table == dp_index
    slot_wanted = jnp.sum(jnp.where(owner_hit, reuse_table % slot_count, 0), axis=1)
    outgoing = jnp.take(passage_kv, slot_wanted, axis=0)
    incoming = lax.all_to_all(outgoing, "dp", split_axis=0, concat_axis=0, tiled=True)
    my_refs = lax.dynamic_index_in_dim(reuse_table, dp_index, 0, keepdims=False)
    my_owners = my_refs // slot_count
    my_blocks = passage_blocks[:, 0, :].reshape(-1)[my_refs]
    gathered = jnp.take(incoming, my_owners, axis=0).reshape(
        samples, ref_count * slot_len, 2, channels
    )
    pad_rows = jnp.zeros((BLOCK - query_len, 2, channels), jnp.bfloat16)

    def per_sample(item):
        queries, out_grad, own_rows, passage_rows, block_counts = item
        key_rows = jnp.concatenate([passage_rows, own_rows, pad_rows], axis=0)
        return attend(queries, out_grad, key_rows, key_valid(block_counts, query_len, slot_len))

    dq_all, dkv_all = lax.map(
        per_sample,
        (question_q, question_grad, question_kv, gathered, my_blocks.reshape(samples, ref_count)),
    )
    key_split = ref_count * slot_len
    own_grads = dkv_all[:, key_split : key_split + query_len]
    partials = dkv_all[:, :key_split].reshape(samples * ref_count, slot_len, 2, channels)
    peer_ids = jnp.arange(peer_count, dtype=jnp.int32)
    ref_ids = jnp.arange(samples * ref_count, dtype=jnp.int32)
    position = jnp.sum(
        jnp.where(my_owners[None, :] == peer_ids[:, None], ref_ids[None, :], 0), axis=1
    )
    returned = lax.all_to_all(
        jnp.take(partials, position, axis=0), "dp", split_axis=0, concat_axis=0, tiled=True
    )
    slot_ids = jnp.arange(slot_count, dtype=jnp.int32)
    owner_onehot = (slot_wanted[:, None] == slot_ids[None, :]).astype(jnp.bfloat16)
    passage_grad = jnp.einsum(
        "rs,rlkc->slkc", owner_onehot, returned, preferred_element_type=jnp.float32
    ).astype(jnp.bfloat16)
    model_width = passage_hidden.shape[2]
    full_pass, full_query = (
        lax.all_gather(passage_hidden, "tensor", axis=1, tiled=True),
        lax.all_gather(question_hidden, "tensor", axis=1, tiled=True),
    )
    flat_pass = full_pass.reshape(-1, model_width)
    flat_query = full_query.reshape(-1, model_width)
    grads_pass = passage_grad.reshape(flat_pass.shape[0], -1)
    grads_query = own_grads.reshape(flat_query.shape[0], -1)
    row_share = model_width // (lax.axis_size("dp") * lax.axis_size("pass"))
    block_part = lax.psum_scatter(
        weight_terms(
            flat_pass,
            grads_pass,
            flat_query,
            grads_query,
            row_share * lax.axis_size(("dp", "pass")),
        ),
        ("dp", "pass"),
        scatter_dimension=0,
        tiled=True,
    )
    weight_grad = lax.all_to_all(block_part, "tensor", split_axis=0, concat_axis=2, tiled=True)
    return (dq_all, own_grads, passage_grad, weight_grad)


def solution(mesh):
    in_specs = (
        P(("dp", "pass"), None, "tensor"),
        P(("dp", "pass"), None, "tensor"),
        P(("dp", "pass"), None, None, "tensor"),
        P(("dp", "pass"), None, None, "tensor"),
        P(("dp", "pass"), "tensor", None),
        P(("dp", "pass"), "tensor", None),
        P(None, "pass", None),
        P(None, "pass", None),
    )
    out_specs = (
        P(("dp", "pass"), None, "tensor"),
        P(("dp", "pass"), None, None, "tensor"),
        P(("dp", "pass"), None, None, "tensor"),
        P(("dp", "pass", "tensor"), None, None),
    )
    return jax.shard_map(local, mesh=mesh, in_specs=in_specs, out_specs=out_specs, check_vma=False)
```

profile of v0, /device:TPU:1, one launch (start us, length us, event | category | flops | bytes accessed | tf_op | source)
XLA Modules:
  0.0 592.9 jit_solution(14972902945835727237)
XLA Ops:
  8.2 9.8 %gather_fusion = bf16[16,256,2,256]{3,2,1,0:T(2,128)(2,1)} fusion(bf16[2,256,2,256]{3,2,1,0:T(2,128)(2,1)S(1)} %copy-done, s32[1024]{0:T(1024)S(1)} %pad_clamp_fusion.3), kind=kCustom, calls=%fused_computation.2 | custom fusion | bytes 8388672 | tf_op jit(solution)/shard_map/jit(_take)/gather | solution.py:89
  18.0 7.9 %broadcast_select_fusion = bf16[16,256,2,256]{3,2,1,0:T(2,128)(2,1)} fusion(bf16[16,256,2,256]{3,2,1,0:T(2,128)(2,1)} %gather_fusion, pred[16]{0:T(512)(128)(4,1)S(1)} %compare_and_fusion.2), kind=kLoop, calls=%fused_computation.47 | loop fusion | flops 2097152 | bytes 8388624 | tf_op jit(solution)/shard_map/jit(_take)/select_n | solution.py:89
  25.9 7.7 %all-to-all-start = ((bf16[16,256,2,256]{3,2,1,0:T(2,128)(2,1)}), bf16[16,256,2,256]{3,2,1,0:T(2,128)(2,1)}, u32[]{:S(2)}, u32[]{:S(2)}) async-start(bf16[16,256,2,256]{3,2,1,0:T(2,128)(2,1)} %broadcast_select_fusion), calls=%async_computation | async-start | bytes 8388608 | tf_op jit(solution)/shard_map/all_to_all | solution.py:90
  36.8 59.1 %all-to-all-done = bf16[16,256,2,256]{3,2,1,0:T(2,128)(2,1)} async-done(((bf16[16,256,2,256]{3,2,1,0:T(2,128)(2,1)}), bf16[16,256,2,256]{3,2,1,0:T(2,128)(2,1)}, u32[]{:S(2)}, u32[]{:S(2)}) %all-to-all-start) | async-done | bytes 4194336 | tf_op jit(solution)/shard_map/all_to_all | solution.py:90
  96.0 4.9 copy.128
  100.9 4.9 gather_fusion.2
  105.9 2.6 broadcast_select_fusion.2
  108.5 2.3 copy.129
  110.8 83.3 %while.12 = (s32[]{:T(128)}, bf16[4,32,2048]{2,1,0:T(8,128)(2,1)}, bf16[4,1152,2,256]{1,3,2,0:T(8,128)(2,1)}, bf16[4,1024,2,256]{3,1,0,2:T(8,128)(2,1)}, bf16[4,...) while((s32[]{:T(128)}, bf16[4,32,2048]{2,1,0:T(8,128)(2,1)}, ...), condition=%wide.region_5.7_spmd, body=%wide.region_1.6_spmd.sunk | while | flops 769832320 | bytes 47708636 | solution.py:104
  110.8 1.3 constant_dynamic-slice_fusion.7
  113.6 1.2 concatenate.15
  116.5 2.3 fusion.93
  118.8 4.7 fusion.94
  124.3 2.1 fusion.95
  127.0 2.9 fusion.97
  131.6 1.3 constant_dynamic-slice_fusion.7
  134.4 1.2 concatenate.15
  137.3 2.3 fusion.93
  139.6 4.7 fusion.94
  145.1 2.1 fusion.95
  147.8 2.9 fusion.97
  152.4 1.3 constant_dynamic-slice_fusion.7
  155.2 1.2 concatenate.15
  158.2 2.3 fusion.93
  160.5 4.7 fusion.94
  166.0 2.1 fusion.95
  168.6 2.9 fusion.97
  173.2 1.3 constant_dynamic-slice_fusion.7
  179.0 2.3 fusion.93
  181.2 4.7 fusion.94
  186.7 2.1 fusion.95
  189.4 2.9 fusion.97
  192.9 1.2 maximum_dynamic-update-slice_fusion.2
  194.1 6.7 %copy.134 = bf16[4,1152,2,256]{3,1,0,2:T(8,128)(2,1)} copy(bf16[4,1152,2,256]{1,3,2,0:T(8,128)(2,1)} %get-tuple-element.49) | data formatting | bytes 9437184 | tf_op jit(solution)/shard_map/while | solution.py:104
  200.8 2.2 slice-done
  203.0 2.3 copy.135
  205.2 4.9 gather_fusion.3
  210.1 2.6 broadcast_select_fusion.1
  212.8 6.3 %copy.136 = bf16[16,256,2,256]{3,2,1,0:T(2,128)(2,1)} copy(bf16[16,256,2,256]{3,1,2,0:T(8,128)(2,1)S(1)} %broadcast_select_fusion.1) | data formatting | bytes 8388608 | tf_op jit(solution)/shard_map/jit(_take)/select_n | solution.py:117
  219.1 4.5 all-to-all-start.1
  224.4 12.7 %copy.133 = bf16[4,1152,2,256]{3,2,1,0:T(2,128)(2,1)} copy(bf16[4,1152,2,256]{1,3,2,0:T(8,128)(2,1)} %get-tuple-element.49) | data formatting | bytes 9437184 | tf_op jit(solution)/shard_map/while | solution.py:104
  238.1 44.9 %all-to-all-done.1 = bf16[16,256,2,256]{3,2,1,0:T(2,128)(2,1)} async-done(((bf16[16,256,2,256]{3,2,1,0:T(2,128)(2,1)}), bf16[16,256,2,256]{3,2,1,0:T(2,128)(2,1)}, u32[]{:S(2)}, u32[]{:S(2)}) %all-to-all-start.1) | async-done | bytes 4194336 | tf_op jit(solution)/shard_map/all_to_all | solution.py:116
  283.1 4.7 fusion.33
  288.3 7.9 %fusion.51 = f32[512,4096]{1,0:T(8,128)} fusion(bf16[512,512]{1,0:T(8,128)(2,1)S(1)} %bitcast.161, bf16[512,4096]{1,0:T(8,128)(2,1)} %bitcast.160), kind=kOutput, calls=%fused_computation.94 | convolution fusion | flops 2147483648 | bytes 13107200 | tf_op jit(solution)/shard_map/dot_general | solution.py:60
  296.2 8.3 %convolution_add_fusion = f32[512,4096]{1,0:T(8,128)} fusion(f32[512,4096]{1,0:T(8,128)} %fusion.51, bf16[128,512]{1,0:T(8,128)(2,1)S(1)} %bitcast.164, bf16[128,4096]{1,0:T(8,128)(2,1)} %bitcast.163), kind=kOutput, calls=%fused_computation.48 | convolution fusion | flops 538968064 | bytes 17956864 | tf_op jit(solution)/shard_map/dot_general | solution.py:61
  304.6 13.2 %copy.139 = f32[4096,2,256]{2,1,0:T(2,128)} copy(f32[4096,2,256]{0,2,1:T(8,128)} %bitcast.150) | data formatting | bytes 16777216 | tf_op jit(solution)/shard_map/reshape | solution.py:64
  319.6 260.7 %all-reduce.3.cloned.1.call-done = f32[4096,2,256]{2,1,0:T(2,128)} async-done(((f32[4096,2,256]{2,1,0:T(2,128)}), f32[4096,2,256]{2,1,0:T(2,128)}) %all-reduce.3.cloned.1.call-update) | async-done | bytes 8388624
  581.2 4.4 all_to_all.28
  (141 shorter events, 34.1 us)
Async XLA Ops:
  7.2 1.1 copy-start
  25.9 8.5 %copy-start.5 = (s32[16,1,2]{0,2,1:T(2,128)S(1)}, s32[16,1,2]{0,2,1:T(2,128)}, u32[]{:S(2)}) copy-start(s32[16,1,2]{0,2,1:T(2,128)} %param.19) | copy-start | bytes 388
  25.9 70.1 %all-to-all-start = ((bf16[16,256,2,256]{3,2,1,0:T(2,128)(2,1)}), bf16[16,256,2,256]{3,2,1,0:T(2,128)(2,1)}, u32[]{:S(2)}, u32[]{:S(2)}) async-start(bf16[16,256,2,256]{3,2,1,0:T(2,128)(2,1)} %broadcast_select_fusion), calls=%async_computation | async-start | bytes 8388608 | tf_op jit(solution)/shard_map/all_to_all | solution.py:90
  33.6 254.6 %all-gather.3.cloned.1.call-start = ((), (), s32[]{:S(2)}) async-start(), calls=%async_computation.3 | async-start | bytes 6291456 | tf_op jit(solution)/shard_map/all_gather | solution.py:126
  124.3 2.6 copy-start.2
  145.1 2.6 copy-start.2
  165.9 2.6 copy-start.2
  186.7 2.6 copy-start.2
  200.8 2.2 slice-start
  219.1 64.0 %all-to-all-start.1 = ((bf16[16,256,2,256]{3,2,1,0:T(2,128)(2,1)}), bf16[16,256,2,256]{3,2,1,0:T(2,128)(2,1)}, u32[]{:S(2)}, u32[]{:S(2)}) async-start(bf16[16,256,2,256]{3,2,1,0:T(2,128)(2,1)} %copy.136), calls=%async_computation.1 | async-start | bytes 8388608 | tf_op jit(solution)/shard_map/all_to_all | solution.py:116
  223.6 72.6 %all-gather.5.cloned.1.call-start = ((), (), s32[]{:S(2)}) async-start(), calls=%async_computation.4 | async-start | bytes 1572864 | tf_op jit(solution)/shard_map/all_gather | solution.py:127
  224.4 355.9 %all-reduce.3.cloned.1.call-start = ((), (), s32[]{:S(2)}) async-start(), calls=%async_computation.5 | async-start | bytes 16777216
  238.1 49.7 %copy-start.4 = (bf16[4,32,2,256]{3,2,1,0:T(2,128)(2,1)}, bf16[4,32,2,256]{3,2,1,0:T(2,128)(2,1)S(1)}, u32[]{:S(2)}) copy-start(bf16[4,32,2,256]{3,2,1,0:T(2,128)(2,1)S(1)} %slice.24) | copy-start | bytes 393220
  288.2 8.1 %copy-start.3 = (bf16[2,256,2,256]{3,2,1,0:T(2,128)(2,1)}, bf16[2,256,2,256]{3,2,1,0:T(2,128)(2,1)S(1)}, u32[]{:S(2)}) copy-start(bf16[2,256,2,256]{3,2,1,0:T(2,128)(2,1)S(1)} %copy.142) | copy-start | bytes 1572868
  317.7 0.7 copy-start.6
  317.8 268.6 %copy-start.1 = (bf16[2,256,2,256]{3,2,1,0:T(2,128)(2,1)S(1)}, bf16[2,256,2,256]{3,2,1,0:T(2,128)(2,1)}, u32[]{:S(2)}) copy-start(bf16[2,256,2,256]{3,2,1,0:T(2,128)(2,1)} %param.15) | copy-start | bytes 1572868
Sparse Core Ops, SparseCore 0:
  36.3 23.1 all-gather.2
  226.3 19.4 all-gather.4
  317.9 262.3 all-reduce.2
where the time goes:
time: 595 us; the launch traced here: 593 us
  waiting for transfers between devices  366 us (62%)
  local copies, waits for them, and re-layouts  99.1 us (17%)
  matrix products  55 us (9%)
  other arithmetic  40.6 us (7%)
  between operations  14.6 us (2%)
  starting transfers between devices  12.4 us (2%)
    unnamed x4, waiting for transfers between devices  262 us
    all_to_all x1, waiting for transfers between devices, local(): lax.all_to_all(outgoing, 'dp', split_axis=0, concat_axis=0, tiled=True)  59.1 us
    all_to_all x1, waiting for transfers between devices, local(): lax.all_to_all(jnp.take(partials, position, axis=0), 'dp', split_axis=0,...  44.9 us
    while x2, local copies, waits for them, and re-layouts, local(): lax.map(per_sample, (question_q, question_grad, question_kv, gathered, my...  19.3 us
    dot_general x4, matrix products, attend(): jnp.einsum('grqk,kgd->qgrd', dscore, key_heads, preferred_element_type=jn...  18.8 us
    reshape x1, local copies, waits for them, and re-layouts, weight_terms(): return summed.reshape(count, 2, -1)  13.2 us
  transfers between devices with their start and end apart: 5, of which 3 were waited for; matrix products, arithmetic and copies ran while one was open for 25% of the time, Pallas kernels for 0%

commit v1 on v0

v1 whole, which is shorter than its diff:
```python
import functools

import jax
import jax.numpy as jnp
from jax import lax
from jax.experimental import pallas as pl
from jax.experimental.pallas import tpu as pltpu
from jax.sharding import PartitionSpec as P

HD = 128
BLOCK = 128
NEG_FILL = -1e30
SCALE = HD ** (-0.5)
VMEM_LIMIT = 48 * 1024 * 1024
NT = (((1,), (1,)), ((), ()))
TN = (((0,), (0,)), ((), ()))
F32 = jnp.float32
BF16 = jnp.bfloat16


def params():
    return pltpu.CompilerParams(vmem_limit_bytes=VMEM_LIMIT)


def whole():
    return pl.BlockSpec(memory_space=pltpu.VMEM)


def smem():
    return pl.BlockSpec(memory_space=pltpu.SMEM)


def cost(flops, nbytes, trans=0):
    return pl.CostEstimate(flops=flops, bytes_accessed=nbytes, transcendentals=trans)


def head_rows(block, head, group):
    first = head * group
    return jnp.concatenate(
        [block[:, (first + r) * HD : (first + r + 1) * HD] for r in range(group)], axis=0
    )


def send_kernel(slots, refs, me, q_ref, g_ref, out_ref, sems):
    peers = out_ref.shape[0]
    rows = q_ref.shape[1]
    per = peers // q_ref.shape[0]
    copies = []
    for j in range(peers):
        dest = refs[me[0], j] // slots
        for part, src in enumerate((q_ref, g_ref)):
            copy = pltpu.make_async_copy(
                src.at[j // per],
                out_ref.at[dest, pl.ds(part * rows, rows)],
                sems.at[j, part],
            )
            copy.start()
            copies.append(copy)
    for copy in copies:
        copy.wait()


def pack_queries(refs, me, question_q, question_grad, slots):
    samples, rows, width = question_q.shape
    peers = refs.shape[0]
    return pl.pallas_call(
        functools.partial(send_kernel, slots),
        out_shape=jax.ShapeDtypeStruct((peers, 2 * rows, width), BF16),
        in_specs=[smem(), smem(), whole(), whole()],
        out_specs=pl.BlockSpec(memory_space=pl.ANY),
        scratch_shapes=[pltpu.SemaphoreType.DMA((peers, 2))],
        compiler_params=params(),
        cost_estimate=cost(0, 6 * 2**20),
        name="pack_queries",
    )(refs, me, question_q, question_grad)


def scores_t(keys, queries, valid):
    scores = lax.dot_general(keys, queries, NT, preferred_element_type=F32) * SCALE
    return jnp.where(valid, scores, NEG_FILL)


def put_stats(out_ref, index, head, heads, scores, prob_grad):
    top = jnp.max(scores, axis=0, keepdims=True)
    shifted = jnp.exp(scores - top)
    total = jnp.sum(shifted, axis=0, keepdims=True)
    weighted = jnp.sum(shifted * prob_grad, axis=0, keepdims=True)
    out_ref[index, head : head + 1] = top + jnp.log(total)
    out_ref[index, heads + head : heads + head + 1] = weighted / total


def owner_stats_kernel(group, slot_of, blocks, got_ref, k_ref, v_ref, out_ref):
    slot = slot_of[pl.program_id(0)]
    rows = got_ref.shape[1] // 2
    slot_len = k_ref.shape[1]
    heads = k_ref.shape[2] // HD
    shape = (slot_len, group * rows)
    valid = lax.broadcasted_iota(jnp.int32, shape, 0) < blocks[slot] * BLOCK
    for head in range(heads):
        lanes = slice(head * HD, (head + 1) * HD)
        queries = head_rows(got_ref[0, :rows], head, group)
        grads = head_rows(got_ref[0, rows:], head, group)
        scores = scores_t(k_ref[slot, :, lanes], queries, valid)
        prob_grad = lax.dot_general(v_ref[slot, :, lanes], grads, NT, preferred_element_type=F32)
        put_stats(out_ref, 0, head, heads, scores, prob_grad)


def owner_stats(slot_of, blocks, got, keys, values, group):
    peers, both, width = got.shape
    heads = keys.shape[2] // HD
    columns = group * both // 2
    return pl.pallas_call(
        functools.partial(owner_stats_kernel, group),
        out_shape=jax.ShapeDtypeStruct((peers, 2 * heads, columns), F32),
        grid_spec=pltpu.PrefetchScalarGridSpec(
            num_scalar_prefetch=2,
            grid=(peers,),
            in_specs=[
                pl.BlockSpec((1, both, width), lambda r, s, b: (r, 0, 0)),
                whole(),
                whole(),
            ],
            out_specs=pl.BlockSpec((1, 2 * heads, columns), lambda r, s, b: (r, 0, 0)),
        ),
        compiler_params=params(),
        cost_estimate=cost(2 * 10**9, 5 * 2**20, 2 * 10**6),
        name="owner_stats",
    )(slot_of, blocks, got, keys, values)


def own_valid(own_rows, rows, group):
    shape = (own_rows, group * rows)
    key_row = lax.broadcasted_iota(jnp.int32, shape, 0)
    query_row = lax.rem(lax.broadcasted_iota(jnp.int32, shape, 1), jnp.int32(rows))
    return key_row <= query_row


def own_stats_kernel(group, q_ref, g_ref, k_ref, v_ref, out_ref):
    samples, rows, _ = q_ref.shape
    heads = k_ref.shape[2] // HD
    valid = own_valid(rows, rows, group)
    for sample in range(samples):
        for head in range(heads):
            lanes = slice(head * HD, (head + 1) * HD)
            queries = head_rows(q_ref[sample], head, group)
            grads = head_rows(g_ref[sample], head, group)
            scores = scores_t(k_ref[sample, :, lanes], queries, valid)
            prob_grad = lax.dot_general(
                v_ref[sample, :, lanes], grads, NT, preferred_element_type=F32
            )
            put_stats(out_ref, sample, head, heads, scores, prob_grad)


def own_stats(question_q, question_grad, keys, values, group):
    samples, rows, _ = question_q.shape
    heads = keys.shape[2] // HD
    return pl.pallas_call(
        functools.partial(own_stats_kernel, group),
        out_shape=jax.ShapeDtypeStruct((samples, 2 * heads, group * rows), F32),
        in_specs=[whole()] * 4,
        out_specs=whole(),
        compiler_params=params(),
        cost_estimate=cost(10**8, 2**20, 10**5),
        name="own_stats",
    )(question_q, question_grad, keys, values)


def merge_kernel(slots, refs, me, st_ref, own_ref, back_ref, merged_ref):
    samples, stat_rows, _ = own_ref.shape
    heads = stat_rows // 2
    per = st_ref.shape[0] // samples
    for sample in range(samples):
        owners = [refs[me[0], sample * per + k] // slots for k in range(per)]
        parts = [own_ref[sample]] + [st_ref[owner] for owner in owners]
        logs = [part[:heads] for part in parts]
        top = functools.reduce(jnp.maximum, logs)
        total = sum(jnp.exp(one - top) for one in logs)
        joint = top + jnp.log(total)
        delta = sum(jnp.exp(one - joint) * part[heads:] for one, part in zip(logs, parts))
        both = jnp.concatenate([joint, delta], axis=0)
        merged_ref[sample] = both
        for owner in owners:
            back_ref[owner] = both


def merge(refs, me, stats, own, slots):
    return pl.pallas_call(
        functools.partial(merge_kernel, slots),
        out_shape=(
            jax.ShapeDtypeStruct(stats.shape, F32),
            jax.ShapeDtypeStruct(own.shape, F32),
        ),
        in_specs=[smem(), smem(), whole(), whole()],
        out_specs=(whole(), whole()),
        compiler_params=params(),
        cost_estimate=cost(10**5, 2**17, 10**4),
        name="merge_stats",
    )(refs, me, stats, own)


def probs_and_dscore(scores, prob_grad, joint, delta):
    probs = jnp.exp(scores - joint)
    dscore = (probs * (prob_grad - delta) * SCALE).astype(BF16)
    return probs.astype(BF16), dscore


def owner_grads_kernel(
    group, slot_of, blocks, got_ref, joint_ref, k_ref, v_ref, grad_ref, dq_ref, acc_ref
):
    step = pl.program_id(0)
    slot = slot_of[step]
    rows = got_ref.shape[1] // 2
    slot_len = k_ref.shape[1]
    width = k_ref.shape[2]
    heads = width // HD
    shape = (slot_len, group * rows)
    valid = lax.broadcasted_iota(jnp.int32, shape, 0) < blocks[slot] * BLOCK

    @pl.when(step == 0)
    def _():
        acc_ref[...] = jnp.zeros_like(acc_ref)

    for head in range(heads):
        lanes = slice(head * HD, (head + 1) * HD)
        value_lanes = slice(width + head * HD, width + (head + 1) * HD)
        queries = head_rows(got_ref[0, :rows], head, group)
        grads = head_rows(got_ref[0, rows:], head, group)
        keys = k_ref[slot, :, lanes]
        scores = scores_t(keys, queries, valid)
        prob_grad = lax.dot_general(v_ref[slot, :, lanes], grads, NT, preferred_element_type=F32)
        joint = joint_ref[0, head : head + 1]
        delta = joint_ref[0, heads + head : heads + head + 1]
        probs, dscore = probs_and_dscore(scores, prob_grad, joint, delta)
        acc_ref[slot, :, lanes] += jnp.dot(dscore, queries, preferred_element_type=F32)
        acc_ref[slot, :, value_lanes] += jnp.dot(probs, grads, preferred_element_type=F32)
        dq = lax.dot_general(dscore, keys, TN, preferred_element_type=F32).astype(BF16)
        for r in range(group):
            column = (head * group + r) * HD
            dq_ref[0, :, column : column + HD] = dq[r * rows : (r + 1) * rows]

    @pl.when(step == pl.num_programs(0) - 1)
    def _():
        for one in range(acc_ref.shape[0]):
            grad_ref[one * slot_len : (one + 1) * slot_len] = acc_ref[one].astype(BF16)


def owner_grads(slot_of, blocks, got, joint, keys, values, group):
    peers, both, width = got.shape
    slots, slot_len, key_width = keys.shape
    stat_rows, columns = joint.shape[1:]
    return pl.pallas_call(
        functools.partial(owner_grads_kernel, group),
        out_shape=(
            jax.ShapeDtypeStruct((slots * slot_len, 2 * key_width), BF16),
            jax.ShapeDtypeStruct((peers, both // 2, width), BF16),
        ),
        grid_spec=pltpu.PrefetchScalarGridSpec(
            num_scalar_prefetch=2,
            grid=(peers,),
            in_specs=[
                pl.BlockSpec((1, both, width), lambda r, s, b: (r, 0, 0)),
                pl.BlockSpec((1, stat_rows, columns), lambda r, s, b: (r, 0, 0)),
                whole(),
                whole(),
            ],
            out_specs=(
                pl.BlockSpec((slots * slot_len, 2 * key_width), lambda r, s, b: (0, 0)),
                pl.BlockSpec((1, both // 2, width), lambda r, s, b: (r, 0, 0)),
            ),
            scratch_shapes=[pltpu.VMEM((slots, slot_len, 2 * key_width), F32)],
        ),
        compiler_params=params(),
        cost_estimate=cost(5 * 10**9, 8 * 2**20, 2 * 10**6),
        name="owner_grads",
    )(slot_of, blocks, got, joint, keys, values)


def own_grads_kernel(group, q_ref, g_ref, k_ref, v_ref, joint_ref, grad_ref, dq_ref):
    samples, rows, _ = q_ref.shape
    width = k_ref.shape[2]
    heads = width // HD
    valid = own_valid(rows, rows, group)
    for sample in range(samples):
        token = slice(sample * rows, (sample + 1) * rows)
        for head in range(heads):
            lanes = slice(head * HD, (head + 1) * HD)
            value_lanes = slice(width + head * HD, width + (head + 1) * HD)
            queries = head_rows(q_ref[sample], head, group)
            grads = head_rows(g_ref[sample], head, group)
            keys = k_ref[sample, :, lanes]
            scores = scores_t(keys, queries, valid)
            prob_grad = lax.dot_general(
                v_ref[sample, :, lanes], grads, NT, preferred_element_type=F32
            )
            joint = joint_ref[sample, head : head + 1]
            delta = joint_ref[sample, heads + head : heads + head + 1]
            probs, dscore = probs_and_dscore(scores, prob_grad, joint, delta)
            key_grad = jnp.dot(dscore, queries, preferred_element_type=F32)
            value_grad = jnp.dot(probs, grads, preferred_element_type=F32)
            grad_ref[token, lanes] = key_grad.astype(BF16)
            grad_ref[token, value_lanes] = value_grad.astype(BF16)
            dq = lax.dot_general(dscore, keys, TN, preferred_element_type=F32)
            for r in range(group):
                column = (head * group + r) * HD
                dq_ref[sample, :, column : column + HD] = dq[r * rows : (r + 1) * rows]


def own_grads(question_q, question_grad, keys, values, joint, group):
    samples, rows, width = question_q.shape
    key_width = keys.shape[2]
    return pl.pallas_call(
        functools.partial(own_grads_kernel, group),
        out_shape=(
            jax.ShapeDtypeStruct((samples * rows, 2 * key_width), BF16),
            jax.ShapeDtypeStruct((samples, rows, width), F32),
        ),
        in_specs=[whole()] * 5,
        out_specs=(whole(), whole()),
        compiler_params=params(),
        cost_estimate=cost(3 * 10**8, 3 * 2**20, 10**5),
        name="own_grads",
    )(question_q, question_grad, keys, values, joint)


def sum_dq_kernel(owners, *refs):
    out_ref = refs[-1]
    total = refs[-2][0]
    for ref in refs[:-2]:
        total = total + ref[0].astype(F32)
    out_ref[0] = total.astype(BF16)


def sum_dq(owners, returned, own):
    samples, rows, width = own.shape
    per = returned.shape[0] // samples

    def from_owner(k):
        return pl.BlockSpec((1, rows, width), lambda s, o: (o[s * per + k], 0, 0))

    return pl.pallas_call(
        sum_dq_kernel,
        out_shape=jax.ShapeDtypeStruct((samples, rows, width), BF16),
        grid_spec=pltpu.PrefetchScalarGridSpec(
            num_scalar_prefetch=1,
            grid=(samples,),
            in_specs=[from_owner(k) for k in range(per)]
            + [pl.BlockSpec((1, rows, width), lambda s, o: (s, 0, 0))],
            out_specs=pl.BlockSpec((1, rows, width), lambda s, o: (s, 0, 0)),
        ),
        compiler_params=params(),
        cost_estimate=cost(2 * 10**6, 4 * 2**20),
        name="sum_dq",
    )(owners, *([returned] * per), own)


def transpose_kernel(p_ref, q_ref, out_ref):
    split = p_ref.shape[0]
    out_ref[:, :split] = p_ref[...].T
    out_ref[:, split:] = q_ref[...].T


def transpose_hidden(flat_pass, flat_query):
    count, width = flat_pass.shape
    extra = flat_query.shape[0]
    tile = 512
    return pl.pallas_call(
        transpose_kernel,
        out_shape=jax.ShapeDtypeStruct((width, count + extra), BF16),
        grid=(width // tile,),
        in_specs=[
            pl.BlockSpec((count, tile), lambda i: (0, i)),
            pl.BlockSpec((extra, tile), lambda i: (0, i)),
        ],
        out_specs=pl.BlockSpec((tile, count + extra), lambda i: (i, 0)),
        compiler_params=params(),
        cost_estimate=cost(0, 12 * 2**20),
        name="transpose_hidden",
    )(flat_pass, flat_query)


def weight_kernel(h_ref, p_ref, q_ref, out_ref):
    split = p_ref.shape[0]
    groups, owners, rows, width = out_ref.shape
    total = jnp.dot(h_ref[:, :split], p_ref[...], preferred_element_type=F32)
    total = total + jnp.dot(h_ref[:, split:], q_ref[...], preferred_element_type=F32)
    total = total.astype(BF16)
    for owner in range(owners):
        for group in range(groups):
            first = (owner * groups + group) * rows
            out_ref[group, owner] = total[first : first + rows]


def weight_terms(hidden_t, grads_pass, grads_query, owners, groups):
    model_width, tokens = hidden_t.shape
    width = grads_pass.shape[1]
    rows = model_width // (owners * groups)
    per = 2
    return pl.pallas_call(
        weight_kernel,
        out_shape=jax.ShapeDtypeStruct((groups, owners, rows, width), BF16),
        grid=(owners // per,),
        in_specs=[
            pl.BlockSpec((per * groups * rows, tokens), lambda i: (i, 0)),
            whole(),
            whole(),
        ],
        out_specs=pl.BlockSpec((groups, per, rows, width), lambda i: (0, i, 0, 0)),
        compiler_params=params(),
        cost_estimate=cost(2 * model_width * tokens * width, 10 * 2**20),
        name="weight_terms",
    )(hidden_t, grads_pass, grads_query)


def finish_kernel(x_ref, out_ref):
    owners, cores, rows, width = x_ref.shape
    half = width // 2
    for core in range(cores):
        total = x_ref[0, core].astype(F32)
        for owner in range(1, owners):
            total = total + x_ref[owner, core].astype(F32)
        lanes = slice(core * half, (core + 1) * half)
        out_ref[:, 0, lanes] = total[:, :half]
        out_ref[:, 1, lanes] = total[:, half:]


def finish_weights(parts):
    owners, cores, rows, width = parts.shape
    return pl.pallas_call(
        finish_kernel,
        out_shape=jax.ShapeDtypeStruct((rows, 2, cores * width // 2), F32),
        in_specs=[whole()],
        out_specs=whole(),
        compiler_params=params(),
        cost_estimate=cost(10**6, 2**20),
        name="finish_weights",
    )(parts)


def local(
    question_q,
    question_grad,
    question_kv,
    passage_kv,
    question_hidden,
    passage_hidden,
    reuse,
    passage_blocks,
):
    me = lax.axis_index("dp")
    me_array = me.reshape(1)
    peers = lax.axis_size("dp")
    groups = lax.axis_size("pass")
    cores = lax.axis_size("tensor")
    slots, slot_len, _, channels = passage_kv.shape
    samples, rows, width = question_q.shape
    group = width // channels
    refs = reuse.reshape(reuse.shape[0], reuse.shape[2])

    def exchange(x):
        return lax.all_to_all(x, "dp", split_axis=0, concat_axis=0, tiled=True)

    packed = pack_queries(refs, me_array, question_q, question_grad, slots)
    got = exchange(packed)

    slot_of = jnp.sum(jnp.where(refs // slots == me, refs % slots, 0), axis=1)
    owners = lax.dynamic_index_in_dim(refs, me, 0, keepdims=False) // slots
    blocks = lax.dynamic_index_in_dim(passage_blocks, me, 0, keepdims=False).reshape(slots)
    keys, values = passage_kv[:, :, 0], passage_kv[:, :, 1]
    own_keys, own_values = question_kv[:, :, 0], question_kv[:, :, 1]
    own = own_stats(question_q, question_grad, own_keys, own_values, group)

    full_pass = lax.all_gather(passage_hidden, "tensor", axis=1, tiled=True)
    full_query = lax.all_gather(question_hidden, "tensor", axis=1, tiled=True)
    model_width = passage_hidden.shape[2]
    hidden_t = transpose_hidden(
        full_pass.reshape(-1, model_width), full_query.reshape(-1, model_width)
    )

    stats = owner_stats(slot_of, blocks, got, keys, values, group)
    back, merged = merge(refs, me_array, exchange(stats), own, slots)
    joint = exchange(back)
    grads_query, own_dq = own_grads(
        question_q, question_grad, own_keys, own_values, merged, group
    )
    grads_pass, dq_parts = owner_grads(slot_of, blocks, got, joint, keys, values, group)

    terms = weight_terms(hidden_t, grads_pass, grads_query, peers, groups)
    summed = lax.psum_scatter(terms, "pass", scatter_dimension=0, tiled=False)
    question_dq = sum_dq(owners, exchange(dq_parts), own_dq)

    share = summed.shape[1] // cores
    parts = lax.all_to_all(
        summed.reshape(peers * cores, share, -1),
        ("dp", "tensor"),
        split_axis=0,
        concat_axis=0,
        tiled=True,
    )
    weight_grad = finish_weights(parts.reshape(peers, cores, share, -1))
    question_dkv = grads_query.reshape(samples, rows, 2, channels)
    passage_dkv = grads_pass.reshape(slots, slot_len, 2, channels)
    return (question_dq, question_dkv, passage_dkv, weight_grad)


def solution(mesh):
    in_specs = (
        P(("dp", "pass"), None, "tensor"),
        P(("dp", "pass"), None, "tensor"),
        P(("dp", "pass"), None, None, "tensor"),
        P(("dp", "pass"), None, None, "tensor"),
        P(("dp", "pass"), "tensor", None),
        P(("dp", "pass"), "tensor", None),
        P(None, "pass", None),
        P(None, "pass", None),
    )
    out_specs = (
        P(("dp", "pass"), None, "tensor"),
        P(("dp", "pass"), None, None, "tensor"),
        P(("dp", "pass"), None, None, "tensor"),
        P(("dp", "pass", "tensor"), None, None),
    )
    return jax.shard_map(local, mesh=mesh, in_specs=in_specs, out_specs=out_specs, check_vma=False)
```

time: 595 us -> 246 us (0.41)
  waiting for transfers between devices: 366 us -> 108 us
  local copies, waits for them, and re-layouts: 99.1 us -> 16.5 us
  matrix products: 55 us -> 0 us
  Pallas kernels: 0 us -> 54.2 us
  other arithmetic: 40.6 us -> 0.14 us
  blocking collectives: 4.4 us -> 28 us
  starting transfers between devices: 12.4 us -> 23.2 us
    unnamed x4 -> x3, waiting for transfers between devices: 262 us -> 1.39 us
    pallas_call x0 -> x10, Pallas kernels: none -> 54.2 us  [the longest x1 15.8 us: owner_grads(): pl.pallas_call(functools.partial(owner_grads_kernel, group), out_shape=(j...]
    dot_general x19 -> x0, matrix products: 45.8 us -> none  [the longest x4 18.8 us: attend(): jnp.einsum('grqk,kgd->qgrd', dscore, key_heads, preferred_element_type=jn...]
    reduce_scatter x0 -> x1, waiting for transfers between devices: none -> 30.5 us  [local(): summed = lax.psum_scatter(terms, 'pass', scatter_dimension=0, tiled=False)]
    all_to_all x2 -> x4, waiting for transfers between devices: 104 us -> 76.3 us  [the longest x3 69.7 us: exchange(): return lax.all_to_all(x, 'dp', split_axis=0, concat_axis=0, tiled=True)]
    all_to_all x1, blocking collectives: 4.4 us -> 28 us  [exchange(): return lax.all_to_all(x, 'dp', split_axis=0, concat_axis=0, tiled=True)]
    while x22 -> x0, local copies, waits for them, and re-layouts: 23.5 us -> none  [the longest x2 19.3 us: local(): lax.map(per_sample, (question_q, question_grad, question_kv, gathered, my...]
    gather x4 -> x0, local copies, waits for them, and re-layouts: 20.3 us -> none  [the longest x1 9.79 us: local(): outgoing = jnp.take(passage_kv, slot_wanted, axis=0)]
  transfers between devices with their start and end apart: 5 -> 7, of which waited for: 3 -> 5; matrix products, arithmetic and copies ran while one was open for 25% -> 1% of each run, Pallas kernels for 0% -> 17%
where the time goes in v1:
time: 246 us; the launch traced here: 244 us
  waiting for transfers between devices  108 us (44%)
  Pallas kernels  54.2 us (22%)
  blocking collectives  28 us (11%)
  starting transfers between devices  23.2 us (9%)
  local copies, waits for them, and re-layouts  16.5 us (7%)
  between operations  14 us (6%)
    all_to_all x3, waiting for transfers between devices, exchange(): return lax.all_to_all(x, 'dp', split_axis=0, concat_axis=0, tiled=True)  69.7 us
    reduce_scatter x1, waiting for transfers between devices, local(): summed = lax.psum_scatter(terms, 'pass', scatter_dimension=0, tiled=False)  30.5 us
    all_to_all x1, blocking collectives, exchange(): return lax.all_to_all(x, 'dp', split_axis=0, concat_axis=0, tiled=True)  28 us
    pallas_call x1, Pallas kernels, owner_grads(): pl.pallas_call(functools.partial(owner_grads_kernel, group), out_shape=(j...  15.8 us
    all_to_all x3, starting transfers between devices, exchange(): return lax.all_to_all(x, 'dp', split_axis=0, concat_axis=0, tiled=True)  15.6 us
    unnamed x32, local copies, waits for them, and re-layouts  13.7 us
    pallas_call x1, Pallas kernels, owner_stats(): pl.pallas_call(functools.partial(owner_stats_kernel, group), out_shape=ja...  12.9 us
    all_to_all x1, starting transfers between devices, local(): lax.all_to_all(summed.reshape(peers * cores, share, -1), ('dp', 'tensor')...  7.46 us
  transfers between devices with their start and end apart: 7, of which 5 were waited for; matrix products, arithmetic and copies ran while one was open for 1% of the time, Pallas kernels for 17%

profile of v1, /device:TPU:1, one launch (start us, length us, event | category | flops | bytes accessed | tf_op | source)
XLA Modules:
  0.0 244.2 jit_solution(8577499200775237274)
XLA Ops:
  7.2 0.0 copy-start
  7.2 0.0 all-gather.5.cloned.1.call-start
  7.2 0.7 all-gather.5.cloned.1.call-update
  7.9 0.0 copy-start.3
  7.9 1.0 copy-done.3
  9.0 1.0 copy-done.5
  10.0 0.7 copy-done.12
  10.7 6.6 %pack_queries.1 = bf16[16,64,2048]{2,1,0:T(8,128)(2,1)S(1)} custom-call(s32[16,16]{1,0:T(8,128)S(1)} %bitcast.25, s32[1]{0:T(128)} %bitcast.2.me, bf16[4,32,2048]{2,1,0:T(8,128)(2,1)S(1)} %copy-done.3, bf16[4,32,2048]{2,1,0:T(8,128)(2,1)S(1)} %copy-done.5), custom_call_target="tpu_custom_call" | custom-call | bytes 6291456 | tf_op jit(solution)/shard_map/pack_queries/pallas_call | solution.py:66
  17.3 2.0 copy-done.1
  19.3 7.8 %all-to-all-start = ((bf16[16,64,2048]{2,1,0:T(8,128)(2,1)}), bf16[16,64,2048]{2,1,0:T(8,128)(2,1)}, u32[]{:S(2)}, u32[]{:S(2)}) async-start(bf16[16,64,2048]{2,1,0:T(8,128)(2,1)} %copy-done.1), calls=%async_computation | async-start | bytes 8388608 | tf_op jit(solution)/shard_map/all_to_all | solution.py:460
  27.1 0.0 all-gather.3.cloned.1.call-start
  27.2 0.7 all-gather.3.cloned.1.call-update
  27.9 0.2 dynamic-slice_reduce_fusion.blocks
  28.1 0.0 copy-done.13
  28.1 0.1 fusion.2.slot_of
  28.2 0.2 fusion.6
  28.4 0.7 fusion.5
  29.1 0.1 copy_bitcast_fusion
  29.2 0.0 copy-start.4
  29.2 0.0 copy-start.6
  29.2 60.2 %all-to-all-done.got_ref = bf16[16,64,2048]{2,1,0:T(8,128)(2,1)} async-done(((bf16[16,64,2048]{2,1,0:T(8,128)(2,1)}), bf16[16,64,2048]{2,1,0:T(8,128)(2,1)}, u32[]{:S(2)}, u32[]{:S(2)}) %all-to-all-start) | async-done | bytes 4194336 | tf_op jit(solution)/shard_map/all_to_all | solution.py:460
  89.5 12.9 %owner_stats.1 = f32[16,4,256]{2,1,0:T(4,128)} custom-call(s32[16]{0:T(128)S(1)} %fusion.2.slot_of, s32[2]{0:T(128)S(1)} %dynamic-slice_reduce_fusion.blocks, bf16[16,64,2048]{2,1,0:T(8,128)(2,1)} %all-to-all-done.got_ref, bf16[2,256,256]{2,1,0:T(8,128)(2,1)S(1)} %get-tuple-element.21.k_ref, bf16[2,256,256]{2,1,0:T(8,128)(2,1)S(1)} %get-tuple-element.20.v_ref), custom_call_target="tpu_custom_call" | custom-call | flops 2000000000 | bytes 5242880 | tf_op jit(solution)/shard_map/owner_stats/pallas_call | solution.py:112
  102.3 4.3 %all-to-all-start.1 = ((f32[16,4,256]{2,1,0:T(4,128)}), f32[16,4,256]{2,1,0:T(4,128)S(1)}, u32[]{:S(2)}, u32[]{:S(2)}) async-start(f32[16,4,256]{2,1,0:T(4,128)} %owner_stats.1), calls=%async_computation.1 | async-start | bytes 131072 | tf_op jit(solution)/shard_map/all_to_all | solution.py:460
  106.7 0.5 own_stats.1.own_ref
  107.2 6.0 %all-to-all-done.1.st_ref = f32[16,4,256]{2,1,0:T(4,128)S(1)} async-done(((f32[16,4,256]{2,1,0:T(4,128)}), f32[16,4,256]{2,1,0:T(4,128)S(1)}, u32[]{:S(2)}, u32[]{:S(2)}) %all-to-all-start.1) | async-done | bytes 65568 | tf_op jit(solution)/shard_map/all_to_all | solution.py:460
  113.2 1.4 merge_stats.1
  114.6 3.5 %all-to-all-start.2 = ((f32[16,4,256]{2,1,0:T(4,128)}), f32[16,4,256]{2,1,0:T(4,128)S(1)}, u32[]{:S(2)}, u32[]{:S(2)}) async-start(f32[16,4,256]{2,1,0:T(4,128)} %get-tuple-element.10), calls=%async_computation.2 | async-start | bytes 131072 | tf_op jit(solution)/shard_map/all_to_all | solution.py:460
  118.1 0.0 reduce-scatter.2.cloned.1.call-start
  118.2 1.9 own_grads.1
  120.0 1.0 copy-done.10
  121.1 3.5 %all-to-all-done.2.joint_ref = f32[16,4,256]{2,1,0:T(4,128)S(1)} async-done(((f32[16,4,256]{2,1,0:T(4,128)}), f32[16,4,256]{2,1,0:T(4,128)S(1)}, u32[]{:S(2)}, u32[]{:S(2)}) %all-to-all-start.2) | async-done | bytes 65568 | tf_op jit(solution)/shard_map/all_to_all | solution.py:460
  124.6 15.8 %owner_grads.1 = (bf16[512,512]{1,0:T(8,128)(2,1)S(1)}, bf16[16,32,2048]{2,1,0:T(8,128)(2,1)S(1)}) custom-call(s32[16]{0:T(128)S(1)} %fusion.2.slot_of, s32[2]{0:T(128)S(1)} %dynamic-slice_reduce_fusion.blocks, bf16[16,64,2048]{2,1,0:T(8,128)(2,1)} %all-to-all-done.got_ref, f32[16,4,256]{2,1,0:T(4,128)S(1)} %all-to-all-done.2.joint_ref, ...), custom_call_target="tpu_custom_call" | custom-call | flops 5000000000 | bytes 8388608 | tf_op jit(solution)/shard_map/owner_grads/pallas_call | solution.py:251
  140.4 1.3 copy-done.8
  141.7 2.2 copy-done.7
  143.9 1.2 copy-done.9
  145.1 4.8 %transpose_hidden.1.h_ref = bf16[4096,640]{1,0:T(8,128)(2,1)} custom-call(bf16[512,4096]{1,0:T(8,128)(2,1)S(1)} %bitcast.22, bf16[128,4096]{1,0:T(8,128)(2,1)S(1)} %bitcast.24), custom_call_target="tpu_custom_call" | custom-call | bytes 12582912 | tf_op jit(solution)/shard_map/transpose_hidden/pallas_call | solution.py:366
  149.9 7.4 %weight_terms.1 = bf16[8,16,32,512]{3,2,1,0:T(8,128)(2,1)S(1)} custom-call(bf16[4096,640]{1,0:T(8,128)(2,1)} %transpose_hidden.1.h_ref, bf16[512,512]{1,0:T(8,128)(2,1)S(1)} %get-tuple-element.15.p_ref, bf16[128,512]{1,0:T(8,128)(2,1)S(1)} %get-tuple-element.14.q_ref), custom_call_target="tpu_custom_call" | custom-call | flops 2684354560 | bytes 10485760 | tf_op jit(solution)/shard_map/weight_terms/pallas_call | solution.py:398
  157.4 2.0 copy-done.2
  159.4 0.0 reduce-scatter.2.cloned.1.call-update
  159.4 28.0 %all_to_all.25.refs_0_.refs_1_.refs_2_.refs_3_ = bf16[16,32,2048]{2,1,0:T(8,128)(2,1)S(1)} all-to-all(bf16[16,32,2048]{2,1,0:T(8,128)(2,1)} %copy-done.8), channel_id=1, replica_groups=mesh['dp'=16,'pass'=8,'tensor'=2] {'dp'}, dimensions={0} | all-to-all | bytes 4194304 | tf_op jit(solution)/shard_map/all_to_all | solution.py:460
  187.4 30.5 %reduce-scatter.2.cloned.1.call-done = bf16[1,16,32,512]{3,2,1,0:T(8,128)(2,1)} async-done(((bf16[8,16,32,512]{3,2,1,0:T(8,128)(2,1)}), bf16[1,16,32,512]{3,2,1,0:T(8,128)(2,1)}) %reduce-scatter.2.cloned.1.call-update) | async-done | bytes 524304 | tf_op jit(solution)/shard_map/reduce_scatter | solution.py:488
  217.9 7.5 %all-to-all-start.4 = ((bf16[32,16,512]{2,1,0:T(8,128)(2,1)}), bf16[32,16,512]{2,1,0:T(8,128)(2,1)S(1)}, u32[]{:S(2)}, u32[]{:S(2)}) async-start(bf16[32,16,512]{2,1,0:T(8,128)(2,1)} %bitcast.28), calls=%async_computation.5 | async-start | bytes 1048576 | tf_op jit(solution)/shard_map/all_to_all | solution.py:492
  225.4 0.7 reshape.38
  226.1 0.9 reshape.39
  227.0 1.2 copy-done.11
  228.3 2.1 sum_dq.1
  230.4 6.6 %all-to-all-done.4 = bf16[32,16,512]{2,1,0:T(8,128)(2,1)S(1)} async-done(((bf16[32,16,512]{2,1,0:T(8,128)(2,1)}), bf16[32,16,512]{2,1,0:T(8,128)(2,1)S(1)}, u32[]{:S(2)}, u32[]{:S(2)}) %all-to-all-start.4) | async-done | bytes 524320 | tf_op jit(solution)/shard_map/all_to_all | solution.py:492
  236.9 0.7 finish_weights.1
  (21 shorter events, 0.1 us)
Async XLA Ops:
  7.2 20.7 %copy-start = (s32[16,1,2]{0,2,1:T(2,128)S(1)}, s32[16,1,2]{0,2,1:T(2,128)}, u32[]{:S(2)}) copy-start(s32[16,1,2]{0,2,1:T(2,128)} %param.15) | copy-start | bytes 388
  7.2 134.5 %all-gather.5.cloned.1.call-start = ((), (), s32[]{:S(2)}) async-start(), calls=%async_computation.7 | async-start | bytes 1572864 | tf_op jit(solution)/shard_map/all_gather | solution.py:473
  7.9 1.0 copy-start.3
  9.0 1.0 copy-start.5
  10.0 0.7 copy-start.12
  17.3 2.0 copy-start.1
  19.3 8.7 %copy-start.13 = (s32[16,1,16]{2,1,0:T(1,128)S(1)}, s32[16,1,16]{2,1,0:T(1,128)}, u32[]{:S(2)}) copy-start(s32[16,1,16]{2,1,0:T(1,128)} %param.14) | copy-start | bytes 3076
  19.3 8.9 %copy-start.15 = (bf16[4,32,2,256]{3,2,1,0:T(2,128)(2,1)S(1)}, bf16[4,32,2,256]{3,2,1,0:T(2,128)(2,1)}, u32[]{:S(2)}) copy-start(bf16[4,32,2,256]{3,2,1,0:T(2,128)(2,1)} %param.10) | copy-start | bytes 393220
  19.3 9.1 %copy-start.14 = (bf16[2,256,2,256]{3,2,1,0:T(2,128)(2,1)S(1)}, bf16[2,256,2,256]{3,2,1,0:T(2,128)(2,1)}, u32[]{:S(2)}) copy-start(bf16[2,256,2,256]{3,2,1,0:T(2,128)(2,1)} %param.11) | copy-start | bytes 1572868
  19.3 70.1 %all-to-all-start = ((bf16[16,64,2048]{2,1,0:T(8,128)(2,1)}), bf16[16,64,2048]{2,1,0:T(8,128)(2,1)}, u32[]{:S(2)}, u32[]{:S(2)}) async-start(bf16[16,64,2048]{2,1,0:T(8,128)(2,1)} %copy-done.1), calls=%async_computation | async-start | bytes 8388608 | tf_op jit(solution)/shard_map/all_to_all | solution.py:460
  27.1 114.6 %all-gather.3.cloned.1.call-start = ((), (), s32[]{:S(2)}) async-start(), calls=%async_computation.6 | async-start | bytes 6291456 | tf_op jit(solution)/shard_map/all_gather | solution.py:472
  29.2 77.5 %copy-start.4 = (bf16[4,32,2048]{2,1,0:T(8,128)(2,1)S(1)}, bf16[4,32,2048]{2,1,0:T(8,128)(2,1)}, u32[]{:S(2)}) copy-start(bf16[4,32,2048]{2,1,0:T(8,128)(2,1)} %q_ref.5) | copy-start | bytes 1572868
  29.2 77.5 %copy-start.6 = (bf16[4,32,2048]{2,1,0:T(8,128)(2,1)S(1)}, bf16[4,32,2048]{2,1,0:T(8,128)(2,1)}, u32[]{:S(2)}) copy-start(bf16[4,32,2048]{2,1,0:T(8,128)(2,1)} %g_ref.5) | copy-start | bytes 1572868
  102.3 10.8 %all-to-all-start.1 = ((f32[16,4,256]{2,1,0:T(4,128)}), f32[16,4,256]{2,1,0:T(4,128)S(1)}, u32[]{:S(2)}, u32[]{:S(2)}) async-start(f32[16,4,256]{2,1,0:T(4,128)} %owner_stats.1), calls=%async_computation.1 | async-start | bytes 131072 | tf_op jit(solution)/shard_map/all_to_all | solution.py:460
  114.6 10.0 %all-to-all-start.2 = ((f32[16,4,256]{2,1,0:T(4,128)}), f32[16,4,256]{2,1,0:T(4,128)S(1)}, u32[]{:S(2)}, u32[]{:S(2)}) async-start(f32[16,4,256]{2,1,0:T(4,128)} %get-tuple-element.10), calls=%async_computation.2 | async-start | bytes 131072 | tf_op jit(solution)/shard_map/all_to_all | solution.py:460
  118.1 99.8 %reduce-scatter.2.cloned.1.call-start = ((), (), s32[]{:S(2)}) async-start(), calls=%async_computation.8 | async-start | bytes 4718592 | tf_op jit(solution)/shard_map/reduce_scatter | solution.py:488
  120.0 1.0 copy-start.10
  140.4 1.3 copy-start.8
  141.7 2.2 copy-start.7
  143.9 1.2 copy-start.9
  157.4 2.0 copy-start.2
  217.9 19.0 %all-to-all-start.4 = ((bf16[32,16,512]{2,1,0:T(8,128)(2,1)}), bf16[32,16,512]{2,1,0:T(8,128)(2,1)S(1)}, u32[]{:S(2)}, u32[]{:S(2)}) async-start(bf16[32,16,512]{2,1,0:T(8,128)(2,1)} %bitcast.28), calls=%async_computation.5 | async-start | bytes 1048576 | tf_op jit(solution)/shard_map/all_to_all | solution.py:492
  227.0 1.2 copy-start.11
Sparse Core Ops, SparseCore 0:
  9.8 18.8 all-gather.4
  30.5 22.3 all-gather.2
  159.5 58.3 reduce-scatter.1

commit v2 on v1

v2 whole, which is shorter than its diff:
```python
import functools
import math

import jax
import jax.numpy as jnp
from jax import lax
from jax.experimental import pallas as pl
from jax.experimental.pallas import tpu as pltpu
from jax.sharding import PartitionSpec as P

HD = 128
BLOCK = 128
NEG_FILL = -1e30
SCALE = HD ** (-0.5)
SCALE_LOG2 = SCALE * math.log2(math.e)
VMEM_LIMIT = 48 * 1024 * 1024
NT = (((1,), (1,)), ((), ()))
TN = (((0,), (0,)), ((), ()))
F32 = jnp.float32
BF16 = jnp.bfloat16


def params():
    return pltpu.CompilerParams(vmem_limit_bytes=VMEM_LIMIT)


def whole():
    return pl.BlockSpec(memory_space=pltpu.VMEM)


def smem():
    return pl.BlockSpec(memory_space=pltpu.SMEM)


def anywhere():
    return pl.BlockSpec(memory_space=pl.ANY)


def cost(flops, nbytes, trans=0):
    return pl.CostEstimate(flops=flops, bytes_accessed=nbytes, transcendentals=trans)


def quotient(value, divisor):
    return lax.div(value, jnp.int32(divisor))


def head_rows(block, head, group):
    first = head * group
    return jnp.concatenate(
        [block[:, (first + r) * HD : (first + r + 1) * HD] for r in range(group)], axis=0
    )


def pack_kernel(slots, refs, me, q_ref, g_ref, out_ref, held, load_sems, sems):
    peers = out_ref.shape[0]
    samples, rows, _ = q_ref.shape
    per = peers // samples
    loads = []
    for sample in range(samples):
        pair = []
        for part, src in enumerate((q_ref, g_ref)):
            pair.append(
                pltpu.make_async_copy(
                    src.at[sample],
                    held.at[sample, pl.ds(part * rows, rows)],
                    load_sems.at[sample, part],
                )
            )
            pair[-1].start()
        loads.append(pair)
    copies = []
    for j in range(peers):
        sample = j // per
        if j % per == 0:
            for copy in loads[sample]:
                copy.wait()
        dest = quotient(refs[me[0], j], slots)
        copy = pltpu.make_async_copy(held.at[sample], out_ref.at[dest], sems.at[j])
        copy.start()
        copies.append(copy)
    for copy in copies:
        copy.wait()


def pack_queries(refs, me, question_q, question_grad, slots):
    samples, rows, width = question_q.shape
    peers = refs.shape[0]
    return pl.pallas_call(
        functools.partial(pack_kernel, slots),
        out_shape=jax.ShapeDtypeStruct((peers, 2 * rows, width), BF16),
        in_specs=[smem(), smem(), anywhere(), anywhere()],
        out_specs=anywhere(),
        scratch_shapes=[
            pltpu.VMEM((samples, 2 * rows, width), BF16),
            pltpu.SemaphoreType.DMA((samples, 2)),
            pltpu.SemaphoreType.DMA((peers,)),
        ],
        compiler_params=params(),
        cost_estimate=cost(0, 6 * 2**20),
        name="pack_queries",
    )(refs, me, question_q, question_grad)


def scores_t(keys, queries, valid):
    scores = lax.dot_general(keys, queries, NT, preferred_element_type=F32) * SCALE_LOG2
    return jnp.where(valid, scores, NEG_FILL)


def part_stats(scores, prob_grad):
    top = jnp.max(scores, axis=0, keepdims=True)
    shifted = jnp.exp2(scores - top)
    total = jnp.sum(shifted, axis=0, keepdims=True)
    weighted = jnp.sum(shifted * prob_grad, axis=0, keepdims=True)
    return top + jnp.log2(total), weighted / total


def passage_valid(blocks, slot, slot_len, columns):
    shape = (slot_len, columns)
    return lax.broadcasted_iota(jnp.int32, shape, 0) < blocks[slot] * BLOCK


def owner_stats_kernel(group, slot_of, blocks, got_ref, k_ref, v_ref, own_ref, out_ref):
    step = pl.program_id(0)
    last = pl.num_programs(0) - 1
    per, both, _ = got_ref.shape
    rows = both // 2
    peers = out_ref.shape[0]
    slot_len = k_ref.shape[1]
    heads = k_ref.shape[2] // HD
    columns = group * rows

    @pl.when(step < last)
    def _():
        for one in range(per):
            slot = slot_of[step * per + one]
            valid = passage_valid(blocks, slot, slot_len, columns)
            logs, deltas = [], []
            for head in range(heads):
                lanes = slice(head * HD, (head + 1) * HD)
                queries = head_rows(got_ref[one, :rows], head, group)
                grads = head_rows(got_ref[one, rows:], head, group)
                scores = scores_t(k_ref[slot, :, lanes], queries, valid)
                prob_grad = lax.dot_general(
                    v_ref[slot, :, lanes], grads, NT, preferred_element_type=F32
                )
                log, delta = part_stats(scores, prob_grad)
                logs.append(log)
                deltas.append(delta)
            both_stats = jnp.concatenate(logs + deltas, axis=0)
            for peer in range(peers):
                out_ref[peer, one] = both_stats

    @pl.when(step == last)
    def _():
        for peer in range(peers):
            out_ref[peer] = own_ref[...]


def owner_stats(slot_of, blocks, got, keys, values, own, group):
    peers, both, width = got.shape
    samples, stat_rows, columns = own.shape
    steps = peers // samples
    return pl.pallas_call(
        functools.partial(owner_stats_kernel, group),
        out_shape=jax.ShapeDtypeStruct((peers, peers + samples, stat_rows, columns), F32),
        grid_spec=pltpu.PrefetchScalarGridSpec(
            num_scalar_prefetch=2,
            grid=(steps + 1,),
            in_specs=[
                pl.BlockSpec(
                    (samples, both, width), lambda r, s, b: (jnp.minimum(r, steps - 1), 0, 0)
                ),
                whole(),
                whole(),
                whole(),
            ],
            out_specs=pl.BlockSpec(
                (peers, samples, stat_rows, columns), lambda r, s, b: (0, r, 0, 0)
            ),
        ),
        compiler_params=params(),
        cost_estimate=cost(2 * 10**9, 6 * 2**20, 2 * 10**6),
        name="owner_stats",
    )(slot_of, blocks, got, keys, values, own)


def own_valid(own_rows, rows, group):
    shape = (own_rows, group * rows)
    key_row = lax.broadcasted_iota(jnp.int32, shape, 0)
    query_row = lax.rem(lax.broadcasted_iota(jnp.int32, shape, 1), jnp.int32(rows))
    return key_row <= query_row


def own_stats_kernel(group, q_ref, g_ref, k_ref, v_ref, out_ref):
    samples, rows, _ = q_ref.shape
    heads = k_ref.shape[2] // HD
    valid = own_valid(rows, rows, group)
    for sample in range(samples):
        logs, deltas = [], []
        for head in range(heads):
            lanes = slice(head * HD, (head + 1) * HD)
            queries = head_rows(q_ref[sample], head, group)
            grads = head_rows(g_ref[sample], head, group)
            scores = scores_t(k_ref[sample, :, lanes], queries, valid)
            prob_grad = lax.dot_general(
                v_ref[sample, :, lanes], grads, NT, preferred_element_type=F32
            )
            log, delta = part_stats(scores, prob_grad)
            logs.append(log)
            deltas.append(delta)
        out_ref[sample] = jnp.concatenate(logs + deltas, axis=0)


def own_stats(question_q, question_grad, keys, values, group):
    samples, rows, _ = question_q.shape
    heads = keys.shape[2] // HD
    return pl.pallas_call(
        functools.partial(own_stats_kernel, group),
        out_shape=jax.ShapeDtypeStruct((samples, 2 * heads, group * rows), F32),
        in_specs=[whole()] * 4,
        out_specs=whole(),
        compiler_params=params(),
        cost_estimate=cost(10**8, 2**20, 10**5),
        name="own_stats",
    )(question_q, question_grad, keys, values)


def joint_stats(all_ref, refs, reader, sample, per, slots, head, heads):
    peers = all_ref.shape[0]
    parts = [all_ref[reader, peers + sample]]
    for k in range(per):
        parts.append(all_ref[quotient(refs[reader, sample * per + k], slots), reader])
    logs = [part[head : head + 1] for part in parts]
    deltas = [part[heads + head : heads + head + 1] for part in parts]
    top = functools.reduce(jnp.maximum, logs)
    weights = [jnp.exp2(log - top) for log in logs]
    total = sum(weights)
    delta = sum(weight * one for weight, one in zip(weights, deltas)) / total
    return top + jnp.log2(total), delta


def probs_and_dscore(scores, prob_grad, joint, delta):
    probs = jnp.exp2(scores - joint)
    dscore = (probs * (prob_grad - delta) * SCALE).astype(BF16)
    return probs.astype(BF16), dscore


def owner_grads_kernel(
    group,
    slots,
    head,
    slot_of,
    blocks,
    refs,
    entry_of,
    got_ref,
    all_ref,
    k_ref,
    v_ref,
    grad_ref,
    dq_ref,
    acc_ref,
):
    step = pl.program_id(0)
    per, both, _ = got_ref.shape
    rows = both // 2
    slot_len = k_ref.shape[1]
    heads = k_ref.shape[2] // HD
    peers = all_ref.shape[0]
    entries = peers // (all_ref.shape[1] - peers)
    lanes = slice(head * HD, (head + 1) * HD)

    @pl.when(step == 0)
    def _():
        acc_ref[...] = jnp.zeros_like(acc_ref)

    for one in range(per):
        reader = step * per + one
        slot = slot_of[reader]
        sample = quotient(entry_of[reader], entries)
        joint, delta = joint_stats(all_ref, refs, reader, sample, entries, slots, head, heads)
        valid = passage_valid(blocks, slot, slot_len, group * rows)
        queries = head_rows(got_ref[one, :rows], 0, group)
        grads = head_rows(got_ref[one, rows:], 0, group)
        keys = k_ref[slot, :, lanes]
        scores = scores_t(keys, queries, valid)
        prob_grad = lax.dot_general(v_ref[slot, :, lanes], grads, NT, preferred_element_type=F32)
        probs, dscore = probs_and_dscore(scores, prob_grad, joint, delta)
        acc_ref[slot, :, :HD] += jnp.dot(dscore, queries, preferred_element_type=F32)
        acc_ref[slot, :, HD:] += jnp.dot(probs, grads, preferred_element_type=F32)
        dq = lax.dot_general(dscore, keys, TN, preferred_element_type=F32).astype(BF16)
        for r in range(group):
            dq_ref[one, :, r * HD : (r + 1) * HD] = dq[r * rows : (r + 1) * rows]

    @pl.when(step == pl.num_programs(0) - 1)
    def _():
        for one in range(acc_ref.shape[0]):
            grad_ref[one * slot_len : (one + 1) * slot_len] = acc_ref[one].astype(BF16)


def owner_grads(head, slot_of, blocks, refs, entry_of, got, stats, keys, values, group):
    peers, both, _ = got.shape
    slots, slot_len, _ = keys.shape
    per = stats.shape[1] - peers
    width = group * HD
    return pl.pallas_call(
        functools.partial(owner_grads_kernel, group, slots, head),
        out_shape=(
            jax.ShapeDtypeStruct((slots * slot_len, 2 * HD), BF16),
            jax.ShapeDtypeStruct((peers, both // 2, width), BF16),
        ),
        grid_spec=pltpu.PrefetchScalarGridSpec(
            num_scalar_prefetch=4,
            grid=(peers // per,),
            in_specs=[
                pl.BlockSpec((per, both, width), lambda r, *_: (r, 0, head)),
                whole(),
                whole(),
                whole(),
            ],
            out_specs=(
                pl.BlockSpec((slots * slot_len, 2 * HD), lambda r, *_: (0, 0)),
                pl.BlockSpec((per, both // 2, width), lambda r, *_: (r, 0, 0)),
            ),
            scratch_shapes=[pltpu.VMEM((slots, slot_len, 2 * HD), F32)],
        ),
        compiler_params=params(),
        cost_estimate=cost(5 * 10**9, 8 * 2**20, 2 * 10**6),
        name=f"owner_grads_{head}",
    )(slot_of, blocks, refs, entry_of, got, stats, keys, values)


def own_grads_kernel(
    group, slots, refs, me, q_ref, g_ref, k_ref, v_ref, all_ref, grad_ref, dq_ref
):
    samples, rows, _ = q_ref.shape
    heads = k_ref.shape[2] // HD
    entries = all_ref.shape[0] // samples
    valid = own_valid(rows, rows, group)
    for sample in range(samples):
        token = slice(sample * rows, (sample + 1) * rows)
        for head in range(heads):
            lanes = slice(head * HD, (head + 1) * HD)
            joint, delta = joint_stats(all_ref, refs, me[0], sample, entries, slots, head, heads)
            queries = head_rows(q_ref[sample], head, group)
            grads = head_rows(g_ref[sample], head, group)
            keys = k_ref[sample, :, lanes]
            scores = scores_t(keys, queries, valid)
            prob_grad = lax.dot_general(
                v_ref[sample, :, lanes], grads, NT, preferred_element_type=F32
            )
            probs, dscore = probs_and_dscore(scores, prob_grad, joint, delta)
            key_grad = jnp.dot(dscore, queries, preferred_element_type=F32)
            value_grad = jnp.dot(probs, grads, preferred_element_type=F32)
            grad_ref[head, token, :HD] = key_grad.astype(BF16)
            grad_ref[head, token, HD:] = value_grad.astype(BF16)
            dq = lax.dot_general(dscore, keys, TN, preferred_element_type=F32)
            for r in range(group):
                column = (head * group + r) * HD
                dq_ref[sample, :, column : column + HD] = dq[r * rows : (r + 1) * rows]


def own_grads(refs, me, question_q, question_grad, keys, values, stats, group, slots):
    samples, rows, width = question_q.shape
    heads = keys.shape[2] // HD
    return pl.pallas_call(
        functools.partial(own_grads_kernel, group, slots),
        out_shape=(
            jax.ShapeDtypeStruct((heads, samples * rows, 2 * HD), BF16),
            jax.ShapeDtypeStruct((samples, rows, width), F32),
        ),
        in_specs=[smem(), smem()] + [whole()] * 5,
        out_specs=(whole(), whole()),
        compiler_params=params(),
        cost_estimate=cost(3 * 10**8, 3 * 2**20, 10**5),
        name="own_grads",
    )(refs, me, question_q, question_grad, keys, values, stats)


def sum_dq_kernel(heads, owners, *refs):
    out_ref = refs[-1]
    own_ref = refs[-2]
    per = (len(refs) - 2) // heads
    width = refs[0].shape[2]
    for head in range(heads):
        lanes = slice(head * width, (head + 1) * width)
        total = own_ref[0, :, lanes]
        for ref in refs[head * per : (head + 1) * per]:
            total = total + ref[0].astype(F32)
        out_ref[0, :, lanes] = total.astype(BF16)


def sum_dq(owners, returned, own):
    samples, rows, width = own.shape
    per = owners.shape[0] // samples
    heads = len(returned)

    def from_owner(k):
        return pl.BlockSpec((1, rows, width // heads), lambda s, o: (o[s * per + k], 0, 0))

    return pl.pallas_call(
        functools.partial(sum_dq_kernel, heads),
        out_shape=jax.ShapeDtypeStruct((samples, rows, width), BF16),
        grid_spec=pltpu.PrefetchScalarGridSpec(
            num_scalar_prefetch=1,
            grid=(samples,),
            in_specs=[from_owner(k) for k in range(per)] * heads
            + [pl.BlockSpec((1, rows, width), lambda s, o: (s, 0, 0))],
            out_specs=pl.BlockSpec((1, rows, width), lambda s, o: (s, 0, 0)),
        ),
        compiler_params=params(),
        cost_estimate=cost(2 * 10**6, 4 * 2**20),
        name="sum_dq",
    )(owners, *[one for one in returned for _ in range(per)], own)


def transpose_kernel(slots, samples, owners, core, mine_p, other_p, mine_q, other_q, out_ref):
    groups, share, _ = out_ref.shape
    lower = core[0] == 0
    first_p = jnp.where(lower, mine_p[...], other_p[...])
    second_p = jnp.where(lower, other_p[...], mine_p[...])
    first_q = jnp.where(lower, mine_q[...], other_q[...])
    second_q = jnp.where(lower, other_q[...], mine_q[...])
    half = first_p.shape[0] // slots
    part = first_q.shape[0] // samples
    pieces = []
    for slot in range(slots):
        pieces.append(first_p[slot * half : (slot + 1) * half])
        pieces.append(second_p[slot * half : (slot + 1) * half])
    for sample in range(samples):
        pieces.append(first_q[sample * part : (sample + 1) * part])
        pieces.append(second_q[sample * part : (sample + 1) * part])
    turned = jnp.concatenate(pieces, axis=0).T
    rows = share // owners
    for owner in range(owners):
        for group in range(groups):
            first = (owner * groups + group) * rows
            out_ref[group, owner * rows : (owner + 1) * rows] = turned[first : first + rows]


def transpose_hidden(core, mine_p, other_p, mine_q, other_q, slots, samples, owners, groups):
    width = mine_p.shape[1]
    tokens = 2 * (mine_p.shape[0] + mine_q.shape[0])
    per = 2
    tile = per * width // owners
    return pl.pallas_call(
        functools.partial(transpose_kernel, slots, samples, per),
        out_shape=jax.ShapeDtypeStruct((groups, width // groups, tokens), BF16),
        grid_spec=pltpu.PrefetchScalarGridSpec(
            num_scalar_prefetch=1,
            grid=(width // tile,),
            in_specs=[
                pl.BlockSpec((one.shape[0], tile), lambda i, c: (0, i))
                for one in (mine_p, other_p, mine_q, other_q)
            ],
            out_specs=pl.BlockSpec((groups, tile // groups, tokens), lambda i, c: (0, i, 0)),
        ),
        compiler_params=params(),
        cost_estimate=cost(0, 12 * 2**20),
        name="transpose_hidden",
    )(core, mine_p, other_p, mine_q, other_q)


def weight_kernel(h_ref, p_ref, q_ref, out_ref):
    split = p_ref.shape[0]
    for one in range(h_ref.shape[0]):
        total = jnp.dot(h_ref[one, :, :split], p_ref[...], preferred_element_type=F32)
        total = total + jnp.dot(h_ref[one, :, split:], q_ref[...], preferred_element_type=F32)
        out_ref[one] = total.astype(BF16)


def weight_terms(hidden_t, grads_pass, grads_query, head):
    groups, share, tokens = hidden_t.shape
    width = grads_pass.shape[1]
    per = 2
    return pl.pallas_call(
        weight_kernel,
        out_shape=jax.ShapeDtypeStruct((groups, share, width), BF16),
        grid=(groups // per,),
        in_specs=[
            pl.BlockSpec((per, share, tokens), lambda i: (i, 0, 0)),
            whole(),
            whole(),
        ],
        out_specs=pl.BlockSpec((per, share, width), lambda i: (i, 0, 0)),
        compiler_params=params(),
        cost_estimate=cost(2 * groups * share * tokens * width, 8 * 2**20),
        name=f"weight_terms_{head}",
    )(hidden_t, grads_pass, grads_query)


def add_low(one, other):
    return (one.astype(F32) + other.astype(F32)).astype(BF16)


def reduce_over_pass(sets):
    me = lax.axis_index("pass")
    count = lax.axis_size("pass")
    right = [(i, (i + 1) % count) for i in range(count)]
    left = [(i, (i - 1) % count) for i in range(count)]
    far = count // 2

    def pick(one, distance):
        return lax.dynamic_index_in_dim(one, lax.rem(me + distance + count, count), 0, False)

    ahead = [pick(one, far) for one in sets]
    behind = [pick(one, 1 - far) for one in sets]
    for distance in range(far - 1, -1, -1):
        for i, one in enumerate(sets):
            ahead[i] = lax.ppermute(ahead[i], "pass", right)
            if distance:
                ahead[i] = add_low(ahead[i], pick(one, distance))
            if distance < far - 1:
                behind[i] = lax.ppermute(behind[i], "pass", left)
                if distance:
                    behind[i] = add_low(behind[i], pick(one, -distance))
    return [
        (a.astype(F32) + b.astype(F32) + pick(one, 0).astype(F32)).astype(BF16)
        for a, b, one in zip(ahead, behind, sets)
    ]


def finish_kernel(heads, x_ref, out_ref):
    owners, cores, _, _ = x_ref.shape
    for core in range(cores):
        total = x_ref[0, core].astype(F32)
        for owner in range(1, owners):
            total = total + x_ref[owner, core].astype(F32)
        for head in range(heads):
            lanes = slice((core * heads + head) * HD, (core * heads + head + 1) * HD)
            for part in range(2):
                first = (head * 2 + part) * HD
                out_ref[:, part, lanes] = total[:, first : first + HD]


def finish_weights(parts):
    owners, cores, rows, width = parts.shape
    return pl.pallas_call(
        functools.partial(finish_kernel, width // (2 * HD)),
        out_shape=jax.ShapeDtypeStruct((rows, 2, cores * width // 2), F32),
        in_specs=[whole()],
        out_specs=whole(),
        compiler_params=params(),
        cost_estimate=cost(10**6, 2**20),
        name="finish_weights",
    )(parts)


def local(
    question_q,
    question_grad,
    question_kv,
    passage_kv,
    question_hidden,
    passage_hidden,
    reuse,
    passage_blocks,
):
    me = lax.axis_index("dp")
    me_array = me.reshape(1)
    peers = lax.axis_size("dp")
    groups = lax.axis_size("pass")
    cores = lax.axis_size("tensor")
    slots, slot_len, _, channels = passage_kv.shape
    samples, rows, width = question_q.shape
    heads = channels // HD
    group = width // channels
    refs = reuse.reshape(reuse.shape[0], reuse.shape[2])
    model_width = passage_hidden.shape[2]

    def exchange(x):
        return lax.all_to_all(x, "dp", split_axis=0, concat_axis=0, tiled=True)

    def from_partner(x):
        return lax.ppermute(x, "tensor", [(i, cores - 1 - i) for i in range(cores)])

    packed = pack_queries(refs, me_array, question_q, question_grad, slots)
    got = exchange(packed)

    hit = quotient(refs, slots) == me
    slot_of = jnp.sum(jnp.where(hit, lax.rem(refs, jnp.int32(slots)), 0), axis=1)
    order = jnp.arange(refs.shape[1], dtype=jnp.int32)
    entry_of = jnp.sum(jnp.where(hit, order[None, :], 0), axis=1)
    owners = quotient(lax.dynamic_index_in_dim(refs, me, 0, keepdims=False), slots)
    blocks = lax.dynamic_index_in_dim(passage_blocks, me, 0, keepdims=False).reshape(slots)
    keys, values = passage_kv[:, :, 0], passage_kv[:, :, 1]
    own_keys, own_values = question_kv[:, :, 0], question_kv[:, :, 1]
    own = own_stats(question_q, question_grad, own_keys, own_values, group)
    hidden_t = transpose_hidden(
        lax.axis_index("tensor").reshape(1),
        passage_hidden.reshape(-1, model_width),
        from_partner(passage_hidden).reshape(-1, model_width),
        question_hidden.reshape(-1, model_width),
        from_partner(question_hidden).reshape(-1, model_width),
        slots,
        samples,
        peers,
        groups,
    )
    got, hidden_t, own, keys, values = lax.optimization_barrier(
        (got, hidden_t, own, keys, values)
    )

    stats = exchange(owner_stats(slot_of, blocks, got, keys, values, own, group))
    grads_query, own_dq = own_grads(
        refs, me_array, question_q, question_grad, own_keys, own_values, stats, group, slots
    )
    grads_pass, dq_parts, terms = [], [], []
    for head in range(heads):
        one, dq = owner_grads(
            head, slot_of, blocks, refs, entry_of, got, stats, keys, values, group
        )
        grads_pass.append(one)
        dq_parts.append(dq)
        terms.append(weight_terms(hidden_t, one, grads_query[head], head))
    summed = jnp.concatenate(reduce_over_pass(terms), axis=-1)
    returned = exchange(jnp.concatenate(dq_parts, axis=-1))
    question_dq = sum_dq(owners, [returned], own_dq)

    share = summed.shape[0] // (peers * cores)
    parts = lax.all_to_all(
        summed.reshape(peers * cores, share, -1),
        ("dp", "tensor"),
        split_axis=0,
        concat_axis=0,
        tiled=True,
    )
    weight_grad = finish_weights(parts.reshape(peers, cores, share, -1))
    question_dkv = jnp.concatenate(
        [grads_query[head].reshape(samples, rows, 2, HD) for head in range(heads)], axis=-1
    )
    passage_dkv = jnp.concatenate(
        [one.reshape(slots, slot_len, 2, HD) for one in grads_pass], axis=-1
    )
    return (question_dq, question_dkv, passage_dkv, weight_grad)


def solution(mesh):
    in_specs = (
        P(("dp", "pass"), None, "tensor"),
        P(("dp", "pass"), None, "tensor"),
        P(("dp", "pass"), None, None, "tensor"),
        P(("dp", "pass"), None, None, "tensor"),
        P(("dp", "pass"), "tensor", None),
        P(("dp", "pass"), "tensor", None),
        P(None, "pass", None),
        P(None, "pass", None),
    )
    out_specs = (
        P(("dp", "pass"), None, "tensor"),
        P(("dp", "pass"), None, None, "tensor"),
        P(("dp", "pass"), None, None, "tensor"),
        P(("dp", "pass", "tensor"), None, None),
    )
    return jax.shard_map(local, mesh=mesh, in_specs=in_specs, out_specs=out_specs, check_vma=False)
```

time: 246 us -> 257 us (1.045)
  blocking collectives: 28 us -> 0 us
  starting transfers between devices: 23.2 us -> 47.4 us
  other arithmetic: 0.14 us -> 19.9 us
  between operations: 14 us -> 1.01 us
  waiting for transfers between devices: 108 us -> 118 us
  Pallas kernels: 54.2 us -> 45.9 us
  local copies, waits for them, and re-layouts: 16.5 us -> 24.1 us
    reduce_scatter x1 -> x0, waiting for transfers between devices: 30.5 us -> none  [local(): summed = lax.psum_scatter(terms, 'pass', scatter_dimension=0, tiled=False)]
    all_to_all x1 -> x0, blocking collectives: 28 us -> none  [exchange(): return lax.all_to_all(x, 'dp', split_axis=0, concat_axis=0, tiled=True)]
    all_to_all x3, waiting for transfers between devices: 69.7 us -> 95.3 us  [exchange(): return lax.all_to_all(x, 'dp', split_axis=0, concat_axis=0, tiled=True)]
    ppermute x0 -> x16, starting transfers between devices: none -> 18.8 us  [the longest x6 13.2 us: reduce_over_pass(): behind[i] = lax.ppermute(behind[i], 'pass', left)]
    convert_element_type x0 -> x8, other arithmetic: none -> 13.4 us  [the longest x6 11.1 us: add_low(): return (one.astype(F32) + other.astype(F32)).astype(BF16)]
    ppermute x0 -> x16, waiting for transfers between devices: none -> 13.3 us  [the longest x8 11.1 us: reduce_over_pass(): ahead[i] = lax.ppermute(ahead[i], 'pass', right)]
    pallas_call x1, Pallas kernels: 12.9 us -> 6.23 us  [owner_stats(): pl.pallas_call(functools.partial(owner_stats_kernel, group), out_shape=ja...]
    concatenate x0 -> x4, other arithmetic: none -> 5.73 us  [the longest x1 2.75 us: local(): returned = exchange(jnp.concatenate(dq_parts, axis=-1))]
  transfers between devices with their start and end apart: 7 -> 20, of which waited for: 5 -> 12; matrix products, arithmetic and copies ran while one was open for 1% -> 9% of each run, Pallas kernels for 17% -> 8%
where the time goes in v2:
time: 257 us; the launch traced here: 256 us
  waiting for transfers between devices  118 us (46%)
  starting transfers between devices  47.4 us (18%)
  Pallas kernels  45.9 us (18%)
  local copies, waits for them, and re-layouts  24.1 us (9%)
  other arithmetic  19.9 us (8%)
    all_to_all x3, waiting for transfers between devices, exchange(): return lax.all_to_all(x, 'dp', split_axis=0, concat_axis=0, tiled=True)  95.3 us
    unnamed x68, local copies, waits for them, and re-layouts  17.5 us
    all_to_all x3, starting transfers between devices, exchange(): return lax.all_to_all(x, 'dp', split_axis=0, concat_axis=0, tiled=True)  15.9 us
    pallas_call x2, Pallas kernels, owner_grads(): pl.pallas_call(functools.partial(owner_grads_kernel, group, slots, head),...  14.9 us
    ppermute x6, starting transfers between devices, reduce_over_pass(): behind[i] = lax.ppermute(behind[i], 'pass', left)  13.2 us
    all_to_all x1, starting transfers between devices, local(): lax.all_to_all(summed.reshape(peers * cores, share, -1), ('dp', 'tensor')...  12.6 us
    convert_element_type x6, other arithmetic, add_low(): return (one.astype(F32) + other.astype(F32)).astype(BF16)  11.1 us
    ppermute x8, waiting for transfers between devices, reduce_over_pass(): ahead[i] = lax.ppermute(ahead[i], 'pass', right)  11.1 us
  transfers between devices with their start and end apart: 20, of which 12 were waited for; matrix products, arithmetic and copies ran while one was open for 9% of the time, Pallas kernels for 8%

profile of v2, /device:TPU:1, one launch (start us, length us, event | category | flops | bytes accessed | tf_op | source)
XLA Modules:
  0.0 255.8 jit_solution(12956203395962744399)
XLA Ops:
  1.7 1.0 copy-done.5
  3.4 2.7 %pack_queries.1 = bf16[16,64,2048]{2,1,0:T(8,128)(2,1)S(1)} custom-call(s32[16,16]{1,0:T(8,128)S(1)} %bitcast.72, s32[1]{0:T(128)} %bitcast.2.me, bf16[4,32,2048]{2,1,0:T(8,128)(2,1)S(1)} %copy-done.3, bf16[4,32,2048]{2,1,0:T(8,128)(2,1)S(1)} %copy-done.5), custom_call_target="tpu_custom_call" | custom-call | bytes 6291456 | tf_op jit(solution)/shard_map/pack_queries/pallas_call | solution.py:88
  6.2 2.1 copy-done.1
  8.3 7.9 %all-to-all-start = ((bf16[16,64,2048]{2,1,0:T(8,128)(2,1)}), bf16[16,64,2048]{2,1,0:T(8,128)(2,1)}, u32[]{:S(2)}, u32[]{:S(2)}) async-start(bf16[16,64,2048]{2,1,0:T(8,128)(2,1)} %copy-done.1), calls=%async_computation | async-start | bytes 8388608 | tf_op jit(solution)/shard_map/all_to_all | solution.py:572
  16.2 1.0 collective-permute-start
  19.6 2.2 fusion.18
  22.6 7.2 %transpose_hidden.1.h_ref = bf16[8,512,640]{2,1,0:T(8,128)(2,1)} custom-call(s32[1]{0:T(128)} %bitcast.3.core, bf16[256,4096]{1,0:T(8,128)(2,1)S(1)} %bitcast.70, bf16[256,4096]{1,0:T(8,128)(2,1)} %bitcast.5.other_p, bf16[64,4096]{1,0:T(8,128)(2,1)S(1)} %bitcast.71, bf16[64,4096]{1,0:T(8,128)(2,1)} %bitcast.7.other_q), custom_call_target="tpu_custom_call" | custom-call | bytes 12582912 | tf_op jit(solution)/shard_map/transpose_hidden/pallas_call | solution.py:446
  29.8 48.8 %all-to-all-done.got_ref = bf16[16,64,2048]{2,1,0:T(8,128)(2,1)} async-done(((bf16[16,64,2048]{2,1,0:T(8,128)(2,1)}), bf16[16,64,2048]{2,1,0:T(8,128)(2,1)}, u32[]{:S(2)}, u32[]{:S(2)}) %all-to-all-start) | async-done | bytes 4194336 | tf_op jit(solution)/shard_map/all_to_all | solution.py:572
  81.6 6.2 %owner_stats.1 = f32[16,20,4,256]{3,2,1,0:T(4,128)S(1)} custom-call(s32[16]{0:T(128)S(1)} %copy-done.27, s32[2]{0:T(128)S(1)} %copy-done.29, bf16[16,64,2048]{2,1,0:T(8,128)(2,1)} %all-to-all-done.got_ref, bf16[2,256,256]{2,1,0:T(8,128)(2,1)S(1)} %copy-done.21, bf16[2,256,256]{2,1,0:T(8,128)(2,1)S(1)} %get-tuple-element.17.v_ref, f32[4,4,256]{2,1,0:T(4,128)S(1)} %copy-done.26), custom_call_target="tpu_custom_call" | custom-call | flops 2000000000 | bytes 6291456 | tf_op jit(solution)/shard_map/owner_stats/pallas_call | solution.py:163
  87.8 1.1 copy-done.8
  88.9 4.3 %all-to-all-start.1 = ((f32[16,20,4,256]{3,2,1,0:T(4,128)}), f32[16,20,4,256]{3,2,1,0:T(4,128)S(1)}, u32[]{:S(2)}, u32[]{:S(2)}) async-start(f32[16,20,4,256]{3,2,1,0:T(4,128)} %copy-done.8), calls=%async_computation.1 | async-start | bytes 2621440 | tf_op jit(solution)/shard_map/all_to_all | solution.py:572
  93.2 17.6 %all-to-all-done.1.all_ref = f32[16,20,4,256]{3,2,1,0:T(4,128)S(1)} async-done(((f32[16,20,4,256]{3,2,1,0:T(4,128)}), f32[16,20,4,256]{3,2,1,0:T(4,128)S(1)}, u32[]{:S(2)}, u32[]{:S(2)}) %all-to-all-start.1) | async-done | bytes 1310752 | tf_op jit(solution)/shard_map/all_to_all | solution.py:572
  110.8 2.5 own_grads.1
  117.4 7.4 %owner_grads_1.1 = (bf16[512,256]{1,0:T(8,128)(2,1)S(1)}, bf16[16,32,1024]{2,1,0:T(8,128)(2,1)S(1)}) custom-call(s32[16]{0:T(128)S(1)} %copy-done.28, s32[2]{0:T(128)S(1)} %copy-done.30, s32[16,16]{1,0:T(8,128)S(1)} %bitcast.75, s32[16]{0:T(128)S(1)} %get-tuple-element.26.entry_of, bf16[16,64,2048]{2,1,0:T(8,128)(2,1)} %all-to-all-done.got_ref, ...), custom_call_target="tpu_custom_call" | custom-call | flops 5000000000 | bytes 8388608 | tf_op jit(solution)/shard_map/owner_grads_1/pallas_call | solution.py:306
  125.8 4.5 %weight_terms_1.1 = bf16[8,512,256]{2,1,0:T(8,128)(2,1)S(1)} custom-call(bf16[8,512,640]{2,1,0:T(8,128)(2,1)} %transpose_hidden.1.h_ref, bf16[512,256]{1,0:T(8,128)(2,1)S(1)} %get-tuple-element.24.p_ref, bf16[128,256]{1,0:T(8,128)(2,1)S(1)} %get-tuple-element.43.q_ref), custom_call_target="tpu_custom_call" | custom-call | flops 1342177280 | bytes 8388608 | tf_op jit(solution)/shard_map/weight_terms_1/pallas_call | solution.py:476
  131.2 1.6 collective-permute-start.9
  132.8 7.4 %owner_grads_0.1 = (bf16[512,256]{1,0:T(8,128)(2,1)S(1)}, bf16[16,32,1024]{2,1,0:T(8,128)(2,1)S(1)}) custom-call(s32[16]{0:T(128)S(1)} %copy-done.28, s32[2]{0:T(128)S(1)} %copy-done.30, s32[16,16]{1,0:T(8,128)S(1)} %bitcast.76, s32[16]{0:T(128)S(1)} %get-tuple-element.26.entry_of, bf16[16,64,2048]{2,1,0:T(8,128)(2,1)} %all-to-all-done.got_ref, ...), custom_call_target="tpu_custom_call" | custom-call | flops 5000000000 | bytes 8388608 | tf_op jit(solution)/shard_map/owner_grads_0/pallas_call | solution.py:306
  141.3 4.6 %weight_terms_0.1 = bf16[8,512,256]{2,1,0:T(8,128)(2,1)S(1)} custom-call(bf16[8,512,640]{2,1,0:T(8,128)(2,1)} %transpose_hidden.1.h_ref, bf16[512,256]{1,0:T(8,128)(2,1)S(1)} %get-tuple-element.23.p_ref, bf16[128,256]{1,0:T(8,128)(2,1)S(1)} %get-tuple-element.42.q_ref), custom_call_target="tpu_custom_call" | custom-call | flops 1342177280 | bytes 8388608 | tf_op jit(solution)/shard_map/weight_terms_0/pallas_call | solution.py:476
  145.9 1.3 copy-done.2
  147.2 1.7 collective-permute-start.2
  149.0 2.6 %collective-permute-start.13 = (bf16[512,256]{1,0:T(8,128)(2,1)S(1)}, bf16[512,256]{1,0:T(8,128)(2,1)S(1)}, u32[]{:S(2)}, u32[]{:S(2)}) collective-permute-start(bf16[512,256]{1,0:T(8,128)(2,1)S(1)} %copy-done.32), channel_id=1, source_target_pairs={{0,14},{2,0},{4,2},{6,4},{8,6},{10,8},{12,10},{14,12},{1,15},{3,1}... | collective-permute-start | bytes 786440 | tf_op jit(solution)/shard_map/ppermute | solution.py:514
  151.6 1.7 fusion.5
  153.3 2.7 %collective-permute-start.6 = (bf16[512,256]{1,0:T(8,128)(2,1)S(1)}, bf16[512,256]{1,0:T(8,128)(2,1)S(1)}, u32[]{:S(2)}, u32[]{:S(2)}) collective-permute-start(bf16[512,256]{1,0:T(8,128)(2,1)S(1)} %get-tuple-element.33), channel_id=1, source_target_pairs={{0,14},{2,0},{4,2},{6,4},{8,6},{10,8},{12,10},{14,12},{1,15},{3,1}... | collective-permute-start | bytes 786440 | tf_op jit(solution)/shard_map/ppermute | solution.py:514
  156.0 1.8 fusion.11
  157.8 4.5 %collective-permute-done.10 = bf16[512,256]{1,0:T(8,128)(2,1)} collective-permute-done((bf16[512,256]{1,0:T(8,128)(2,1)}, bf16[512,256]{1,0:T(8,128)(2,1)}, u32[]{:S(2)}, u32[]{:S(2)}) %collective-permute-start.10) | collective-permute-done | bytes 262176 | tf_op jit(solution)/shard_map/ppermute | solution.py:510
  162.3 1.8 fusion.4
  164.1 2.7 %collective-permute-start.14 = (bf16[512,256]{1,0:T(8,128)(2,1)S(1)}, bf16[512,256]{1,0:T(8,128)(2,1)}, u32[]{:S(2)}, u32[]{:S(2)}) collective-permute-start(bf16[512,256]{1,0:T(8,128)(2,1)S(1)} %get-tuple-element.37), channel_id=1, source_target_pairs={{0,14},{2,0},{4,2},{6,4},{8,6},{10,8},{12,10},{14,12},{1,15},{3,1}... | collective-permute-start | bytes 786440 | tf_op jit(solution)/shard_map/ppermute | solution.py:514
  167.7 1.9 fusion.10
  169.6 2.7 %collective-permute-start.7 = (bf16[512,256]{1,0:T(8,128)(2,1)S(1)}, bf16[512,256]{1,0:T(8,128)(2,1)S(1)}, u32[]{:S(2)}, u32[]{:S(2)}) collective-permute-start(bf16[512,256]{1,0:T(8,128)(2,1)S(1)} %get-tuple-element.31), channel_id=1, source_target_pairs={{0,14},{2,0},{4,2},{6,4},{8,6},{10,8},{12,10},{14,12},{1,15},{3,1}... | collective-permute-start | bytes 786440 | tf_op jit(solution)/shard_map/ppermute | solution.py:514
  172.3 1.3 collective-permute-done.11
  173.5 1.9 fusion.3
  175.7 1.2 collective-permute-start.12
  176.9 1.7 collective-permute-done.4
  178.6 2.0 fusion.9
  180.6 2.2 collective-permute-start.8
  183.7 1.4 collective-permute-done.12
  185.0 1.1 fusion
  186.2 2.2 collective-permute-done.8
  188.3 1.2 collective-permute-done.5
  189.6 1.2 fusion.6
  191.6 12.6 %all-to-all-start.3 = ((bf16[32,16,512]{2,1,0:T(8,128)(2,1)}), bf16[32,16,512]{2,1,0:T(8,128)(2,1)S(1)}, u32[]{:S(2)}, u32[]{:S(2)}) async-start(bf16[32,16,512]{2,1,0:T(8,128)(2,1)} %bitcast.30), calls=%async_computation.3 | async-start | bytes 1048576 | tf_op jit(solution)/shard_map/all_to_all | solution.py:621
  204.3 2.8 %pad_maximum_fusion = bf16[16,32,2048]{2,1,0:T(8,128)(2,1)} fusion(bf16[16,32,1024]{2,1,0:T(8,128)(2,1)S(1)} %copy-done.12, bf16[16,32,1024]{2,1,0:T(8,128)(2,1)} %copy-done.13), kind=kLoop, calls=%fused_computation | loop fusion | flops 4194304 | bytes 4194304 | tf_op jit(solution)/shard_map/concatenate | solution.py:617
  207.0 8.9 %all-to-all-done.3 = bf16[32,16,512]{2,1,0:T(8,128)(2,1)S(1)} async-done(((bf16[32,16,512]{2,1,0:T(8,128)(2,1)}), bf16[32,16,512]{2,1,0:T(8,128)(2,1)S(1)}, u32[]{:S(2)}, u32[]{:S(2)}) %all-to-all-start.3) | async-done | bytes 524320 | tf_op jit(solution)/shard_map/all_to_all | solution.py:621
  215.9 3.7 %all-to-all-start.2 = ((bf16[16,32,2048]{2,1,0:T(8,128)(2,1)}), bf16[16,32,2048]{2,1,0:T(8,128)(2,1)S(1)}, u32[]{:S(2)}, u32[]{:S(2)}) async-start(bf16[16,32,2048]{2,1,0:T(8,128)(2,1)} %pad_maximum_fusion), calls=%async_computation.2 | async-start | bytes 4194304 | tf_op jit(solution)/shard_map/all_to_all | solution.py:572
  221.5 1.3 pad_maximum_fusion.1
  223.6 28.9 %all-to-all-done.2.refs_0_.refs_1_.refs_2_.refs_3_ = bf16[16,32,2048]{2,1,0:T(8,128)(2,1)S(1)} async-done(((bf16[16,32,2048]{2,1,0:T(8,128)(2,1)}), bf16[16,32,2048]{2,1,0:T(8,128)(2,1)S(1)}, u32[]{:S(2)}, u32[]{:S(2)}) %all-to-all-start.2) | async-done | bytes 2097184 | tf_op jit(solution)/shard_map/all_to_all | solution.py:572
  252.5 1.2 copy-done.10
  253.7 2.1 sum_dq.1
  (97 shorter events, 20.3 us)
Async XLA Ops:
  0.6 17.6 %copy-start = (s32[16,1,2]{0,2,1:T(2,128)S(1)}, s32[16,1,2]{0,2,1:T(2,128)}, u32[]{:S(2)}) copy-start(s32[16,1,2]{0,2,1:T(2,128)} %param.15) | copy-start | bytes 388
  0.7 1.0 copy-start.3
  1.7 1.0 copy-start.5
  6.2 2.1 copy-start.1
  8.2 7.9 %copy-start.7 = (bf16[2,128,4096]{2,1,0:T(8,128)(2,1)S(1)}, bf16[2,128,4096]{2,1,0:T(8,128)(2,1)}, u32[]{:S(2)}) copy-start(bf16[2,128,4096]{2,1,0:T(8,128)(2,1)} %param.13) | copy-start | bytes 6291460
  8.2 9.1 %copy-start.24 = (s32[16,1,16]{2,1,0:T(1,128)S(1)}, s32[16,1,16]{2,1,0:T(1,128)}, u32[]{:S(2)}) copy-start(s32[16,1,16]{2,1,0:T(1,128)} %param.14) | copy-start | bytes 3076
  8.2 9.8 %copy-start.31 = (bf16[4,32,2,256]{3,2,1,0:T(2,128)(2,1)S(1)}, bf16[4,32,2,256]{3,2,1,0:T(2,128)(2,1)}, u32[]{:S(2)}) copy-start(bf16[4,32,2,256]{3,2,1,0:T(2,128)(2,1)} %param.10) | copy-start | bytes 393220
  8.3 10.8 %copy-start.4 = (bf16[4,32,2048]{2,1,0:T(8,128)(2,1)S(1)}, bf16[4,32,2048]{2,1,0:T(8,128)(2,1)}, u32[]{:S(2)}) copy-start(bf16[4,32,2048]{2,1,0:T(8,128)(2,1)} %q_ref.5) | copy-start | bytes 1572868
  8.3 10.8 %copy-start.6 = (bf16[4,32,2048]{2,1,0:T(8,128)(2,1)S(1)}, bf16[4,32,2048]{2,1,0:T(8,128)(2,1)}, u32[]{:S(2)}) copy-start(bf16[4,32,2048]{2,1,0:T(8,128)(2,1)} %g_ref.5) | copy-start | bytes 1572868
  8.3 70.3 %all-to-all-start = ((bf16[16,64,2048]{2,1,0:T(8,128)(2,1)}), bf16[16,64,2048]{2,1,0:T(8,128)(2,1)}, u32[]{:S(2)}, u32[]{:S(2)}) async-start(bf16[16,64,2048]{2,1,0:T(8,128)(2,1)} %copy-done.1), calls=%async_computation | async-start | bytes 8388608 | tf_op jit(solution)/shard_map/all_to_all | solution.py:572
  16.2 6.4 %collective-permute-start = (bf16[2,128,4096]{2,1,0:T(8,128)(2,1)S(1)}, bf16[2,128,4096]{2,1,0:T(8,128)(2,1)}, u32[]{:S(2)}, u32[]{:S(2)}) collective-permute-start(bf16[2,128,4096]{2,1,0:T(8,128)(2,1)S(1)} %copy-done.7), channel_id=1, source_target_pairs={{0,1},{1,0},{2,3},{3,2},{4,5},{5,4},{6,7},{7,6},{8,9},{9,8},{10,11... | collective-permute-start | bytes 6291464 | tf_op jit(solution)/shard_map/ppermute | solution.py:575
  17.2 5.3 %collective-permute-start.1 = (bf16[4,16,4096]{2,1,0:T(8,128)(2,1)}, bf16[4,16,4096]{2,1,0:T(8,128)(2,1)}, u32[]{:S(2)}, u32[]{:S(2)}) collective-permute-start(bf16[4,16,4096]{2,1,0:T(8,128)(2,1)} %param.12), channel_id=1, source_target_pairs={{0,1},{1,0},{2,3},{3,2},{4,5},{5,4},{6,7},{7,6},{8,9},{9,8},{10,11... | collective-permute-start | bytes 1572872 | tf_op jit(solution)/shard_map/ppermute | solution.py:575
  19.6 2.2 copy-start.25
  19.6 3.0 %copy-start.18 = (bf16[4,16,4096]{2,1,0:T(8,128)(2,1)S(1)}, bf16[4,16,4096]{2,1,0:T(8,128)(2,1)}, u32[]{:S(2)}) copy-start(bf16[4,16,4096]{2,1,0:T(8,128)(2,1)} %param.12) | copy-start | bytes 1572868
  22.6 56.0 %copy-start.19 = (bf16[2,256,256]{2,1,0:T(8,128)(2,1)}, bf16[2,256,256]{2,1,0:T(8,128)(2,1)S(1)}, u32[]{:S(2)}) copy-start(bf16[2,256,256]{2,1,0:T(8,128)(2,1)S(1)} %get-tuple-element.17.v_ref) | copy-start | bytes 786436
  78.5 1.0 copy-start.21
  87.8 1.1 copy-start.8
  88.9 22.0 %all-to-all-start.1 = ((f32[16,20,4,256]{3,2,1,0:T(4,128)}), f32[16,20,4,256]{3,2,1,0:T(4,128)S(1)}, u32[]{:S(2)}, u32[]{:S(2)}) async-start(f32[16,20,4,256]{3,2,1,0:T(4,128)} %copy-done.8), calls=%async_computation.1 | async-start | bytes 2621440 | tf_op jit(solution)/shard_map/all_to_all | solution.py:572
  113.4 11.5 %copy-start.9 = (f32[4,32,2048]{2,1,0:T(8,128)}, f32[4,32,2048]{2,1,0:T(8,128)S(1)}, u32[]{:S(2)}) copy-start(f32[4,32,2048]{2,1,0:T(8,128)S(1)} %get-tuple-element.21.refs_4_) | copy-start | bytes 3145732
  114.1 0.9 copy-start.20
  115.1 0.9 copy-start.22
  124.8 1.0 copy-start.11
  125.8 4.6 %copy-start.14 = (bf16[512,256]{1,0:T(8,128)(2,1)}, bf16[512,256]{1,0:T(8,128)(2,1)S(1)}, u32[]{:S(2)}) copy-start(bf16[512,256]{1,0:T(8,128)(2,1)S(1)} %get-tuple-element.24.p_ref) | copy-start | bytes 786436
  131.2 20.4 %collective-permute-start.9 = (bf16[512,256]{1,0:T(8,128)(2,1)}, bf16[512,256]{1,0:T(8,128)(2,1)}, u32[]{:S(2)}, u32[]{:S(2)}) collective-permute-start(bf16[512,256]{1,0:T(8,128)(2,1)} %get-tuple-element.38), channel_id=1, source_target_pairs={{0,2},{2,4},{4,6},{6,8},{8,10},{10,12},{12,14},{14,0},{1,3},{3,5},... | collective-permute-start | bytes 786440 | tf_op jit(solution)/shard_map/ppermute | solution.py:510
  140.3 1.0 copy-start.13
  141.3 4.6 %copy-start.16 = (bf16[512,256]{1,0:T(8,128)(2,1)}, bf16[512,256]{1,0:T(8,128)(2,1)S(1)}, u32[]{:S(2)}) copy-start(bf16[512,256]{1,0:T(8,128)(2,1)S(1)} %get-tuple-element.23.p_ref) | copy-start | bytes 786436
  141.3 7.7 %copy-start.32 = (bf16[512,256]{1,0:T(8,128)(2,1)S(1)}, bf16[512,256]{1,0:T(8,128)(2,1)}, u32[]{:S(2)}) copy-start(bf16[512,256]{1,0:T(8,128)(2,1)} %get-tuple-element.39) | copy-start | bytes 786436
  145.9 1.3 copy-start.2
  147.2 8.7 %collective-permute-start.2 = (bf16[512,256]{1,0:T(8,128)(2,1)S(1)}, bf16[512,256]{1,0:T(8,128)(2,1)}, u32[]{:S(2)}, u32[]{:S(2)}) collective-permute-start(bf16[512,256]{1,0:T(8,128)(2,1)S(1)} %get-tuple-element.32), channel_id=1, source_target_pairs={{0,2},{2,4},{4,6},{6,8},{8,10},{10,12},{12,14},{14,0},{1,3},{3,5},... | collective-permute-start | bytes 786440 | tf_op jit(solution)/shard_map/ppermute | solution.py:510
  149.0 8.8 %collective-permute-start.13 = (bf16[512,256]{1,0:T(8,128)(2,1)S(1)}, bf16[512,256]{1,0:T(8,128)(2,1)S(1)}, u32[]{:S(2)}, u32[]{:S(2)}) collective-permute-start(bf16[512,256]{1,0:T(8,128)(2,1)S(1)} %copy-done.32), channel_id=1, source_target_pairs={{0,14},{2,0},{4,2},{6,4},{8,6},{10,8},{12,10},{14,12},{1,15},{3,1}... | collective-permute-start | bytes 786440 | tf_op jit(solution)/shard_map/ppermute | solution.py:514
  153.3 9.0 %collective-permute-start.10 = (bf16[512,256]{1,0:T(8,128)(2,1)}, bf16[512,256]{1,0:T(8,128)(2,1)}, u32[]{:S(2)}, u32[]{:S(2)}) collective-permute-start(bf16[512,256]{1,0:T(8,128)(2,1)} %fusion.5), channel_id=1, source_target_pairs={{0,2},{2,4},{4,6},{6,8},{8,10},{10,12},{12,14},{14,0},{1,3},{3,5},... | collective-permute-start | bytes 786440 | tf_op jit(solution)/shard_map/ppermute | solution.py:510
  153.3 13.5 %collective-permute-start.6 = (bf16[512,256]{1,0:T(8,128)(2,1)S(1)}, bf16[512,256]{1,0:T(8,128)(2,1)S(1)}, u32[]{:S(2)}, u32[]{:S(2)}) collective-permute-start(bf16[512,256]{1,0:T(8,128)(2,1)S(1)} %get-tuple-element.33), channel_id=1, source_target_pairs={{0,14},{2,0},{4,2},{6,4},{8,6},{10,8},{12,10},{14,12},{1,15},{3,1}... | collective-permute-start | bytes 786440 | tf_op jit(solution)/shard_map/ppermute | solution.py:514
  157.8 10.0 %collective-permute-start.3 = (bf16[512,256]{1,0:T(8,128)(2,1)}, bf16[512,256]{1,0:T(8,128)(2,1)S(1)}, u32[]{:S(2)}, u32[]{:S(2)}) collective-permute-start(bf16[512,256]{1,0:T(8,128)(2,1)} %fusion.11), channel_id=1, source_target_pairs={{0,2},{2,4},{4,6},{6,8},{8,10},{10,12},{12,14},{14,0},{1,3},{3,5},... | collective-permute-start | bytes 786440 | tf_op jit(solution)/shard_map/ppermute | solution.py:510
  164.1 9.4 %collective-permute-start.11 = (bf16[512,256]{1,0:T(8,128)(2,1)}, bf16[512,256]{1,0:T(8,128)(2,1)S(1)}, u32[]{:S(2)}, u32[]{:S(2)}) collective-permute-start(bf16[512,256]{1,0:T(8,128)(2,1)} %get-tuple-element.36), channel_id=1, source_target_pairs={{0,2},{2,4},{4,6},{6,8},{8,10},{10,12},{12,14},{14,0},{1,3},{3,5},... | collective-permute-start | bytes 786440 | tf_op jit(solution)/shard_map/ppermute | solution.py:510
  164.1 9.4 %collective-permute-start.14 = (bf16[512,256]{1,0:T(8,128)(2,1)S(1)}, bf16[512,256]{1,0:T(8,128)(2,1)}, u32[]{:S(2)}, u32[]{:S(2)}) collective-permute-start(bf16[512,256]{1,0:T(8,128)(2,1)S(1)} %get-tuple-element.37), channel_id=1, source_target_pairs={{0,14},{2,0},{4,2},{6,4},{8,6},{10,8},{12,10},{14,12},{1,15},{3,1}... | collective-permute-start | bytes 786440 | tf_op jit(solution)/shard_map/ppermute | solution.py:514
  169.6 9.0 %collective-permute-start.4 = (bf16[512,256]{1,0:T(8,128)(2,1)}, bf16[512,256]{1,0:T(8,128)(2,1)S(1)}, u32[]{:S(2)}, u32[]{:S(2)}) collective-permute-start(bf16[512,256]{1,0:T(8,128)(2,1)} %get-tuple-element.30), channel_id=1, source_target_pairs={{0,2},{2,4},{4,6},{6,8},{8,10},{10,12},{12,14},{14,0},{1,3},{3,5},... | collective-permute-start | bytes 786440 | tf_op jit(solution)/shard_map/ppermute | solution.py:510
  169.6 9.0 %collective-permute-start.7 = (bf16[512,256]{1,0:T(8,128)(2,1)S(1)}, bf16[512,256]{1,0:T(8,128)(2,1)S(1)}, u32[]{:S(2)}, u32[]{:S(2)}) collective-permute-start(bf16[512,256]{1,0:T(8,128)(2,1)S(1)} %get-tuple-element.31), channel_id=1, source_target_pairs={{0,14},{2,0},{4,2},{6,4},{8,6},{10,8},{12,10},{14,12},{1,15},{3,1}... | collective-permute-start | bytes 786440 | tf_op jit(solution)/shard_map/ppermute | solution.py:514
  175.4 7.5 %collective-permute-start.15 = (bf16[512,256]{1,0:T(8,128)(2,1)}, bf16[512,256]{1,0:T(8,128)(2,1)S(1)}, u32[]{:S(2)}, u32[]{:S(2)}) collective-permute-start(bf16[512,256]{1,0:T(8,128)(2,1)} %get-tuple-element.35), channel_id=1, source_target_pairs={{0,14},{2,0},{4,2},{6,4},{8,6},{10,8},{12,10},{14,12},{1,15},{3,1}... | collective-permute-start | bytes 786440 | tf_op jit(solution)/shard_map/ppermute | solution.py:514
  175.7 9.3 %collective-permute-start.12 = (bf16[512,256]{1,0:T(8,128)(2,1)}, bf16[512,256]{1,0:T(8,128)(2,1)}, u32[]{:S(2)}, u32[]{:S(2)}) collective-permute-start(bf16[512,256]{1,0:T(8,128)(2,1)} %get-tuple-element.34), channel_id=1, source_target_pairs={{0,2},{2,4},{4,6},{6,8},{8,10},{10,12},{12,14},{14,0},{1,3},{3,5},... | collective-permute-start | bytes 786440 | tf_op jit(solution)/shard_map/ppermute | solution.py:510
  180.6 7.8 %collective-permute-start.8 = (bf16[512,256]{1,0:T(8,128)(2,1)}, bf16[512,256]{1,0:T(8,128)(2,1)}, u32[]{:S(2)}, u32[]{:S(2)}) collective-permute-start(bf16[512,256]{1,0:T(8,128)(2,1)} %get-tuple-element.29), channel_id=1, source_target_pairs={{0,14},{2,0},{4,2},{6,4},{8,6},{10,8},{12,10},{14,12},{1,15},{3,1}... | collective-permute-start | bytes 786440 | tf_op jit(solution)/shard_map/ppermute | solution.py:514
  182.8 6.7 %collective-permute-start.5 = (bf16[512,256]{1,0:T(8,128)(2,1)}, bf16[512,256]{1,0:T(8,128)(2,1)}, u32[]{:S(2)}, u32[]{:S(2)}) collective-permute-start(bf16[512,256]{1,0:T(8,128)(2,1)} %get-tuple-element.28), channel_id=1, source_target_pairs={{0,2},{2,4},{4,6},{6,8},{8,10},{10,12},{12,14},{14,0},{1,3},{3,5},... | collective-permute-start | bytes 786440 | tf_op jit(solution)/shard_map/ppermute | solution.py:510
  182.8 21.4 %copy-start.12 = (bf16[16,32,1024]{2,1,0:T(8,128)(2,1)S(1)}, bf16[16,32,1024]{2,1,0:T(8,128)(2,1)}, u32[]{:S(2)}) copy-start(bf16[16,32,1024]{2,1,0:T(8,128)(2,1)} %copy-done.11) | copy-start | bytes 3145732
  182.9 0.7 copy-start.33
  191.6 24.3 %all-to-all-start.3 = ((bf16[32,16,512]{2,1,0:T(8,128)(2,1)}), bf16[32,16,512]{2,1,0:T(8,128)(2,1)S(1)}, u32[]{:S(2)}, u32[]{:S(2)}) async-start(bf16[32,16,512]{2,1,0:T(8,128)(2,1)} %bitcast.30), calls=%async_computation.3 | async-start | bytes 1048576 | tf_op jit(solution)/shard_map/all_to_all | solution.py:621
  207.0 12.6 %copy-start.15 = (bf16[512,256]{1,0:T(8,128)(2,1)S(1)}, bf16[512,256]{1,0:T(8,128)(2,1)}, u32[]{:S(2)}) copy-start(bf16[512,256]{1,0:T(8,128)(2,1)} %copy-done.14) | copy-start | bytes 786436
  207.0 12.7 %copy-start.17 = (bf16[512,256]{1,0:T(8,128)(2,1)S(1)}, bf16[512,256]{1,0:T(8,128)(2,1)}, u32[]{:S(2)}) copy-start(bf16[512,256]{1,0:T(8,128)(2,1)} %copy-done.16) | copy-start | bytes 786436
  215.9 36.5 %all-to-all-start.2 = ((bf16[16,32,2048]{2,1,0:T(8,128)(2,1)}), bf16[16,32,2048]{2,1,0:T(8,128)(2,1)S(1)}, u32[]{:S(2)}, u32[]{:S(2)}) async-start(bf16[16,32,2048]{2,1,0:T(8,128)(2,1)} %pad_maximum_fusion), calls=%async_computation.2 | async-start | bytes 4194304 | tf_op jit(solution)/shard_map/all_to_all | solution.py:572
  252.5 1.2 copy-start.10
  (6 other events, 4.1 us)

commit v3 on v2

--- a/solution.py
+++ b/solution.py
@@ -13,15 +13,15 @@
 NEG_FILL = -1e30
 SCALE = HD ** (-0.5)
 SCALE_LOG2 = SCALE * math.log2(math.e)
-VMEM_LIMIT = 48 * 1024 * 1024
+VMEM_LIMIT = 24 * 1024 * 1024
 NT = (((1,), (1,)), ((), ()))
 TN = (((0,), (0,)), ((), ()))
 F32 = jnp.float32
 BF16 = jnp.bfloat16
 
 
-def params():
-    return pltpu.CompilerParams(vmem_limit_bytes=VMEM_LIMIT)
+def params(limit=VMEM_LIMIT):
+    return pltpu.CompilerParams(vmem_limit_bytes=limit)
 
 
 def whole():
@@ -32,8 +32,8 @@
     return pl.BlockSpec(memory_space=pltpu.SMEM)
 
 
-def anywhere():
-    return pl.BlockSpec(memory_space=pl.ANY)
+def in_hbm():
+    return pl.BlockSpec(memory_space=pltpu.HBM)
 
 
 def cost(flops, nbytes, trans=0):
@@ -51,10 +51,11 @@
     )
 
 
-def pack_kernel(slots, refs, me, q_ref, g_ref, out_ref, held, load_sems, sems):
+def pack_kernel(slots, refs, q_ref, g_ref, out_ref, held, load_sems, sems):
     peers = out_ref.shape[0]
     samples, rows, _ = q_ref.shape
     per = peers // samples
+    me = lax.axis_index("dp")
     loads = []
     for sample in range(samples):
         pair = []
@@ -74,7 +75,7 @@
         if j % per == 0:
             for copy in loads[sample]:
                 copy.wait()
-        dest = quotient(refs[me[0], j], slots)
+        dest = quotient(refs[me, j], slots)
         copy = pltpu.make_async_copy(held.at[sample], out_ref.at[dest], sems.at[j])
         copy.start()
         copies.append(copy)
@@ -82,23 +83,23 @@
         copy.wait()
 
 
-def pack_queries(refs, me, question_q, question_grad, slots):
+def pack_queries(refs, question_q, question_grad, slots):
     samples, rows, width = question_q.shape
     peers = refs.shape[0]
     return pl.pallas_call(
         functools.partial(pack_kernel, slots),
         out_shape=jax.ShapeDtypeStruct((peers, 2 * rows, width), BF16),
-        in_specs=[smem(), smem(), anywhere(), anywhere()],
-        out_specs=anywhere(),
+        in_specs=[smem(), in_hbm(), in_hbm()],
+        out_specs=in_hbm(),
         scratch_shapes=[
             pltpu.VMEM((samples, 2 * rows, width), BF16),
             pltpu.SemaphoreType.DMA((samples, 2)),
             pltpu.SemaphoreType.DMA((peers,)),
         ],
-        compiler_params=params(),
+        compiler_params=params(60 * 1024 * 1024),
         cost_estimate=cost(0, 6 * 2**20),
         name="pack_queries",
-    )(refs, me, question_q, question_grad)
+    )(refs, question_q, question_grad)
 
 
 def scores_t(keys, queries, valid):
@@ -119,69 +120,53 @@
     return lax.broadcasted_iota(jnp.int32, shape, 0) < blocks[slot] * BLOCK
 
 
-def owner_stats_kernel(group, slot_of, blocks, got_ref, k_ref, v_ref, own_ref, out_ref):
+def owner_stats_kernel(group, slot_of, blocks, got_ref, k_ref, v_ref, out_ref):
     step = pl.program_id(0)
-    last = pl.num_programs(0) - 1
     per, both, _ = got_ref.shape
     rows = both // 2
-    peers = out_ref.shape[0]
     slot_len = k_ref.shape[1]
     heads = k_ref.shape[2] // HD
     columns = group * rows
-
-    @pl.when(step < last)
-    def _():
-        for one in range(per):
-            slot = slot_of[step * per + one]
-            valid = passage_valid(blocks, slot, slot_len, columns)
-            logs, deltas = [], []
-            for head in range(heads):
-                lanes = slice(head * HD, (head + 1) * HD)
-                queries = head_rows(got_ref[one, :rows], head, group)
-                grads = head_rows(got_ref[one, rows:], head, group)
-                scores = scores_t(k_ref[slot, :, lanes], queries, valid)
-                prob_grad = lax.dot_general(
-                    v_ref[slot, :, lanes], grads, NT, preferred_element_type=F32
-                )
-                log, delta = part_stats(scores, prob_grad)
-                logs.append(log)
-                deltas.append(delta)
-            both_stats = jnp.concatenate(logs + deltas, axis=0)
-            for peer in range(peers):
-                out_ref[peer, one] = both_stats
-
-    @pl.when(step == last)
-    def _():
-        for peer in range(peers):
-            out_ref[peer] = own_ref[...]
-
-
-def owner_stats(slot_of, blocks, got, keys, values, own, group):
+    for one in range(per):
+        slot = slot_of[step * per + one]
+        valid = passage_valid(blocks, slot, slot_len, columns)
+        logs, deltas = [], []
+        for head in range(heads):
+            lanes = slice(head * HD, (head + 1) * HD)
+            queries = head_rows(got_ref[one, :rows], head, group)
+            grads = head_rows(got_ref[one, rows:], head, group)
+            scores = scores_t(k_ref[slot, :, lanes], queries, valid)
+            prob_grad = lax.dot_general(
+                v_ref[slot, :, lanes], grads, NT, preferred_element_type=F32
+            )
+            log, delta = part_stats(scores, prob_grad)
+            logs.append(log)
+            deltas.append(delta)
+        out_ref[one] = jnp.concatenate(logs + deltas, axis=0)
+
+
+def owner_stats(slot_of, blocks, got, keys, values, group):
     peers, both, width = got.shape
-    samples, stat_rows, columns = own.shape
-    steps = peers // samples
+    heads = keys.shape[2] // HD
+    columns = group * both // 2
+    per = 4
     return pl.pallas_call(
         functools.partial(owner_stats_kernel, group),
-        out_shape=jax.ShapeDtypeStruct((peers, peers + samples, stat_rows, columns), F32),
+        out_shape=jax.ShapeDtypeStruct((peers, 2 * heads, columns), F32),
         grid_spec=pltpu.PrefetchScalarGridSpec(
             num_scalar_prefetch=2,
-            grid=(steps + 1,),
+            grid=(peers // per,),
             in_specs=[
-                pl.BlockSpec(
-                    (samples, both, width), lambda r, s, b: (jnp.minimum(r, steps - 1), 0, 0)
-                ),
-                whole(),
+                pl.BlockSpec((per, both, width), lambda r, s, b: (r, 0, 0)),
                 whole(),
                 whole(),
             ],
-            out_specs=pl.BlockSpec(
-                (peers, samples, stat_rows, columns), lambda r, s, b: (0, r, 0, 0)
-            ),
+            out_specs=pl.BlockSpec((per, 2 * heads, columns), lambda r, s, b: (r, 0, 0)),
         ),
         compiler_params=params(),
         cost_estimate=cost(2 * 10**9, 6 * 2**20, 2 * 10**6),
         name="owner_stats",
-    )(slot_of, blocks, got, keys, values, own)
+    )(slot_of, blocks, got, keys, values)
 
 
 def own_valid(own_rows, rows, group):
@@ -225,18 +210,38 @@
     )(question_q, question_grad, keys, values)
 
 
-def joint_stats(all_ref, refs, reader, sample, per, slots, head, heads):
-    peers = all_ref.shape[0]
-    parts = [all_ref[reader, peers + sample]]
-    for k in range(per):
-        parts.append(all_ref[quotient(refs[reader, sample * per + k], slots), reader])
-    logs = [part[head : head + 1] for part in parts]
-    deltas = [part[heads + head : heads + head + 1] for part in parts]
-    top = functools.reduce(jnp.maximum, logs)
-    weights = [jnp.exp2(log - top) for log in logs]
-    total = sum(weights)
-    delta = sum(weight * one for weight, one in zip(weights, deltas)) / total
-    return top + jnp.log2(total), delta
+def merge_kernel(slots, refs, st_ref, own_ref, back_ref, merged_ref):
+    samples, stat_rows, _ = own_ref.shape
+    heads = stat_rows // 2
+    per = st_ref.shape[0] // samples
+    me = lax.axis_index("dp")
+    for sample in range(samples):
+        owners = [quotient(refs[me, sample * per + k], slots) for k in range(per)]
+        parts = [own_ref[sample]] + [st_ref[owner] for owner in owners]
+        logs = [part[:heads] for part in parts]
+        top = functools.reduce(jnp.maximum, logs)
+        weights = [jnp.exp2(log - top) for log in logs]
+        total = sum(weights)
+        delta = sum(weight * part[heads:] for weight, part in zip(weights, parts)) / total
+        joint = jnp.concatenate([top + jnp.log2(total), delta], axis=0)
+        merged_ref[sample] = joint
+        for owner in owners:
+            back_ref[owner] = joint
+
+
+def merge(refs, stats, own, slots):
+    return pl.pallas_call(
+        functools.partial(merge_kernel, slots),
+        out_shape=(
+            jax.ShapeDtypeStruct(stats.shape, F32),
+            jax.ShapeDtypeStruct(own.shape, F32),
+        ),
+        in_specs=[smem(), whole(), whole()],
+        out_specs=(whole(), whole()),
+        compiler_params=params(),
+        cost_estimate=cost(10**5, 2**17, 10**4),
+        name="merge_stats",
+    )(refs, stats, own)
 
 
 def probs_and_dscore(scores, prob_grad, joint, delta):
@@ -245,29 +250,13 @@
     return probs.astype(BF16), dscore
 
 
-def owner_grads_kernel(
-    group,
-    slots,
-    head,
-    slot_of,
-    blocks,
-    refs,
-    entry_of,
-    got_ref,
-    all_ref,
-    k_ref,
-    v_ref,
-    grad_ref,
-    dq_ref,
-    acc_ref,
-):
+def owner_grads_kernel(group, head, slot_of, blocks, got_ref, joint_ref, k_ref, v_ref, *rest):
+    grad_ref, dq_ref, acc_ref = rest[-3:]
     step = pl.program_id(0)
     per, both, _ = got_ref.shape
     rows = both // 2
     slot_len = k_ref.shape[1]
     heads = k_ref.shape[2] // HD
-    peers = all_ref.shape[0]
-    entries = peers // (all_ref.shape[1] - peers)
     lanes = slice(head * HD, (head + 1) * HD)
 
     @pl.when(step == 0)
@@ -275,16 +264,15 @@
         acc_ref[...] = jnp.zeros_like(acc_ref)
 
     for one in range(per):
-        reader = step * per + one
-        slot = slot_of[reader]
-        sample = quotient(entry_of[reader], entries)
-        joint, delta = joint_stats(all_ref, refs, reader, sample, entries, slots, head, heads)
+        slot = slot_of[step * per + one]
         valid = passage_valid(blocks, slot, slot_len, group * rows)
         queries = head_rows(got_ref[one, :rows], 0, group)
         grads = head_rows(got_ref[one, rows:], 0, group)
         keys = k_ref[slot, :, lanes]
         scores = scores_t(keys, queries, valid)
         prob_grad = lax.dot_general(v_ref[slot, :, lanes], grads, NT, preferred_element_type=F32)
+        joint = joint_ref[one, head : head + 1]
+        delta = joint_ref[one, heads + head : heads + head + 1]
         probs, dscore = probs_and_dscore(scores, prob_grad, joint, delta)
         acc_ref[slot, :, :HD] += jnp.dot(dscore, queries, preferred_element_type=F32)
         acc_ref[slot, :, HD:] += jnp.dot(probs, grads, preferred_element_type=F32)
@@ -298,50 +286,57 @@
             grad_ref[one * slot_len : (one + 1) * slot_len] = acc_ref[one].astype(BF16)
 
 
-def owner_grads(head, slot_of, blocks, refs, entry_of, got, stats, keys, values, group):
-    peers, both, _ = got.shape
+def owner_grads(head, slot_of, blocks, got, joint, keys, values, dq, group):
+    peers, both, width = got.shape
     slots, slot_len, _ = keys.shape
-    per = stats.shape[1] - peers
-    width = group * HD
-    return pl.pallas_call(
-        functools.partial(owner_grads_kernel, group, slots, head),
+    stat_rows, columns = joint.shape[1:]
+    per = 4
+    lanes = group * HD
+    operands = [slot_of, blocks, got, joint, keys, values]
+    in_specs = [
+        pl.BlockSpec((per, both, lanes), lambda r, *_: (r, 0, head)),
+        pl.BlockSpec((per, stat_rows, columns), lambda r, *_: (r, 0, 0)),
+        whole(),
+        whole(),
+    ]
+    aliases = {}
+    if dq is not None:
+        aliases = {len(operands): 1}
+        operands.append(dq)
+        in_specs.append(in_hbm())
+    return pl.pallas_call(
+        functools.partial(owner_grads_kernel, group, head),
         out_shape=(
             jax.ShapeDtypeStruct((slots * slot_len, 2 * HD), BF16),
             jax.ShapeDtypeStruct((peers, both // 2, width), BF16),
         ),
         grid_spec=pltpu.PrefetchScalarGridSpec(
-            num_scalar_prefetch=4,
+            num_scalar_prefetch=2,
             grid=(peers // per,),
-            in_specs=[
-                pl.BlockSpec((per, both, width), lambda r, *_: (r, 0, head)),
-                whole(),
-                whole(),
-                whole(),
-            ],
+            in_specs=in_specs,
             out_specs=(
                 pl.BlockSpec((slots * slot_len, 2 * HD), lambda r, *_: (0, 0)),
-                pl.BlockSpec((per, both // 2, width), lambda r, *_: (r, 0, 0)),
+                pl.BlockSpec((per, both // 2, lanes), lambda r, *_: (r, 0, head)),
             ),
             scratch_shapes=[pltpu.VMEM((slots, slot_len, 2 * HD), F32)],
         ),
+        input_output_aliases=aliases,
         compiler_params=params(),
         cost_estimate=cost(5 * 10**9, 8 * 2**20, 2 * 10**6),
         name=f"owner_grads_{head}",
-    )(slot_of, blocks, refs, entry_of, got, stats, keys, values)
-
-
-def own_grads_kernel(
-    group, slots, refs, me, q_ref, g_ref, k_ref, v_ref, all_ref, grad_ref, dq_ref
-):
+    )(*operands)
+
+
+def own_grads_kernel(group, q_ref, g_ref, k_ref, v_ref, joint_ref, grad_ref, dq_ref):
     samples, rows, _ = q_ref.shape
     heads = k_ref.shape[2] // HD
-    entries = all_ref.shape[0] // samples
     valid = own_valid(rows, rows, group)
     for sample in range(samples):
         token = slice(sample * rows, (sample + 1) * rows)
         for head in range(heads):
             lanes = slice(head * HD, (head + 1) * HD)
-            joint, delta = joint_stats(all_ref, refs, me[0], sample, entries, slots, head, heads)
+            joint = joint_ref[sample, head : head + 1]
+            delta = joint_ref[sample, heads + head : heads + head + 1]
             queries = head_rows(q_ref[sample], head, group)
             grads = head_rows(g_ref[sample], head, group)
             keys = k_ref[sample, :, lanes]
@@ -360,21 +355,21 @@
                 dq_ref[sample, :, column : column + HD] = dq[r * rows : (r + 1) * rows]
 
 
-def own_grads(refs, me, question_q, question_grad, keys, values, stats, group, slots):
+def own_grads(question_q, question_grad, keys, values, joint, group):
     samples, rows, width = question_q.shape
     heads = keys.shape[2] // HD
     return pl.pallas_call(
-        functools.partial(own_grads_kernel, group, slots),
+        functools.partial(own_grads_kernel, group),
         out_shape=(
             jax.ShapeDtypeStruct((heads, samples * rows, 2 * HD), BF16),
             jax.ShapeDtypeStruct((samples, rows, width), F32),
         ),
-        in_specs=[smem(), smem()] + [whole()] * 5,
+        in_specs=[whole()] * 5,
         out_specs=(whole(), whole()),
         compiler_params=params(),
         cost_estimate=cost(3 * 10**8, 3 * 2**20, 10**5),
         name="own_grads",
-    )(refs, me, question_q, question_grad, keys, values, stats)
+    )(question_q, question_grad, keys, values, joint)
 
 
 def sum_dq_kernel(heads, owners, *refs):
@@ -461,63 +456,97 @@
     )(core, mine_p, other_p, mine_q, other_q)
 
 
-def weight_kernel(h_ref, p_ref, q_ref, out_ref):
+def weight_block(h_ref, place, p_ref, q_ref, sums):
+    count, _, _ = h_ref.shape
     split = p_ref.shape[0]
-    for one in range(h_ref.shape[0]):
-        total = jnp.dot(h_ref[one, :, :split], p_ref[...], preferred_element_type=F32)
-        total = total + jnp.dot(h_ref[one, :, split:], q_ref[...], preferred_element_type=F32)
-        out_ref[one] = total.astype(BF16)
-
-
-def weight_terms(hidden_t, grads_pass, grads_query, head):
-    groups, share, tokens = hidden_t.shape
+    group = lax.rem(lax.axis_index("pass") + (place + count), count)
+    total = jnp.dot(h_ref[group, :, :split], p_ref[...], preferred_element_type=F32)
+    total = total + jnp.dot(h_ref[group, :, split:], q_ref[...], preferred_element_type=F32)
+    for one in sums:
+        total = total + one[...].astype(F32)
+    return total.astype(BF16)
+
+
+def weight_kernel(places, arrived, h_ref, p_ref, q_ref, *refs):
+    sums, outs = list(refs[: -len(places)]), refs[-len(places) :]
+    for place, extra, out_ref in zip(places, arrived, outs):
+        out_ref[...] = weight_block(h_ref, place, p_ref, q_ref, [sums.pop(0) for _ in range(extra)])
+
+
+def weight_blocks(hidden_t, grads_pass, grads_query, places, arrived, name):
+    _, share, tokens = hidden_t.shape
     width = grads_pass.shape[1]
-    per = 2
-    return pl.pallas_call(
-        weight_kernel,
-        out_shape=jax.ShapeDtypeStruct((groups, share, width), BF16),
-        grid=(groups // per,),
-        in_specs=[
-            pl.BlockSpec((per, share, tokens), lambda i: (i, 0, 0)),
-            whole(),
-            whole(),
-        ],
-        out_specs=pl.BlockSpec((per, share, width), lambda i: (i, 0, 0)),
-        compiler_params=params(),
-        cost_estimate=cost(2 * groups * share * tokens * width, 8 * 2**20),
-        name=f"weight_terms_{head}",
-    )(hidden_t, grads_pass, grads_query)
-
-
-def add_low(one, other):
-    return (one.astype(F32) + other.astype(F32)).astype(BF16)
-
-
-def reduce_over_pass(sets):
-    me = lax.axis_index("pass")
+    count = len(places)
+    extras = [one for block in arrived for one in block]
+    return pl.pallas_call(
+        functools.partial(weight_kernel, places, tuple(len(block) for block in arrived)),
+        out_shape=tuple(jax.ShapeDtypeStruct((share, width), BF16) for _ in range(count)),
+        in_specs=[whole()] * (3 + len(extras)),
+        out_specs=tuple(whole() for _ in range(count)),
+        compiler_params=params(),
+        cost_estimate=cost(2 * count * share * tokens * width, 2 * count * share * 2 * width),
+        name=name,
+    )(hidden_t, grads_pass, grads_query, *extras)
+
+
+def last_kernel(h_ref, *refs):
+    out_ref = refs[-1]
+    per = 4
+    for head in range((len(refs) - 1) // per):
+        p_ref, q_ref, ahead, behind = refs[head * per : (head + 1) * per]
+        width = p_ref.shape[1]
+        out_ref[:, head * width : (head + 1) * width] = weight_block(
+            h_ref, 0, p_ref, q_ref, [ahead, behind]
+        )
+
+
+def last_blocks(hidden_t, chains):
+    _, share, tokens = hidden_t.shape
+    width = sum(chain[0].shape[1] for chain in chains)
+    operands = [one for chain in chains for one in chain]
+    return pl.pallas_call(
+        last_kernel,
+        out_shape=jax.ShapeDtypeStruct((share, width), BF16),
+        in_specs=[whole()] * (1 + len(operands)),
+        out_specs=whole(),
+        compiler_params=params(),
+        cost_estimate=cost(2 * share * tokens * width, 2 * share * 3 * width),
+        name="weights_last",
+    )(hidden_t, *operands)
+
+
+def ring(head):
     count = lax.axis_size("pass")
-    right = [(i, (i + 1) % count) for i in range(count)]
-    left = [(i, (i - 1) % count) for i in range(count)]
-    far = count // 2
-
-    def pick(one, distance):
-        return lax.dynamic_index_in_dim(one, lax.rem(me + distance + count, count), 0, False)
-
-    ahead = [pick(one, far) for one in sets]
-    behind = [pick(one, 1 - far) for one in sets]
-    for distance in range(far - 1, -1, -1):
-        for i, one in enumerate(sets):
-            ahead[i] = lax.ppermute(ahead[i], "pass", right)
-            if distance:
-                ahead[i] = add_low(ahead[i], pick(one, distance))
-            if distance < far - 1:
-                behind[i] = lax.ppermute(behind[i], "pass", left)
-                if distance:
-                    behind[i] = add_low(behind[i], pick(one, -distance))
-    return [
-        (a.astype(F32) + b.astype(F32) + pick(one, 0).astype(F32)).astype(BF16)
-        for a, b, one in zip(ahead, behind, sets)
-    ]
+    sign = 1 if head % 2 == 0 else -1
+    ahead_to = [(i, (i + sign) % count) for i in range(count)]
+    behind_to = [(i, (i - sign) % count) for i in range(count)]
+    return sign, ahead_to, behind_to
+
+
+def farthest(hidden_t, grads_pass, grads_query, head):
+    sign, ahead_to, _ = ring(head)
+    far = lax.axis_size("pass") // 2
+    (block,) = weight_blocks(
+        hidden_t, grads_pass, grads_query, (sign * far,), ([],), f"weights_{head}_{far}"
+    )
+    return block, lax.ppermute(block, "pass", ahead_to)
+
+
+def sums_over_pass(hidden_t, grads_pass, grads_query, ahead, head):
+    sign, ahead_to, behind_to = ring(head)
+    behind = []
+    for distance in range(lax.axis_size("pass") // 2 - 1, 0, -1):
+        sums = weight_blocks(
+            hidden_t,
+            grads_pass,
+            grads_query,
+            (sign * distance, -sign * distance),
+            ([ahead], behind),
+            f"weights_{head}_{distance}",
+        )
+        ahead = lax.ppermute(sums[0], "pass", ahead_to)
+        behind = [lax.ppermute(sums[1], "pass", behind_to)]
+    return ahead, behind[0]
 
 
 def finish_kernel(heads, x_ref, out_ref):
@@ -557,7 +586,6 @@
     passage_blocks,
 ):
     me = lax.axis_index("dp")
-    me_array = me.reshape(1)
     peers = lax.axis_size("dp")
     groups = lax.axis_size("pass")
     cores = lax.axis_size("tensor")
@@ -574,13 +602,11 @@
     def from_partner(x):
         return lax.ppermute(x, "tensor", [(i, cores - 1 - i) for i in range(cores)])
 
-    packed = pack_queries(refs, me_array, question_q, question_grad, slots)
+    packed = pack_queries(refs, question_q, question_grad, slots)
     got = exchange(packed)
 
     hit = quotient(refs, slots) == me
     slot_of = jnp.sum(jnp.where(hit, lax.rem(refs, jnp.int32(slots)), 0), axis=1)
-    order = jnp.arange(refs.shape[1], dtype=jnp.int32)
-    entry_of = jnp.sum(jnp.where(hit, order[None, :], 0), axis=1)
     owners = quotient(lax.dynamic_index_in_dim(refs, me, 0, keepdims=False), slots)
     blocks = lax.dynamic_index_in_dim(passage_blocks, me, 0, keepdims=False).reshape(slots)
     keys, values = passage_kv[:, :, 0], passage_kv[:, :, 1]
@@ -597,24 +623,34 @@
         peers,
         groups,
     )
-    got, hidden_t, own, keys, values = lax.optimization_barrier(
-        (got, hidden_t, own, keys, values)
-    )
-
-    stats = exchange(owner_stats(slot_of, blocks, got, keys, values, own, group))
+    got, hidden_t, own = lax.optimization_barrier((got, hidden_t, own))
+
+    stats = exchange(owner_stats(slot_of, blocks, got, keys, values, group))
+    back, merged = merge(refs, stats, own, slots)
+    joint = exchange(back)
     grads_query, own_dq = own_grads(
-        refs, me_array, question_q, question_grad, own_keys, own_values, stats, group, slots
-    )
-    grads_pass, dq_parts, terms = [], [], []
+        question_q, question_grad, own_keys, own_values, merged, group
+    )
+    joint, grads_query, own_dq = lax.optimization_barrier((joint, grads_query, own_dq))
+    grads_pass, first = [], []
+    dq_parts = None
     for head in range(heads):
-        one, dq = owner_grads(
-            head, slot_of, blocks, refs, entry_of, got, stats, keys, values, group
+        one, dq_parts = owner_grads(
+            head, slot_of, blocks, got, joint, keys, values, dq_parts, group
         )
         grads_pass.append(one)
-        dq_parts.append(dq)
-        terms.append(weight_terms(hidden_t, one, grads_query[head], head))
-    summed = jnp.concatenate(reduce_over_pass(terms), axis=-1)
-    returned = exchange(jnp.concatenate(dq_parts, axis=-1))
+        block, ahead = farthest(hidden_t, one, grads_query[head], head)
+        first.append(ahead)
+        dq_parts, _ = lax.optimization_barrier((dq_parts, block))
+    returned = exchange(dq_parts)
+    chains = []
+    for head in range(heads):
+        ends = sums_over_pass(
+            hidden_t, grads_pass[head], grads_query[head], first[head], head
+        )
+        chains.append((grads_pass[head], grads_query[head], *ends))
+    summed = last_blocks(hidden_t, chains)
+    summed, returned = lax.optimization_barrier((summed, returned))
     question_dq = sum_dq(owners, [returned], own_dq)
 
     share = summed.shape[0] // (peers * cores)

time: 257 us -> 204 us (0.79)
  waiting for transfers between devices: 118 us -> 83 us
  other arithmetic: 19.9 us -> 2.27 us
  blocking collectives: 0 us -> 10.6 us
  local copies, waits for them, and re-layouts: 24.1 us -> 13.6 us
  Pallas kernels: 45.9 us -> 42.4 us
  starting transfers between devices: 47.4 us -> 50.1 us
    all_to_all x3, waiting for transfers between devices: 95.3 us -> 52.3 us  [exchange(): return lax.all_to_all(x, 'dp', split_axis=0, concat_axis=0, tiled=True)]
    convert_element_type x8 -> x0, other arithmetic: 13.4 us -> none  [the longest x6 11.1 us: add_low(): return (one.astype(F32) + other.astype(F32)).astype(BF16)]
    all_to_all x0 -> x1, blocking collectives: none -> 10.6 us  [exchange(): return lax.all_to_all(x, 'dp', split_axis=0, concat_axis=0, tiled=True)]
    ppermute x14, waiting for transfers between devices: 13.3 us -> 22.9 us  [the longest x6 12.3 us: sums_over_pass(): ahead = lax.ppermute(sums[0], 'pass', ahead_to)]
    unnamed x68 -> x52, local copies, waits for them, and re-layouts: 17.5 us -> 10.7 us
    all_to_all x1, waiting for transfers between devices: 8.9 us -> 5 us  [local(): lax.all_to_all(summed.reshape(peers * cores, share, -1), ('dp', 'tensor')...]
    concatenate x2 -> x0, other arithmetic: 3.59 us -> none  [the longest x1 2.75 us: local(): returned = exchange(jnp.concatenate(dq_parts, axis=-1))]
    pallas_call x5 -> x13, Pallas kernels: 26.5 us -> 23.4 us  [the longest x2 14.7 us: owner_grads(): pl.pallas_call(functools.partial(owner_grads_kernel, group, head), out_sh...]
  transfers between devices with their start and end apart: 20 -> 20, of which waited for: 12 -> 13; matrix products, arithmetic and copies ran while one was open for 9% -> 2% of each run, Pallas kernels for 8% -> 7%
where the time goes in v3:
time: 204 us; the launch traced here: 203 us
  waiting for transfers between devices  83 us (41%)
  starting transfers between devices  50.1 us (25%)
  Pallas kernels  42.4 us (21%)
  local copies, waits for them, and re-layouts  13.6 us (7%)
  blocking collectives  10.6 us (5%)
  other arithmetic  2.27 us (1%)
    all_to_all x3, waiting for transfers between devices, exchange(): return lax.all_to_all(x, 'dp', split_axis=0, concat_axis=0, tiled=True)  52.3 us
    all_to_all x3, starting transfers between devices, exchange(): return lax.all_to_all(x, 'dp', split_axis=0, concat_axis=0, tiled=True)  15 us
    pallas_call x2, Pallas kernels, owner_grads(): pl.pallas_call(functools.partial(owner_grads_kernel, group, head), out_sh...  14.7 us
    all_to_all x1, starting transfers between devices, local(): lax.all_to_all(summed.reshape(peers * cores, share, -1), ('dp', 'tensor')...  13.6 us
    ppermute x6, waiting for transfers between devices, sums_over_pass(): ahead = lax.ppermute(sums[0], 'pass', ahead_to)  12.3 us
    ppermute x6, starting transfers between devices, sums_over_pass(): behind = [lax.ppermute(sums[1], 'pass', behind_to)]  11 us
    unnamed x52, local copies, waits for them, and re-layouts  10.7 us
    all_to_all x1, blocking collectives, exchange(): return lax.all_to_all(x, 'dp', split_axis=0, concat_axis=0, tiled=True)  10.6 us
  transfers between devices with their start and end apart: 20, of which 13 were waited for; matrix products, arithmetic and copies ran while one was open for 2% of the time, Pallas kernels for 7%

profile of v3, /device:TPU:1, one launch (start us, length us, event | category | flops | bytes accessed | tf_op | source)
XLA Modules:
  0.0 203.2 jit_solution(6290817740443916736)
XLA Ops:
  0.6 4.2 %pack_queries.1 = bf16[16,64,2048]{2,1,0:T(8,128)(2,1)} custom-call(s32[16,16]{1,0:T(8,128)} %bitcast.30, bf16[4,32,2048]{2,1,0:T(8,128)(2,1)} %q_ref.5, bf16[4,32,2048]{2,1,0:T(8,128)(2,1)} %g_ref.5), custom_call_target="tpu_custom_call" | custom-call | bytes 6291456 | tf_op jit(solution)/shard_map/pack_queries/pallas_call | solution.py:89
  4.9 7.7 %all-to-all-start = ((bf16[16,64,2048]{2,1,0:T(8,128)(2,1)}), bf16[16,64,2048]{2,1,0:T(8,128)(2,1)}, u32[]{:S(2)}, u32[]{:S(2)}) async-start(bf16[16,64,2048]{2,1,0:T(8,128)(2,1)} %pack_queries.1), calls=%async_computation | async-start | bytes 8388608 | tf_op jit(solution)/shard_map/all_to_all | solution.py:600
  12.6 1.0 collective-permute-start
  14.9 0.7 fusion.4
  15.7 2.3 %collective-permute-done.1 = bf16[4,16,4096]{2,1,0:T(8,128)(2,1)S(1)} collective-permute-done((bf16[4,16,4096]{2,1,0:T(8,128)(2,1)S(1)}, bf16[4,16,4096]{2,1,0:T(8,128)(2,1)S(1)}, u32[]{:S(2)}, u32[]{:S(2)}) %collective-permute-start.1) | collective-permute-done | bytes 524320 | tf_op jit(solution)/shard_map/ppermute | solution.py:603
  18.6 5.4 %transpose_hidden.1.h_ref = bf16[8,512,640]{2,1,0:T(8,128)(2,1)S(1)} custom-call(s32[1]{0:T(128)} %bitcast.2.core, bf16[256,4096]{1,0:T(8,128)(2,1)S(1)} %bitcast.27, bf16[256,4096]{1,0:T(8,128)(2,1)} %bitcast.4.other_p, bf16[64,4096]{1,0:T(8,128)(2,1)S(1)} %bitcast.28, bf16[64,4096]{1,0:T(8,128)(2,1)S(1)} %bitcast.29), custom_call_target="tpu_custom_call" | custom-call | bytes 12582912 | tf_op jit(solution)/shard_map/transpose_hidden/pallas_call | solution.py:441
  24.0 2.3 %copy-done.1 = bf16[8,512,640]{2,1,0:T(8,128)(2,1)} copy-done((bf16[8,512,640]{2,1,0:T(8,128)(2,1)}, bf16[8,512,640]{2,1,0:T(8,128)(2,1)S(1)}, u32[]{:S(2)}) %copy-start.1) | copy-done | bytes 5242904
  26.3 48.7 %all-to-all-done.got_ref = bf16[16,64,2048]{2,1,0:T(8,128)(2,1)} async-done(((bf16[16,64,2048]{2,1,0:T(8,128)(2,1)}), bf16[16,64,2048]{2,1,0:T(8,128)(2,1)}, u32[]{:S(2)}, u32[]{:S(2)}) %all-to-all-start) | async-done | bytes 4194336 | tf_op jit(solution)/shard_map/all_to_all | solution.py:600
  75.0 6.1 %owner_stats.1 = f32[16,4,256]{2,1,0:T(4,128)S(1)} custom-call(s32[16]{0:T(128)S(1)} %fusion.2.slot_of, s32[2]{0:T(128)S(1)} %dynamic-slice_reduce_fusion.blocks, bf16[16,64,2048]{2,1,0:T(8,128)(2,1)} %all-to-all-done.got_ref, bf16[2,256,256]{2,1,0:T(8,128)(2,1)S(1)} %get-tuple-element.75.k_ref, bf16[2,256,256]{2,1,0:T(8,128)(2,1)S(1)} %get-tuple-element.74.v_ref), custom_call_target="tpu_custom_call" | custom-call | flops 2000000000 | bytes 6291456 | tf_op jit(solution)/shard_map/owner_stats/pallas_call | solution.py:153
  81.1 10.6 %all_to_all.25.st_ref = f32[16,4,256]{2,1,0:T(4,128)S(1)} all-to-all(f32[16,4,256]{2,1,0:T(4,128)S(1)} %owner_stats.1), channel_id=1, replica_groups=mesh['dp'=16,'pass'=8,'tensor'=2] {'dp'}, dimensions={0} | all-to-all | bytes 131072 | tf_op jit(solution)/shard_map/all_to_all | solution.py:600
  91.7 1.4 merge_stats.1
  93.1 3.5 %all-to-all-start.2 = ((f32[16,4,256]{2,1,0:T(4,128)}), f32[16,4,256]{2,1,0:T(4,128)S(1)}, u32[]{:S(2)}, u32[]{:S(2)}) async-start(f32[16,4,256]{2,1,0:T(4,128)} %get-tuple-element.37), calls=%async_computation.2 | async-start | bytes 131072 | tf_op jit(solution)/shard_map/all_to_all | solution.py:600
  96.6 1.9 own_grads.1
  98.5 1.0 copy-done.7
  99.4 3.6 %all-to-all-done.2.joint_ref = f32[16,4,256]{2,1,0:T(4,128)S(1)} async-done(((f32[16,4,256]{2,1,0:T(4,128)}), f32[16,4,256]{2,1,0:T(4,128)S(1)}, u32[]{:S(2)}, u32[]{:S(2)}) %all-to-all-start.2) | async-done | bytes 65568 | tf_op jit(solution)/shard_map/all_to_all | solution.py:600
  103.1 0.7 fusion.5
  103.7 1.4 copy-done.11
  105.1 0.7 copy-done.17
  105.8 7.3 %owner_grads_0.1 = (bf16[512,256]{1,0:T(8,128)(2,1)S(1)}, bf16[16,32,2048]{2,1,0:T(8,128)(2,1)S(1)}) custom-call(s32[16]{0:T(128)S(1)} %fusion.2.slot_of, s32[2]{0:T(128)S(1)} %copy-done.17, bf16[16,64,2048]{2,1,0:T(8,128)(2,1)} %all-to-all-done.got_ref, f32[16,4,256]{2,1,0:T(4,128)S(1)} %all-to-all-done.2.joint_ref, bf16[2,256,256]{2,1,0:T(8,128)(2,1)S(1)} %copy-done.11, ...), custom_call_target="tpu_custom_call" | custom-call | flops 5000000000 | bytes 8388608 | tf_op jit(solution)/shard_map/owner_grads_0/pallas_call | solution.py:307
  113.5 0.6 copy-done.12
  114.1 7.3 %owner_grads_1.1 = (bf16[512,256]{1,0:T(8,128)(2,1)S(1)}, bf16[16,32,2048]{2,1,0:T(8,128)(2,1)S(1)}) custom-call(s32[16]{0:T(128)S(1)} %fusion.2.slot_of, s32[2]{0:T(128)S(1)} %copy-done.18, bf16[16,64,2048]{2,1,0:T(8,128)(2,1)} %all-to-all-done.got_ref, f32[16,4,256]{2,1,0:T(4,128)S(1)} %copy-done.15, ...), custom_call_target="tpu_custom_call", output_to_operand_aliasing={{1}: (6, {})} | custom-call | flops 5000000000 | bytes 8388608 | tf_op jit(solution)/shard_map/owner_grads_1/pallas_call | solution.py:307
  121.8 1.0 copy-done.5
  122.8 3.7 %all-to-all-start.3 = ((bf16[16,32,2048]{2,1,0:T(8,128)(2,1)}), bf16[16,32,2048]{2,1,0:T(8,128)(2,1)S(1)}, u32[]{:S(2)}, u32[]{:S(2)}) async-start(bf16[16,32,2048]{2,1,0:T(8,128)(2,1)} %copy-done.5), calls=%async_computation.3 | async-start | bytes 4194304 | tf_op jit(solution)/shard_map/all_to_all | solution.py:600
  126.5 5.7 %collective-permute-start.9 = (bf16[512,256]{1,0:T(8,128)(2,1)S(1)}, bf16[512,256]{1,0:T(8,128)(2,1)S(1)}, u32[]{:S(2)}, u32[]{:S(2)}) collective-permute-start(bf16[512,256]{1,0:T(8,128)(2,1)S(1)} %weights_1_4.1), channel_id=1, source_target_pairs={{0,14},{2,0},{4,2},{6,4},{8,6},{10,8},{12,10},{14,12},{1,15},{3,1}... | collective-permute-start | bytes 786440 | tf_op jit(solution)/shard_map/ppermute | solution.py:532
  132.2 3.3 %collective-permute-done.9.refs_0_ = bf16[512,256]{1,0:T(8,128)(2,1)S(1)} collective-permute-done((bf16[512,256]{1,0:T(8,128)(2,1)S(1)}, bf16[512,256]{1,0:T(8,128)(2,1)S(1)}, u32[]{:S(2)}, u32[]{:S(2)}) %collective-permute-start.9) | collective-permute-done | bytes 262176 | tf_op jit(solution)/shard_map/ppermute | solution.py:532
  135.5 2.5 %copy-done.2 = bf16[8,512,640]{2,1,0:T(8,128)(2,1)S(1)} copy-done((bf16[8,512,640]{2,1,0:T(8,128)(2,1)S(1)}, bf16[8,512,640]{2,1,0:T(8,128)(2,1)}, u32[]{:S(2)}) %copy-start.2) | copy-done | bytes 5242904
  138.6 3.4 %collective-permute-start.10 = (bf16[512,256]{1,0:T(8,128)(2,1)S(1)}, bf16[512,256]{1,0:T(8,128)(2,1)S(1)}, u32[]{:S(2)}, u32[]{:S(2)}) collective-permute-start(bf16[512,256]{1,0:T(8,128)(2,1)S(1)} %get-tuple-element.53), channel_id=1, source_target_pairs={{0,14},{2,0},{4,2},{6,4},{8,6},{10,8},{12,10},{14,12},{1,15},{3,1}... | collective-permute-start | bytes 786440 | tf_op jit(solution)/shard_map/ppermute | solution.py:547
  142.6 2.7 %collective-permute-start.4 = (bf16[512,256]{1,0:T(8,128)(2,1)S(1)}, bf16[512,256]{1,0:T(8,128)(2,1)S(1)}, u32[]{:S(2)}, u32[]{:S(2)}) collective-permute-start(bf16[512,256]{1,0:T(8,128)(2,1)S(1)} %get-tuple-element.45), channel_id=1, source_target_pairs={{0,14},{2,0},{4,2},{6,4},{8,6},{10,8},{12,10},{14,12},{1,15},{3,1}... | collective-permute-start | bytes 786440 | tf_op jit(solution)/shard_map/ppermute | solution.py:548
  145.4 3.3 %collective-permute-done.11.refs_1_ = bf16[512,256]{1,0:T(8,128)(2,1)S(1)} collective-permute-done((bf16[512,256]{1,0:T(8,128)(2,1)S(1)}, bf16[512,256]{1,0:T(8,128)(2,1)S(1)}, u32[]{:S(2)}, u32[]{:S(2)}) %collective-permute-start.11) | collective-permute-done | bytes 262176 | tf_op jit(solution)/shard_map/ppermute | solution.py:548
  149.3 1.5 collective-permute-start.13
  150.8 0.7 collective-permute-done.3.refs_0_
  152.2 2.7 %collective-permute-start.6 = (bf16[512,256]{1,0:T(8,128)(2,1)S(1)}, bf16[512,256]{1,0:T(8,128)(2,1)S(1)}, u32[]{:S(2)}, u32[]{:S(2)}) collective-permute-start(bf16[512,256]{1,0:T(8,128)(2,1)S(1)} %get-tuple-element.47), channel_id=1, source_target_pairs={{0,14},{2,0},{4,2},{6,4},{8,6},{10,8},{12,10},{14,12},{1,15},{3,1}... | collective-permute-start | bytes 786440 | tf_op jit(solution)/shard_map/ppermute | solution.py:548
  154.8 2.5 %collective-permute-done.12.refs_0_ = bf16[512,256]{1,0:T(8,128)(2,1)S(1)} collective-permute-done((bf16[512,256]{1,0:T(8,128)(2,1)S(1)}, bf16[512,256]{1,0:T(8,128)(2,1)S(1)}, u32[]{:S(2)}, u32[]{:S(2)}) %collective-permute-start.12) | collective-permute-done | bytes 262176 | tf_op jit(solution)/shard_map/ppermute | solution.py:547
  157.3 1.7 collective-permute-done.13.refs_1_
  159.6 1.5 collective-permute-start.15
  161.1 3.5 %collective-permute-done.5.refs_0_ = bf16[512,256]{1,0:T(8,128)(2,1)S(1)} collective-permute-done((bf16[512,256]{1,0:T(8,128)(2,1)S(1)}, bf16[512,256]{1,0:T(8,128)(2,1)S(1)}, u32[]{:S(2)}, u32[]{:S(2)}) %collective-permute-start.5) | collective-permute-done | bytes 262176 | tf_op jit(solution)/shard_map/ppermute | solution.py:547
  165.2 2.7 %collective-permute-start.8 = (bf16[512,256]{1,0:T(8,128)(2,1)S(1)}, bf16[512,256]{1,0:T(8,128)(2,1)S(1)}, u32[]{:S(2)}, u32[]{:S(2)}) collective-permute-start(bf16[512,256]{1,0:T(8,128)(2,1)S(1)} %get-tuple-element.49), channel_id=1, source_target_pairs={{0,14},{2,0},{4,2},{6,4},{8,6},{10,8},{12,10},{14,12},{1,15},{3,1}... | collective-permute-start | bytes 786440 | tf_op jit(solution)/shard_map/ppermute | solution.py:548
  167.9 2.3 %collective-permute-done.15.refs_7_ = bf16[512,256]{1,0:T(8,128)(2,1)S(1)} collective-permute-done((bf16[512,256]{1,0:T(8,128)(2,1)S(1)}, bf16[512,256]{1,0:T(8,128)(2,1)S(1)}, u32[]{:S(2)}, u32[]{:S(2)}) %collective-permute-start.15) | collective-permute-done | bytes 262176 | tf_op jit(solution)/shard_map/ppermute | solution.py:548
  170.2 5.6 %collective-permute-done.7.refs_2_ = bf16[512,256]{1,0:T(8,128)(2,1)S(1)} collective-permute-done((bf16[512,256]{1,0:T(8,128)(2,1)S(1)}, bf16[512,256]{1,0:T(8,128)(2,1)S(1)}, u32[]{:S(2)}, u32[]{:S(2)}) %collective-permute-start.7) | collective-permute-done | bytes 262176 | tf_op jit(solution)/shard_map/ppermute | solution.py:547
  175.8 1.4 weights_last.1
  177.3 13.6 %all-to-all-start.4 = ((bf16[32,16,512]{2,1,0:T(8,128)(2,1)}), bf16[32,16,512]{2,1,0:T(8,128)(2,1)S(1)}, u32[]{:S(2)}, u32[]{:S(2)}) async-start(bf16[32,16,512]{2,1,0:T(8,128)(2,1)} %bitcast.13), calls=%async_computation.4 | async-start | bytes 1048576 | tf_op jit(solution)/shard_map/all_to_all | solution.py:657
  191.0 0.9 reshape_squeeze.6
  191.9 0.8 pad_maximum_fusion.1
  192.7 1.3 pad_maximum_fusion
  194.1 1.2 copy-done.8
  195.3 2.1 %sum_dq.1 = bf16[4,32,2048]{2,1,0:T(8,128)(2,1)} custom-call(s32[16]{0:T(128)S(1)} %compare_select_fusion.owners, bf16[16,32,2048]{2,1,0:T(8,128)(2,1)S(1)} %all-to-all-done.3.refs_0_.refs_1_.refs_2_.refs_3_, bf16[16,32,2048]{2,1,0:T(8,128)(2,1)S(1)} %all-to-all-done.3.refs_0_.refs_1_.refs_2_.refs_3_, ...), custom_call_target="tpu_custom_call" | custom-call | flops 2000000 | bytes 4194304 | tf_op jit(solution)/shard_map/sum_dq/pallas_call | solution.py:396
  197.4 5.0 %all-to-all-done.4 = bf16[32,16,512]{2,1,0:T(8,128)(2,1)S(1)} async-done(((bf16[32,16,512]{2,1,0:T(8,128)(2,1)}), bf16[32,16,512]{2,1,0:T(8,128)(2,1)S(1)}, u32[]{:S(2)}, u32[]{:S(2)}) %all-to-all-start.4) | async-done | bytes 524320 | tf_op jit(solution)/shard_map/all_to_all | solution.py:657
  202.4 0.7 finish_weights.1
  (80 shorter events, 6.5 us)
Async XLA Ops:
  0.6 13.5 %copy-start = (s32[16,1,2]{0,2,1:T(2,128)S(1)}, s32[16,1,2]{0,2,1:T(2,128)}, u32[]{:S(2)}) copy-start(s32[16,1,2]{0,2,1:T(2,128)} %param.15) | copy-start | bytes 388
  4.8 8.9 %copy-start.9 = (bf16[4,16,4096]{2,1,0:T(8,128)(2,1)S(1)}, bf16[4,16,4096]{2,1,0:T(8,128)(2,1)}, u32[]{:S(2)}) copy-start(bf16[4,16,4096]{2,1,0:T(8,128)(2,1)} %param.12) | copy-start | bytes 1572868
  4.8 9.0 %copy-start.13 = (s32[16,1,16]{2,1,0:T(1,128)S(1)}, s32[16,1,16]{2,1,0:T(1,128)}, u32[]{:S(2)}) copy-start(s32[16,1,16]{2,1,0:T(1,128)} %param.14) | copy-start | bytes 3076
  4.9 9.1 %copy-start.20 = (bf16[4,32,2,256]{3,2,1,0:T(2,128)(2,1)S(1)}, bf16[4,32,2,256]{3,2,1,0:T(2,128)(2,1)}, u32[]{:S(2)}) copy-start(bf16[4,32,2,256]{3,2,1,0:T(2,128)(2,1)} %param.10) | copy-start | bytes 393220
  4.9 9.5 %copy-start.3 = (bf16[4,32,2048]{2,1,0:T(8,128)(2,1)S(1)}, bf16[4,32,2048]{2,1,0:T(8,128)(2,1)}, u32[]{:S(2)}) copy-start(bf16[4,32,2048]{2,1,0:T(8,128)(2,1)} %q_ref.5) | copy-start | bytes 1572868
  4.9 9.5 %copy-start.4 = (bf16[4,32,2048]{2,1,0:T(8,128)(2,1)S(1)}, bf16[4,32,2048]{2,1,0:T(8,128)(2,1)}, u32[]{:S(2)}) copy-start(bf16[4,32,2048]{2,1,0:T(8,128)(2,1)} %g_ref.5) | copy-start | bytes 1572868
  4.9 70.1 %all-to-all-start = ((bf16[16,64,2048]{2,1,0:T(8,128)(2,1)}), bf16[16,64,2048]{2,1,0:T(8,128)(2,1)}, u32[]{:S(2)}, u32[]{:S(2)}) async-start(bf16[16,64,2048]{2,1,0:T(8,128)(2,1)} %pack_queries.1), calls=%async_computation | async-start | bytes 8388608 | tf_op jit(solution)/shard_map/all_to_all | solution.py:600
  12.6 2.2 %copy-start.19 = (bf16[2,256,2,256]{3,2,1,0:T(2,128)(2,1)S(1)}, bf16[2,256,2,256]{3,2,1,0:T(2,128)(2,1)}, u32[]{:S(2)}) copy-start(bf16[2,256,2,256]{3,2,1,0:T(2,128)(2,1)} %param.11) | copy-start | bytes 1572868
  12.6 5.9 %collective-permute-start = (bf16[2,128,4096]{2,1,0:T(8,128)(2,1)}, bf16[2,128,4096]{2,1,0:T(8,128)(2,1)}, u32[]{:S(2)}, u32[]{:S(2)}) collective-permute-start(bf16[2,128,4096]{2,1,0:T(8,128)(2,1)} %param.13), channel_id=1, source_target_pairs={{0,1},{1,0},{2,3},{3,2},{4,5},{5,4},{6,7},{7,6},{8,9},{9,8},{10,11... | collective-permute-start | bytes 6291464 | tf_op jit(solution)/shard_map/ppermute | solution.py:603
  13.7 4.4 %collective-permute-start.1 = (bf16[4,16,4096]{2,1,0:T(8,128)(2,1)S(1)}, bf16[4,16,4096]{2,1,0:T(8,128)(2,1)S(1)}, u32[]{:S(2)}, u32[]{:S(2)}) collective-permute-start(bf16[4,16,4096]{2,1,0:T(8,128)(2,1)S(1)} %copy-done.9), channel_id=1, source_target_pairs={{0,1},{1,0},{2,3},{3,2},{4,5},{5,4},{6,7},{7,6},{8,9},{9,8},{10,11... | collective-permute-start | bytes 1572872 | tf_op jit(solution)/shard_map/ppermute | solution.py:603
  14.3 60.6 %copy-start.16 = (s32[2]{0:T(128)}, s32[2]{0:T(128)S(1)}, u32[]{:S(2)}) copy-start(s32[2]{0:T(128)S(1)} %dynamic-slice_reduce_fusion.blocks) | copy-start | bytes 28
  14.9 3.7 %copy-start.6 = (bf16[2,128,4096]{2,1,0:T(8,128)(2,1)S(1)}, bf16[2,128,4096]{2,1,0:T(8,128)(2,1)}, u32[]{:S(2)}) copy-start(bf16[2,128,4096]{2,1,0:T(8,128)(2,1)} %param.13) | copy-start | bytes 6291460
  15.7 59.3 %copy-start.10 = (bf16[2,256,256]{2,1,0:T(8,128)(2,1)}, bf16[2,256,256]{2,1,0:T(8,128)(2,1)S(1)}, u32[]{:S(2)}) copy-start(bf16[2,256,256]{2,1,0:T(8,128)(2,1)S(1)} %get-tuple-element.75.k_ref) | copy-start | bytes 786436
  23.9 2.3 %copy-start.1 = (bf16[8,512,640]{2,1,0:T(8,128)(2,1)}, bf16[8,512,640]{2,1,0:T(8,128)(2,1)S(1)}, u32[]{:S(2)}) copy-start(bf16[8,512,640]{2,1,0:T(8,128)(2,1)S(1)} %transpose_hidden.1.h_ref) | copy-start | bytes 15728644
  93.1 10.0 %all-to-all-start.2 = ((f32[16,4,256]{2,1,0:T(4,128)}), f32[16,4,256]{2,1,0:T(4,128)S(1)}, u32[]{:S(2)}, u32[]{:S(2)}) async-start(f32[16,4,256]{2,1,0:T(4,128)} %get-tuple-element.37), calls=%async_computation.2 | async-start | bytes 131072 | tf_op jit(solution)/shard_map/all_to_all | solution.py:600
  98.5 1.0 copy-start.7
  103.1 10.0 %copy-start.14 = (f32[16,4,256]{2,1,0:T(4,128)}, f32[16,4,256]{2,1,0:T(4,128)S(1)}, u32[]{:S(2)}) copy-start(f32[16,4,256]{2,1,0:T(4,128)S(1)} %all-to-all-done.2.joint_ref) | copy-start | bytes 196612
  103.1 10.1 %slice-start = ((s8[5242880]{0:T(1024)(128)(4,1)}), s8[4194304]{0:T(1024)(128)(4,1)S(1)}, s32[]{:S(2)}) async-start(s8[5242880]{0:T(1024)(128)(4,1)} %bitcast.22), calls=%async_computation.5 | async-start | bytes 8388608
  103.7 1.4 copy-start.11
  105.1 0.7 copy-start.17
  105.8 7.4 %slice-start.1 = ((s8[5242880]{0:T(1024)(128)(4,1)}), s8[1048576]{0:T(1024)(128)(4,1)S(1)}, s32[]{:S(2)}) async-start(s8[5242880]{0:T(1024)(128)(4,1)} %bitcast.22), calls=%async_computation.6 | async-start | bytes 2097152
  113.1 1.0 copy-start.12
  113.2 0.9 copy-start.15
  113.2 0.9 copy-start.18
  121.5 1.3 copy-start.5
  122.8 54.5 %all-to-all-start.3 = ((bf16[16,32,2048]{2,1,0:T(8,128)(2,1)}), bf16[16,32,2048]{2,1,0:T(8,128)(2,1)S(1)}, u32[]{:S(2)}, u32[]{:S(2)}) async-start(bf16[16,32,2048]{2,1,0:T(8,128)(2,1)} %copy-done.5), calls=%async_computation.3 | async-start | bytes 4194304 | tf_op jit(solution)/shard_map/all_to_all | solution.py:600
  126.5 9.0 %collective-permute-start.9 = (bf16[512,256]{1,0:T(8,128)(2,1)S(1)}, bf16[512,256]{1,0:T(8,128)(2,1)S(1)}, u32[]{:S(2)}, u32[]{:S(2)}) collective-permute-start(bf16[512,256]{1,0:T(8,128)(2,1)S(1)} %weights_1_4.1), channel_id=1, source_target_pairs={{0,14},{2,0},{4,2},{6,4},{8,6},{10,8},{12,10},{14,12},{1,15},{3,1}... | collective-permute-start | bytes 786440 | tf_op jit(solution)/shard_map/ppermute | solution.py:532
  132.2 9.7 %collective-permute-start.2 = (bf16[512,256]{1,0:T(8,128)(2,1)S(1)}, bf16[512,256]{1,0:T(8,128)(2,1)S(1)}, u32[]{:S(2)}, u32[]{:S(2)}) collective-permute-start(bf16[512,256]{1,0:T(8,128)(2,1)S(1)} %weights_0_4.1), channel_id=1, source_target_pairs={{0,2},{2,4},{4,6},{6,8},{8,10},{10,12},{12,14},{14,0},{1,3},{3,5},... | collective-permute-start | bytes 786440 | tf_op jit(solution)/shard_map/ppermute | solution.py:532
  135.5 2.5 %copy-start.2 = (bf16[8,512,640]{2,1,0:T(8,128)(2,1)S(1)}, bf16[8,512,640]{2,1,0:T(8,128)(2,1)}, u32[]{:S(2)}) copy-start(bf16[8,512,640]{2,1,0:T(8,128)(2,1)} %copy-done.1) | copy-start | bytes 15728644
  138.6 6.8 %collective-permute-start.10 = (bf16[512,256]{1,0:T(8,128)(2,1)S(1)}, bf16[512,256]{1,0:T(8,128)(2,1)S(1)}, u32[]{:S(2)}, u32[]{:S(2)}) collective-permute-start(bf16[512,256]{1,0:T(8,128)(2,1)S(1)} %get-tuple-element.53), channel_id=1, source_target_pairs={{0,14},{2,0},{4,2},{6,4},{8,6},{10,8},{12,10},{14,12},{1,15},{3,1}... | collective-permute-start | bytes 786440 | tf_op jit(solution)/shard_map/ppermute | solution.py:547
  141.9 6.7 %collective-permute-start.11 = (bf16[512,256]{1,0:T(8,128)(2,1)S(1)}, bf16[512,256]{1,0:T(8,128)(2,1)S(1)}, u32[]{:S(2)}, u32[]{:S(2)}) collective-permute-start(bf16[512,256]{1,0:T(8,128)(2,1)S(1)} %get-tuple-element.54), channel_id=1, source_target_pairs={{0,2},{2,4},{4,6},{6,8},{8,10},{10,12},{12,14},{14,0},{1,3},{3,5},... | collective-permute-start | bytes 786440 | tf_op jit(solution)/shard_map/ppermute | solution.py:548
  142.5 9.0 %collective-permute-start.3 = (bf16[512,256]{1,0:T(8,128)(2,1)S(1)}, bf16[512,256]{1,0:T(8,128)(2,1)S(1)}, u32[]{:S(2)}, u32[]{:S(2)}) collective-permute-start(bf16[512,256]{1,0:T(8,128)(2,1)S(1)} %get-tuple-element.44), channel_id=1, source_target_pairs={{0,2},{2,4},{4,6},{6,8},{8,10},{10,12},{12,14},{14,0},{1,3},{3,5},... | collective-permute-start | bytes 786440 | tf_op jit(solution)/shard_map/ppermute | solution.py:547
  142.6 8.9 %collective-permute-start.4 = (bf16[512,256]{1,0:T(8,128)(2,1)S(1)}, bf16[512,256]{1,0:T(8,128)(2,1)S(1)}, u32[]{:S(2)}, u32[]{:S(2)}) collective-permute-start(bf16[512,256]{1,0:T(8,128)(2,1)S(1)} %get-tuple-element.45), channel_id=1, source_target_pairs={{0,14},{2,0},{4,2},{6,4},{8,6},{10,8},{12,10},{14,12},{1,15},{3,1}... | collective-permute-start | bytes 786440 | tf_op jit(solution)/shard_map/ppermute | solution.py:548
  149.2 8.1 %collective-permute-start.12 = (bf16[512,256]{1,0:T(8,128)(2,1)S(1)}, bf16[512,256]{1,0:T(8,128)(2,1)S(1)}, u32[]{:S(2)}, u32[]{:S(2)}) collective-permute-start(bf16[512,256]{1,0:T(8,128)(2,1)S(1)} %get-tuple-element.55), channel_id=1, source_target_pairs={{0,14},{2,0},{4,2},{6,4},{8,6},{10,8},{12,10},{14,12},{1,15},{3,1}... | collective-permute-start | bytes 786440 | tf_op jit(solution)/shard_map/ppermute | solution.py:547
  149.3 9.6 %collective-permute-start.13 = (bf16[512,256]{1,0:T(8,128)(2,1)S(1)}, bf16[512,256]{1,0:T(8,128)(2,1)S(1)}, u32[]{:S(2)}, u32[]{:S(2)}) collective-permute-start(bf16[512,256]{1,0:T(8,128)(2,1)S(1)} %get-tuple-element.56), channel_id=1, source_target_pairs={{0,2},{2,4},{4,6},{6,8},{8,10},{10,12},{12,14},{14,0},{1,3},{3,5},... | collective-permute-start | bytes 786440 | tf_op jit(solution)/shard_map/ppermute | solution.py:548
  151.5 24.3 %slice-start.2 = ((s8[5242880]{0:T(1024)(128)(4,1)}), s8[4194304]{0:T(1024)(128)(4,1)S(1)}, s32[]{:S(2)}) async-start(s8[5242880]{0:T(1024)(128)(4,1)} %bitcast.24), calls=%async_computation.7 | async-start | bytes 8388608
  152.1 12.5 %collective-permute-start.5 = (bf16[512,256]{1,0:T(8,128)(2,1)S(1)}, bf16[512,256]{1,0:T(8,128)(2,1)S(1)}, u32[]{:S(2)}, u32[]{:S(2)}) collective-permute-start(bf16[512,256]{1,0:T(8,128)(2,1)S(1)} %get-tuple-element.46), channel_id=1, source_target_pairs={{0,2},{2,4},{4,6},{6,8},{8,10},{10,12},{12,14},{14,0},{1,3},{3,5},... | collective-permute-start | bytes 786440 | tf_op jit(solution)/shard_map/ppermute | solution.py:547
  152.1 23.7 %slice-start.3 = ((s8[5242880]{0:T(1024)(128)(4,1)}), s8[1048576]{0:T(1024)(128)(4,1)S(1)}, s32[]{:S(2)}) async-start(s8[5242880]{0:T(1024)(128)(4,1)} %bitcast.24), calls=%async_computation.8 | async-start | bytes 2097152
  152.2 12.4 %collective-permute-start.6 = (bf16[512,256]{1,0:T(8,128)(2,1)S(1)}, bf16[512,256]{1,0:T(8,128)(2,1)S(1)}, u32[]{:S(2)}, u32[]{:S(2)}) collective-permute-start(bf16[512,256]{1,0:T(8,128)(2,1)S(1)} %get-tuple-element.47), channel_id=1, source_target_pairs={{0,14},{2,0},{4,2},{6,4},{8,6},{10,8},{12,10},{14,12},{1,15},{3,1}... | collective-permute-start | bytes 786440 | tf_op jit(solution)/shard_map/ppermute | solution.py:548
  159.5 8.4 %collective-permute-start.14 = (bf16[512,256]{1,0:T(8,128)(2,1)S(1)}, bf16[512,256]{1,0:T(8,128)(2,1)S(1)}, u32[]{:S(2)}, u32[]{:S(2)}) collective-permute-start(bf16[512,256]{1,0:T(8,128)(2,1)S(1)} %get-tuple-element.57), channel_id=1, source_target_pairs={{0,14},{2,0},{4,2},{6,4},{8,6},{10,8},{12,10},{14,12},{1,15},{3,1}... | collective-permute-start | bytes 786440 | tf_op jit(solution)/shard_map/ppermute | solution.py:547
  159.6 10.6 %collective-permute-start.15 = (bf16[512,256]{1,0:T(8,128)(2,1)S(1)}, bf16[512,256]{1,0:T(8,128)(2,1)S(1)}, u32[]{:S(2)}, u32[]{:S(2)}) collective-permute-start(bf16[512,256]{1,0:T(8,128)(2,1)S(1)} %get-tuple-element.58), channel_id=1, source_target_pairs={{0,2},{2,4},{4,6},{6,8},{8,10},{10,12},{12,14},{14,0},{1,3},{3,5},... | collective-permute-start | bytes 786440 | tf_op jit(solution)/shard_map/ppermute | solution.py:548
  165.2 10.7 %collective-permute-start.7 = (bf16[512,256]{1,0:T(8,128)(2,1)S(1)}, bf16[512,256]{1,0:T(8,128)(2,1)S(1)}, u32[]{:S(2)}, u32[]{:S(2)}) collective-permute-start(bf16[512,256]{1,0:T(8,128)(2,1)S(1)} %get-tuple-element.48), channel_id=1, source_target_pairs={{0,2},{2,4},{4,6},{6,8},{8,10},{10,12},{12,14},{14,0},{1,3},{3,5},... | collective-permute-start | bytes 786440 | tf_op jit(solution)/shard_map/ppermute | solution.py:547
  165.2 10.6 %collective-permute-start.8 = (bf16[512,256]{1,0:T(8,128)(2,1)S(1)}, bf16[512,256]{1,0:T(8,128)(2,1)S(1)}, u32[]{:S(2)}, u32[]{:S(2)}) collective-permute-start(bf16[512,256]{1,0:T(8,128)(2,1)S(1)} %get-tuple-element.49), channel_id=1, source_target_pairs={{0,14},{2,0},{4,2},{6,4},{8,6},{10,8},{12,10},{14,12},{1,15},{3,1}... | collective-permute-start | bytes 786440 | tf_op jit(solution)/shard_map/ppermute | solution.py:548
  177.3 14.6 %copy-start.21 = (bf16[1,128,256]{2,1,0:T(8,128)(2,1)S(1)}, bf16[1,128,256]{2,1,0:T(8,128)(2,1)}, u32[]{:S(2)}) copy-start(bf16[1,128,256]{2,1,0:T(8,128)(2,1)} %get-tuple-element.69) | copy-start | bytes 196612
  177.3 25.1 %all-to-all-start.4 = ((bf16[32,16,512]{2,1,0:T(8,128)(2,1)}), bf16[32,16,512]{2,1,0:T(8,128)(2,1)S(1)}, u32[]{:S(2)}, u32[]{:S(2)}) async-start(bf16[32,16,512]{2,1,0:T(8,128)(2,1)} %bitcast.13), calls=%async_computation.4 | async-start | bytes 1048576 | tf_op jit(solution)/shard_map/all_to_all | solution.py:657
  194.1 1.2 copy-start.8

commit v4 on v3

--- a/solution.py
+++ b/solution.py
@@ -14,6 +14,7 @@
 SCALE = HD ** (-0.5)
 SCALE_LOG2 = SCALE * math.log2(math.e)
 VMEM_LIMIT = 24 * 1024 * 1024
+VMEM_MOST = 60 * 1024 * 1024
 NT = (((1,), (1,)), ((), ()))
 TN = (((0,), (0,)), ((), ()))
 F32 = jnp.float32
@@ -96,7 +97,7 @@
             pltpu.SemaphoreType.DMA((samples, 2)),
             pltpu.SemaphoreType.DMA((peers,)),
         ],
-        compiler_params=params(60 * 1024 * 1024),
+        compiler_params=params(VMEM_MOST),
         cost_estimate=cost(0, 6 * 2**20),
         name="pack_queries",
     )(refs, question_q, question_grad)
@@ -115,29 +116,30 @@
     return top + jnp.log2(total), weighted / total
 
 
-def passage_valid(blocks, slot, slot_len, columns):
+def passage_valid(blocks, slot_len, columns):
     shape = (slot_len, columns)
-    return lax.broadcasted_iota(jnp.int32, shape, 0) < blocks[slot] * BLOCK
-
-
-def owner_stats_kernel(group, slot_of, blocks, got_ref, k_ref, v_ref, out_ref):
+    return lax.broadcasted_iota(jnp.int32, shape, 0) < blocks * BLOCK
+
+
+def owner_stats_kernel(group, table, got_ref, kv_ref, out_ref):
     step = pl.program_id(0)
     per, both, _ = got_ref.shape
+    peers = per * pl.num_programs(0)
     rows = both // 2
-    slot_len = k_ref.shape[1]
-    heads = k_ref.shape[2] // HD
+    slot_len = kv_ref.shape[2]
+    heads = kv_ref.shape[3] // HD
     columns = group * rows
     for one in range(per):
-        slot = slot_of[step * per + one]
-        valid = passage_valid(blocks, slot, slot_len, columns)
+        slot = table[step * per + one]
+        valid = passage_valid(table[peers + slot], slot_len, columns)
         logs, deltas = [], []
         for head in range(heads):
             lanes = slice(head * HD, (head + 1) * HD)
             queries = head_rows(got_ref[one, :rows], head, group)
             grads = head_rows(got_ref[one, rows:], head, group)
-            scores = scores_t(k_ref[slot, :, lanes], queries, valid)
+            scores = scores_t(kv_ref[0, slot, :, lanes], queries, valid)
             prob_grad = lax.dot_general(
-                v_ref[slot, :, lanes], grads, NT, preferred_element_type=F32
+                kv_ref[1, slot, :, lanes], grads, NT, preferred_element_type=F32
             )
             log, delta = part_stats(scores, prob_grad)
             logs.append(log)
@@ -145,28 +147,24 @@
         out_ref[one] = jnp.concatenate(logs + deltas, axis=0)
 
 
-def owner_stats(slot_of, blocks, got, keys, values, group):
+def owner_stats(table, got, kv, group):
     peers, both, width = got.shape
-    heads = keys.shape[2] // HD
+    heads = kv.shape[3] // HD
     columns = group * both // 2
     per = 4
     return pl.pallas_call(
         functools.partial(owner_stats_kernel, group),
         out_shape=jax.ShapeDtypeStruct((peers, 2 * heads, columns), F32),
         grid_spec=pltpu.PrefetchScalarGridSpec(
-            num_scalar_prefetch=2,
+            num_scalar_prefetch=1,
             grid=(peers // per,),
-            in_specs=[
-                pl.BlockSpec((per, both, width), lambda r, s, b: (r, 0, 0)),
-                whole(),
-                whole(),
-            ],
-            out_specs=pl.BlockSpec((per, 2 * heads, columns), lambda r, s, b: (r, 0, 0)),
+            in_specs=[pl.BlockSpec((per, both, width), lambda r, t: (r, 0, 0)), whole()],
+            out_specs=pl.BlockSpec((per, 2 * heads, columns), lambda r, t: (r, 0, 0)),
         ),
-        compiler_params=params(),
+        compiler_params=params(VMEM_MOST),
         cost_estimate=cost(2 * 10**9, 6 * 2**20, 2 * 10**6),
         name="owner_stats",
-    )(slot_of, blocks, got, keys, values)
+    )(table, got, kv)
 
 
 def own_valid(own_rows, rows, group):
@@ -250,27 +248,34 @@
     return probs.astype(BF16), dscore
 
 
-def owner_grads_kernel(group, head, slot_of, blocks, got_ref, joint_ref, k_ref, v_ref, *rest):
-    grad_ref, dq_ref, acc_ref = rest[-3:]
+def owner_grads_kernel(
+    group, head, places, table, got_ref, joint_ref, kv_ref, own_ref, hidden_ref, *rest
+):
+    grad_ref, dq_ref, *block_refs, acc_ref, h_ref, h_sem = rest[-5 - len(places) :]
+    load = pltpu.make_async_copy(hidden_ref, h_ref, h_sem)
     step = pl.program_id(0)
     per, both, _ = got_ref.shape
+    peers = per * pl.num_programs(0)
     rows = both // 2
-    slot_len = k_ref.shape[1]
-    heads = k_ref.shape[2] // HD
+    slot_len = kv_ref.shape[2]
+    heads = kv_ref.shape[3] // HD
     lanes = slice(head * HD, (head + 1) * HD)
 
     @pl.when(step == 0)
     def _():
+        load.start()
         acc_ref[...] = jnp.zeros_like(acc_ref)
 
     for one in range(per):
-        slot = slot_of[step * per + one]
-        valid = passage_valid(blocks, slot, slot_len, group * rows)
+        slot = table[step * per + one]
+        valid = passage_valid(table[peers + slot], slot_len, group * rows)
         queries = head_rows(got_ref[one, :rows], 0, group)
         grads = head_rows(got_ref[one, rows:], 0, group)
-        keys = k_ref[slot, :, lanes]
+        keys = kv_ref[0, slot, :, lanes]
         scores = scores_t(keys, queries, valid)
-        prob_grad = lax.dot_general(v_ref[slot, :, lanes], grads, NT, preferred_element_type=F32)
+        prob_grad = lax.dot_general(
+            kv_ref[1, slot, :, lanes], grads, NT, preferred_element_type=F32
+        )
         joint = joint_ref[one, head : head + 1]
         delta = joint_ref[one, heads + head : heads + head + 1]
         probs, dscore = probs_and_dscore(scores, prob_grad, joint, delta)
@@ -284,20 +289,25 @@
     def _():
         for one in range(acc_ref.shape[0]):
             grad_ref[one * slot_len : (one + 1) * slot_len] = acc_ref[one].astype(BF16)
-
-
-def owner_grads(head, slot_of, blocks, got, joint, keys, values, dq, group):
+        load.wait()
+        for place, block_ref in zip(places, block_refs):
+            block_ref[...] = weight_block(h_ref, place, grad_ref, own_ref, head)
+
+
+def owner_grads(head, places, table, got, joint, kv, hidden_t, grads_query, dq, group):
     peers, both, width = got.shape
-    slots, slot_len, _ = keys.shape
+    _, slots, slot_len, _ = kv.shape
     stat_rows, columns = joint.shape[1:]
+    share = hidden_t.shape[1]
     per = 4
     lanes = group * HD
-    operands = [slot_of, blocks, got, joint, keys, values]
+    operands = [table, got, joint, kv, grads_query, hidden_t]
     in_specs = [
-        pl.BlockSpec((per, both, lanes), lambda r, *_: (r, 0, head)),
-        pl.BlockSpec((per, stat_rows, columns), lambda r, *_: (r, 0, 0)),
+        pl.BlockSpec((per, both, lanes), lambda r, t: (r, 0, head)),
+        pl.BlockSpec((per, stat_rows, columns), lambda r, t: (r, 0, 0)),
         whole(),
         whole(),
+        in_hbm(),
     ]
     aliases = {}
     if dq is not None:
@@ -305,23 +315,29 @@
         operands.append(dq)
         in_specs.append(in_hbm())
     return pl.pallas_call(
-        functools.partial(owner_grads_kernel, group, head),
+        functools.partial(owner_grads_kernel, group, head, places),
         out_shape=(
             jax.ShapeDtypeStruct((slots * slot_len, 2 * HD), BF16),
             jax.ShapeDtypeStruct((peers, both // 2, width), BF16),
+            *[jax.ShapeDtypeStruct((share, 2 * HD), BF16) for _ in places],
         ),
         grid_spec=pltpu.PrefetchScalarGridSpec(
-            num_scalar_prefetch=2,
+            num_scalar_prefetch=1,
             grid=(peers // per,),
             in_specs=in_specs,
             out_specs=(
-                pl.BlockSpec((slots * slot_len, 2 * HD), lambda r, *_: (0, 0)),
-                pl.BlockSpec((per, both // 2, lanes), lambda r, *_: (r, 0, head)),
+                pl.BlockSpec((slots * slot_len, 2 * HD), lambda r, t: (0, 0)),
+                pl.BlockSpec((per, both // 2, lanes), lambda r, t: (r, 0, head)),
+                *[pl.BlockSpec((share, 2 * HD), lambda r, t: (0, 0)) for _ in places],
             ),
-            scratch_shapes=[pltpu.VMEM((slots, slot_len, 2 * HD), F32)],
+            scratch_shapes=[
+                pltpu.VMEM((slots, slot_len, 2 * HD), F32),
+                pltpu.VMEM(hidden_t.shape, BF16),
+                pltpu.SemaphoreType.DMA,
+            ],
         ),
         input_output_aliases=aliases,
-        compiler_params=params(),
+        compiler_params=params(VMEM_MOST),
         cost_estimate=cost(5 * 10**9, 8 * 2**20, 2 * 10**6),
         name=f"owner_grads_{head}",
     )(*operands)
@@ -450,103 +466,73 @@
             ],
             out_specs=pl.BlockSpec((groups, tile // groups, tokens), lambda i, c: (0, i, 0)),
         ),
-        compiler_params=params(),
+        compiler_params=params(VMEM_MOST),
         cost_estimate=cost(0, 12 * 2**20),
         name="transpose_hidden",
     )(core, mine_p, other_p, mine_q, other_q)
 
 
-def weight_block(h_ref, place, p_ref, q_ref, sums):
+def weight_block(h_ref, place, p_ref, q_ref, head):
     count, _, _ = h_ref.shape
     split = p_ref.shape[0]
     group = lax.rem(lax.axis_index("pass") + (place + count), count)
     total = jnp.dot(h_ref[group, :, :split], p_ref[...], preferred_element_type=F32)
-    total = total + jnp.dot(h_ref[group, :, split:], q_ref[...], preferred_element_type=F32)
-    for one in sums:
-        total = total + one[...].astype(F32)
+    total = total + jnp.dot(h_ref[group, :, split:], q_ref[head], preferred_element_type=F32)
     return total.astype(BF16)
 
 
-def weight_kernel(places, arrived, h_ref, p_ref, q_ref, *refs):
-    sums, outs = list(refs[: -len(places)]), refs[-len(places) :]
-    for place, extra, out_ref in zip(places, arrived, outs):
-        out_ref[...] = weight_block(h_ref, place, p_ref, q_ref, [sums.pop(0) for _ in range(extra)])
-
-
-def weight_blocks(hidden_t, grads_pass, grads_query, places, arrived, name):
-    _, share, tokens = hidden_t.shape
-    width = grads_pass.shape[1]
-    count = len(places)
-    extras = [one for block in arrived for one in block]
-    return pl.pallas_call(
-        functools.partial(weight_kernel, places, tuple(len(block) for block in arrived)),
-        out_shape=tuple(jax.ShapeDtypeStruct((share, width), BF16) for _ in range(count)),
-        in_specs=[whole()] * (3 + len(extras)),
-        out_specs=tuple(whole() for _ in range(count)),
+def add_kernel(*refs):
+    outs = refs[2 * (len(refs) // 3) + 1 :]
+    for k, out_ref in enumerate(outs):
+        total = refs[2 * k][...].astype(F32) + refs[2 * k + 1][...].astype(F32)
+        out_ref[...] = total.astype(BF16)
+
+
+def add_arrived(blocks, arrived, after, name):
+    return pl.pallas_call(
+        add_kernel,
+        out_shape=tuple(jax.ShapeDtypeStruct(one.shape, BF16) for one in blocks),
+        in_specs=[whole()] * (2 * len(blocks)) + [pl.BlockSpec(memory_space=pl.ANY)],
+        out_specs=tuple(whole() for _ in blocks),
         compiler_params=params(),
-        cost_estimate=cost(2 * count * share * tokens * width, 2 * count * share * 2 * width),
+        cost_estimate=cost(8 * 10**9, 2**20),
         name=name,
-    )(hidden_t, grads_pass, grads_query, *extras)
-
-
-def last_kernel(h_ref, *refs):
+    )(*[one for pair in zip(blocks, arrived) for one in pair], after)
+
+
+def last_kernel(*refs):
     out_ref = refs[-1]
-    per = 4
+    per = 3
     for head in range((len(refs) - 1) // per):
-        p_ref, q_ref, ahead, behind = refs[head * per : (head + 1) * per]
-        width = p_ref.shape[1]
-        out_ref[:, head * width : (head + 1) * width] = weight_block(
-            h_ref, 0, p_ref, q_ref, [ahead, behind]
-        )
-
-
-def last_blocks(hidden_t, chains):
-    _, share, tokens = hidden_t.shape
-    width = sum(chain[0].shape[1] for chain in chains)
-    operands = [one for chain in chains for one in chain]
+        total = sum(ref[...].astype(F32) for ref in refs[head * per : (head + 1) * per])
+        width = total.shape[1]
+        out_ref[:, head * width : (head + 1) * width] = total.astype(BF16)
+
+
+def last_sums(chains):
+    share, width = chains[0][0].shape
     return pl.pallas_call(
         last_kernel,
-        out_shape=jax.ShapeDtypeStruct((share, width), BF16),
-        in_specs=[whole()] * (1 + len(operands)),
+        out_shape=jax.ShapeDtypeStruct((share, len(chains) * width), BF16),
+        in_specs=[whole()] * (3 * len(chains)),
         out_specs=whole(),
         compiler_params=params(),
-        cost_estimate=cost(2 * share * tokens * width, 2 * share * 3 * width),
+        cost_estimate=cost(10**6, 2**21),
         name="weights_last",
-    )(hidden_t, *operands)
-
-
-def ring(head):
+    )(*[one for chain in chains for one in chain])
+
+
+def travel(blocks, head):
     count = lax.axis_size("pass")
-    sign = 1 if head % 2 == 0 else -1
-    ahead_to = [(i, (i + sign) % count) for i in range(count)]
-    behind_to = [(i, (i - sign) % count) for i in range(count)]
-    return sign, ahead_to, behind_to
-
-
-def farthest(hidden_t, grads_pass, grads_query, head):
-    sign, ahead_to, _ = ring(head)
-    far = lax.axis_size("pass") // 2
-    (block,) = weight_blocks(
-        hidden_t, grads_pass, grads_query, (sign * far,), ([],), f"weights_{head}_{far}"
-    )
-    return block, lax.ppermute(block, "pass", ahead_to)
-
-
-def sums_over_pass(hidden_t, grads_pass, grads_query, ahead, head):
-    sign, ahead_to, behind_to = ring(head)
-    behind = []
-    for distance in range(lax.axis_size("pass") // 2 - 1, 0, -1):
-        sums = weight_blocks(
-            hidden_t,
-            grads_pass,
-            grads_query,
-            (sign * distance, -sign * distance),
-            ([ahead], behind),
-            f"weights_{head}_{distance}",
-        )
-        ahead = lax.ppermute(sums[0], "pass", ahead_to)
-        behind = [lax.ppermute(sums[1], "pass", behind_to)]
-    return ahead, behind[0]
+    ways = [direction(head), -direction(head)]
+    return [
+        lax.ppermute(block, "pass", [(i, (i + way) % count) for i in range(count)])
+        for block, way in zip(blocks, ways)
+    ]
+
+
+def direction(head):
+    return 1 if head % 2 == 0 else -1
 
 
 def finish_kernel(heads, x_ref, out_ref):
@@ -609,7 +595,8 @@
     slot_of = jnp.sum(jnp.where(hit, lax.rem(refs, jnp.int32(slots)), 0), axis=1)
     owners = quotient(lax.dynamic_index_in_dim(refs, me, 0, keepdims=False), slots)
     blocks = lax.dynamic_index_in_dim(passage_blocks, me, 0, keepdims=False).reshape(slots)
-    keys, values = passage_kv[:, :, 0], passage_kv[:, :, 1]
+    table = jnp.concatenate([slot_of, blocks])
+    kv = jnp.transpose(passage_kv, (2, 0, 1, 3))
     own_keys, own_values = question_kv[:, :, 0], question_kv[:, :, 1]
     own = own_stats(question_q, question_grad, own_keys, own_values, group)
     hidden_t = transpose_hidden(
@@ -625,31 +612,46 @@
     )
     got, hidden_t, own = lax.optimization_barrier((got, hidden_t, own))
 
-    stats = exchange(owner_stats(slot_of, blocks, got, keys, values, group))
+    stats = exchange(owner_stats(table, got, kv, group))
     back, merged = merge(refs, stats, own, slots)
     joint = exchange(back)
     grads_query, own_dq = own_grads(
         question_q, question_grad, own_keys, own_values, merged, group
     )
     joint, grads_query, own_dq = lax.optimization_barrier((joint, grads_query, own_dq))
-    grads_pass, first = [], []
+    far = groups // 2
+    distances = list(range(far, 0, -1))
+    grads_pass, blocks_of, sums = [], [], []
     dq_parts = None
     for head in range(heads):
-        one, dq_parts = owner_grads(
-            head, slot_of, blocks, got, joint, keys, values, dq_parts, group
+        way = direction(head)
+        places = [way * one for one in distances] + [-way * one for one in distances[1:]] + [0]
+        one, dq_parts, *weights = owner_grads(
+            head, tuple(places), table, got, joint, kv, hidden_t, grads_query, dq_parts, group
         )
         grads_pass.append(one)
-        block, ahead = farthest(hidden_t, one, grads_query[head], head)
-        first.append(ahead)
-        dq_parts, _ = lax.optimization_barrier((dq_parts, block))
+        blocks_of.append(dict(zip([place * way for place in places], weights)))
+        sums.append(travel([blocks_of[head][far], blocks_of[head][1 - far]], head))
+    ends = [None] * heads
+    after = grads_pass[-1]
+    for distance in distances[1:]:
+        for head in range(heads):
+            places = [distance, 1 - distance]
+            if distance == 1:
+                places = places[:1]
+                ends[head] = sums[head][1]
+            added = add_arrived(
+                [blocks_of[head][place] for place in places],
+                sums[head][: len(places)],
+                after,
+                f"add_{head}_{distance}",
+            )
+            after = added[0]
+            sums[head] = travel(added, head)
+        if distance == far - 1:
+            dq_parts, after = lax.optimization_barrier((dq_parts, after))
     returned = exchange(dq_parts)
-    chains = []
-    for head in range(heads):
-        ends = sums_over_pass(
-            hidden_t, grads_pass[head], grads_query[head], first[head], head
-        )
-        chains.append((grads_pass[head], grads_query[head], *ends))
-    summed = last_blocks(hidden_t, chains)
+    summed = last_sums([(blocks_of[h][0], sums[h][0], ends[h]) for h in range(heads)])
     summed, returned = lax.optimization_barrier((summed, returned))
     question_dq = sum_dq(owners, [returned], own_dq)
 

time: 204 us -> 199 us (0.975)
  waiting for transfers between devices: 83 us -> 74.3 us
  Pallas kernels: 42.4 us -> 50.8 us
  local copies, waits for them, and re-layouts: 13.6 us -> 8.96 us
    ppermute x14, waiting for transfers between devices: 22.9 us -> 15.5 us  [travel(): lax.ppermute(block, 'pass', [(i, (i + way) % count) for i in range(count)])]
    pallas_call x11 -> x9, Pallas kernels: 20.2 us -> 25.5 us  [the longest x2 22.2 us: owner_grads(): pl.pallas_call(functools.partial(owner_grads_kernel, group, head, places)...]
    ppermute x14, starting transfers between devices: 20.5 us -> 17 us  [travel(): lax.ppermute(block, 'pass', [(i, (i + way) % count) for i in range(count)])]
    all_to_all x1, starting transfers between devices: 13.6 us -> 16 us  [local(): lax.all_to_all(summed.reshape(peers * cores, share, -1), ('dp', 'tensor')...]
    pallas_call x1, Pallas kernels: 5.37 us -> 7.67 us  [transpose_hidden(): pl.pallas_call(functools.partial(transpose_kernel, slots, samples, per),...]
    unnamed x52 -> x53, local copies, waits for them, and re-layouts: 10.7 us -> 8.38 us
  transfers between devices with their start and end apart: 20 -> 20, of which waited for: 13 -> 13; matrix products, arithmetic and copies ran while one was open for 2% -> 3% of each run, Pallas kernels for 7% -> 13%
where the time goes in v4:
time: 199 us; the launch traced here: 198 us
  waiting for transfers between devices  74.3 us (37%)
  Pallas kernels  50.8 us (26%)
  starting transfers between devices  49.2 us (25%)
  blocking collectives  10.8 us (5%)
  local copies, waits for them, and re-layouts  8.96 us (5%)
  other arithmetic  2.88 us (1%)
    all_to_all x3, waiting for transfers between devices, exchange(): return lax.all_to_all(x, 'dp', split_axis=0, concat_axis=0, tiled=True)  51.9 us
    pallas_call x2, Pallas kernels, owner_grads(): pl.pallas_call(functools.partial(owner_grads_kernel, group, head, places)...  22.2 us
    ppermute x14, starting transfers between devices, travel(): lax.ppermute(block, 'pass', [(i, (i + way) % count) for i in range(count)])  17 us
    all_to_all x1, starting transfers between devices, local(): lax.all_to_all(summed.reshape(peers * cores, share, -1), ('dp', 'tensor')...  16 us
    ppermute x14, waiting for transfers between devices, travel(): lax.ppermute(block, 'pass', [(i, (i + way) % count) for i in range(count)])  15.5 us
    all_to_all x3, starting transfers between devices, exchange(): return lax.all_to_all(x, 'dp', split_axis=0, concat_axis=0, tiled=True)  15 us
    all_to_all x1, blocking collectives, exchange(): return lax.all_to_all(x, 'dp', split_axis=0, concat_axis=0, tiled=True)  10.8 us
    unnamed x53, local copies, waits for them, and re-layouts  8.38 us
  transfers between devices with their start and end apart: 20, of which 13 were waited for; matrix products, arithmetic and copies ran while one was open for 3% of the time, Pallas kernels for 13%

profile of v4, /device:TPU:1, one launch (start us, length us, event | category | flops | bytes accessed | tf_op | source)
XLA Modules:
  0.0 198.0 jit_solution(7566457159313050536)
XLA Ops:
  0.6 4.1 %pack_queries.1 = bf16[16,64,2048]{2,1,0:T(8,128)(2,1)} custom-call(s32[16,16]{1,0:T(8,128)} %bitcast.18, bf16[4,32,2048]{2,1,0:T(8,128)(2,1)} %q_ref.5, bf16[4,32,2048]{2,1,0:T(8,128)(2,1)} %g_ref.5), custom_call_target="tpu_custom_call" | custom-call | bytes 6291456 | tf_op jit(solution)/shard_map/pack_queries/pallas_call | solution.py:90
  4.8 7.8 %all-to-all-start = ((bf16[16,64,2048]{2,1,0:T(8,128)(2,1)}), bf16[16,64,2048]{2,1,0:T(8,128)(2,1)}, u32[]{:S(2)}, u32[]{:S(2)}) async-start(bf16[16,64,2048]{2,1,0:T(8,128)(2,1)} %pack_queries.1), calls=%async_computation | async-start | bytes 8388608 | tf_op jit(solution)/shard_map/all_to_all | solution.py:586
  12.7 1.0 collective-permute-start
  14.0 1.9 copy.21
  16.1 0.5 own_stats.1.own_ref
  16.8 0.6 pad_add_fusion.table
  17.4 1.1 collective-permute-done.1
  18.5 7.7 %transpose_hidden.1.hidden_ref = bf16[8,512,640]{2,1,0:T(8,128)(2,1)} custom-call(s32[1]{0:T(128)} %bitcast.2.core, bf16[256,4096]{1,0:T(8,128)(2,1)} %bitcast.21, bf16[256,4096]{1,0:T(8,128)(2,1)} %bitcast.4.other_p, bf16[64,4096]{1,0:T(8,128)(2,1)} %bitcast.25, bf16[64,4096]{1,0:T(8,128)(2,1)} %bitcast.6.other_q), custom_call_target="tpu_custom_call" | custom-call | bytes 12582912 | tf_op jit(solution)/shard_map/transpose_hidden/pallas_call | solution.py:457
  26.1 48.8 %all-to-all-done.got_ref = bf16[16,64,2048]{2,1,0:T(8,128)(2,1)} async-done(((bf16[16,64,2048]{2,1,0:T(8,128)(2,1)}), bf16[16,64,2048]{2,1,0:T(8,128)(2,1)}, u32[]{:S(2)}, u32[]{:S(2)}) %all-to-all-start) | async-done | bytes 4194336 | tf_op jit(solution)/shard_map/all_to_all | solution.py:586
  75.0 6.9 %owner_stats.1 = f32[16,4,256]{2,1,0:T(4,128)} custom-call(s32[18]{0:T(128)} %pad_add_fusion.table, bf16[16,64,2048]{2,1,0:T(8,128)(2,1)} %all-to-all-done.got_ref, bf16[2,2,256,256]{3,2,1,0:T(8,128)(2,1)} %bitcast.22), custom_call_target="tpu_custom_call" | custom-call | flops 2000000000 | bytes 6291456 | tf_op jit(solution)/shard_map/owner_stats/pallas_call | solution.py:155
  81.9 10.8 %all_to_all.25.st_ref = f32[16,4,256]{2,1,0:T(4,128)S(1)} all-to-all(f32[16,4,256]{2,1,0:T(4,128)} %owner_stats.1), channel_id=1, replica_groups=mesh['dp'=16,'pass'=8,'tensor'=2] {'dp'}, dimensions={0} | all-to-all | bytes 131072 | tf_op jit(solution)/shard_map/all_to_all | solution.py:586
  92.7 1.4 merge_stats.1
  94.1 3.5 %all-to-all-start.2 = ((f32[16,4,256]{2,1,0:T(4,128)}), f32[16,4,256]{2,1,0:T(4,128)S(1)}, u32[]{:S(2)}, u32[]{:S(2)}) async-start(f32[16,4,256]{2,1,0:T(4,128)} %get-tuple-element.48), calls=%async_computation.2 | async-start | bytes 131072 | tf_op jit(solution)/shard_map/all_to_all | solution.py:586
  97.6 1.9 own_grads.1
  99.5 1.0 copy-done.3
  100.5 0.7 copy-done.9
  101.2 2.9 %all-to-all-done.2.joint_ref = f32[16,4,256]{2,1,0:T(4,128)S(1)} async-done(((f32[16,4,256]{2,1,0:T(4,128)}), f32[16,4,256]{2,1,0:T(4,128)S(1)}, u32[]{:S(2)}, u32[]{:S(2)}) %all-to-all-start.2) | async-done | bytes 65568 | tf_op jit(solution)/shard_map/all_to_all | solution.py:586
  104.1 0.6 copy-done.25
  104.7 11.0 %owner_grads_0.1 = (bf16[512,256]{1,0:T(8,128)(2,1)}, bf16[16,32,2048]{2,1,0:T(8,128)(2,1)}, bf16[512,256]{1,0:T(8,128)(2,1)}, bf16[512,256]{1,0:T(8,128)(2,1)},...) custom-call(s32[18]{0:T(128)} %pad_add_fusion.table, ...), custom_call_target="tpu_custom_call" | custom-call | flops 5000000000 | bytes 8388608 | tf_op jit(solution)/shard_map/owner_grads_0/pallas_call | solution.py:317
  115.7 1.7 collective-permute-start.2
  117.4 4.0 %collective-permute-start.3 = (bf16[512,256]{1,0:T(8,128)(2,1)}, bf16[512,256]{1,0:T(8,128)(2,1)S(1)}, u32[]{:S(2)}, u32[]{:S(2)}) collective-permute-start(bf16[512,256]{1,0:T(8,128)(2,1)} %get-tuple-element.61), channel_id=1, source_target_pairs={{0,14},{2,0},{4,2},{6,4},{8,6},{10,8},{12,10},{14,12},{1,15},{3,1}... | collective-permute-start | bytes 786440 | tf_op jit(solution)/shard_map/ppermute | solution.py:529
  121.5 11.2 %owner_grads_1.1 = (bf16[512,256]{1,0:T(8,128)(2,1)}, bf16[16,32,2048]{2,1,0:T(8,128)(2,1)}, bf16[512,256]{1,0:T(8,128)(2,1)}, bf16[512,256]{1,0:T(8,128)(2,1)},...) custom-call(s32[18]{0:T(128)} %pad_add_fusion.table, ...), custom_call_target="tpu_custom_call", output_to_operand_aliasing={{1}: (6, {})} | custom-call | flops 5000000000 | bytes 8388608 | tf_op jit(solution)/shard_map/owner_grads_1/pallas_call | solution.py:317
  132.6 1.6 collective-permute-start.6
  134.4 0.9 copy-done.5
  135.6 2.7 %collective-permute-start.5 = (bf16[512,256]{1,0:T(8,128)(2,1)S(1)}, bf16[512,256]{1,0:T(8,128)(2,1)S(1)}, u32[]{:S(2)}, u32[]{:S(2)}) collective-permute-start(bf16[512,256]{1,0:T(8,128)(2,1)S(1)} %get-tuple-element.66), channel_id=1, source_target_pairs={{0,14},{2,0},{4,2},{6,4},{8,6},{10,8},{12,10},{14,12},{1,15},{3,1}... | collective-permute-start | bytes 786440 | tf_op jit(solution)/shard_map/ppermute | solution.py:529
  138.3 2.6 %collective-permute-done.7.refs_3_ = bf16[512,256]{1,0:T(8,128)(2,1)S(1)} collective-permute-done((bf16[512,256]{1,0:T(8,128)(2,1)}, bf16[512,256]{1,0:T(8,128)(2,1)S(1)}, u32[]{:S(2)}, u32[]{:S(2)}) %collective-permute-start.7) | collective-permute-done | bytes 262176 | tf_op jit(solution)/shard_map/ppermute | solution.py:529
  140.9 0.8 add_1_3.1
  141.8 1.5 collective-permute-start.10
  143.2 3.7 %all-to-all-start.3 = ((bf16[16,32,2048]{2,1,0:T(8,128)(2,1)}), bf16[16,32,2048]{2,1,0:T(8,128)(2,1)S(1)}, u32[]{:S(2)}, u32[]{:S(2)}) async-start(bf16[16,32,2048]{2,1,0:T(8,128)(2,1)} %get-tuple-element.83), calls=%async_computation.3 | async-start | bytes 4194304 | tf_op jit(solution)/shard_map/all_to_all | solution.py:586
  147.0 0.9 copy-done.18
  147.9 0.9 copy-done.19
  149.1 2.5 %collective-permute-done.10.refs_3_ = bf16[512,256]{1,0:T(8,128)(2,1)} collective-permute-done((bf16[512,256]{1,0:T(8,128)(2,1)}, bf16[512,256]{1,0:T(8,128)(2,1)}, u32[]{:S(2)}, u32[]{:S(2)}) %collective-permute-start.10) | collective-permute-done | bytes 262176 | tf_op jit(solution)/shard_map/ppermute | solution.py:529
  151.6 1.1 add_1_2.1
  153.0 1.3 collective-permute-start.15
  154.3 1.4 collective-permute-start.12
  156.1 2.3 %collective-permute-done.13.refs_1_ = bf16[512,256]{1,0:T(8,128)(2,1)S(1)} collective-permute-done((bf16[512,256]{1,0:T(8,128)(2,1)S(1)}, bf16[512,256]{1,0:T(8,128)(2,1)S(1)}, u32[]{:S(2)}, u32[]{:S(2)}) %collective-permute-start.13) | collective-permute-done | bytes 262176 | tf_op jit(solution)/shard_map/ppermute | solution.py:529
  158.5 2.3 %collective-permute-start.14 = (bf16[512,256]{1,0:T(8,128)(2,1)S(1)}, bf16[512,256]{1,0:T(8,128)(2,1)S(1)}, u32[]{:S(2)}, u32[]{:S(2)}) collective-permute-start(bf16[512,256]{1,0:T(8,128)(2,1)S(1)} %add_1_1.1), channel_id=1, source_target_pairs={{0,14},{2,0},{4,2},{6,4},{8,6},{10,8},{12,10},{14,12},{1,15},{3,1}... | collective-permute-start | bytes 786440 | tf_op jit(solution)/shard_map/ppermute | solution.py:529
  160.8 0.6 collective-permute-done.15.refs_5_
  161.4 3.9 %collective-permute-done.14.refs_4_ = bf16[512,256]{1,0:T(8,128)(2,1)S(1)} collective-permute-done((bf16[512,256]{1,0:T(8,128)(2,1)S(1)}, bf16[512,256]{1,0:T(8,128)(2,1)S(1)}, u32[]{:S(2)}, u32[]{:S(2)}) %collective-permute-start.14) | collective-permute-done | bytes 262176 | tf_op jit(solution)/shard_map/ppermute | solution.py:529
  165.4 3.1 %collective-permute-done.11.refs_1_ = bf16[512,256]{1,0:T(8,128)(2,1)S(1)} collective-permute-done((bf16[512,256]{1,0:T(8,128)(2,1)S(1)}, bf16[512,256]{1,0:T(8,128)(2,1)S(1)}, u32[]{:S(2)}, u32[]{:S(2)}) %collective-permute-start.11) | collective-permute-done | bytes 262176 | tf_op jit(solution)/shard_map/ppermute | solution.py:529
  168.5 1.0 weights_last.1
  169.7 16.0 %all-to-all-start.4 = ((bf16[32,16,512]{2,1,0:T(8,128)(2,1)}), bf16[32,16,512]{2,1,0:T(8,128)(2,1)S(1)}, u32[]{:S(2)}, u32[]{:S(2)}) async-start(bf16[32,16,512]{2,1,0:T(8,128)(2,1)} %bitcast.10), calls=%async_computation.4 | async-start | bytes 1048576 | tf_op jit(solution)/shard_map/all_to_all | solution.py:659
  186.0 0.8 pad_maximum_fusion.1
  186.8 1.3 pad_maximum_fusion
  188.1 1.2 copy-done.4
  189.3 2.1 %sum_dq.1 = bf16[4,32,2048]{2,1,0:T(8,128)(2,1)} custom-call(s32[16]{0:T(128)S(1)} %compare_select_fusion.owners, bf16[16,32,2048]{2,1,0:T(8,128)(2,1)S(1)} %all-to-all-done.3.refs_0_.refs_1_.refs_2_.refs_3_, bf16[16,32,2048]{2,1,0:T(8,128)(2,1)S(1)} %all-to-all-done.3.refs_0_.refs_1_.refs_2_.refs_3_, ...), custom_call_target="tpu_custom_call" | custom-call | flops 2000000 | bytes 4194304 | tf_op jit(solution)/shard_map/sum_dq/pallas_call | solution.py:412
  191.4 5.8 %all-to-all-done.4 = bf16[32,16,512]{2,1,0:T(8,128)(2,1)S(1)} async-done(((bf16[32,16,512]{2,1,0:T(8,128)(2,1)}), bf16[32,16,512]{2,1,0:T(8,128)(2,1)S(1)}, u32[]{:S(2)}, u32[]{:S(2)}) %all-to-all-start.4) | async-done | bytes 524320 | tf_op jit(solution)/shard_map/all_to_all | solution.py:659
  197.3 0.7 finish_weights.1
  (76 shorter events, 2.5 us)
Async XLA Ops:
  0.6 15.3 %copy-start = (s32[16,1,2]{0,2,1:T(2,128)S(1)}, s32[16,1,2]{0,2,1:T(2,128)}, u32[]{:S(2)}) copy-start(s32[16,1,2]{0,2,1:T(2,128)} %param.15) | copy-start | bytes 388
  4.8 7.9 %copy-start.22 = (bf16[2,128,4096]{2,1,0:T(8,128)(2,1)S(1)}, bf16[2,128,4096]{2,1,0:T(8,128)(2,1)}, u32[]{:S(2)}) copy-start(bf16[2,128,4096]{2,1,0:T(8,128)(2,1)} %param.13) | copy-start | bytes 6291460
  4.8 9.0 %copy-start.23 = (bf16[4,32,2,256]{3,2,1,0:T(2,128)(2,1)S(1)}, bf16[4,32,2,256]{3,2,1,0:T(2,128)(2,1)}, u32[]{:S(2)}) copy-start(bf16[4,32,2,256]{3,2,1,0:T(2,128)(2,1)} %param.10) | copy-start | bytes 393220
  4.8 70.2 %all-to-all-start = ((bf16[16,64,2048]{2,1,0:T(8,128)(2,1)}), bf16[16,64,2048]{2,1,0:T(8,128)(2,1)}, u32[]{:S(2)}, u32[]{:S(2)}) async-start(bf16[16,64,2048]{2,1,0:T(8,128)(2,1)} %pack_queries.1), calls=%async_computation | async-start | bytes 8388608 | tf_op jit(solution)/shard_map/all_to_all | solution.py:586
  12.6 3.5 %copy-start.1 = (bf16[4,32,2048]{2,1,0:T(8,128)(2,1)S(1)}, bf16[4,32,2048]{2,1,0:T(8,128)(2,1)}, u32[]{:S(2)}) copy-start(bf16[4,32,2048]{2,1,0:T(8,128)(2,1)} %q_ref.5) | copy-start | bytes 1572868
  12.6 3.5 %copy-start.2 = (bf16[4,32,2048]{2,1,0:T(8,128)(2,1)S(1)}, bf16[4,32,2048]{2,1,0:T(8,128)(2,1)}, u32[]{:S(2)}) copy-start(bf16[4,32,2048]{2,1,0:T(8,128)(2,1)} %g_ref.5) | copy-start | bytes 1572868
  12.7 4.0 %copy-start.11 = (s32[16,1,16]{2,1,0:T(1,128)S(1)}, s32[16,1,16]{2,1,0:T(1,128)}, u32[]{:S(2)}) copy-start(s32[16,1,16]{2,1,0:T(1,128)} %param.14) | copy-start | bytes 3076
  12.7 5.8 %collective-permute-start = (bf16[2,128,4096]{2,1,0:T(8,128)(2,1)S(1)}, bf16[2,128,4096]{2,1,0:T(8,128)(2,1)}, u32[]{:S(2)}, u32[]{:S(2)}) collective-permute-start(bf16[2,128,4096]{2,1,0:T(8,128)(2,1)S(1)} %copy-done.22), channel_id=1, source_target_pairs={{0,1},{1,0},{2,3},{3,2},{4,5},{5,4},{6,7},{7,6},{8,9},{9,8},{10,11... | collective-permute-start | bytes 6291464 | tf_op jit(solution)/shard_map/ppermute | solution.py:589
  13.7 4.7 %collective-permute-start.1 = (bf16[4,16,4096]{2,1,0:T(8,128)(2,1)}, bf16[4,16,4096]{2,1,0:T(8,128)(2,1)}, u32[]{:S(2)}, u32[]{:S(2)}) collective-permute-start(bf16[4,16,4096]{2,1,0:T(8,128)(2,1)} %param.12), channel_id=1, source_target_pairs={{0,1},{1,0},{2,3},{3,2},{4,5},{5,4},{6,7},{7,6},{8,9},{9,8},{10,11... | collective-permute-start | bytes 1572872 | tf_op jit(solution)/shard_map/ppermute | solution.py:589
  94.1 10.0 %all-to-all-start.2 = ((f32[16,4,256]{2,1,0:T(4,128)}), f32[16,4,256]{2,1,0:T(4,128)S(1)}, u32[]{:S(2)}, u32[]{:S(2)}) async-start(f32[16,4,256]{2,1,0:T(4,128)} %get-tuple-element.48), calls=%async_computation.2 | async-start | bytes 131072 | tf_op jit(solution)/shard_map/all_to_all | solution.py:586
  99.5 1.0 copy-start.3
  100.5 0.7 copy-start.9
  104.1 0.6 copy-start.25
  115.7 18.6 %collective-permute-start.2 = (bf16[512,256]{1,0:T(8,128)(2,1)}, bf16[512,256]{1,0:T(8,128)(2,1)S(1)}, u32[]{:S(2)}, u32[]{:S(2)}) collective-permute-start(bf16[512,256]{1,0:T(8,128)(2,1)} %get-tuple-element.59), channel_id=1, source_target_pairs={{0,2},{2,4},{4,6},{6,8},{8,10},{10,12},{12,14},{14,0},{1,3},{3,5},... | collective-permute-start | bytes 786440 | tf_op jit(solution)/shard_map/ppermute | solution.py:529
  117.4 17.0 %collective-permute-start.3 = (bf16[512,256]{1,0:T(8,128)(2,1)}, bf16[512,256]{1,0:T(8,128)(2,1)S(1)}, u32[]{:S(2)}, u32[]{:S(2)}) collective-permute-start(bf16[512,256]{1,0:T(8,128)(2,1)} %get-tuple-element.61), channel_id=1, source_target_pairs={{0,14},{2,0},{4,2},{6,4},{8,6},{10,8},{12,10},{14,12},{1,15},{3,1}... | collective-permute-start | bytes 786440 | tf_op jit(solution)/shard_map/ppermute | solution.py:529
  121.5 12.9 %copy-start.20 = (bf16[512,256]{1,0:T(8,128)(2,1)S(1)}, bf16[512,256]{1,0:T(8,128)(2,1)}, u32[]{:S(2)}) copy-start(bf16[512,256]{1,0:T(8,128)(2,1)} %get-tuple-element.58.refs_0_) | copy-start | bytes 786436
  121.5 12.9 %copy-start.21 = (bf16[512,256]{1,0:T(8,128)(2,1)S(1)}, bf16[512,256]{1,0:T(8,128)(2,1)}, u32[]{:S(2)}) copy-start(bf16[512,256]{1,0:T(8,128)(2,1)} %get-tuple-element.60.refs_2_) | copy-start | bytes 786436
  132.6 5.7 %collective-permute-start.6 = (bf16[512,256]{1,0:T(8,128)(2,1)}, bf16[512,256]{1,0:T(8,128)(2,1)S(1)}, u32[]{:S(2)}, u32[]{:S(2)}) collective-permute-start(bf16[512,256]{1,0:T(8,128)(2,1)} %get-tuple-element.69), channel_id=1, source_target_pairs={{0,14},{2,0},{4,2},{6,4},{8,6},{10,8},{12,10},{14,12},{1,15},{3,1}... | collective-permute-start | bytes 786440 | tf_op jit(solution)/shard_map/ppermute | solution.py:529
  134.3 6.6 %collective-permute-start.7 = (bf16[512,256]{1,0:T(8,128)(2,1)}, bf16[512,256]{1,0:T(8,128)(2,1)S(1)}, u32[]{:S(2)}, u32[]{:S(2)}) collective-permute-start(bf16[512,256]{1,0:T(8,128)(2,1)} %get-tuple-element.71), channel_id=1, source_target_pairs={{0,2},{2,4},{4,6},{6,8},{8,10},{10,12},{12,14},{14,0},{1,3},{3,5},... | collective-permute-start | bytes 786440 | tf_op jit(solution)/shard_map/ppermute | solution.py:529
  134.4 1.0 copy-start.5
  135.3 5.6 %copy-start.15 = (bf16[512,256]{1,0:T(8,128)(2,1)S(1)}, bf16[512,256]{1,0:T(8,128)(2,1)}, u32[]{:S(2)}) copy-start(bf16[512,256]{1,0:T(8,128)(2,1)} %get-tuple-element.68.refs_0_) | copy-start | bytes 786436
  135.3 5.6 %copy-start.16 = (bf16[512,256]{1,0:T(8,128)(2,1)S(1)}, bf16[512,256]{1,0:T(8,128)(2,1)}, u32[]{:S(2)}) copy-start(bf16[512,256]{1,0:T(8,128)(2,1)} %get-tuple-element.70.refs_2_) | copy-start | bytes 786436
  135.5 11.5 %collective-permute-start.4 = (bf16[512,256]{1,0:T(8,128)(2,1)S(1)}, bf16[512,256]{1,0:T(8,128)(2,1)S(1)}, u32[]{:S(2)}, u32[]{:S(2)}) collective-permute-start(bf16[512,256]{1,0:T(8,128)(2,1)S(1)} %get-tuple-element.64.refs_4_), channel_id=1, source_target_pairs={{0,2},{2,4},{4,6},{6,8},{8,10},{10,12},{12,14},{14,0},{1,3},{3,5},... | collective-permute-start | bytes 786440 | tf_op jit(solution)/shard_map/ppermute | solution.py:529
  135.6 11.4 %collective-permute-start.5 = (bf16[512,256]{1,0:T(8,128)(2,1)S(1)}, bf16[512,256]{1,0:T(8,128)(2,1)S(1)}, u32[]{:S(2)}, u32[]{:S(2)}) collective-permute-start(bf16[512,256]{1,0:T(8,128)(2,1)S(1)} %get-tuple-element.66), channel_id=1, source_target_pairs={{0,14},{2,0},{4,2},{6,4},{8,6},{10,8},{12,10},{14,12},{1,15},{3,1}... | collective-permute-start | bytes 786440 | tf_op jit(solution)/shard_map/ppermute | solution.py:529
  141.8 9.8 %collective-permute-start.9 = (bf16[512,256]{1,0:T(8,128)(2,1)}, bf16[512,256]{1,0:T(8,128)(2,1)S(1)}, u32[]{:S(2)}, u32[]{:S(2)}) collective-permute-start(bf16[512,256]{1,0:T(8,128)(2,1)} %get-tuple-element.73.refs_4_), channel_id=1, source_target_pairs={{0,14},{2,0},{4,2},{6,4},{8,6},{10,8},{12,10},{14,12},{1,15},{3,1}... | collective-permute-start | bytes 786440 | tf_op jit(solution)/shard_map/ppermute | solution.py:529
  141.8 9.8 %collective-permute-start.10 = (bf16[512,256]{1,0:T(8,128)(2,1)}, bf16[512,256]{1,0:T(8,128)(2,1)}, u32[]{:S(2)}, u32[]{:S(2)}) collective-permute-start(bf16[512,256]{1,0:T(8,128)(2,1)} %get-tuple-element.77), channel_id=1, source_target_pairs={{0,2},{2,4},{4,6},{6,8},{8,10},{10,12},{12,14},{14,0},{1,3},{3,5},... | collective-permute-start | bytes 786440 | tf_op jit(solution)/shard_map/ppermute | solution.py:529
  143.2 26.4 %all-to-all-start.3 = ((bf16[16,32,2048]{2,1,0:T(8,128)(2,1)}), bf16[16,32,2048]{2,1,0:T(8,128)(2,1)S(1)}, u32[]{:S(2)}, u32[]{:S(2)}) async-start(bf16[16,32,2048]{2,1,0:T(8,128)(2,1)} %get-tuple-element.83), calls=%async_computation.3 | async-start | bytes 4194304 | tf_op jit(solution)/shard_map/all_to_all | solution.py:586
  147.0 1.0 copy-start.18
  147.9 0.9 copy-start.19
  148.9 2.7 %copy-start.13 = (bf16[512,256]{1,0:T(8,128)(2,1)S(1)}, bf16[512,256]{1,0:T(8,128)(2,1)}, u32[]{:S(2)}) copy-start(bf16[512,256]{1,0:T(8,128)(2,1)} %get-tuple-element.75.refs_0_) | copy-start | bytes 786436
  148.9 2.7 %copy-start.14 = (bf16[512,256]{1,0:T(8,128)(2,1)S(1)}, bf16[512,256]{1,0:T(8,128)(2,1)}, u32[]{:S(2)}) copy-start(bf16[512,256]{1,0:T(8,128)(2,1)} %get-tuple-element.76.refs_2_) | copy-start | bytes 786436
  149.0 7.0 %collective-permute-start.8 = (bf16[512,256]{1,0:T(8,128)(2,1)S(1)}, bf16[512,256]{1,0:T(8,128)(2,1)S(1)}, u32[]{:S(2)}, u32[]{:S(2)}) collective-permute-start(bf16[512,256]{1,0:T(8,128)(2,1)S(1)} %get-tuple-element.74.refs_4_), channel_id=1, source_target_pairs={{0,2},{2,4},{4,6},{6,8},{8,10},{10,12},{12,14},{14,0},{1,3},{3,5},... | collective-permute-start | bytes 786440 | tf_op jit(solution)/shard_map/ppermute | solution.py:529
  151.6 4.5 %copy-start.17 = (bf16[512,256]{1,0:T(8,128)(2,1)S(1)}, bf16[512,256]{1,0:T(8,128)(2,1)}, u32[]{:S(2)}) copy-start(bf16[512,256]{1,0:T(8,128)(2,1)} %get-tuple-element.56.refs_0_) | copy-start | bytes 786436
  152.7 5.7 %collective-permute-start.13 = (bf16[512,256]{1,0:T(8,128)(2,1)S(1)}, bf16[512,256]{1,0:T(8,128)(2,1)S(1)}, u32[]{:S(2)}, u32[]{:S(2)}) collective-permute-start(bf16[512,256]{1,0:T(8,128)(2,1)S(1)} %get-tuple-element.78.refs_2_), channel_id=1, source_target_pairs={{0,14},{2,0},{4,2},{6,4},{8,6},{10,8},{12,10},{14,12},{1,15},{3,1}... | collective-permute-start | bytes 786440 | tf_op jit(solution)/shard_map/ppermute | solution.py:529
  153.0 8.4 %collective-permute-start.15 = (bf16[512,256]{1,0:T(8,128)(2,1)S(1)}, bf16[512,256]{1,0:T(8,128)(2,1)S(1)}, u32[]{:S(2)}, u32[]{:S(2)}) collective-permute-start(bf16[512,256]{1,0:T(8,128)(2,1)S(1)} %get-tuple-element.82), channel_id=1, source_target_pairs={{0,2},{2,4},{4,6},{6,8},{8,10},{10,12},{12,14},{14,0},{1,3},{3,5},... | collective-permute-start | bytes 786440 | tf_op jit(solution)/shard_map/ppermute | solution.py:529
  154.3 7.1 %collective-permute-start.12 = (bf16[512,256]{1,0:T(8,128)(2,1)S(1)}, bf16[512,256]{1,0:T(8,128)(2,1)S(1)}, u32[]{:S(2)}, u32[]{:S(2)}) collective-permute-start(bf16[512,256]{1,0:T(8,128)(2,1)S(1)} %get-tuple-element.79), channel_id=1, source_target_pairs={{0,14},{2,0},{4,2},{6,4},{8,6},{10,8},{12,10},{14,12},{1,15},{3,1}... | collective-permute-start | bytes 786440 | tf_op jit(solution)/shard_map/ppermute | solution.py:529
  156.1 2.4 %copy-start.12 = (bf16[512,256]{1,0:T(8,128)(2,1)S(1)}, bf16[512,256]{1,0:T(8,128)(2,1)}, u32[]{:S(2)}) copy-start(bf16[512,256]{1,0:T(8,128)(2,1)} %get-tuple-element.81.refs_0_) | copy-start | bytes 786436
  158.5 10.1 %copy-start.7 = (bf16[512,256]{1,0:T(8,128)(2,1)S(1)}, bf16[512,256]{1,0:T(8,128)(2,1)}, u32[]{:S(2)}) copy-start(bf16[512,256]{1,0:T(8,128)(2,1)} %get-tuple-element.55.refs_0_) | copy-start | bytes 786436
  158.5 10.1 %copy-start.8 = (bf16[512,256]{1,0:T(8,128)(2,1)S(1)}, bf16[512,256]{1,0:T(8,128)(2,1)}, u32[]{:S(2)}) copy-start(bf16[512,256]{1,0:T(8,128)(2,1)} %get-tuple-element.80.refs_3_) | copy-start | bytes 786436
  158.5 27.2 %copy-start.6 = (bf16[512,256]{1,0:T(8,128)(2,1)S(1)}, bf16[512,256]{1,0:T(8,128)(2,1)}, u32[]{:S(2)}) copy-start(bf16[512,256]{1,0:T(8,128)(2,1)} %get-tuple-element.63.refs_4_) | copy-start | bytes 786436
  158.5 27.3 %copy-start.24 = (bf16[512,256]{1,0:T(8,128)(2,1)S(1)}, bf16[512,256]{1,0:T(8,128)(2,1)}, u32[]{:S(2)}) copy-start(bf16[512,256]{1,0:T(8,128)(2,1)} %get-tuple-element.86) | copy-start | bytes 786436
  158.5 6.8 %collective-permute-start.14 = (bf16[512,256]{1,0:T(8,128)(2,1)S(1)}, bf16[512,256]{1,0:T(8,128)(2,1)S(1)}, u32[]{:S(2)}, u32[]{:S(2)}) collective-permute-start(bf16[512,256]{1,0:T(8,128)(2,1)S(1)} %add_1_1.1), channel_id=1, source_target_pairs={{0,14},{2,0},{4,2},{6,4},{8,6},{10,8},{12,10},{14,12},{1,15},{3,1}... | collective-permute-start | bytes 786440 | tf_op jit(solution)/shard_map/ppermute | solution.py:529
  160.8 7.7 %collective-permute-start.11 = (bf16[512,256]{1,0:T(8,128)(2,1)S(1)}, bf16[512,256]{1,0:T(8,128)(2,1)S(1)}, u32[]{:S(2)}, u32[]{:S(2)}) collective-permute-start(bf16[512,256]{1,0:T(8,128)(2,1)S(1)} %add_0_1.1.refs_2_), channel_id=1, source_target_pairs={{0,2},{2,4},{4,6},{6,8},{8,10},{10,12},{12,14},{14,0},{1,3},{3,5},... | collective-permute-start | bytes 786440 | tf_op jit(solution)/shard_map/ppermute | solution.py:529
  168.5 17.4 %copy-start.10 = (bf16[2,128,256]{2,1,0:T(8,128)(2,1)S(1)}, bf16[2,128,256]{2,1,0:T(8,128)(2,1)}, u32[]{:S(2)}) copy-start(bf16[2,128,256]{2,1,0:T(8,128)(2,1)} %copy-done.9) | copy-start | bytes 393220
  169.7 27.6 %all-to-all-start.4 = ((bf16[32,16,512]{2,1,0:T(8,128)(2,1)}), bf16[32,16,512]{2,1,0:T(8,128)(2,1)S(1)}, u32[]{:S(2)}, u32[]{:S(2)}) async-start(bf16[32,16,512]{2,1,0:T(8,128)(2,1)} %bitcast.10), calls=%async_computation.4 | async-start | bytes 1048576 | tf_op jit(solution)/shard_map/all_to_all | solution.py:659
  188.1 1.2 copy-start.4

commit v5 on v4

--- a/solution.py
+++ b/solution.py
@@ -121,46 +121,66 @@
     return lax.broadcasted_iota(jnp.int32, shape, 0) < blocks * BLOCK
 
 
-def owner_stats_kernel(group, table, got_ref, kv_ref, out_ref):
-    step = pl.program_id(0)
-    per, both, _ = got_ref.shape
-    peers = per * pl.num_programs(0)
+def load_groups(src, held, sems):
+    count = sems.shape[0]
+    per = src.shape[0] // count
+    return [
+        pltpu.make_async_copy(
+            src.at[pl.ds(i * per, per)], held.at[pl.ds(i * per, per)], sems.at[i]
+        )
+        for i in range(count)
+    ]
+
+
+def wait_group(i, src, held, sems):
+    per = src.shape[0] // sems.shape[0]
+    rows = pl.ds(i * per, per)
+    pltpu.make_async_copy(src.at[rows], held.at[rows], sems.at[i]).wait()
+
+
+def owner_stats_kernel(group, table, got_hbm, kv_ref, out_ref, got_ref, sems):
+    peers, both, _ = got_ref.shape
+    steps = sems.shape[0]
+    per = peers // steps
     rows = both // 2
     slot_len = kv_ref.shape[2]
     heads = kv_ref.shape[3] // HD
     columns = group * rows
-    for one in range(per):
-        slot = table[step * per + one]
-        valid = passage_valid(table[peers + slot], slot_len, columns)
-        logs, deltas = [], []
-        for head in range(heads):
-            lanes = slice(head * HD, (head + 1) * HD)
-            queries = head_rows(got_ref[one, :rows], head, group)
-            grads = head_rows(got_ref[one, rows:], head, group)
-            scores = scores_t(kv_ref[0, slot, :, lanes], queries, valid)
-            prob_grad = lax.dot_general(
-                kv_ref[1, slot, :, lanes], grads, NT, preferred_element_type=F32
-            )
-            log, delta = part_stats(scores, prob_grad)
-            logs.append(log)
-            deltas.append(delta)
-        out_ref[one] = jnp.concatenate(logs + deltas, axis=0)
+    for load in load_groups(got_hbm, got_ref, sems):
+        load.start()
+
+    @pl.loop(0, steps)
+    def _(step):
+        wait_group(step, got_hbm, got_ref, sems)
+        for one in range(per):
+            reader = step * per + one
+            slot = table[reader]
+            valid = passage_valid(table[peers + slot], slot_len, columns)
+            logs, deltas = [], []
+            for head in range(heads):
+                lanes = slice(head * HD, (head + 1) * HD)
+                queries = head_rows(got_ref[reader, :rows], head, group)
+                grads = head_rows(got_ref[reader, rows:], head, group)
+                scores = scores_t(kv_ref[0, slot, :, lanes], queries, valid)
+                prob_grad = lax.dot_general(
+                    kv_ref[1, slot, :, lanes], grads, NT, preferred_element_type=F32
+                )
+                log, delta = part_stats(scores, prob_grad)
+                logs.append(log)
+                deltas.append(delta)
+            out_ref[reader] = jnp.concatenate(logs + deltas, axis=0)
 
 
 def owner_stats(table, got, kv, group):
     peers, both, width = got.shape
     heads = kv.shape[3] // HD
     columns = group * both // 2
-    per = 4
     return pl.pallas_call(
         functools.partial(owner_stats_kernel, group),
         out_shape=jax.ShapeDtypeStruct((peers, 2 * heads, columns), F32),
-        grid_spec=pltpu.PrefetchScalarGridSpec(
-            num_scalar_prefetch=1,
-            grid=(peers // per,),
-            in_specs=[pl.BlockSpec((per, both, width), lambda r, t: (r, 0, 0)), whole()],
-            out_specs=pl.BlockSpec((per, 2 * heads, columns), lambda r, t: (r, 0, 0)),
-        ),
+        in_specs=[smem(), in_hbm(), whole()],
+        out_specs=whole(),
+        scratch_shapes=[pltpu.VMEM(got.shape, BF16), pltpu.SemaphoreType.DMA((4,))],
         compiler_params=params(VMEM_MOST),
         cost_estimate=cost(2 * 10**9, 6 * 2**20, 2 * 10**6),
         name="owner_stats",
@@ -249,98 +269,130 @@
 
 
 def owner_grads_kernel(
-    group, head, places, table, got_ref, joint_ref, kv_ref, own_ref, hidden_ref, *rest
+    group,
+    places,
+    table,
+    got_hbm,
+    joint_ref,
+    kv_ref,
+    turned_ref,
+    own_ref,
+    hidden_ref,
+    grad_out,
+    dq_out,
+    *rest,
 ):
-    grad_ref, dq_ref, *block_refs, acc_ref, h_ref, h_sem = rest[-5 - len(places) :]
-    load = pltpu.make_async_copy(hidden_ref, h_ref, h_sem)
-    step = pl.program_id(0)
-    per, both, _ = got_ref.shape
-    peers = per * pl.num_programs(0)
+    outs = rest[:-11]
+    acc_ref, got_ref, h_ref, grad_ref, dq_ref, block_ref = rest[-11:-5]
+    got_sems, h_sem, grad_sem, dq_sems, sems = rest[-5:]
+    peers, both, _ = got_ref.shape
+    steps = got_sems.shape[0]
+    per = peers // steps
     rows = both // 2
     slot_len = kv_ref.shape[2]
     heads = kv_ref.shape[3] // HD
-    lanes = slice(head * HD, (head + 1) * HD)
-
-    @pl.when(step == 0)
-    def _():
+    for load in load_groups(got_hbm, got_ref, got_sems):
         load.start()
-        acc_ref[...] = jnp.zeros_like(acc_ref)
-
-    for one in range(per):
-        slot = table[step * per + one]
-        valid = passage_valid(table[peers + slot], slot_len, group * rows)
-        queries = head_rows(got_ref[one, :rows], 0, group)
-        grads = head_rows(got_ref[one, rows:], 0, group)
-        keys = kv_ref[0, slot, :, lanes]
-        scores = scores_t(keys, queries, valid)
-        prob_grad = lax.dot_general(
-            kv_ref[1, slot, :, lanes], grads, NT, preferred_element_type=F32
+    hidden_load = pltpu.make_async_copy(hidden_ref, h_ref, h_sem)
+    hidden_load.start()
+    acc_ref[...] = jnp.zeros_like(acc_ref)
+
+    @pl.loop(0, steps)
+    def _(step):
+        wait_group(step, got_hbm, got_ref, got_sems)
+        for one in range(per):
+            reader = step * per + one
+            slot = table[reader]
+            valid = passage_valid(table[peers + slot], slot_len, group * rows)
+            for head in range(heads):
+                lanes = slice(head * HD, (head + 1) * HD)
+                key_lanes = slice(2 * head * HD, (2 * head + 1) * HD)
+                value_lanes = slice((2 * head + 1) * HD, (2 * head + 2) * HD)
+                queries = head_rows(got_ref[reader, :rows], head, group)
+                grads = head_rows(got_ref[reader, rows:], head, group)
+                scores = scores_t(kv_ref[0, slot, :, lanes], queries, valid)
+                prob_grad = lax.dot_general(
+                    kv_ref[1, slot, :, lanes], grads, NT, preferred_element_type=F32
+                )
+                joint = joint_ref[reader, head : head + 1]
+                delta = joint_ref[reader, heads + head : heads + head + 1]
+                probs, dscore = probs_and_dscore(scores, prob_grad, joint, delta)
+                acc_ref[slot, :, key_lanes] += jnp.dot(
+                    dscore, queries, preferred_element_type=F32
+                )
+                acc_ref[slot, :, value_lanes] += jnp.dot(
+                    probs, grads, preferred_element_type=F32
+                )
+                dq = jnp.dot(turned_ref[slot, lanes], dscore, preferred_element_type=F32)
+                dq = dq.astype(BF16).T
+                for r in range(group):
+                    column = (head * group + r) * HD
+                    dq_ref[reader, :, column : column + HD] = dq[r * rows : (r + 1) * rows]
+        part = pl.ds(step * per, per)
+        pltpu.make_async_copy(dq_ref.at[part], dq_out.at[part], dq_sems.at[step]).start()
+
+    for one in range(acc_ref.shape[0]):
+        grad_ref[one * slot_len : (one + 1) * slot_len] = acc_ref[one].astype(BF16)
+    copies = [pltpu.make_async_copy(grad_ref, grad_out, grad_sem)]
+    copies[0].start()
+    hidden_load.wait()
+    count = h_ref.shape[0]
+    tokens = grad_ref.shape[0]
+    k = 0
+    for place, uses in places:
+        pass_group = lax.rem(lax.axis_index("pass") + (place + count), count)
+        total = jnp.dot(h_ref[pass_group, :, :tokens], grad_ref[...], preferred_element_type=F32)
+        total = total + jnp.dot(
+            h_ref[pass_group, :, tokens:], own_ref[...], preferred_element_type=F32
         )
-        joint = joint_ref[one, head : head + 1]
-        delta = joint_ref[one, heads + head : heads + head + 1]
-        probs, dscore = probs_and_dscore(scores, prob_grad, joint, delta)
-        acc_ref[slot, :, :HD] += jnp.dot(dscore, queries, preferred_element_type=F32)
-        acc_ref[slot, :, HD:] += jnp.dot(probs, grads, preferred_element_type=F32)
-        dq = lax.dot_general(dscore, keys, TN, preferred_element_type=F32).astype(BF16)
-        for r in range(group):
-            dq_ref[one, :, r * HD : (r + 1) * HD] = dq[r * rows : (r + 1) * rows]
-
-    @pl.when(step == pl.num_programs(0) - 1)
-    def _():
-        for one in range(acc_ref.shape[0]):
-            grad_ref[one * slot_len : (one + 1) * slot_len] = acc_ref[one].astype(BF16)
-        load.wait()
-        for place, block_ref in zip(places, block_refs):
-            block_ref[...] = weight_block(h_ref, place, grad_ref, own_ref, head)
-
-
-def owner_grads(head, places, table, got, joint, kv, hidden_t, grads_query, dq, group):
+        for head, out, row in uses:
+            lanes = slice(2 * head * HD, 2 * (head + 1) * HD)
+            block_ref[k] = total[:, lanes].astype(BF16)
+            copies.append(
+                pltpu.make_async_copy(block_ref.at[k], outs[out].at[row], sems.at[k])
+            )
+            copies[-1].start()
+            k += 1
+    for copy in copies:
+        copy.wait()
+    for step in range(steps):
+        wait_group(step, dq_ref, dq_out, dq_sems)
+
+
+def owner_grads(places, depths, table, got, joint, kv, turned, hidden_t, grads_query):
     peers, both, width = got.shape
-    _, slots, slot_len, _ = kv.shape
-    stat_rows, columns = joint.shape[1:]
+    _, slots, slot_len, channels = kv.shape
+    columns = joint.shape[2]
     share = hidden_t.shape[1]
-    per = 4
-    lanes = group * HD
-    operands = [table, got, joint, kv, grads_query, hidden_t]
-    in_specs = [
-        pl.BlockSpec((per, both, lanes), lambda r, t: (r, 0, head)),
-        pl.BlockSpec((per, stat_rows, columns), lambda r, t: (r, 0, 0)),
-        whole(),
-        whole(),
-        in_hbm(),
-    ]
-    aliases = {}
-    if dq is not None:
-        aliases = {len(operands): 1}
-        operands.append(dq)
-        in_specs.append(in_hbm())
-    return pl.pallas_call(
-        functools.partial(owner_grads_kernel, group, head, places),
+    count = sum(depths)
+    grads = jax.ShapeDtypeStruct((slots * slot_len, 2 * channels), BF16)
+    dq = jax.ShapeDtypeStruct((peers, both // 2, width), BF16)
+    return pl.pallas_call(
+        functools.partial(owner_grads_kernel, 2 * columns // both, places),
         out_shape=(
-            jax.ShapeDtypeStruct((slots * slot_len, 2 * HD), BF16),
-            jax.ShapeDtypeStruct((peers, both // 2, width), BF16),
-            *[jax.ShapeDtypeStruct((share, 2 * HD), BF16) for _ in places],
+            grads,
+            dq,
+            *[jax.ShapeDtypeStruct((depth, share, 2 * HD), BF16) for depth in depths],
         ),
-        grid_spec=pltpu.PrefetchScalarGridSpec(
-            num_scalar_prefetch=1,
-            grid=(peers // per,),
-            in_specs=in_specs,
-            out_specs=(
-                pl.BlockSpec((slots * slot_len, 2 * HD), lambda r, t: (0, 0)),
-                pl.BlockSpec((per, both // 2, lanes), lambda r, t: (r, 0, head)),
-                *[pl.BlockSpec((share, 2 * HD), lambda r, t: (0, 0)) for _ in places],
-            ),
-            scratch_shapes=[
-                pltpu.VMEM((slots, slot_len, 2 * HD), F32),
-                pltpu.VMEM(hidden_t.shape, BF16),
-                pltpu.SemaphoreType.DMA,
-            ],
-        ),
-        input_output_aliases=aliases,
+        in_specs=[smem(), in_hbm(), whole(), whole(), whole(), whole(), in_hbm()],
+        out_specs=tuple(in_hbm() for _ in range(2 + len(depths))),
+        scratch_shapes=[
+            pltpu.VMEM((slots, slot_len, 2 * channels), F32),
+            pltpu.VMEM(got.shape, BF16),
+            pltpu.VMEM(hidden_t.shape, BF16),
+            pltpu.VMEM(grads.shape, BF16),
+            pltpu.VMEM(dq.shape, BF16),
+            pltpu.VMEM((count, share, 2 * HD), BF16),
+            pltpu.SemaphoreType.DMA((4,)),
+            pltpu.SemaphoreType.DMA,
+            pltpu.SemaphoreType.DMA,
+            pltpu.SemaphoreType.DMA((4,)),
+            pltpu.SemaphoreType.DMA((count,)),
+        ],
         compiler_params=params(VMEM_MOST),
-        cost_estimate=cost(5 * 10**9, 8 * 2**20, 2 * 10**6),
-        name=f"owner_grads_{head}",
-    )(*operands)
+        cost_estimate=cost(16 * 10**9, 24 * 2**20, 2 * 10**6),
+        name="owner_grads",
+    )(table, got, joint, kv, turned, grads_query, hidden_t)
 
 
 def own_grads_kernel(group, q_ref, g_ref, k_ref, v_ref, joint_ref, grad_ref, dq_ref):
@@ -363,9 +415,11 @@
             probs, dscore = probs_and_dscore(scores, prob_grad, joint, delta)
             key_grad = jnp.dot(dscore, queries, preferred_element_type=F32)
             value_grad = jnp.dot(probs, grads, preferred_element_type=F32)
-            grad_ref[head, token, :HD] = key_grad.astype(BF16)
-            grad_ref[head, token, HD:] = value_grad.astype(BF16)
-            dq = lax.dot_general(dscore, keys, TN, preferred_element_type=F32)
+            key_lanes = slice(2 * head * HD, (2 * head + 1) * HD)
+            value_lanes = slice((2 * head + 1) * HD, (2 * head + 2) * HD)
+            grad_ref[token, key_lanes] = key_grad.astype(BF16)
+            grad_ref[token, value_lanes] = value_grad.astype(BF16)
+            dq = lax.dot_general(dscore, keys, TN, preferred_element_type=F32).astype(BF16)
             for r in range(group):
                 column = (head * group + r) * HD
                 dq_ref[sample, :, column : column + HD] = dq[r * rows : (r + 1) * rows]
@@ -377,8 +431,8 @@
     return pl.pallas_call(
         functools.partial(own_grads_kernel, group),
         out_shape=(
-            jax.ShapeDtypeStruct((heads, samples * rows, 2 * HD), BF16),
-            jax.ShapeDtypeStruct((samples, rows, width), F32),
+            jax.ShapeDtypeStruct((samples * rows, 2 * heads * HD), BF16),
+            jax.ShapeDtypeStruct((samples, rows, width), BF16),
         ),
         in_specs=[whole()] * 5,
         out_specs=(whole(), whole()),
@@ -395,7 +449,7 @@
     width = refs[0].shape[2]
     for head in range(heads):
         lanes = slice(head * width, (head + 1) * width)
-        total = own_ref[0, :, lanes]
+        total = own_ref[0, :, lanes].astype(F32)
         for ref in refs[head * per : (head + 1) * per]:
             total = total + ref[0].astype(F32)
         out_ref[0, :, lanes] = total.astype(BF16)
@@ -472,54 +526,46 @@
     )(core, mine_p, other_p, mine_q, other_q)
 
 
-def weight_block(h_ref, place, p_ref, q_ref, head):
-    count, _, _ = h_ref.shape
-    split = p_ref.shape[0]
-    group = lax.rem(lax.axis_index("pass") + (place + count), count)
-    total = jnp.dot(h_ref[group, :, :split], p_ref[...], preferred_element_type=F32)
-    total = total + jnp.dot(h_ref[group, :, split:], q_ref[head], preferred_element_type=F32)
-    return total.astype(BF16)
-
-
-def add_kernel(*refs):
-    outs = refs[2 * (len(refs) // 3) + 1 :]
-    for k, out_ref in enumerate(outs):
-        total = refs[2 * k][...].astype(F32) + refs[2 * k + 1][...].astype(F32)
-        out_ref[...] = total.astype(BF16)
+def add_kernel(count, blocks_ref, *refs):
+    outs = refs[len(refs) - count :]
+    for k, (arrived, out_ref) in enumerate(zip(refs, outs)):
+        out_ref[...] = (blocks_ref[k].astype(F32) + arrived[...].astype(F32)).astype(BF16)
 
 
 def add_arrived(blocks, arrived, after, name):
-    return pl.pallas_call(
-        add_kernel,
-        out_shape=tuple(jax.ShapeDtypeStruct(one.shape, BF16) for one in blocks),
-        in_specs=[whole()] * (2 * len(blocks)) + [pl.BlockSpec(memory_space=pl.ANY)],
-        out_specs=tuple(whole() for _ in blocks),
+    count = len(arrived)
+    return pl.pallas_call(
+        functools.partial(add_kernel, count),
+        out_shape=tuple(jax.ShapeDtypeStruct(one.shape, BF16) for one in arrived),
+        in_specs=[whole()] * (1 + count) + [pl.BlockSpec(memory_space=pl.ANY)],
+        out_specs=(whole(),) * count,
         compiler_params=params(),
         cost_estimate=cost(8 * 10**9, 2**20),
         name=name,
-    )(*[one for pair in zip(blocks, arrived) for one in pair], after)
-
-
-def last_kernel(*refs):
+    )(blocks, *arrived, after)
+
+
+def last_kernel(heads, blocks_ref, *refs):
     out_ref = refs[-1]
-    per = 3
-    for head in range((len(refs) - 1) // per):
-        total = sum(ref[...].astype(F32) for ref in refs[head * per : (head + 1) * per])
+    for head in range(heads):
+        total = blocks_ref[head].astype(F32)
+        for ref in refs[2 * head : 2 * head + 2]:
+            total = total + ref[...].astype(F32)
         width = total.shape[1]
         out_ref[:, head * width : (head + 1) * width] = total.astype(BF16)
 
 
-def last_sums(chains):
-    share, width = chains[0][0].shape
-    return pl.pallas_call(
-        last_kernel,
-        out_shape=jax.ShapeDtypeStruct((share, len(chains) * width), BF16),
-        in_specs=[whole()] * (3 * len(chains)),
+def last_sums(blocks, arrived):
+    heads, share, width = blocks.shape
+    return pl.pallas_call(
+        functools.partial(last_kernel, heads),
+        out_shape=jax.ShapeDtypeStruct((share, heads * width), BF16),
+        in_specs=[whole()] * (1 + 2 * heads),
         out_specs=whole(),
         compiler_params=params(),
         cost_estimate=cost(10**6, 2**21),
         name="weights_last",
-    )(*[one for chain in chains for one in chain])
+    )(blocks, *arrived)
 
 
 def travel(blocks, head):
@@ -597,6 +643,7 @@
     blocks = lax.dynamic_index_in_dim(passage_blocks, me, 0, keepdims=False).reshape(slots)
     table = jnp.concatenate([slot_of, blocks])
     kv = jnp.transpose(passage_kv, (2, 0, 1, 3))
+    turned = jnp.transpose(passage_kv[:, :, 0], (0, 2, 1))
     own_keys, own_values = question_kv[:, :, 0], question_kv[:, :, 1]
     own = own_stats(question_q, question_grad, own_keys, own_values, group)
     hidden_t = transpose_hidden(
@@ -610,7 +657,7 @@
         peers,
         groups,
     )
-    got, hidden_t, own = lax.optimization_barrier((got, hidden_t, own))
+    got, hidden_t, own, turned = lax.optimization_barrier((got, hidden_t, own, turned))
 
     stats = exchange(owner_stats(table, got, kv, group))
     back, merged = merge(refs, stats, own, slots)
@@ -620,38 +667,52 @@
     )
     joint, grads_query, own_dq = lax.optimization_barrier((joint, grads_query, own_dq))
     far = groups // 2
-    distances = list(range(far, 0, -1))
-    grads_pass, blocks_of, sums = [], [], []
-    dq_parts = None
+    depths, homes = [], {}
+
+    def array_of(*blocks):
+        for row, block in enumerate(blocks):
+            homes[block] = (len(depths), row)
+        depths.append(len(blocks))
+        return len(depths) - 1
+
+    firsts, pairs = [], {}
     for head in range(heads):
         way = direction(head)
-        places = [way * one for one in distances] + [-way * one for one in distances[1:]] + [0]
-        one, dq_parts, *weights = owner_grads(
-            head, tuple(places), table, got, joint, kv, hidden_t, grads_query, dq_parts, group
-        )
-        grads_pass.append(one)
-        blocks_of.append(dict(zip([place * way for place in places], weights)))
-        sums.append(travel([blocks_of[head][far], blocks_of[head][1 - far]], head))
+        firsts.append((array_of((far, head)), array_of((way * (1 - far), head))))
+    for distance in range(far - 1, 0, -1):
+        for head in range(heads):
+            way = direction(head)
+            pair = [(way * distance, head), (way * (1 - distance), head)]
+            pairs[distance, head] = array_of(*(pair if distance > 1 else pair[:1]))
+    final = array_of(*[(0, head) for head in range(heads)])
+    places = [
+        (place, [(head, *home) for (one, head), home in homes.items() if one == place])
+        for place in [far, *range(far - 1, -far, -1)]
+    ]
+    grads_pass, dq_parts, *blocks = owner_grads(
+        places, depths, table, got, joint, kv, turned, hidden_t, grads_query
+    )
+    sums = [
+        travel([blocks[ahead][0], blocks[behind][0]], head)
+        for head, (ahead, behind) in enumerate(firsts)
+    ]
     ends = [None] * heads
-    after = grads_pass[-1]
-    for distance in distances[1:]:
+    after = grads_pass
+    for distance in range(far - 1, 0, -1):
         for head in range(heads):
-            places = [distance, 1 - distance]
+            arrived = sums[head]
             if distance == 1:
-                places = places[:1]
-                ends[head] = sums[head][1]
+                ends[head] = arrived[1]
+                arrived = arrived[:1]
             added = add_arrived(
-                [blocks_of[head][place] for place in places],
-                sums[head][: len(places)],
-                after,
-                f"add_{head}_{distance}",
+                blocks[pairs[distance, head]], arrived, after, f"add_{head}_{distance}"
             )
             after = added[0]
             sums[head] = travel(added, head)
-        if distance == far - 1:
-            dq_parts, after = lax.optimization_barrier((dq_parts, after))
     returned = exchange(dq_parts)
-    summed = last_sums([(blocks_of[h][0], sums[h][0], ends[h]) for h in range(heads)])
+    summed = last_sums(
+        blocks[final], [one for head in range(heads) for one in (sums[head][0], ends[head])]
+    )
     summed, returned = lax.optimization_barrier((summed, returned))
     question_dq = sum_dq(owners, [returned], own_dq)
 
@@ -664,12 +725,10 @@
         tiled=True,
     )
     weight_grad = finish_weights(parts.reshape(peers, cores, share, -1))
-    question_dkv = jnp.concatenate(
-        [grads_query[head].reshape(samples, rows, 2, HD) for head in range(heads)], axis=-1
-    )
-    passage_dkv = jnp.concatenate(
-        [one.reshape(slots, slot_len, 2, HD) for one in grads_pass], axis=-1
-    )
+    question_dkv = jnp.swapaxes(grads_query.reshape(samples, rows, heads, 2, HD), 2, 3)
+    question_dkv = question_dkv.reshape(samples, rows, 2, channels)
+    passage_dkv = jnp.swapaxes(grads_pass.reshape(slots, slot_len, heads, 2, HD), 2, 3)
+    passage_dkv = passage_dkv.reshape(slots, slot_len, 2, channels)
     return (question_dq, question_dkv, passage_dkv, weight_grad)
 
 

time: 199 us -> 197 us (0.990)
  Pallas kernels: 50.8 us -> 43.2 us
  waiting for transfers between devices: 74.3 us -> 81.5 us
  other arithmetic: 2.88 us -> 0.71 us
  starting transfers between devices: 49.2 us -> 51.3 us
    pallas_call x9 -> x8, Pallas kernels: 25.5 us -> 17.9 us  [the longest x1 15.3 us: owner_grads(): pl.pallas_call(functools.partial(owner_grads_kernel, 2 * columns // both,...]
    ppermute x14, waiting for transfers between devices: 15.5 us -> 21.1 us  [travel(): lax.ppermute(block, 'pass', [(i, (i + way) % count) for i in range(count)])]
    unnamed x53 -> x40, local copies, waits for them, and re-layouts: 8.38 us -> 4.57 us
    ppermute x14, starting transfers between devices: 17 us -> 20.8 us  [travel(): lax.ppermute(block, 'pass', [(i, (i + way) % count) for i in range(count)])]
    reshape x2, local copies, waits for them, and re-layouts: 0.13 us -> 2.65 us  [the longest x1 1.96 us: local(): grads_pass.reshape(slots, slot_len, heads, 2, HD)]
    concatenate x2 -> x0, other arithmetic: 2.14 us -> none  [the longest x1 1.35 us: local(): jnp.concatenate([one.reshape(slots, slot_len, 2, HD) for one in grads_pas...]
  transfers between devices with their start and end apart: 20 -> 20, of which waited for: 13 -> 14; matrix products, arithmetic and copies ran while one was open for 3% -> 3% of each run, Pallas kernels for 13% -> 8%
where the time goes in v5:
time: 197 us; the launch traced here: 196 us
  waiting for transfers between devices  81.5 us (41%)
  starting transfers between devices  51.3 us (26%)
  Pallas kernels  43.2 us (22%)
  blocking collectives  10.8 us (5%)
  local copies, waits for them, and re-layouts  7.6 us (4%)
    all_to_all x3, waiting for transfers between devices, exchange(): return lax.all_to_all(x, 'dp', split_axis=0, concat_axis=0, tiled=True)  52.4 us
    ppermute x14, waiting for transfers between devices, travel(): lax.ppermute(block, 'pass', [(i, (i + way) % count) for i in range(count)])  21.1 us
    ppermute x14, starting transfers between devices, travel(): lax.ppermute(block, 'pass', [(i, (i + way) % count) for i in range(count)])  20.8 us
    pallas_call x1, Pallas kernels, owner_grads(): pl.pallas_call(functools.partial(owner_grads_kernel, 2 * columns // both,...  15.3 us
    all_to_all x3, starting transfers between devices, exchange(): return lax.all_to_all(x, 'dp', split_axis=0, concat_axis=0, tiled=True)  15.1 us
    all_to_all x1, starting transfers between devices, local(): lax.all_to_all(summed.reshape(peers * cores, share, -1), ('dp', 'tensor')...  14.2 us
    all_to_all x1, blocking collectives, exchange(): return lax.all_to_all(x, 'dp', split_axis=0, concat_axis=0, tiled=True)  10.8 us
    pallas_call x1, Pallas kernels, transpose_hidden(): pl.pallas_call(functools.partial(transpose_kernel, slots, samples, per),...  7.64 us
  transfers between devices with their start and end apart: 20, of which 14 were waited for; matrix products, arithmetic and copies ran while one was open for 3% of the time, Pallas kernels for 8%

profile of v5, /device:TPU:1, one launch (start us, length us, event | category | flops | bytes accessed | tf_op | source)
XLA Modules:
  0.0 196.1 jit_solution(617495293325541422)
XLA Ops:
  0.6 4.1 %pack_queries.1 = bf16[16,64,2048]{2,1,0:T(8,128)(2,1)} custom-call(s32[16,16]{1,0:T(8,128)} %bitcast.32, bf16[4,32,2048]{2,1,0:T(8,128)(2,1)} %q_ref.5, bf16[4,32,2048]{2,1,0:T(8,128)(2,1)} %g_ref.5), custom_call_target="tpu_custom_call" | custom-call | bytes 6291456 | tf_op jit(solution)/shard_map/pack_queries/pallas_call | solution.py:90
  4.8 7.8 %all-to-all-start = ((bf16[16,64,2048]{2,1,0:T(8,128)(2,1)}), bf16[16,64,2048]{2,1,0:T(8,128)(2,1)}, u32[]{:S(2)}, u32[]{:S(2)}) async-start(bf16[16,64,2048]{2,1,0:T(8,128)(2,1)} %pack_queries.1), calls=%async_computation | async-start | bytes 8388608 | tf_op jit(solution)/shard_map/all_to_all | solution.py:632
  12.6 1.0 collective-permute-start
  14.0 0.9 copy.24
  14.9 1.0 copy.20
  16.1 0.5 own_stats.1.own_ref
  16.7 0.6 pad_add_fusion.table
  17.3 0.8 collective-permute-done.1
  18.1 0.5 collective-permute-done
  18.9 7.6 %transpose_hidden.1.hidden_ref = bf16[8,512,640]{2,1,0:T(8,128)(2,1)} custom-call(s32[1]{0:T(128)} %bitcast.2.core, bf16[256,4096]{1,0:T(8,128)(2,1)} %bitcast.36, bf16[256,4096]{1,0:T(8,128)(2,1)} %bitcast.4.other_p, bf16[64,4096]{1,0:T(8,128)(2,1)} %bitcast.40, bf16[64,4096]{1,0:T(8,128)(2,1)} %bitcast.41), custom_call_target="tpu_custom_call" | custom-call | bytes 12582912 | tf_op jit(solution)/shard_map/transpose_hidden/pallas_call | solution.py:511
  26.5 48.4 %all-to-all-done.got_hbm = bf16[16,64,2048]{2,1,0:T(8,128)(2,1)} async-done(((bf16[16,64,2048]{2,1,0:T(8,128)(2,1)}), bf16[16,64,2048]{2,1,0:T(8,128)(2,1)}, u32[]{:S(2)}, u32[]{:S(2)}) %all-to-all-start) | async-done | bytes 4194336 | tf_op jit(solution)/shard_map/all_to_all | solution.py:632
  75.0 6.9 %owner_stats.1 = f32[16,4,256]{2,1,0:T(4,128)} custom-call(s32[18]{0:T(128)} %pad_add_fusion.table, bf16[16,64,2048]{2,1,0:T(8,128)(2,1)} %all-to-all-done.got_hbm, bf16[2,2,256,256]{3,2,1,0:T(8,128)(2,1)} %bitcast.37), custom_call_target="tpu_custom_call" | custom-call | flops 2000000000 | bytes 6291456 | tf_op jit(solution)/shard_map/owner_stats/pallas_call | solution.py:178
  81.9 10.8 %all_to_all.25.st_ref = f32[16,4,256]{2,1,0:T(4,128)S(1)} all-to-all(f32[16,4,256]{2,1,0:T(4,128)} %owner_stats.1), channel_id=1, replica_groups=mesh['dp'=16,'pass'=8,'tensor'=2] {'dp'}, dimensions={0} | all-to-all | bytes 131072 | tf_op jit(solution)/shard_map/all_to_all | solution.py:632
  92.7 1.4 merge_stats.1
  94.1 3.5 %all-to-all-start.2 = ((f32[16,4,256]{2,1,0:T(4,128)}), f32[16,4,256]{2,1,0:T(4,128)S(1)}, u32[]{:S(2)}, u32[]{:S(2)}) async-start(f32[16,4,256]{2,1,0:T(4,128)} %get-tuple-element.40), calls=%async_computation.2 | async-start | bytes 131072 | tf_op jit(solution)/shard_map/all_to_all | solution.py:632
  97.6 1.9 own_grads.1
  99.5 0.6 copy-done.5
  100.2 3.9 %all-to-all-done.2.joint_ref = f32[16,4,256]{2,1,0:T(4,128)S(1)} async-done(((f32[16,4,256]{2,1,0:T(4,128)}), f32[16,4,256]{2,1,0:T(4,128)S(1)}, u32[]{:S(2)}, u32[]{:S(2)}) %all-to-all-start.2) | async-done | bytes 65568 | tf_op jit(solution)/shard_map/all_to_all | solution.py:632
  104.1 0.6 copy-done.18
  104.7 15.3 %owner_grads.1 = (bf16[512,512]{1,0:T(8,128)(2,1)}, bf16[16,32,2048]{2,1,0:T(8,128)(2,1)}, bf16[1,512,256]{2,1,0:T(8,128)(2,1)}, bf16[1,512,256]{2,1,0:T(8,128)(...) custom-call(s32[18]{0:T(128)} %pad_add_fusion.table, ...), custom_call_target="tpu_custom_call" | custom-call | flops 16000000000 | bytes 25165824 | tf_op jit(solution)/shard_map/owner_grads/pallas_call | solution.py:370
  120.0 1.8 collective-permute-start.2
  121.8 4.0 %collective-permute-start.3 = (bf16[512,256]{1,0:T(8,128)(2,1)}, bf16[512,256]{1,0:T(8,128)(2,1)}, u32[]{:S(2)}, u32[]{:S(2)}) collective-permute-start(bf16[512,256]{1,0:T(8,128)(2,1)} %bitcast.46), channel_id=1, source_target_pairs={{0,14},{2,0},{4,2},{6,4},{8,6},{10,8},{12,10},{14,12},{1,15},{3,1}... | collective-permute-start | bytes 786440 | tf_op jit(solution)/shard_map/ppermute | solution.py:575
  125.8 3.8 %all-to-all-start.3 = ((bf16[16,32,2048]{2,1,0:T(8,128)(2,1)}), bf16[16,32,2048]{2,1,0:T(8,128)(2,1)S(1)}, u32[]{:S(2)}, u32[]{:S(2)}) async-start(bf16[16,32,2048]{2,1,0:T(8,128)(2,1)} %get-tuple-element.68), calls=%async_computation.3 | async-start | bytes 4194304 | tf_op jit(solution)/shard_map/all_to_all | solution.py:632
  129.6 1.6 collective-permute-start.6
  131.4 1.0 copy-done.8
  132.4 1.2 add_0_3.1
  133.6 2.7 %collective-permute-start.5 = (bf16[512,256]{1,0:T(8,128)(2,1)S(1)}, bf16[512,256]{1,0:T(8,128)(2,1)S(1)}, u32[]{:S(2)}, u32[]{:S(2)}) collective-permute-start(bf16[512,256]{1,0:T(8,128)(2,1)S(1)} %get-tuple-element.56), channel_id=1, source_target_pairs={{0,14},{2,0},{4,2},{6,4},{8,6},{10,8},{12,10},{14,12},{1,15},{3,1}... | collective-permute-start | bytes 786440 | tf_op jit(solution)/shard_map/ppermute | solution.py:575
  136.2 0.8 collective-permute-done.6.refs_0_
  137.1 0.8 collective-permute-done.7.refs_1_
  138.1 2.7 %collective-permute-start.9 = (bf16[512,256]{1,0:T(8,128)(2,1)S(1)}, bf16[512,256]{1,0:T(8,128)(2,1)S(1)}, u32[]{:S(2)}, u32[]{:S(2)}) collective-permute-start(bf16[512,256]{1,0:T(8,128)(2,1)S(1)} %get-tuple-element.60.refs_2_), channel_id=1, source_target_pairs={{0,14},{2,0},{4,2},{6,4},{8,6},{10,8},{12,10},{14,12},{1,15},{3,1}... | collective-permute-start | bytes 786440 | tf_op jit(solution)/shard_map/ppermute | solution.py:575
  140.8 1.3 collective-permute-done.5.refs_1_
  142.1 2.7 %collective-permute-done.4.refs_0_ = bf16[512,256]{1,0:T(8,128)(2,1)S(1)} collective-permute-done((bf16[512,256]{1,0:T(8,128)(2,1)S(1)}, bf16[512,256]{1,0:T(8,128)(2,1)S(1)}, u32[]{:S(2)}, u32[]{:S(2)}) %collective-permute-start.4) | collective-permute-done | bytes 262176 | tf_op jit(solution)/shard_map/ppermute | solution.py:575
  144.9 0.8 collective-permute-start.12
  145.7 0.8 collective-permute-start.8
  146.5 3.3 %collective-permute-done.10.refs_1_ = bf16[512,256]{1,0:T(8,128)(2,1)S(1)} collective-permute-done((bf16[512,256]{1,0:T(8,128)(2,1)S(1)}, bf16[512,256]{1,0:T(8,128)(2,1)S(1)}, u32[]{:S(2)}, u32[]{:S(2)}) %collective-permute-start.10) | collective-permute-done | bytes 262176 | tf_op jit(solution)/shard_map/ppermute | solution.py:575
  150.1 2.7 %collective-permute-start.13 = (bf16[512,256]{1,0:T(8,128)(2,1)S(1)}, bf16[512,256]{1,0:T(8,128)(2,1)S(1)}, u32[]{:S(2)}, u32[]{:S(2)}) collective-permute-start(bf16[512,256]{1,0:T(8,128)(2,1)S(1)} %get-tuple-element.64.refs_1_), channel_id=1, source_target_pairs={{0,14},{2,0},{4,2},{6,4},{8,6},{10,8},{12,10},{14,12},{1,15},{3,1}... | collective-permute-start | bytes 786440 | tf_op jit(solution)/shard_map/ppermute | solution.py:575
  152.7 2.7 %collective-permute-done.8.refs_0_ = bf16[512,256]{1,0:T(8,128)(2,1)S(1)} collective-permute-done((bf16[512,256]{1,0:T(8,128)(2,1)S(1)}, bf16[512,256]{1,0:T(8,128)(2,1)S(1)}, u32[]{:S(2)}, u32[]{:S(2)}) %collective-permute-start.8) | collective-permute-done | bytes 262176 | tf_op jit(solution)/shard_map/ppermute | solution.py:575
  155.6 3.3 %collective-permute-done.13.refs_0_ = bf16[512,256]{1,0:T(8,128)(2,1)S(1)} collective-permute-done((bf16[512,256]{1,0:T(8,128)(2,1)S(1)}, bf16[512,256]{1,0:T(8,128)(2,1)S(1)}, u32[]{:S(2)}, u32[]{:S(2)}) %collective-permute-start.13) | collective-permute-done | bytes 262176 | tf_op jit(solution)/shard_map/ppermute | solution.py:575
  159.0 3.5 %collective-permute-start.14 = (bf16[512,256]{1,0:T(8,128)(2,1)S(1)}, bf16[512,256]{1,0:T(8,128)(2,1)S(1)}, u32[]{:S(2)}, u32[]{:S(2)}) collective-permute-start(bf16[512,256]{1,0:T(8,128)(2,1)S(1)} %add_1_1.1), channel_id=1, source_target_pairs={{0,14},{2,0},{4,2},{6,4},{8,6},{10,8},{12,10},{14,12},{1,15},{3,1}... | collective-permute-start | bytes 786440 | tf_op jit(solution)/shard_map/ppermute | solution.py:575
  162.5 4.2 %collective-permute-done.11.refs_0_ = bf16[512,256]{1,0:T(8,128)(2,1)S(1)} collective-permute-done((bf16[512,256]{1,0:T(8,128)(2,1)S(1)}, bf16[512,256]{1,0:T(8,128)(2,1)S(1)}, u32[]{:S(2)}, u32[]{:S(2)}) %collective-permute-start.11) | collective-permute-done | bytes 262176 | tf_op jit(solution)/shard_map/ppermute | solution.py:575
  166.7 1.8 collective-permute-done.14.refs_2_
  168.5 1.0 weights_last.1
  169.5 14.2 %all-to-all-start.4 = ((bf16[32,16,512]{2,1,0:T(8,128)(2,1)}), bf16[32,16,512]{2,1,0:T(8,128)(2,1)S(1)}, u32[]{:S(2)}, u32[]{:S(2)}) async-start(bf16[32,16,512]{2,1,0:T(8,128)(2,1)} %bitcast.20), calls=%async_computation.4 | async-start | bytes 1048576 | tf_op jit(solution)/shard_map/all_to_all | solution.py:720
  183.8 0.7 reshape.60
  184.5 2.0 reshape.62
  186.5 2.1 %sum_dq.1 = bf16[4,32,2048]{2,1,0:T(8,128)(2,1)} custom-call(s32[16]{0:T(128)S(1)} %compare_select_fusion.owners, bf16[16,32,2048]{2,1,0:T(8,128)(2,1)S(1)} %all-to-all-done.3.refs_0_.refs_1_.refs_2_.refs_3_, bf16[16,32,2048]{2,1,0:T(8,128)(2,1)S(1)} %all-to-all-done.3.refs_0_.refs_1_.refs_2_.refs_3_, ...), custom_call_target="tpu_custom_call" | custom-call | flops 2000000 | bytes 4194304 | tf_op jit(solution)/shard_map/sum_dq/pallas_call | solution.py:466
  188.6 6.7 %all-to-all-done.4 = bf16[32,16,512]{2,1,0:T(8,128)(2,1)S(1)} async-done(((bf16[32,16,512]{2,1,0:T(8,128)(2,1)}), bf16[32,16,512]{2,1,0:T(8,128)(2,1)S(1)}, u32[]{:S(2)}, u32[]{:S(2)}) %all-to-all-start.4) | async-done | bytes 524320 | tf_op jit(solution)/shard_map/all_to_all | solution.py:720
  195.3 0.7 finish_weights.1
  (57 shorter events, 1.9 us)
Async XLA Ops:
  0.6 15.2 %copy-start = (s32[16,1,2]{0,2,1:T(2,128)S(1)}, s32[16,1,2]{0,2,1:T(2,128)}, u32[]{:S(2)}) copy-start(s32[16,1,2]{0,2,1:T(2,128)} %param.15) | copy-start | bytes 388
  4.8 8.9 %copy-start.16 = (bf16[4,16,4096]{2,1,0:T(8,128)(2,1)S(1)}, bf16[4,16,4096]{2,1,0:T(8,128)(2,1)}, u32[]{:S(2)}) copy-start(bf16[4,16,4096]{2,1,0:T(8,128)(2,1)} %param.12) | copy-start | bytes 1572868
  4.8 9.0 %copy-start.15 = (bf16[4,32,2,256]{3,2,1,0:T(2,128)(2,1)S(1)}, bf16[4,32,2,256]{3,2,1,0:T(2,128)(2,1)}, u32[]{:S(2)}) copy-start(bf16[4,32,2,256]{3,2,1,0:T(2,128)(2,1)} %param.10) | copy-start | bytes 393220
  4.8 9.2 %copy-start.14 = (bf16[2,256,2,256]{3,2,1,0:T(2,128)(2,1)S(1)}, bf16[2,256,2,256]{3,2,1,0:T(2,128)(2,1)}, u32[]{:S(2)}) copy-start(bf16[2,256,2,256]{3,2,1,0:T(2,128)(2,1)} %param.11) | copy-start | bytes 1572868
  4.8 70.1 %all-to-all-start = ((bf16[16,64,2048]{2,1,0:T(8,128)(2,1)}), bf16[16,64,2048]{2,1,0:T(8,128)(2,1)}, u32[]{:S(2)}, u32[]{:S(2)}) async-start(bf16[16,64,2048]{2,1,0:T(8,128)(2,1)} %pack_queries.1), calls=%async_computation | async-start | bytes 8388608 | tf_op jit(solution)/shard_map/all_to_all | solution.py:632
  12.6 3.5 %copy-start.1 = (bf16[4,32,2048]{2,1,0:T(8,128)(2,1)S(1)}, bf16[4,32,2048]{2,1,0:T(8,128)(2,1)}, u32[]{:S(2)}) copy-start(bf16[4,32,2048]{2,1,0:T(8,128)(2,1)} %q_ref.5) | copy-start | bytes 1572868
  12.6 3.5 %copy-start.2 = (bf16[4,32,2048]{2,1,0:T(8,128)(2,1)S(1)}, bf16[4,32,2048]{2,1,0:T(8,128)(2,1)}, u32[]{:S(2)}) copy-start(bf16[4,32,2048]{2,1,0:T(8,128)(2,1)} %g_ref.5) | copy-start | bytes 1572868
  12.6 4.0 %copy-start.7 = (s32[16,1,16]{2,1,0:T(1,128)S(1)}, s32[16,1,16]{2,1,0:T(1,128)}, u32[]{:S(2)}) copy-start(s32[16,1,16]{2,1,0:T(1,128)} %param.14) | copy-start | bytes 3076
  12.6 5.9 %collective-permute-start = (bf16[2,128,4096]{2,1,0:T(8,128)(2,1)}, bf16[2,128,4096]{2,1,0:T(8,128)(2,1)}, u32[]{:S(2)}, u32[]{:S(2)}) collective-permute-start(bf16[2,128,4096]{2,1,0:T(8,128)(2,1)} %param.13), channel_id=1, source_target_pairs={{0,1},{1,0},{2,3},{3,2},{4,5},{5,4},{6,7},{7,6},{8,9},{9,8},{10,11... | collective-permute-start | bytes 6291464 | tf_op jit(solution)/shard_map/ppermute | solution.py:635
  13.7 4.4 %collective-permute-start.1 = (bf16[4,16,4096]{2,1,0:T(8,128)(2,1)S(1)}, bf16[4,16,4096]{2,1,0:T(8,128)(2,1)S(1)}, u32[]{:S(2)}, u32[]{:S(2)}) collective-permute-start(bf16[4,16,4096]{2,1,0:T(8,128)(2,1)S(1)} %copy-done.16), channel_id=1, source_target_pairs={{0,1},{1,0},{2,3},{3,2},{4,5},{5,4},{6,7},{7,6},{8,9},{9,8},{10,11... | collective-permute-start | bytes 1572872 | tf_op jit(solution)/shard_map/ppermute | solution.py:635
  18.1 0.8 copy-start.17
  94.1 10.0 %all-to-all-start.2 = ((f32[16,4,256]{2,1,0:T(4,128)}), f32[16,4,256]{2,1,0:T(4,128)S(1)}, u32[]{:S(2)}, u32[]{:S(2)}) async-start(f32[16,4,256]{2,1,0:T(4,128)} %get-tuple-element.40), calls=%async_computation.2 | async-start | bytes 131072 | tf_op jit(solution)/shard_map/all_to_all | solution.py:632
  99.5 0.7 copy-start.5
  104.1 0.6 copy-start.18
  120.0 11.4 %collective-permute-start.2 = (bf16[512,256]{1,0:T(8,128)(2,1)}, bf16[512,256]{1,0:T(8,128)(2,1)S(1)}, u32[]{:S(2)}, u32[]{:S(2)}) collective-permute-start(bf16[512,256]{1,0:T(8,128)(2,1)} %bitcast.47), channel_id=1, source_target_pairs={{0,2},{2,4},{4,6},{6,8},{8,10},{10,12},{12,14},{14,0},{1,3},{3,5},... | collective-permute-start | bytes 786440 | tf_op jit(solution)/shard_map/ppermute | solution.py:575
  121.8 9.6 %collective-permute-start.3 = (bf16[512,256]{1,0:T(8,128)(2,1)}, bf16[512,256]{1,0:T(8,128)(2,1)}, u32[]{:S(2)}, u32[]{:S(2)}) collective-permute-start(bf16[512,256]{1,0:T(8,128)(2,1)} %bitcast.46), channel_id=1, source_target_pairs={{0,14},{2,0},{4,2},{6,4},{8,6},{10,8},{12,10},{14,12},{1,15},{3,1}... | collective-permute-start | bytes 786440 | tf_op jit(solution)/shard_map/ppermute | solution.py:575
  125.8 5.6 %copy-start.3 = (bf16[512,512]{1,0:T(8,128)(2,1)S(1)}, bf16[512,512]{1,0:T(8,128)(2,1)}, u32[]{:S(2)}) copy-start(bf16[512,512]{1,0:T(8,128)(2,1)} %get-tuple-element.54.refs_2_) | copy-start | bytes 1572868
  125.8 43.8 %all-to-all-start.3 = ((bf16[16,32,2048]{2,1,0:T(8,128)(2,1)}), bf16[16,32,2048]{2,1,0:T(8,128)(2,1)S(1)}, u32[]{:S(2)}, u32[]{:S(2)}) async-start(bf16[16,32,2048]{2,1,0:T(8,128)(2,1)} %get-tuple-element.68), calls=%async_computation.3 | async-start | bytes 4194304 | tf_op jit(solution)/shard_map/all_to_all | solution.py:632
  129.6 7.4 %collective-permute-start.6 = (bf16[512,256]{1,0:T(8,128)(2,1)}, bf16[512,256]{1,0:T(8,128)(2,1)S(1)}, u32[]{:S(2)}, u32[]{:S(2)}) collective-permute-start(bf16[512,256]{1,0:T(8,128)(2,1)} %bitcast.45), channel_id=1, source_target_pairs={{0,14},{2,0},{4,2},{6,4},{8,6},{10,8},{12,10},{14,12},{1,15},{3,1}... | collective-permute-start | bytes 786440 | tf_op jit(solution)/shard_map/ppermute | solution.py:575
  131.3 6.6 %collective-permute-start.7 = (bf16[512,256]{1,0:T(8,128)(2,1)}, bf16[512,256]{1,0:T(8,128)(2,1)S(1)}, u32[]{:S(2)}, u32[]{:S(2)}) collective-permute-start(bf16[512,256]{1,0:T(8,128)(2,1)} %bitcast.44), channel_id=1, source_target_pairs={{0,2},{2,4},{4,6},{6,8},{8,10},{10,12},{12,14},{14,0},{1,3},{3,5},... | collective-permute-start | bytes 786440 | tf_op jit(solution)/shard_map/ppermute | solution.py:575
  131.4 1.0 copy-start.8
  132.4 5.5 %copy-start.11 = (bf16[2,512,256]{2,1,0:T(8,128)(2,1)S(1)}, bf16[2,512,256]{2,1,0:T(8,128)(2,1)}, u32[]{:S(2)}) copy-start(bf16[2,512,256]{2,1,0:T(8,128)(2,1)} %get-tuple-element.57.blocks_ref) | copy-start | bytes 1572868
  133.6 8.5 %collective-permute-start.5 = (bf16[512,256]{1,0:T(8,128)(2,1)S(1)}, bf16[512,256]{1,0:T(8,128)(2,1)S(1)}, u32[]{:S(2)}, u32[]{:S(2)}) collective-permute-start(bf16[512,256]{1,0:T(8,128)(2,1)S(1)} %get-tuple-element.56), channel_id=1, source_target_pairs={{0,14},{2,0},{4,2},{6,4},{8,6},{10,8},{12,10},{14,12},{1,15},{3,1}... | collective-permute-start | bytes 786440 | tf_op jit(solution)/shard_map/ppermute | solution.py:575
  136.2 8.6 %collective-permute-start.4 = (bf16[512,256]{1,0:T(8,128)(2,1)S(1)}, bf16[512,256]{1,0:T(8,128)(2,1)S(1)}, u32[]{:S(2)}, u32[]{:S(2)}) collective-permute-start(bf16[512,256]{1,0:T(8,128)(2,1)S(1)} %get-tuple-element.55.refs_2_), channel_id=1, source_target_pairs={{0,2},{2,4},{4,6},{6,8},{8,10},{10,12},{12,14},{14,0},{1,3},{3,5},... | collective-permute-start | bytes 786440 | tf_op jit(solution)/shard_map/ppermute | solution.py:575
  137.9 6.9 %copy-start.10 = (bf16[2,512,256]{2,1,0:T(8,128)(2,1)S(1)}, bf16[2,512,256]{2,1,0:T(8,128)(2,1)}, u32[]{:S(2)}) copy-start(bf16[2,512,256]{2,1,0:T(8,128)(2,1)} %get-tuple-element.50.blocks_ref) | copy-start | bytes 1572868
  138.0 11.8 %collective-permute-start.10 = (bf16[512,256]{1,0:T(8,128)(2,1)S(1)}, bf16[512,256]{1,0:T(8,128)(2,1)S(1)}, u32[]{:S(2)}, u32[]{:S(2)}) collective-permute-start(bf16[512,256]{1,0:T(8,128)(2,1)S(1)} %get-tuple-element.63), channel_id=1, source_target_pairs={{0,2},{2,4},{4,6},{6,8},{8,10},{10,12},{12,14},{14,0},{1,3},{3,5},... | collective-permute-start | bytes 786440 | tf_op jit(solution)/shard_map/ppermute | solution.py:575
  138.1 11.7 %collective-permute-start.9 = (bf16[512,256]{1,0:T(8,128)(2,1)S(1)}, bf16[512,256]{1,0:T(8,128)(2,1)S(1)}, u32[]{:S(2)}, u32[]{:S(2)}) collective-permute-start(bf16[512,256]{1,0:T(8,128)(2,1)S(1)} %get-tuple-element.60.refs_2_), channel_id=1, source_target_pairs={{0,14},{2,0},{4,2},{6,4},{8,6},{10,8},{12,10},{14,12},{1,15},{3,1}... | collective-permute-start | bytes 786440 | tf_op jit(solution)/shard_map/ppermute | solution.py:575
  144.8 5.0 %copy-start.9 = (bf16[2,512,256]{2,1,0:T(8,128)(2,1)S(1)}, bf16[2,512,256]{2,1,0:T(8,128)(2,1)}, u32[]{:S(2)}) copy-start(bf16[2,512,256]{2,1,0:T(8,128)(2,1)} %get-tuple-element.62.blocks_ref) | copy-start | bytes 1572868
  144.9 17.5 %collective-permute-start.12 = (bf16[512,256]{1,0:T(8,128)(2,1)S(1)}, bf16[512,256]{1,0:T(8,128)(2,1)S(1)}, u32[]{:S(2)}, u32[]{:S(2)}) collective-permute-start(bf16[512,256]{1,0:T(8,128)(2,1)S(1)} %get-tuple-element.65), channel_id=1, source_target_pairs={{0,14},{2,0},{4,2},{6,4},{8,6},{10,8},{12,10},{14,12},{1,15},{3,1}... | collective-permute-start | bytes 786440 | tf_op jit(solution)/shard_map/ppermute | solution.py:575
  145.7 9.7 %collective-permute-start.8 = (bf16[512,256]{1,0:T(8,128)(2,1)S(1)}, bf16[512,256]{1,0:T(8,128)(2,1)S(1)}, u32[]{:S(2)}, u32[]{:S(2)}) collective-permute-start(bf16[512,256]{1,0:T(8,128)(2,1)S(1)} %get-tuple-element.61.refs_2_), channel_id=1, source_target_pairs={{0,2},{2,4},{4,6},{6,8},{8,10},{10,12},{12,14},{14,0},{1,3},{3,5},... | collective-permute-start | bytes 786440 | tf_op jit(solution)/shard_map/ppermute | solution.py:575
  149.8 5.6 %copy-start.13 = (bf16[1,512,256]{2,1,0:T(8,128)(2,1)S(1)}, bf16[1,512,256]{2,1,0:T(8,128)(2,1)}, u32[]{:S(2)}) copy-start(bf16[1,512,256]{2,1,0:T(8,128)(2,1)} %get-tuple-element.49.blocks_ref) | copy-start | bytes 786436
  150.0 12.5 %collective-permute-start.15 = (bf16[512,256]{1,0:T(8,128)(2,1)S(1)}, bf16[512,256]{1,0:T(8,128)(2,1)S(1)}, u32[]{:S(2)}, u32[]{:S(2)}) collective-permute-start(bf16[512,256]{1,0:T(8,128)(2,1)S(1)} %get-tuple-element.67), channel_id=1, source_target_pairs={{0,2},{2,4},{4,6},{6,8},{8,10},{10,12},{12,14},{14,0},{1,3},{3,5},... | collective-permute-start | bytes 786440 | tf_op jit(solution)/shard_map/ppermute | solution.py:575
  150.1 8.9 %collective-permute-start.13 = (bf16[512,256]{1,0:T(8,128)(2,1)S(1)}, bf16[512,256]{1,0:T(8,128)(2,1)S(1)}, u32[]{:S(2)}, u32[]{:S(2)}) collective-permute-start(bf16[512,256]{1,0:T(8,128)(2,1)S(1)} %get-tuple-element.64.refs_1_), channel_id=1, source_target_pairs={{0,14},{2,0},{4,2},{6,4},{8,6},{10,8},{12,10},{14,12},{1,15},{3,1}... | collective-permute-start | bytes 786440 | tf_op jit(solution)/shard_map/ppermute | solution.py:575
  155.4 3.5 %copy-start.12 = (bf16[1,512,256]{2,1,0:T(8,128)(2,1)S(1)}, bf16[1,512,256]{2,1,0:T(8,128)(2,1)}, u32[]{:S(2)}) copy-start(bf16[1,512,256]{2,1,0:T(8,128)(2,1)} %get-tuple-element.66.blocks_ref) | copy-start | bytes 786436
  155.5 11.2 %collective-permute-start.11 = (bf16[512,256]{1,0:T(8,128)(2,1)S(1)}, bf16[512,256]{1,0:T(8,128)(2,1)S(1)}, u32[]{:S(2)}, u32[]{:S(2)}) collective-permute-start(bf16[512,256]{1,0:T(8,128)(2,1)S(1)} %add_0_1.1.refs_1_), channel_id=1, source_target_pairs={{0,2},{2,4},{4,6},{6,8},{8,10},{10,12},{12,14},{14,0},{1,3},{3,5},... | collective-permute-start | bytes 786440 | tf_op jit(solution)/shard_map/ppermute | solution.py:575
  158.9 9.6 %copy-start.4 = (bf16[2,512,256]{2,1,0:T(8,128)(2,1)S(1)}, bf16[2,512,256]{2,1,0:T(8,128)(2,1)}, u32[]{:S(2)}) copy-start(bf16[2,512,256]{2,1,0:T(8,128)(2,1)} %get-tuple-element.48.blocks_ref) | copy-start | bytes 1572868
  159.0 24.8 %copy-start.6 = (bf16[128,512]{1,0:T(8,128)(2,1)S(1)}, bf16[128,512]{1,0:T(8,128)(2,1)}, u32[]{:S(2)}) copy-start(bf16[128,512]{1,0:T(8,128)(2,1)} %copy-done.5) | copy-start | bytes 393220
  159.0 9.5 %collective-permute-start.14 = (bf16[512,256]{1,0:T(8,128)(2,1)S(1)}, bf16[512,256]{1,0:T(8,128)(2,1)S(1)}, u32[]{:S(2)}, u32[]{:S(2)}) collective-permute-start(bf16[512,256]{1,0:T(8,128)(2,1)S(1)} %add_1_1.1), channel_id=1, source_target_pairs={{0,14},{2,0},{4,2},{6,4},{8,6},{10,8},{12,10},{14,12},{1,15},{3,1}... | collective-permute-start | bytes 786440 | tf_op jit(solution)/shard_map/ppermute | solution.py:575
  169.5 25.8 %all-to-all-start.4 = ((bf16[32,16,512]{2,1,0:T(8,128)(2,1)}), bf16[32,16,512]{2,1,0:T(8,128)(2,1)S(1)}, u32[]{:S(2)}, u32[]{:S(2)}) async-start(bf16[32,16,512]{2,1,0:T(8,128)(2,1)} %bitcast.20), calls=%async_computation.4 | async-start | bytes 1048576 | tf_op jit(solution)/shard_map/all_to_all | solution.py:720

commit v6 on v5

--- a/solution.py
+++ b/solution.py
@@ -52,7 +52,7 @@
     )
 
 
-def pack_kernel(slots, refs, q_ref, g_ref, out_ref, held, load_sems, sems):
+def pack_kernel(slots, refs, blocks, q_ref, g_ref, out_ref, table, held, load_sems, sems):
     peers = out_ref.shape[0]
     samples, rows, _ = q_ref.shape
     per = peers // samples
@@ -77,21 +77,38 @@
             for copy in loads[sample]:
                 copy.wait()
         dest = quotient(refs[me, j], slots)
+        table[peers + slots + j] = dest
         copy = pltpu.make_async_copy(held.at[sample], out_ref.at[dest], sems.at[j])
         copy.start()
         copies.append(copy)
+    for slot in range(slots):
+        table[peers + slot] = blocks[me, slot]
+
+    @pl.loop(0, peers)
+    def _(reader):
+        slot = jnp.int32(0)
+        for j in range(peers):
+            entry = refs[reader, j]
+            mine = quotient(entry, slots) == me
+            slot = slot + jnp.where(mine, lax.rem(entry, jnp.int32(slots)), 0)
+        table[reader] = slot
+
     for copy in copies:
         copy.wait()
 
 
-def pack_queries(refs, question_q, question_grad, slots):
+def pack_queries(refs, blocks, question_q, question_grad):
     samples, rows, width = question_q.shape
     peers = refs.shape[0]
+    slots = blocks.shape[1]
     return pl.pallas_call(
         functools.partial(pack_kernel, slots),
-        out_shape=jax.ShapeDtypeStruct((peers, 2 * rows, width), BF16),
-        in_specs=[smem(), in_hbm(), in_hbm()],
-        out_specs=in_hbm(),
+        out_shape=(
+            jax.ShapeDtypeStruct((peers, 2 * rows, width), BF16),
+            jax.ShapeDtypeStruct((2 * peers + slots,), jnp.int32),
+        ),
+        in_specs=[smem(), smem(), in_hbm(), in_hbm()],
+        out_specs=(in_hbm(), smem()),
         scratch_shapes=[
             pltpu.VMEM((samples, 2 * rows, width), BF16),
             pltpu.SemaphoreType.DMA((samples, 2)),
@@ -100,7 +117,7 @@
         compiler_params=params(VMEM_MOST),
         cost_estimate=cost(0, 6 * 2**20),
         name="pack_queries",
-    )(refs, question_q, question_grad)
+    )(refs, blocks, question_q, question_grad)
 
 
 def scores_t(keys, queries, valid):
@@ -275,15 +292,15 @@
     got_hbm,
     joint_ref,
     kv_ref,
-    turned_ref,
     own_ref,
-    hidden_ref,
+    lower_ref,
+    upper_ref,
     grad_out,
     dq_out,
     *rest,
 ):
-    outs = rest[:-11]
-    acc_ref, got_ref, h_ref, grad_ref, dq_ref, block_ref = rest[-11:-5]
+    outs = rest[:-12]
+    acc_ref, got_ref, h_ref, grad_ref, dq_ref, block_ref, turned_ref = rest[-12:-5]
     got_sems, h_sem, grad_sem, dq_sems, sems = rest[-5:]
     peers, both, _ = got_ref.shape
     steps = got_sems.shape[0]
@@ -293,9 +310,16 @@
     heads = kv_ref.shape[3] // HD
     for load in load_groups(got_hbm, got_ref, got_sems):
         load.start()
-    hidden_load = pltpu.make_async_copy(hidden_ref, h_ref, h_sem)
-    hidden_load.start()
+    share = lower_ref.shape[1]
+    hidden_loads = [
+        pltpu.make_async_copy(src, h_ref.at[:, pl.ds(i * share, share)], h_sem.at[i])
+        for i, src in enumerate((lower_ref, upper_ref))
+    ]
+    for load in hidden_loads:
+        load.start()
     acc_ref[...] = jnp.zeros_like(acc_ref)
+    for slot in range(turned_ref.shape[0]):
+        turned_ref[slot] = kv_ref[0, slot].T
 
     @pl.loop(0, steps)
     def _(step):
@@ -335,7 +359,8 @@
         grad_ref[one * slot_len : (one + 1) * slot_len] = acc_ref[one].astype(BF16)
     copies = [pltpu.make_async_copy(grad_ref, grad_out, grad_sem)]
     copies[0].start()
-    hidden_load.wait()
+    for load in hidden_loads:
+        load.wait()
     count = h_ref.shape[0]
     tokens = grad_ref.shape[0]
     k = 0
@@ -359,11 +384,12 @@
         wait_group(step, dq_ref, dq_out, dq_sems)
 
 
-def owner_grads(places, depths, table, got, joint, kv, turned, hidden_t, grads_query):
+def owner_grads(places, depths, table, got, joint, kv, hidden_t, grads_query):
     peers, both, width = got.shape
     _, slots, slot_len, channels = kv.shape
     columns = joint.shape[2]
-    share = hidden_t.shape[1]
+    groups, half, tokens = hidden_t[0].shape
+    share = 2 * half
     count = sum(depths)
     grads = jax.ShapeDtypeStruct((slots * slot_len, 2 * channels), BF16)
     dq = jax.ShapeDtypeStruct((peers, both // 2, width), BF16)
@@ -374,17 +400,18 @@
             dq,
             *[jax.ShapeDtypeStruct((depth, share, 2 * HD), BF16) for depth in depths],
         ),
-        in_specs=[smem(), in_hbm(), whole(), whole(), whole(), whole(), in_hbm()],
+        in_specs=[smem(), in_hbm(), whole(), whole(), whole(), in_hbm(), in_hbm()],
         out_specs=tuple(in_hbm() for _ in range(2 + len(depths))),
         scratch_shapes=[
             pltpu.VMEM((slots, slot_len, 2 * channels), F32),
             pltpu.VMEM(got.shape, BF16),
-            pltpu.VMEM(hidden_t.shape, BF16),
+            pltpu.VMEM((groups, share, tokens), BF16),
             pltpu.VMEM(grads.shape, BF16),
             pltpu.VMEM(dq.shape, BF16),
             pltpu.VMEM((count, share, 2 * HD), BF16),
+            pltpu.VMEM((slots, channels, slot_len), BF16),
             pltpu.SemaphoreType.DMA((4,)),
-            pltpu.SemaphoreType.DMA,
+            pltpu.SemaphoreType.DMA((2,)),
             pltpu.SemaphoreType.DMA,
             pltpu.SemaphoreType.DMA((4,)),
             pltpu.SemaphoreType.DMA((count,)),
@@ -392,7 +419,7 @@
         compiler_params=params(VMEM_MOST),
         cost_estimate=cost(16 * 10**9, 24 * 2**20, 2 * 10**6),
         name="owner_grads",
-    )(table, got, joint, kv, turned, grads_query, hidden_t)
+    )(table, got, joint, kv, grads_query, *hidden_t)
 
 
 def own_grads_kernel(group, q_ref, g_ref, k_ref, v_ref, joint_ref, grad_ref, dq_ref):
@@ -455,13 +482,15 @@
         out_ref[0, :, lanes] = total.astype(BF16)
 
 
-def sum_dq(owners, returned, own):
+def sum_dq(table, returned, own):
     samples, rows, width = own.shape
-    per = owners.shape[0] // samples
+    peers = returned[0].shape[0]
+    per = peers // samples
     heads = len(returned)
+    first = table.shape[0] - peers
 
     def from_owner(k):
-        return pl.BlockSpec((1, rows, width // heads), lambda s, o: (o[s * per + k], 0, 0))
+        return pl.BlockSpec((1, rows, width // heads), lambda s, o: (o[first + s * per + k], 0, 0))
 
     return pl.pallas_call(
         functools.partial(sum_dq_kernel, heads),
@@ -476,7 +505,7 @@
         compiler_params=params(),
         cost_estimate=cost(2 * 10**6, 4 * 2**20),
         name="sum_dq",
-    )(owners, *[one for one in returned for _ in range(per)], own)
+    )(table, *[one for one in returned for _ in range(per)], own)
 
 
 def transpose_kernel(slots, samples, owners, core, mine_p, other_p, mine_q, other_q, out_ref):
@@ -503,27 +532,28 @@
             out_ref[group, owner * rows : (owner + 1) * rows] = turned[first : first + rows]
 
 
-def transpose_hidden(core, mine_p, other_p, mine_q, other_q, slots, samples, owners, groups):
-    width = mine_p.shape[1]
-    tokens = 2 * (mine_p.shape[0] + mine_q.shape[0])
+def transpose_hidden(core, hidden, slots, samples, owners, groups, half):
+    width = hidden[0].shape[1]
+    tokens = sum(one.shape[0] for one in hidden)
     per = 2
     tile = per * width // owners
+    steps = width // tile // 2
     return pl.pallas_call(
         functools.partial(transpose_kernel, slots, samples, per),
-        out_shape=jax.ShapeDtypeStruct((groups, width // groups, tokens), BF16),
+        out_shape=jax.ShapeDtypeStruct((groups, width // groups // 2, tokens), BF16),
         grid_spec=pltpu.PrefetchScalarGridSpec(
             num_scalar_prefetch=1,
-            grid=(width // tile,),
+            grid=(steps,),
             in_specs=[
-                pl.BlockSpec((one.shape[0], tile), lambda i, c: (0, i))
-                for one in (mine_p, other_p, mine_q, other_q)
+                pl.BlockSpec((one.shape[0], tile), lambda i, c: (0, half * steps + i))
+                for one in hidden
             ],
             out_specs=pl.BlockSpec((groups, tile // groups, tokens), lambda i, c: (0, i, 0)),
         ),
         compiler_params=params(VMEM_MOST),
         cost_estimate=cost(0, 12 * 2**20),
-        name="transpose_hidden",
-    )(core, mine_p, other_p, mine_q, other_q)
+        name=f"transpose_hidden_{half}",
+    )(core, *hidden)
 
 
 def add_kernel(count, blocks_ref, *refs):
@@ -617,7 +647,6 @@
     reuse,
     passage_blocks,
 ):
-    me = lax.axis_index("dp")
     peers = lax.axis_size("dp")
     groups = lax.axis_size("pass")
     cores = lax.axis_size("tensor")
@@ -634,38 +663,46 @@
     def from_partner(x):
         return lax.ppermute(x, "tensor", [(i, cores - 1 - i) for i in range(cores)])
 
-    packed = pack_queries(refs, question_q, question_grad, slots)
+    kv = jnp.transpose(passage_kv, (2, 0, 1, 3))
+    blocks = passage_blocks.reshape(peers, slots)
+    packed, table = pack_queries(refs, blocks, question_q, question_grad)
+    packed, table, kv = lax.optimization_barrier((packed, table, kv))
     got = exchange(packed)
-
-    hit = quotient(refs, slots) == me
-    slot_of = jnp.sum(jnp.where(hit, lax.rem(refs, jnp.int32(slots)), 0), axis=1)
-    owners = quotient(lax.dynamic_index_in_dim(refs, me, 0, keepdims=False), slots)
-    blocks = lax.dynamic_index_in_dim(passage_blocks, me, 0, keepdims=False).reshape(slots)
-    table = jnp.concatenate([slot_of, blocks])
-    kv = jnp.transpose(passage_kv, (2, 0, 1, 3))
-    turned = jnp.transpose(passage_kv[:, :, 0], (0, 2, 1))
+    got, passage_hidden, question_hidden, question_kv, question_q, question_grad = (
+        lax.optimization_barrier(
+            (got, passage_hidden, question_hidden, question_kv, question_q, question_grad)
+        )
+    )
     own_keys, own_values = question_kv[:, :, 0], question_kv[:, :, 1]
+
+    parts = owner_stats(table, got, kv, group)
+    parts, own_keys, own_values, passage_hidden, question_hidden = lax.optimization_barrier(
+        (parts, own_keys, own_values, passage_hidden, question_hidden)
+    )
+    stats = exchange(parts)
     own = own_stats(question_q, question_grad, own_keys, own_values, group)
-    hidden_t = transpose_hidden(
-        lax.axis_index("tensor").reshape(1),
-        passage_hidden.reshape(-1, model_width),
-        from_partner(passage_hidden).reshape(-1, model_width),
-        question_hidden.reshape(-1, model_width),
-        from_partner(question_hidden).reshape(-1, model_width),
-        slots,
-        samples,
-        peers,
-        groups,
-    )
-    got, hidden_t, own, turned = lax.optimization_barrier((got, hidden_t, own, turned))
-
-    stats = exchange(owner_stats(table, got, kv, group))
+    hidden = [
+        one.reshape(-1, model_width)
+        for both in (passage_hidden, question_hidden)
+        for one in (both, from_partner(both))
+    ]
+
+    def turned_half(half):
+        core = lax.axis_index("tensor").reshape(1)
+        return transpose_hidden(core, hidden, slots, samples, peers, groups, half)
+
+    lower = turned_half(0)
+    stats, lower = lax.optimization_barrier((stats, lower))
     back, merged = merge(refs, stats, own, slots)
     joint = exchange(back)
     grads_query, own_dq = own_grads(
         question_q, question_grad, own_keys, own_values, merged, group
     )
-    joint, grads_query, own_dq = lax.optimization_barrier((joint, grads_query, own_dq))
+    upper = turned_half(1)
+    joint, grads_query, own_dq, upper = lax.optimization_barrier(
+        (joint, grads_query, own_dq, upper)
+    )
+    hidden_t = [lower, upper]
     far = groups // 2
     depths, homes = [], {}
 
@@ -690,7 +727,7 @@
         for place in [far, *range(far - 1, -far, -1)]
     ]
     grads_pass, dq_parts, *blocks = owner_grads(
-        places, depths, table, got, joint, kv, turned, hidden_t, grads_query
+        places, depths, table, got, joint, kv, hidden_t, grads_query
     )
     sums = [
         travel([blocks[ahead][0], blocks[behind][0]], head)
@@ -714,7 +751,7 @@
         blocks[final], [one for head in range(heads) for one in (sums[head][0], ends[head])]
     )
     summed, returned = lax.optimization_barrier((summed, returned))
-    question_dq = sum_dq(owners, [returned], own_dq)
+    question_dq = sum_dq(table, [returned], own_dq)
 
     share = summed.shape[0] // (peers * cores)
     parts = lax.all_to_all(

time: 197 us -> 192 us (0.975)
  waiting for transfers between devices: 81.5 us -> 28.1 us
  blocking collectives: 10.8 us -> 57.6 us
  Pallas kernels: 43.2 us -> 45.4 us
    all_to_all x3, waiting for transfers between devices: 52.4 us -> 0.59 us  [exchange(): return lax.all_to_all(x, 'dp', split_axis=0, concat_axis=0, tiled=True)]
    all_to_all x1, blocking collectives: 10.8 us -> 57.6 us  [exchange(): return lax.all_to_all(x, 'dp', split_axis=0, concat_axis=0, tiled=True)]
    all_to_all x1, starting transfers between devices: 14.2 us -> 12 us  [local(): lax.all_to_all(summed.reshape(peers * cores, share, -1), ('dp', 'tensor')...]
    pallas_call x1 -> x2, Pallas kernels: 7.64 us -> 8.63 us  [transpose_hidden(): pl.pallas_call(functools.partial(transpose_kernel, slots, samples, per),...]
    unnamed x40 -> x37, local copies, waits for them, and re-layouts: 4.57 us -> 4.61 us
  transfers between devices with their start and end apart: 20 -> 20, of which waited for: 14 -> 12; matrix products, arithmetic and copies ran while one was open for 3% -> 1% of each run, Pallas kernels for 8% -> 8%
where the time goes in v6:
time: 192 us; the launch traced here: 191 us
  blocking collectives  57.6 us (30%)
  starting transfers between devices  50 us (26%)
  Pallas kernels  45.4 us (24%)
  waiting for transfers between devices  28.1 us (15%)
  local copies, waits for them, and re-layouts  8.64 us (4%)
    all_to_all x1, blocking collectives, exchange(): return lax.all_to_all(x, 'dp', split_axis=0, concat_axis=0, tiled=True)  57.6 us
    ppermute x14, waiting for transfers between devices, travel(): lax.ppermute(block, 'pass', [(i, (i + way) % count) for i in range(count)])  20 us
    ppermute x14, starting transfers between devices, travel(): lax.ppermute(block, 'pass', [(i, (i + way) % count) for i in range(count)])  19.9 us
    pallas_call x1, Pallas kernels, owner_grads(): pl.pallas_call(functools.partial(owner_grads_kernel, 2 * columns // both,...  16 us
    all_to_all x3, starting transfers between devices, exchange(): return lax.all_to_all(x, 'dp', split_axis=0, concat_axis=0, tiled=True)  15.9 us
    all_to_all x1, starting transfers between devices, local(): lax.all_to_all(summed.reshape(peers * cores, share, -1), ('dp', 'tensor')...  12 us
    pallas_call x2, Pallas kernels, transpose_hidden(): pl.pallas_call(functools.partial(transpose_kernel, slots, samples, per),...  8.63 us
    pallas_call x1, Pallas kernels, owner_stats(): pl.pallas_call(functools.partial(owner_stats_kernel, group), out_shape=ja...  6.91 us
  transfers between devices with their start and end apart: 20, of which 12 were waited for; matrix products, arithmetic and copies ran while one was open for 1% of the time, Pallas kernels for 8%

profile of v6, /device:TPU:1, one launch (start us, length us, event | category | flops | bytes accessed | tf_op | source)
XLA Modules:
  0.0 190.6 jit_solution(1069294758096114629)
XLA Ops:
  0.6 1.4 copy.12.blocks
  2.0 1.9 copy.19
  3.9 4.6 %pack_queries.1 = (bf16[16,64,2048]{2,1,0:T(8,128)(2,1)}, s32[34]{0:T(128)}) custom-call(s32[16,16]{1,0:T(8,128)} %bitcast.27, s32[16,2]{1,0:T(8,128)} %copy.12.blocks, bf16[4,32,2048]{2,1,0:T(8,128)(2,1)} %q_ref.3, bf16[4,32,2048]{2,1,0:T(8,128)(2,1)} %g_ref.3), custom_call_target="tpu_custom_call" | custom-call | bytes 6291456 | tf_op jit(solution)/shard_map/pack_queries/pallas_call | solution.py:104
  8.6 57.6 %all_to_all.25.got_hbm = bf16[16,64,2048]{2,1,0:T(8,128)(2,1)} all-to-all(bf16[16,64,2048]{2,1,0:T(8,128)(2,1)} %get-tuple-element.56), channel_id=1, replica_groups=mesh['dp'=16,'pass'=8,'tensor'=2] {'dp'}, dimensions={0} | all-to-all | bytes 8388608 | tf_op jit(solution)/shard_map/all_to_all | solution.py:661
  66.3 6.9 %owner_stats.1 = f32[16,4,256]{2,1,0:T(4,128)} custom-call(s32[34]{0:T(128)} %get-tuple-element.55.table.owners, bf16[16,64,2048]{2,1,0:T(8,128)(2,1)} %all_to_all.25.got_hbm, bf16[2,2,256,256]{3,2,1,0:T(8,128)(2,1)} %bitcast.35), custom_call_target="tpu_custom_call" | custom-call | flops 2000000000 | bytes 6291456 | tf_op jit(solution)/shard_map/owner_stats/pallas_call | solution.py:195
  73.2 2.1 %collective-permute-start = (bf16[2,128,4096]{2,1,0:T(8,128)(2,1)}, bf16[2,128,4096]{2,1,0:T(8,128)(2,1)}, u32[]{:S(2)}, u32[]{:S(2)}) collective-permute-start(bf16[2,128,4096]{2,1,0:T(8,128)(2,1)} %param.13), channel_id=1, source_target_pairs={{0,1},{1,0},{2,3},{3,2},{4,5},{5,4},{6,7},{7,6},{8,9},{9,8},{10,11... | collective-permute-start | bytes 6291464 | tf_op jit(solution)/shard_map/ppermute | solution.py:664
  75.4 3.5 %all-to-all-start.1 = ((f32[16,4,256]{2,1,0:T(4,128)}), f32[16,4,256]{2,1,0:T(4,128)S(1)}, u32[]{:S(2)}, u32[]{:S(2)}) async-start(f32[16,4,256]{2,1,0:T(4,128)} %owner_stats.1), calls=%async_computation.1 | async-start | bytes 131072 | tf_op jit(solution)/shard_map/all_to_all | solution.py:661
  78.9 0.5 own_stats.1.own_ref
  79.4 0.3 collective-permute-done.1
  79.7 0.5 collective-permute-done
  80.1 0.3 copy-done.15
  80.5 4.3 %transpose_hidden_0.1.lower_ref = bf16[8,256,640]{2,1,0:T(8,128)(2,1)} custom-call(s32[1]{0:T(128)} %bitcast.5.core, bf16[256,4096]{1,0:T(8,128)(2,1)} %bitcast.29, bf16[256,4096]{1,0:T(8,128)(2,1)} %bitcast.7.other_p, bf16[64,4096]{1,0:T(8,128)(2,1)} %bitcast.31, bf16[64,4096]{1,0:T(8,128)(2,1)} %bitcast.33), custom_call_target="tpu_custom_call" | custom-call | bytes 12582912 | tf_op jit(solution)/shard_map/transpose_hidden_0/pallas_call | solution.py:541
  84.7 0.6 all-to-all-done.1.st_ref
  85.3 1.4 merge_stats.1
  86.7 5.8 %all-to-all-start.2 = ((f32[16,4,256]{2,1,0:T(4,128)}), f32[16,4,256]{2,1,0:T(4,128)S(1)}, u32[]{:S(2)}, u32[]{:S(2)}) async-start(f32[16,4,256]{2,1,0:T(4,128)} %get-tuple-element.70), calls=%async_computation.2 | async-start | bytes 131072 | tf_op jit(solution)/shard_map/all_to_all | solution.py:661
  92.5 4.3 %transpose_hidden_1.1.upper_ref = bf16[8,256,640]{2,1,0:T(8,128)(2,1)} custom-call(s32[1]{0:T(128)} %bitcast.5.core, bf16[256,4096]{1,0:T(8,128)(2,1)} %bitcast.30, bf16[256,4096]{1,0:T(8,128)(2,1)} %bitcast.7.other_p, bf16[64,4096]{1,0:T(8,128)(2,1)} %bitcast.32, bf16[64,4096]{1,0:T(8,128)(2,1)} %bitcast.34), custom_call_target="tpu_custom_call" | custom-call | bytes 12582912 | tf_op jit(solution)/shard_map/transpose_hidden_1/pallas_call | solution.py:541
  96.8 1.9 own_grads.1
  98.7 0.6 copy-done.4
  99.3 0.6 copy-done.17
  100.0 16.0 %owner_grads.1 = (bf16[512,512]{1,0:T(8,128)(2,1)}, bf16[16,32,2048]{2,1,0:T(8,128)(2,1)}, bf16[1,512,256]{2,1,0:T(8,128)(2,1)}, bf16[1,512,256]{2,1,0:T(8,128)(...) custom-call(s32[34]{0:T(128)} %get-tuple-element.55.table.owners, ...), custom_call_target="tpu_custom_call" | custom-call | flops 16000000000 | bytes 25165824 | tf_op jit(solution)/shard_map/owner_grads/pallas_call | solution.py:396
  116.0 1.7 collective-permute-start.2
  117.7 4.0 %collective-permute-start.3 = (bf16[512,256]{1,0:T(8,128)(2,1)}, bf16[512,256]{1,0:T(8,128)(2,1)}, u32[]{:S(2)}, u32[]{:S(2)}) collective-permute-start(bf16[512,256]{1,0:T(8,128)(2,1)} %bitcast.42), channel_id=1, source_target_pairs={{0,14},{2,0},{4,2},{6,4},{8,6},{10,8},{12,10},{14,12},{1,15},{3,1}... | collective-permute-start | bytes 786440 | tf_op jit(solution)/shard_map/ppermute | solution.py:605
  121.7 6.6 %all-to-all-start.3 = ((bf16[16,32,2048]{2,1,0:T(8,128)(2,1)}), bf16[16,32,2048]{2,1,0:T(8,128)(2,1)S(1)}, u32[]{:S(2)}, u32[]{:S(2)}) async-start(bf16[16,32,2048]{2,1,0:T(8,128)(2,1)} %get-tuple-element.98), calls=%async_computation.3 | async-start | bytes 4194304 | tf_op jit(solution)/shard_map/all_to_all | solution.py:661
  128.4 1.6 collective-permute-start.6
  130.1 1.0 copy-done.8
  131.1 1.1 add_0_3.1
  132.3 2.7 %collective-permute-start.5 = (bf16[512,256]{1,0:T(8,128)(2,1)S(1)}, bf16[512,256]{1,0:T(8,128)(2,1)S(1)}, u32[]{:S(2)}, u32[]{:S(2)}) collective-permute-start(bf16[512,256]{1,0:T(8,128)(2,1)S(1)} %get-tuple-element.86), channel_id=1, source_target_pairs={{0,14},{2,0},{4,2},{6,4},{8,6},{10,8},{12,10},{14,12},{1,15},{3,1}... | collective-permute-start | bytes 786440 | tf_op jit(solution)/shard_map/ppermute | solution.py:605
  134.9 2.0 %collective-permute-done.7.refs_1_ = bf16[512,256]{1,0:T(8,128)(2,1)S(1)} collective-permute-done((bf16[512,256]{1,0:T(8,128)(2,1)}, bf16[512,256]{1,0:T(8,128)(2,1)S(1)}, u32[]{:S(2)}, u32[]{:S(2)}) %collective-permute-start.7) | collective-permute-done | bytes 262176 | tf_op jit(solution)/shard_map/ppermute | solution.py:605
  136.9 0.1 add_1_3.1
  137.2 2.7 %collective-permute-start.9 = (bf16[512,256]{1,0:T(8,128)(2,1)S(1)}, bf16[512,256]{1,0:T(8,128)(2,1)S(1)}, u32[]{:S(2)}, u32[]{:S(2)}) collective-permute-start(bf16[512,256]{1,0:T(8,128)(2,1)S(1)} %get-tuple-element.90.refs_2_), channel_id=1, source_target_pairs={{0,14},{2,0},{4,2},{6,4},{8,6},{10,8},{12,10},{14,12},{1,15},{3,1}... | collective-permute-start | bytes 786440 | tf_op jit(solution)/shard_map/ppermute | solution.py:605
  139.8 0.9 collective-permute-done.5.refs_1_
  140.7 2.1 %collective-permute-done.4.refs_0_ = bf16[512,256]{1,0:T(8,128)(2,1)S(1)} collective-permute-done((bf16[512,256]{1,0:T(8,128)(2,1)S(1)}, bf16[512,256]{1,0:T(8,128)(2,1)S(1)}, u32[]{:S(2)}, u32[]{:S(2)}) %collective-permute-start.4) | collective-permute-done | bytes 262176 | tf_op jit(solution)/shard_map/ppermute | solution.py:605
  143.0 0.5 collective-permute-start.12
  143.5 1.0 collective-permute-start.8
  144.5 3.9 %collective-permute-done.10.refs_1_ = bf16[512,256]{1,0:T(8,128)(2,1)S(1)} collective-permute-done((bf16[512,256]{1,0:T(8,128)(2,1)S(1)}, bf16[512,256]{1,0:T(8,128)(2,1)S(1)}, u32[]{:S(2)}, u32[]{:S(2)}) %collective-permute-start.10) | collective-permute-done | bytes 262176 | tf_op jit(solution)/shard_map/ppermute | solution.py:605
  148.5 0.1 add_1_2.1
  148.7 2.7 %collective-permute-start.13 = (bf16[512,256]{1,0:T(8,128)(2,1)S(1)}, bf16[512,256]{1,0:T(8,128)(2,1)S(1)}, u32[]{:S(2)}, u32[]{:S(2)}) collective-permute-start(bf16[512,256]{1,0:T(8,128)(2,1)S(1)} %get-tuple-element.94.refs_1_), channel_id=1, source_target_pairs={{0,14},{2,0},{4,2},{6,4},{8,6},{10,8},{12,10},{14,12},{1,15},{3,1}... | collective-permute-start | bytes 786440 | tf_op jit(solution)/shard_map/ppermute | solution.py:605
  151.3 2.7 %collective-permute-done.8.refs_0_ = bf16[512,256]{1,0:T(8,128)(2,1)S(1)} collective-permute-done((bf16[512,256]{1,0:T(8,128)(2,1)S(1)}, bf16[512,256]{1,0:T(8,128)(2,1)S(1)}, u32[]{:S(2)}, u32[]{:S(2)}) %collective-permute-start.8) | collective-permute-done | bytes 262176 | tf_op jit(solution)/shard_map/ppermute | solution.py:605
  154.2 2.6 %collective-permute-done.13.refs_0_ = bf16[512,256]{1,0:T(8,128)(2,1)S(1)} collective-permute-done((bf16[512,256]{1,0:T(8,128)(2,1)S(1)}, bf16[512,256]{1,0:T(8,128)(2,1)S(1)}, u32[]{:S(2)}, u32[]{:S(2)}) %collective-permute-start.13) | collective-permute-done | bytes 262176 | tf_op jit(solution)/shard_map/ppermute | solution.py:605
  156.9 2.6 %collective-permute-start.14 = (bf16[512,256]{1,0:T(8,128)(2,1)S(1)}, bf16[512,256]{1,0:T(8,128)(2,1)S(1)}, u32[]{:S(2)}, u32[]{:S(2)}) collective-permute-start(bf16[512,256]{1,0:T(8,128)(2,1)S(1)} %add_1_1.1), channel_id=1, source_target_pairs={{0,14},{2,0},{4,2},{6,4},{8,6},{10,8},{12,10},{14,12},{1,15},{3,1}... | collective-permute-start | bytes 786440 | tf_op jit(solution)/shard_map/ppermute | solution.py:605
  159.7 5.6 %collective-permute-done.11.refs_0_ = bf16[512,256]{1,0:T(8,128)(2,1)S(1)} collective-permute-done((bf16[512,256]{1,0:T(8,128)(2,1)S(1)}, bf16[512,256]{1,0:T(8,128)(2,1)S(1)}, u32[]{:S(2)}, u32[]{:S(2)}) %collective-permute-start.11) | collective-permute-done | bytes 262176 | tf_op jit(solution)/shard_map/ppermute | solution.py:605
  165.3 1.0 weights_last.1
  166.3 12.0 %all-to-all-start.4 = ((bf16[32,16,512]{2,1,0:T(8,128)(2,1)}), bf16[32,16,512]{2,1,0:T(8,128)(2,1)S(1)}, u32[]{:S(2)}, u32[]{:S(2)}) async-start(bf16[32,16,512]{2,1,0:T(8,128)(2,1)} %bitcast.18), calls=%async_computation.4 | async-start | bytes 1048576 | tf_op jit(solution)/shard_map/all_to_all | solution.py:757
  178.4 0.7 reshape.55
  179.1 2.0 %reshape.57 = bf16[2,256,2,2,128]{4,3,2,1,0:T(2,128)(2,1)} reshape(bf16[512,512]{1,0:T(8,128)(2,1)} %get-tuple-element.84.refs_2_) | data formatting | bytes 1048576 | tf_op jit(solution)/shard_map/reshape | solution.py:767
  181.0 2.1 %sum_dq.1 = bf16[4,32,2048]{2,1,0:T(8,128)(2,1)} custom-call(s32[34]{0:T(128)S(1)} %copy-done.7, bf16[16,32,2048]{2,1,0:T(8,128)(2,1)S(1)} %all-to-all-done.3.refs_0_.refs_1_.refs_2_.refs_3_, bf16[16,32,2048]{2,1,0:T(8,128)(2,1)S(1)} %all-to-all-done.3.refs_0_.refs_1_.refs_2_.refs_3_, ...), custom_call_target="tpu_custom_call" | custom-call | flops 2000000 | bytes 4194304 | tf_op jit(solution)/shard_map/sum_dq/pallas_call | solution.py:495
  183.2 6.7 %all-to-all-done.4 = bf16[32,16,512]{2,1,0:T(8,128)(2,1)S(1)} async-done(((bf16[32,16,512]{2,1,0:T(8,128)(2,1)}), bf16[32,16,512]{2,1,0:T(8,128)(2,1)S(1)}, u32[]{:S(2)}, u32[]{:S(2)}) %all-to-all-start.4) | async-done | bytes 524320 | tf_op jit(solution)/shard_map/all_to_all | solution.py:757
  189.9 0.7 finish_weights.1
  (52 shorter events, 0.9 us)
Async XLA Ops:
  8.5 57.6 %copy-start.16 = (bf16[4,32,2,256]{3,2,1,0:T(2,128)(2,1)S(1)}, bf16[4,32,2,256]{3,2,1,0:T(2,128)(2,1)}, u32[]{:S(2)}) copy-start(bf16[4,32,2,256]{3,2,1,0:T(2,128)(2,1)} %param.10) | copy-start | bytes 393220
  66.2 9.0 %copy-start.14 = (bf16[4,16,4096]{2,1,0:T(8,128)(2,1)S(1)}, bf16[4,16,4096]{2,1,0:T(8,128)(2,1)}, u32[]{:S(2)}) copy-start(bf16[4,16,4096]{2,1,0:T(8,128)(2,1)} %param.12) | copy-start | bytes 1572868
  66.2 12.6 %copy-start = (bf16[4,32,2048]{2,1,0:T(8,128)(2,1)S(1)}, bf16[4,32,2048]{2,1,0:T(8,128)(2,1)}, u32[]{:S(2)}) copy-start(bf16[4,32,2048]{2,1,0:T(8,128)(2,1)} %q_ref.3) | copy-start | bytes 1572868
  66.3 12.6 %copy-start.1 = (bf16[4,32,2048]{2,1,0:T(8,128)(2,1)S(1)}, bf16[4,32,2048]{2,1,0:T(8,128)(2,1)}, u32[]{:S(2)}) copy-start(bf16[4,32,2048]{2,1,0:T(8,128)(2,1)} %g_ref.3) | copy-start | bytes 1572868
  73.2 6.9 %collective-permute-start = (bf16[2,128,4096]{2,1,0:T(8,128)(2,1)}, bf16[2,128,4096]{2,1,0:T(8,128)(2,1)}, u32[]{:S(2)}, u32[]{:S(2)}) collective-permute-start(bf16[2,128,4096]{2,1,0:T(8,128)(2,1)} %param.13), channel_id=1, source_target_pairs={{0,1},{1,0},{2,3},{3,2},{4,5},{5,4},{6,7},{7,6},{8,9},{9,8},{10,11... | collective-permute-start | bytes 6291464 | tf_op jit(solution)/shard_map/ppermute | solution.py:664
  75.2 4.4 %collective-permute-start.1 = (bf16[4,16,4096]{2,1,0:T(8,128)(2,1)S(1)}, bf16[4,16,4096]{2,1,0:T(8,128)(2,1)S(1)}, u32[]{:S(2)}, u32[]{:S(2)}) collective-permute-start(bf16[4,16,4096]{2,1,0:T(8,128)(2,1)S(1)} %copy-done.14), channel_id=1, source_target_pairs={{0,1},{1,0},{2,3},{3,2},{4,5},{5,4},{6,7},{7,6},{8,9},{9,8},{10,11... | collective-permute-start | bytes 1572872 | tf_op jit(solution)/shard_map/ppermute | solution.py:664
  75.4 10.0 %all-to-all-start.1 = ((f32[16,4,256]{2,1,0:T(4,128)}), f32[16,4,256]{2,1,0:T(4,128)S(1)}, u32[]{:S(2)}, u32[]{:S(2)}) async-start(f32[16,4,256]{2,1,0:T(4,128)} %owner_stats.1), calls=%async_computation.1 | async-start | bytes 131072 | tf_op jit(solution)/shard_map/all_to_all | solution.py:661
  79.7 0.8 copy-start.15
  80.4 4.9 %copy-start.6 = (s32[16,1,16]{2,1,0:T(1,128)S(1)}, s32[16,1,16]{2,1,0:T(1,128)}, u32[]{:S(2)}) copy-start(s32[16,1,16]{2,1,0:T(1,128)} %param.14) | copy-start | bytes 3076
  86.7 12.6 %all-to-all-start.2 = ((f32[16,4,256]{2,1,0:T(4,128)}), f32[16,4,256]{2,1,0:T(4,128)S(1)}, u32[]{:S(2)}, u32[]{:S(2)}) async-start(f32[16,4,256]{2,1,0:T(4,128)} %get-tuple-element.70), calls=%async_computation.2 | async-start | bytes 131072 | tf_op jit(solution)/shard_map/all_to_all | solution.py:661
  98.7 0.7 copy-start.4
  99.3 0.6 copy-start.17
  115.9 14.2 %copy-start.2 = (bf16[512,512]{1,0:T(8,128)(2,1)S(1)}, bf16[512,512]{1,0:T(8,128)(2,1)}, u32[]{:S(2)}) copy-start(bf16[512,512]{1,0:T(8,128)(2,1)} %get-tuple-element.84.refs_2_) | copy-start | bytes 1572868
  116.0 14.1 %collective-permute-start.2 = (bf16[512,256]{1,0:T(8,128)(2,1)}, bf16[512,256]{1,0:T(8,128)(2,1)S(1)}, u32[]{:S(2)}, u32[]{:S(2)}) collective-permute-start(bf16[512,256]{1,0:T(8,128)(2,1)} %bitcast.43), channel_id=1, source_target_pairs={{0,2},{2,4},{4,6},{6,8},{8,10},{10,12},{12,14},{14,0},{1,3},{3,5},... | collective-permute-start | bytes 786440 | tf_op jit(solution)/shard_map/ppermute | solution.py:605
  117.7 12.4 %collective-permute-start.3 = (bf16[512,256]{1,0:T(8,128)(2,1)}, bf16[512,256]{1,0:T(8,128)(2,1)}, u32[]{:S(2)}, u32[]{:S(2)}) collective-permute-start(bf16[512,256]{1,0:T(8,128)(2,1)} %bitcast.42), channel_id=1, source_target_pairs={{0,14},{2,0},{4,2},{6,4},{8,6},{10,8},{12,10},{14,12},{1,15},{3,1}... | collective-permute-start | bytes 786440 | tf_op jit(solution)/shard_map/ppermute | solution.py:605
  121.7 44.6 %all-to-all-start.3 = ((bf16[16,32,2048]{2,1,0:T(8,128)(2,1)}), bf16[16,32,2048]{2,1,0:T(8,128)(2,1)S(1)}, u32[]{:S(2)}, u32[]{:S(2)}) async-start(bf16[16,32,2048]{2,1,0:T(8,128)(2,1)} %get-tuple-element.98), calls=%async_computation.3 | async-start | bytes 4194304 | tf_op jit(solution)/shard_map/all_to_all | solution.py:661
  128.4 6.6 %collective-permute-start.6 = (bf16[512,256]{1,0:T(8,128)(2,1)}, bf16[512,256]{1,0:T(8,128)(2,1)S(1)}, u32[]{:S(2)}, u32[]{:S(2)}) collective-permute-start(bf16[512,256]{1,0:T(8,128)(2,1)} %bitcast.41), channel_id=1, source_target_pairs={{0,14},{2,0},{4,2},{6,4},{8,6},{10,8},{12,10},{14,12},{1,15},{3,1}... | collective-permute-start | bytes 786440 | tf_op jit(solution)/shard_map/ppermute | solution.py:605
  130.0 6.9 %collective-permute-start.7 = (bf16[512,256]{1,0:T(8,128)(2,1)}, bf16[512,256]{1,0:T(8,128)(2,1)S(1)}, u32[]{:S(2)}, u32[]{:S(2)}) collective-permute-start(bf16[512,256]{1,0:T(8,128)(2,1)} %bitcast.40), channel_id=1, source_target_pairs={{0,2},{2,4},{4,6},{6,8},{8,10},{10,12},{12,14},{14,0},{1,3},{3,5},... | collective-permute-start | bytes 786440 | tf_op jit(solution)/shard_map/ppermute | solution.py:605
  130.1 1.0 copy-start.8
  131.1 5.8 %copy-start.11 = (bf16[2,512,256]{2,1,0:T(8,128)(2,1)S(1)}, bf16[2,512,256]{2,1,0:T(8,128)(2,1)}, u32[]{:S(2)}) copy-start(bf16[2,512,256]{2,1,0:T(8,128)(2,1)} %get-tuple-element.87.blocks_ref) | copy-start | bytes 1572868
  132.3 8.4 %collective-permute-start.5 = (bf16[512,256]{1,0:T(8,128)(2,1)S(1)}, bf16[512,256]{1,0:T(8,128)(2,1)S(1)}, u32[]{:S(2)}, u32[]{:S(2)}) collective-permute-start(bf16[512,256]{1,0:T(8,128)(2,1)S(1)} %get-tuple-element.86), channel_id=1, source_target_pairs={{0,14},{2,0},{4,2},{6,4},{8,6},{10,8},{12,10},{14,12},{1,15},{3,1}... | collective-permute-start | bytes 786440 | tf_op jit(solution)/shard_map/ppermute | solution.py:605
  134.9 7.9 %collective-permute-start.4 = (bf16[512,256]{1,0:T(8,128)(2,1)S(1)}, bf16[512,256]{1,0:T(8,128)(2,1)S(1)}, u32[]{:S(2)}, u32[]{:S(2)}) collective-permute-start(bf16[512,256]{1,0:T(8,128)(2,1)S(1)} %get-tuple-element.85.refs_2_), channel_id=1, source_target_pairs={{0,2},{2,4},{4,6},{6,8},{8,10},{10,12},{12,14},{14,0},{1,3},{3,5},... | collective-permute-start | bytes 786440 | tf_op jit(solution)/shard_map/ppermute | solution.py:605
  136.9 5.9 %copy-start.10 = (bf16[2,512,256]{2,1,0:T(8,128)(2,1)S(1)}, bf16[2,512,256]{2,1,0:T(8,128)(2,1)}, u32[]{:S(2)}) copy-start(bf16[2,512,256]{2,1,0:T(8,128)(2,1)} %get-tuple-element.80.blocks_ref) | copy-start | bytes 1572868
  137.1 11.4 %collective-permute-start.10 = (bf16[512,256]{1,0:T(8,128)(2,1)S(1)}, bf16[512,256]{1,0:T(8,128)(2,1)S(1)}, u32[]{:S(2)}, u32[]{:S(2)}) collective-permute-start(bf16[512,256]{1,0:T(8,128)(2,1)S(1)} %get-tuple-element.93), channel_id=1, source_target_pairs={{0,2},{2,4},{4,6},{6,8},{8,10},{10,12},{12,14},{14,0},{1,3},{3,5},... | collective-permute-start | bytes 786440 | tf_op jit(solution)/shard_map/ppermute | solution.py:605
  137.2 11.3 %collective-permute-start.9 = (bf16[512,256]{1,0:T(8,128)(2,1)S(1)}, bf16[512,256]{1,0:T(8,128)(2,1)S(1)}, u32[]{:S(2)}, u32[]{:S(2)}) collective-permute-start(bf16[512,256]{1,0:T(8,128)(2,1)S(1)} %get-tuple-element.90.refs_2_), channel_id=1, source_target_pairs={{0,14},{2,0},{4,2},{6,4},{8,6},{10,8},{12,10},{14,12},{1,15},{3,1}... | collective-permute-start | bytes 786440 | tf_op jit(solution)/shard_map/ppermute | solution.py:605
  142.8 5.6 %copy-start.9 = (bf16[2,512,256]{2,1,0:T(8,128)(2,1)S(1)}, bf16[2,512,256]{2,1,0:T(8,128)(2,1)}, u32[]{:S(2)}) copy-start(bf16[2,512,256]{2,1,0:T(8,128)(2,1)} %get-tuple-element.92.blocks_ref) | copy-start | bytes 1572868
  143.0 16.6 %collective-permute-start.12 = (bf16[512,256]{1,0:T(8,128)(2,1)S(1)}, bf16[512,256]{1,0:T(8,128)(2,1)S(1)}, u32[]{:S(2)}, u32[]{:S(2)}) collective-permute-start(bf16[512,256]{1,0:T(8,128)(2,1)S(1)} %get-tuple-element.95), channel_id=1, source_target_pairs={{0,14},{2,0},{4,2},{6,4},{8,6},{10,8},{12,10},{14,12},{1,15},{3,1}... | collective-permute-start | bytes 786440 | tf_op jit(solution)/shard_map/ppermute | solution.py:605
  143.5 10.6 %collective-permute-start.8 = (bf16[512,256]{1,0:T(8,128)(2,1)S(1)}, bf16[512,256]{1,0:T(8,128)(2,1)S(1)}, u32[]{:S(2)}, u32[]{:S(2)}) collective-permute-start(bf16[512,256]{1,0:T(8,128)(2,1)S(1)} %get-tuple-element.91.refs_2_), channel_id=1, source_target_pairs={{0,2},{2,4},{4,6},{6,8},{8,10},{10,12},{12,14},{14,0},{1,3},{3,5},... | collective-permute-start | bytes 786440 | tf_op jit(solution)/shard_map/ppermute | solution.py:605
  148.4 5.6 %copy-start.13 = (bf16[1,512,256]{2,1,0:T(8,128)(2,1)S(1)}, bf16[1,512,256]{2,1,0:T(8,128)(2,1)}, u32[]{:S(2)}) copy-start(bf16[1,512,256]{2,1,0:T(8,128)(2,1)} %get-tuple-element.79.blocks_ref) | copy-start | bytes 786436
  148.6 11.1 %collective-permute-start.15 = (bf16[512,256]{1,0:T(8,128)(2,1)S(1)}, bf16[512,256]{1,0:T(8,128)(2,1)S(1)}, u32[]{:S(2)}, u32[]{:S(2)}) collective-permute-start(bf16[512,256]{1,0:T(8,128)(2,1)S(1)} %get-tuple-element.97), channel_id=1, source_target_pairs={{0,2},{2,4},{4,6},{6,8},{8,10},{10,12},{12,14},{14,0},{1,3},{3,5},... | collective-permute-start | bytes 786440 | tf_op jit(solution)/shard_map/ppermute | solution.py:605
  148.7 8.2 %collective-permute-start.13 = (bf16[512,256]{1,0:T(8,128)(2,1)S(1)}, bf16[512,256]{1,0:T(8,128)(2,1)S(1)}, u32[]{:S(2)}, u32[]{:S(2)}) collective-permute-start(bf16[512,256]{1,0:T(8,128)(2,1)S(1)} %get-tuple-element.94.refs_1_), channel_id=1, source_target_pairs={{0,14},{2,0},{4,2},{6,4},{8,6},{10,8},{12,10},{14,12},{1,15},{3,1}... | collective-permute-start | bytes 786440 | tf_op jit(solution)/shard_map/ppermute | solution.py:605
  154.1 2.8 %copy-start.12 = (bf16[1,512,256]{2,1,0:T(8,128)(2,1)S(1)}, bf16[1,512,256]{2,1,0:T(8,128)(2,1)}, u32[]{:S(2)}) copy-start(bf16[1,512,256]{2,1,0:T(8,128)(2,1)} %get-tuple-element.96.blocks_ref) | copy-start | bytes 786436
  154.1 11.2 %collective-permute-start.11 = (bf16[512,256]{1,0:T(8,128)(2,1)S(1)}, bf16[512,256]{1,0:T(8,128)(2,1)S(1)}, u32[]{:S(2)}, u32[]{:S(2)}) collective-permute-start(bf16[512,256]{1,0:T(8,128)(2,1)S(1)} %add_0_1.1.refs_1_), channel_id=1, source_target_pairs={{0,2},{2,4},{4,6},{6,8},{8,10},{10,12},{12,14},{14,0},{1,3},{3,5},... | collective-permute-start | bytes 786440 | tf_op jit(solution)/shard_map/ppermute | solution.py:605
  156.9 8.4 %copy-start.3 = (bf16[2,512,256]{2,1,0:T(8,128)(2,1)S(1)}, bf16[2,512,256]{2,1,0:T(8,128)(2,1)}, u32[]{:S(2)}) copy-start(bf16[2,512,256]{2,1,0:T(8,128)(2,1)} %get-tuple-element.78.blocks_ref) | copy-start | bytes 1572868
  156.9 21.4 %copy-start.5 = (bf16[128,512]{1,0:T(8,128)(2,1)S(1)}, bf16[128,512]{1,0:T(8,128)(2,1)}, u32[]{:S(2)}) copy-start(bf16[128,512]{1,0:T(8,128)(2,1)} %copy-done.4) | copy-start | bytes 393220
  156.9 24.1 %copy-start.7 = (s32[34]{0:T(128)S(1)}, s32[34]{0:T(128)}, u32[]{:S(2)}) copy-start(s32[34]{0:T(128)} %get-tuple-element.55.table.owners) | copy-start | bytes 412
  156.9 8.4 %collective-permute-start.14 = (bf16[512,256]{1,0:T(8,128)(2,1)S(1)}, bf16[512,256]{1,0:T(8,128)(2,1)S(1)}, u32[]{:S(2)}, u32[]{:S(2)}) collective-permute-start(bf16[512,256]{1,0:T(8,128)(2,1)S(1)} %add_1_1.1), channel_id=1, source_target_pairs={{0,14},{2,0},{4,2},{6,4},{8,6},{10,8},{12,10},{14,12},{1,15},{3,1}... | collective-permute-start | bytes 786440 | tf_op jit(solution)/shard_map/ppermute | solution.py:605
  166.3 23.6 %all-to-all-start.4 = ((bf16[32,16,512]{2,1,0:T(8,128)(2,1)}), bf16[32,16,512]{2,1,0:T(8,128)(2,1)S(1)}, u32[]{:S(2)}, u32[]{:S(2)}) async-start(bf16[32,16,512]{2,1,0:T(8,128)(2,1)} %bitcast.18), calls=%async_computation.4 | async-start | bytes 1048576 | tf_op jit(solution)/shard_map/all_to_all | solution.py:757

commit v7 on v6

--- a/solution.py
+++ b/solution.py
@@ -293,14 +293,17 @@
     joint_ref,
     kv_ref,
     own_ref,
-    lower_ref,
-    upper_ref,
+    mine_pass,
+    other_pass,
+    mine_query,
+    other_query,
     grad_out,
     dq_out,
     *rest,
 ):
-    outs = rest[:-12]
-    acc_ref, got_ref, h_ref, grad_ref, dq_ref, block_ref, turned_ref = rest[-12:-5]
+    outs = rest[:-14]
+    acc_ref, got_ref, h_ref, grad_ref, dq_ref, block_ref, turned_ref, mixed_ref = rest[-14:-6]
+    plain_ref = rest[-6]
     got_sems, h_sem, grad_sem, dq_sems, sems = rest[-5:]
     peers, both, _ = got_ref.shape
     steps = got_sems.shape[0]
@@ -310,13 +313,26 @@
     heads = kv_ref.shape[3] // HD
     for load in load_groups(got_hbm, got_ref, got_sems):
         load.start()
-    share = lower_ref.shape[1]
-    hidden_loads = [
-        pltpu.make_async_copy(src, h_ref.at[:, pl.ds(i * share, share)], h_sem.at[i])
-        for i, src in enumerate((lower_ref, upper_ref))
-    ]
-    for load in hidden_loads:
-        load.start()
+    groups, share, _ = h_ref.shape
+    tile = groups * share // peers
+    part = share // peers
+
+    def hidden_loads(step):
+        lanes = pl.ds(pl.multiple_of(step * per * tile, per * tile), per * tile)
+        loads, row = [], 0
+        for k, src in enumerate((mine_pass, other_pass, mine_query, other_query)):
+            rows_here = pl.ds(row, src.shape[0])
+            loads.append(
+                pltpu.make_async_copy(
+                    src.at[:, lanes], plain_ref.at[rows_here, lanes], h_sem.at[step, k]
+                )
+            )
+            row += src.shape[0]
+        return loads
+
+    for step in range(steps):
+        for load in hidden_loads(step):
+            load.start()
     acc_ref[...] = jnp.zeros_like(acc_ref)
     for slot in range(turned_ref.shape[0]):
         turned_ref[slot] = kv_ref[0, slot].T
@@ -324,8 +340,15 @@
     @pl.loop(0, steps)
     def _(step):
         wait_group(step, got_hbm, got_ref, got_sems)
+        for load in hidden_loads(step):
+            load.wait()
         for one in range(per):
             reader = step * per + one
+            first = pl.multiple_of(reader * tile, tile)
+            turned = plain_ref[:, pl.ds(first, tile)].T
+            for k in range(groups):
+                place = pl.ds(pl.multiple_of(reader * part, part), part)
+                h_ref[k, place] = turned[k * part : (k + 1) * part]
             slot = table[reader]
             valid = passage_valid(table[peers + slot], slot_len, group * rows)
             for head in range(heads):
@@ -352,24 +375,20 @@
                 for r in range(group):
                     column = (head * group + r) * HD
                     dq_ref[reader, :, column : column + HD] = dq[r * rows : (r + 1) * rows]
-        part = pl.ds(step * per, per)
-        pltpu.make_async_copy(dq_ref.at[part], dq_out.at[part], dq_sems.at[step]).start()
+        done = pl.ds(step * per, per)
+        pltpu.make_async_copy(dq_ref.at[done], dq_out.at[done], dq_sems.at[step]).start()
 
     for one in range(acc_ref.shape[0]):
         grad_ref[one * slot_len : (one + 1) * slot_len] = acc_ref[one].astype(BF16)
     copies = [pltpu.make_async_copy(grad_ref, grad_out, grad_sem)]
     copies[0].start()
-    for load in hidden_loads:
-        load.wait()
     count = h_ref.shape[0]
-    tokens = grad_ref.shape[0]
+    mix_tokens(grad_ref, mixed_ref, 0, acc_ref.shape[0])
+    mix_tokens(own_ref, mixed_ref, grad_ref.shape[0], own_ref.shape[0] // rows)
     k = 0
     for place, uses in places:
         pass_group = lax.rem(lax.axis_index("pass") + (place + count), count)
-        total = jnp.dot(h_ref[pass_group, :, :tokens], grad_ref[...], preferred_element_type=F32)
-        total = total + jnp.dot(
-            h_ref[pass_group, :, tokens:], own_ref[...], preferred_element_type=F32
-        )
+        total = jnp.dot(h_ref[pass_group], mixed_ref[...], preferred_element_type=F32)
         for head, out, row in uses:
             lanes = slice(2 * head * HD, 2 * (head + 1) * HD)
             block_ref[k] = total[:, lanes].astype(BF16)
@@ -384,12 +403,23 @@
         wait_group(step, dq_ref, dq_out, dq_sems)
 
 
-def owner_grads(places, depths, table, got, joint, kv, hidden_t, grads_query):
+def mix_tokens(src, out_ref, start, pieces):
+    half = src.shape[0] // pieces // 2
+    core = lax.axis_index("tensor")
+    for k, side in enumerate((core, 1 - core)):
+        for piece in range(pieces):
+            first = pl.multiple_of((2 * piece + side) * half, half)
+            row = start + (k * pieces + piece) * half
+            out_ref[row : row + half] = src[pl.ds(first, half)]
+
+
+def owner_grads(places, depths, table, got, joint, kv, hidden, grads_query, groups):
     peers, both, width = got.shape
     _, slots, slot_len, channels = kv.shape
     columns = joint.shape[2]
-    groups, half, tokens = hidden_t[0].shape
-    share = 2 * half
+    tokens = sum(one.shape[0] for one in hidden)
+    model_width = hidden[0].shape[1]
+    share = model_width // groups
     count = sum(depths)
     grads = jax.ShapeDtypeStruct((slots * slot_len, 2 * channels), BF16)
     dq = jax.ShapeDtypeStruct((peers, both // 2, width), BF16)
@@ -400,7 +430,7 @@
             dq,
             *[jax.ShapeDtypeStruct((depth, share, 2 * HD), BF16) for depth in depths],
         ),
-        in_specs=[smem(), in_hbm(), whole(), whole(), whole(), in_hbm(), in_hbm()],
+        in_specs=[smem(), in_hbm(), whole(), whole(), whole()] + [in_hbm()] * 4,
         out_specs=tuple(in_hbm() for _ in range(2 + len(depths))),
         scratch_shapes=[
             pltpu.VMEM((slots, slot_len, 2 * channels), F32),
@@ -410,8 +440,10 @@
             pltpu.VMEM(dq.shape, BF16),
             pltpu.VMEM((count, share, 2 * HD), BF16),
             pltpu.VMEM((slots, channels, slot_len), BF16),
+            pltpu.VMEM((tokens, 2 * channels), BF16),
+            pltpu.VMEM((tokens, model_width), BF16),
             pltpu.SemaphoreType.DMA((4,)),
-            pltpu.SemaphoreType.DMA((2,)),
+            pltpu.SemaphoreType.DMA((4, 4)),
             pltpu.SemaphoreType.DMA,
             pltpu.SemaphoreType.DMA((4,)),
             pltpu.SemaphoreType.DMA((count,)),
@@ -419,7 +451,7 @@
         compiler_params=params(VMEM_MOST),
         cost_estimate=cost(16 * 10**9, 24 * 2**20, 2 * 10**6),
         name="owner_grads",
-    )(table, got, joint, kv, grads_query, *hidden_t)
+    )(table, got, joint, kv, grads_query, *hidden)
 
 
 def own_grads_kernel(group, q_ref, g_ref, k_ref, v_ref, joint_ref, grad_ref, dq_ref):
@@ -508,54 +540,6 @@
     )(table, *[one for one in returned for _ in range(per)], own)
 
 
-def transpose_kernel(slots, samples, owners, core, mine_p, other_p, mine_q, other_q, out_ref):
-    groups, share, _ = out_ref.shape
-    lower = core[0] == 0
-    first_p = jnp.where(lower, mine_p[...], other_p[...])
-    second_p = jnp.where(lower, other_p[...], mine_p[...])
-    first_q = jnp.where(lower, mine_q[...], other_q[...])
-    second_q = jnp.where(lower, other_q[...], mine_q[...])
-    half = first_p.shape[0] // slots
-    part = first_q.shape[0] // samples
-    pieces = []
-    for slot in range(slots):
-        pieces.append(first_p[slot * half : (slot + 1) * half])
-        pieces.append(second_p[slot * half : (slot + 1) * half])
-    for sample in range(samples):
-        pieces.append(first_q[sample * part : (sample + 1) * part])
-        pieces.append(second_q[sample * part : (sample + 1) * part])
-    turned = jnp.concatenate(pieces, axis=0).T
-    rows = share // owners
-    for owner in range(owners):
-        for group in range(groups):
-            first = (owner * groups + group) * rows
-            out_ref[group, owner * rows : (owner + 1) * rows] = turned[first : first + rows]
-
-
-def transpose_hidden(core, hidden, slots, samples, owners, groups, half):
-    width = hidden[0].shape[1]
-    tokens = sum(one.shape[0] for one in hidden)
-    per = 2
-    tile = per * width // owners
-    steps = width // tile // 2
-    return pl.pallas_call(
-        functools.partial(transpose_kernel, slots, samples, per),
-        out_shape=jax.ShapeDtypeStruct((groups, width // groups // 2, tokens), BF16),
-        grid_spec=pltpu.PrefetchScalarGridSpec(
-            num_scalar_prefetch=1,
-            grid=(steps,),
-            in_specs=[
-                pl.BlockSpec((one.shape[0], tile), lambda i, c: (0, half * steps + i))
-                for one in hidden
-            ],
-            out_specs=pl.BlockSpec((groups, tile // groups, tokens), lambda i, c: (0, i, 0)),
-        ),
-        compiler_params=params(VMEM_MOST),
-        cost_estimate=cost(0, 12 * 2**20),
-        name=f"transpose_hidden_{half}",
-    )(core, *hidden)
-
-
 def add_kernel(count, blocks_ref, *refs):
     outs = refs[len(refs) - count :]
     for k, (arrived, out_ref) in enumerate(zip(refs, outs)):
@@ -687,22 +671,13 @@
         for one in (both, from_partner(both))
     ]
 
-    def turned_half(half):
-        core = lax.axis_index("tensor").reshape(1)
-        return transpose_hidden(core, hidden, slots, samples, peers, groups, half)
-
-    lower = turned_half(0)
-    stats, lower = lax.optimization_barrier((stats, lower))
+    stats, *hidden = lax.optimization_barrier((stats, *hidden))
     back, merged = merge(refs, stats, own, slots)
     joint = exchange(back)
     grads_query, own_dq = own_grads(
         question_q, question_grad, own_keys, own_values, merged, group
     )
-    upper = turned_half(1)
-    joint, grads_query, own_dq, upper = lax.optimization_barrier(
-        (joint, grads_query, own_dq, upper)
-    )
-    hidden_t = [lower, upper]
+    joint, grads_query, own_dq = lax.optimization_barrier((joint, grads_query, own_dq))
     far = groups // 2
     depths, homes = [], {}
 
@@ -727,7 +702,7 @@
         for place in [far, *range(far - 1, -far, -1)]
     ]
     grads_pass, dq_parts, *blocks = owner_grads(
-        places, depths, table, got, joint, kv, hidden_t, grads_query
+        places, depths, table, got, joint, kv, hidden, grads_query, groups
     )
     sums = [
         travel([blocks[ahead][0], blocks[behind][0]], head)

time: 192 us -> 188 us (0.979)
  waiting for transfers between devices: 28.1 us -> 38.4 us
  Pallas kernels: 45.4 us -> 37.7 us
  starting transfers between devices: 50 us -> 44.3 us
    all_to_all x3, waiting for transfers between devices: 0.59 us -> 9.86 us  [exchange(): return lax.all_to_all(x, 'dp', split_axis=0, concat_axis=0, tiled=True)]
    pallas_call x2 -> x0, Pallas kernels: 8.63 us -> none  [transpose_hidden(): pl.pallas_call(functools.partial(transpose_kernel, slots, samples, per),...]
    all_to_all x3, starting transfers between devices: 15.9 us -> 10.9 us  [exchange(): return lax.all_to_all(x, 'dp', split_axis=0, concat_axis=0, tiled=True)]
  transfers between devices with their start and end apart: 20 -> 20, of which waited for: 12 -> 11; matrix products, arithmetic and copies ran while one was open for 1% -> 1% of each run, Pallas kernels for 8% -> 4%
where the time goes in v7:
time: 188 us; the launch traced here: 187 us
  blocking collectives  57.7 us (31%)
  starting transfers between devices  44.3 us (24%)
  waiting for transfers between devices  38.4 us (20%)
  Pallas kernels  37.7 us (20%)
  local copies, waits for them, and re-layouts  8.32 us (4%)
    all_to_all x1, blocking collectives, exchange(): return lax.all_to_all(x, 'dp', split_axis=0, concat_axis=0, tiled=True)  57.7 us
    ppermute x14, waiting for transfers between devices, travel(): lax.ppermute(block, 'pass', [(i, (i + way) % count) for i in range(count)])  21.8 us
    ppermute x14, starting transfers between devices, travel(): lax.ppermute(block, 'pass', [(i, (i + way) % count) for i in range(count)])  19.3 us
    pallas_call x1, Pallas kernels, owner_grads(): pl.pallas_call(functools.partial(owner_grads_kernel, 2 * columns // both,...  16.9 us
    all_to_all x1, starting transfers between devices, local(): lax.all_to_all(summed.reshape(peers * cores, share, -1), ('dp', 'tensor')...  12 us
    all_to_all x3, starting transfers between devices, exchange(): return lax.all_to_all(x, 'dp', split_axis=0, concat_axis=0, tiled=True)  10.9 us
    all_to_all x3, waiting for transfers between devices, exchange(): return lax.all_to_all(x, 'dp', split_axis=0, concat_axis=0, tiled=True)  9.86 us
    pallas_call x1, Pallas kernels, owner_stats(): pl.pallas_call(functools.partial(owner_stats_kernel, group), out_shape=ja...  6.91 us
  transfers between devices with their start and end apart: 20, of which 11 were waited for; matrix products, arithmetic and copies ran while one was open for 1% of the time, Pallas kernels for 4%

profile of v7, /device:TPU:1, one launch (start us, length us, event | category | flops | bytes accessed | tf_op | source)
XLA Modules:
  0.0 187.3 jit_solution(16509763105232843637)
XLA Ops:
  0.6 1.4 copy.12.blocks
  2.0 1.9 %copy.19 = bf16[2,256,2,256]{3,1,0,2:T(8,128)(2,1)} copy(bf16[2,256,2,256]{3,2,1,0:T(2,128)(2,1)} %param.11) | data formatting | bytes 1048576 | tf_op args[3]
  3.9 4.6 %pack_queries.1 = (bf16[16,64,2048]{2,1,0:T(8,128)(2,1)}, s32[34]{0:T(128)}) custom-call(s32[16,16]{1,0:T(8,128)} %bitcast.26, s32[16,2]{1,0:T(8,128)} %copy.12.blocks, bf16[4,32,2048]{2,1,0:T(8,128)(2,1)} %q_ref.3, bf16[4,32,2048]{2,1,0:T(8,128)(2,1)} %g_ref.3), custom_call_target="tpu_custom_call" | custom-call | bytes 6291456 | tf_op jit(solution)/shard_map/pack_queries/pallas_call | solution.py:104
  8.5 57.7 %all_to_all.25.got_hbm = bf16[16,64,2048]{2,1,0:T(8,128)(2,1)} all-to-all(bf16[16,64,2048]{2,1,0:T(8,128)(2,1)} %get-tuple-element.58), channel_id=1, replica_groups=mesh['dp'=16,'pass'=8,'tensor'=2] {'dp'}, dimensions={0} | all-to-all | bytes 8388608 | tf_op jit(solution)/shard_map/all_to_all | solution.py:645
  66.3 6.9 %owner_stats.1 = f32[16,4,256]{2,1,0:T(4,128)} custom-call(s32[34]{0:T(128)} %get-tuple-element.57.table.owners, bf16[16,64,2048]{2,1,0:T(8,128)(2,1)} %all_to_all.25.got_hbm, bf16[2,2,256,256]{3,2,1,0:T(8,128)(2,1)} %bitcast.28), custom_call_target="tpu_custom_call" | custom-call | flops 2000000000 | bytes 6291456 | tf_op jit(solution)/shard_map/owner_stats/pallas_call | solution.py:195
  73.2 2.1 %collective-permute-start = (bf16[2,128,4096]{2,1,0:T(8,128)(2,1)}, bf16[2,128,4096]{2,1,0:T(8,128)(2,1)}, u32[]{:S(2)}, u32[]{:S(2)}) collective-permute-start(bf16[2,128,4096]{2,1,0:T(8,128)(2,1)} %param.13), channel_id=1, source_target_pairs={{0,1},{1,0},{2,3},{3,2},{4,5},{5,4},{6,7},{7,6},{8,9},{9,8},{10,11... | collective-permute-start | bytes 6291464 | tf_op jit(solution)/shard_map/ppermute | solution.py:648
  75.3 0.1 collective-permute-start.1
  75.4 3.5 %all-to-all-start.1 = ((f32[16,4,256]{2,1,0:T(4,128)}), f32[16,4,256]{2,1,0:T(4,128)S(1)}, u32[]{:S(2)}, u32[]{:S(2)}) async-start(f32[16,4,256]{2,1,0:T(4,128)} %owner_stats.1), calls=%async_computation.1 | async-start | bytes 131072 | tf_op jit(solution)/shard_map/all_to_all | solution.py:645
  78.9 0.5 own_stats.1.own_ref
  79.4 5.9 %all-to-all-done.1.st_ref = f32[16,4,256]{2,1,0:T(4,128)S(1)} async-done(((f32[16,4,256]{2,1,0:T(4,128)}), f32[16,4,256]{2,1,0:T(4,128)S(1)}, u32[]{:S(2)}, u32[]{:S(2)}) %all-to-all-start.1) | async-done | bytes 65568 | tf_op jit(solution)/shard_map/all_to_all | solution.py:645
  85.4 1.4 merge_stats.1
  86.8 3.5 %all-to-all-start.2 = ((f32[16,4,256]{2,1,0:T(4,128)}), f32[16,4,256]{2,1,0:T(4,128)S(1)}, u32[]{:S(2)}, u32[]{:S(2)}) async-start(f32[16,4,256]{2,1,0:T(4,128)} %get-tuple-element.72), calls=%async_computation.2 | async-start | bytes 131072 | tf_op jit(solution)/shard_map/all_to_all | solution.py:645
  90.3 1.9 own_grads.1
  92.2 0.6 copy-done.4
  92.8 3.9 %all-to-all-done.2.joint_ref = f32[16,4,256]{2,1,0:T(4,128)S(1)} async-done(((f32[16,4,256]{2,1,0:T(4,128)}), f32[16,4,256]{2,1,0:T(4,128)S(1)}, u32[]{:S(2)}, u32[]{:S(2)}) %all-to-all-start.2) | async-done | bytes 65568 | tf_op jit(solution)/shard_map/all_to_all | solution.py:645
  96.7 0.6 copy-done.15
  97.4 16.9 %owner_grads.1 = (bf16[512,512]{1,0:T(8,128)(2,1)}, bf16[16,32,2048]{2,1,0:T(8,128)(2,1)}, bf16[1,512,256]{2,1,0:T(8,128)(2,1)}, bf16[1,512,256]{2,1,0:T(8,128)(...) custom-call(s32[34]{0:T(128)} %get-tuple-element.57.table.owners, ...), custom_call_target="tpu_custom_call" | custom-call | flops 16000000000 | bytes 25165824 | tf_op jit(solution)/shard_map/owner_grads/pallas_call | solution.py:426
  114.3 1.8 collective-permute-start.2
  116.1 4.0 %collective-permute-start.3 = (bf16[512,256]{1,0:T(8,128)(2,1)}, bf16[512,256]{1,0:T(8,128)(2,1)}, u32[]{:S(2)}, u32[]{:S(2)}) collective-permute-start(bf16[512,256]{1,0:T(8,128)(2,1)} %bitcast.38), channel_id=1, source_target_pairs={{0,14},{2,0},{4,2},{6,4},{8,6},{10,8},{12,10},{14,12},{1,15},{3,1}... | collective-permute-start | bytes 786440 | tf_op jit(solution)/shard_map/ppermute | solution.py:589
  120.0 3.8 %all-to-all-start.3 = ((bf16[16,32,2048]{2,1,0:T(8,128)(2,1)}), bf16[16,32,2048]{2,1,0:T(8,128)(2,1)S(1)}, u32[]{:S(2)}, u32[]{:S(2)}) async-start(bf16[16,32,2048]{2,1,0:T(8,128)(2,1)} %get-tuple-element.102), calls=%async_computation.3 | async-start | bytes 4194304 | tf_op jit(solution)/shard_map/all_to_all | solution.py:645
  123.9 1.6 collective-permute-start.6
  125.5 0.1 collective-permute-start.7
  125.7 1.0 copy-done.8
  126.7 1.1 add_0_3.1
  127.8 2.7 %collective-permute-start.5 = (bf16[512,256]{1,0:T(8,128)(2,1)S(1)}, bf16[512,256]{1,0:T(8,128)(2,1)S(1)}, u32[]{:S(2)}, u32[]{:S(2)}) collective-permute-start(bf16[512,256]{1,0:T(8,128)(2,1)S(1)} %get-tuple-element.90), channel_id=1, source_target_pairs={{0,14},{2,0},{4,2},{6,4},{8,6},{10,8},{12,10},{14,12},{1,15},{3,1}... | collective-permute-start | bytes 786440 | tf_op jit(solution)/shard_map/ppermute | solution.py:589
  130.5 2.0 %collective-permute-done.7.refs_1_ = bf16[512,256]{1,0:T(8,128)(2,1)S(1)} collective-permute-done((bf16[512,256]{1,0:T(8,128)(2,1)}, bf16[512,256]{1,0:T(8,128)(2,1)S(1)}, u32[]{:S(2)}, u32[]{:S(2)}) %collective-permute-start.7) | collective-permute-done | bytes 262176 | tf_op jit(solution)/shard_map/ppermute | solution.py:589
  132.5 0.1 add_1_3.1
  132.6 0.1 collective-permute-start.10
  132.7 2.7 %collective-permute-start.9 = (bf16[512,256]{1,0:T(8,128)(2,1)S(1)}, bf16[512,256]{1,0:T(8,128)(2,1)S(1)}, u32[]{:S(2)}, u32[]{:S(2)}) collective-permute-start(bf16[512,256]{1,0:T(8,128)(2,1)S(1)} %get-tuple-element.94.refs_2_), channel_id=1, source_target_pairs={{0,14},{2,0},{4,2},{6,4},{8,6},{10,8},{12,10},{14,12},{1,15},{3,1}... | collective-permute-start | bytes 786440 | tf_op jit(solution)/shard_map/ppermute | solution.py:589
  135.4 0.9 collective-permute-done.5.refs_1_
  136.2 3.3 %collective-permute-done.4.refs_0_ = bf16[512,256]{1,0:T(8,128)(2,1)S(1)} collective-permute-done((bf16[512,256]{1,0:T(8,128)(2,1)S(1)}, bf16[512,256]{1,0:T(8,128)(2,1)S(1)}, u32[]{:S(2)}, u32[]{:S(2)}) %collective-permute-start.4) | collective-permute-done | bytes 262176 | tf_op jit(solution)/shard_map/ppermute | solution.py:589
  139.6 0.1 add_0_2.1
  139.8 1.5 collective-permute-start.8
  141.2 3.9 %collective-permute-done.10.refs_1_ = bf16[512,256]{1,0:T(8,128)(2,1)S(1)} collective-permute-done((bf16[512,256]{1,0:T(8,128)(2,1)S(1)}, bf16[512,256]{1,0:T(8,128)(2,1)S(1)}, u32[]{:S(2)}, u32[]{:S(2)}) %collective-permute-start.10) | collective-permute-done | bytes 262176 | tf_op jit(solution)/shard_map/ppermute | solution.py:589
  145.2 0.1 add_1_2.1
  145.4 2.7 %collective-permute-start.13 = (bf16[512,256]{1,0:T(8,128)(2,1)S(1)}, bf16[512,256]{1,0:T(8,128)(2,1)S(1)}, u32[]{:S(2)}, u32[]{:S(2)}) collective-permute-start(bf16[512,256]{1,0:T(8,128)(2,1)S(1)} %get-tuple-element.98.refs_1_), channel_id=1, source_target_pairs={{0,14},{2,0},{4,2},{6,4},{8,6},{10,8},{12,10},{14,12},{1,15},{3,1}... | collective-permute-start | bytes 786440 | tf_op jit(solution)/shard_map/ppermute | solution.py:589
  148.1 2.7 %collective-permute-done.8.refs_0_ = bf16[512,256]{1,0:T(8,128)(2,1)S(1)} collective-permute-done((bf16[512,256]{1,0:T(8,128)(2,1)S(1)}, bf16[512,256]{1,0:T(8,128)(2,1)S(1)}, u32[]{:S(2)}, u32[]{:S(2)}) %collective-permute-start.8) | collective-permute-done | bytes 262176 | tf_op jit(solution)/shard_map/ppermute | solution.py:589
  150.9 2.6 %collective-permute-done.13.refs_0_ = bf16[512,256]{1,0:T(8,128)(2,1)S(1)} collective-permute-done((bf16[512,256]{1,0:T(8,128)(2,1)S(1)}, bf16[512,256]{1,0:T(8,128)(2,1)S(1)}, u32[]{:S(2)}, u32[]{:S(2)}) %collective-permute-start.13) | collective-permute-done | bytes 262176 | tf_op jit(solution)/shard_map/ppermute | solution.py:589
  153.7 2.1 %collective-permute-start.14 = (bf16[512,256]{1,0:T(8,128)(2,1)S(1)}, bf16[512,256]{1,0:T(8,128)(2,1)S(1)}, u32[]{:S(2)}, u32[]{:S(2)}) collective-permute-start(bf16[512,256]{1,0:T(8,128)(2,1)S(1)} %add_1_1.1), channel_id=1, source_target_pairs={{0,14},{2,0},{4,2},{6,4},{8,6},{10,8},{12,10},{14,12},{1,15},{3,1}... | collective-permute-start | bytes 786440 | tf_op jit(solution)/shard_map/ppermute | solution.py:589
  155.7 0.7 collective-permute-done.15.refs_3_
  156.4 5.6 %collective-permute-done.11.refs_0_ = bf16[512,256]{1,0:T(8,128)(2,1)S(1)} collective-permute-done((bf16[512,256]{1,0:T(8,128)(2,1)S(1)}, bf16[512,256]{1,0:T(8,128)(2,1)S(1)}, u32[]{:S(2)}, u32[]{:S(2)}) %collective-permute-start.11) | collective-permute-done | bytes 262176 | tf_op jit(solution)/shard_map/ppermute | solution.py:589
  162.0 1.0 weights_last.1
  163.0 12.0 %all-to-all-start.4 = ((bf16[32,16,512]{2,1,0:T(8,128)(2,1)}), bf16[32,16,512]{2,1,0:T(8,128)(2,1)S(1)}, u32[]{:S(2)}, u32[]{:S(2)}) async-start(bf16[32,16,512]{2,1,0:T(8,128)(2,1)} %bitcast.17), calls=%async_computation.4 | async-start | bytes 1048576 | tf_op jit(solution)/shard_map/all_to_all | solution.py:732
  175.0 0.7 reshape.50
  175.7 2.0 %reshape.52 = bf16[2,256,2,2,128]{4,3,2,1,0:T(2,128)(2,1)} reshape(bf16[512,512]{1,0:T(8,128)(2,1)} %get-tuple-element.88.refs_2_) | data formatting | bytes 1048576 | tf_op jit(solution)/shard_map/reshape | solution.py:742
  177.7 2.1 %sum_dq.1 = bf16[4,32,2048]{2,1,0:T(8,128)(2,1)} custom-call(s32[34]{0:T(128)S(1)} %copy-done.7, bf16[16,32,2048]{2,1,0:T(8,128)(2,1)S(1)} %all-to-all-done.3.refs_0_.refs_1_.refs_2_.refs_3_, bf16[16,32,2048]{2,1,0:T(8,128)(2,1)S(1)} %all-to-all-done.3.refs_0_.refs_1_.refs_2_.refs_3_, ...), custom_call_target="tpu_custom_call" | custom-call | flops 2000000 | bytes 4194304 | tf_op jit(solution)/shard_map/sum_dq/pallas_call | solution.py:527
  179.8 6.7 %all-to-all-done.4 = bf16[32,16,512]{2,1,0:T(8,128)(2,1)S(1)} async-done(((bf16[32,16,512]{2,1,0:T(8,128)(2,1)}), bf16[32,16,512]{2,1,0:T(8,128)(2,1)S(1)}, u32[]{:S(2)}, u32[]{:S(2)}) %all-to-all-start.4) | async-done | bytes 524320 | tf_op jit(solution)/shard_map/all_to_all | solution.py:732
  186.6 0.7 finish_weights.1
  (50 shorter events, 0.5 us)
Async XLA Ops:
  8.5 57.7 %copy-start.14 = (bf16[4,32,2,256]{3,2,1,0:T(2,128)(2,1)S(1)}, bf16[4,32,2,256]{3,2,1,0:T(2,128)(2,1)}, u32[]{:S(2)}) copy-start(bf16[4,32,2,256]{3,2,1,0:T(2,128)(2,1)} %param.10) | copy-start | bytes 393220
  66.3 9.0 %copy-start.16 = (bf16[4,16,4096]{2,1,0:T(8,128)(2,1)S(1)}, bf16[4,16,4096]{2,1,0:T(8,128)(2,1)}, u32[]{:S(2)}) copy-start(bf16[4,16,4096]{2,1,0:T(8,128)(2,1)} %param.12) | copy-start | bytes 1572868
  66.3 12.6 %copy-start = (bf16[4,32,2048]{2,1,0:T(8,128)(2,1)S(1)}, bf16[4,32,2048]{2,1,0:T(8,128)(2,1)}, u32[]{:S(2)}) copy-start(bf16[4,32,2048]{2,1,0:T(8,128)(2,1)} %q_ref.3) | copy-start | bytes 1572868
  66.3 12.6 %copy-start.1 = (bf16[4,32,2048]{2,1,0:T(8,128)(2,1)S(1)}, bf16[4,32,2048]{2,1,0:T(8,128)(2,1)}, u32[]{:S(2)}) copy-start(bf16[4,32,2048]{2,1,0:T(8,128)(2,1)} %g_ref.3) | copy-start | bytes 1572868
  66.3 19.1 %copy-start.6 = (s32[16,1,16]{2,1,0:T(1,128)S(1)}, s32[16,1,16]{2,1,0:T(1,128)}, u32[]{:S(2)}) copy-start(s32[16,1,16]{2,1,0:T(1,128)} %param.14) | copy-start | bytes 3076
  73.2 12.2 %collective-permute-start = (bf16[2,128,4096]{2,1,0:T(8,128)(2,1)}, bf16[2,128,4096]{2,1,0:T(8,128)(2,1)}, u32[]{:S(2)}, u32[]{:S(2)}) collective-permute-start(bf16[2,128,4096]{2,1,0:T(8,128)(2,1)} %param.13), channel_id=1, source_target_pairs={{0,1},{1,0},{2,3},{3,2},{4,5},{5,4},{6,7},{7,6},{8,9},{9,8},{10,11... | collective-permute-start | bytes 6291464 | tf_op jit(solution)/shard_map/ppermute | solution.py:648
  75.3 10.1 %collective-permute-start.1 = (bf16[4,16,4096]{2,1,0:T(8,128)(2,1)S(1)}, bf16[4,16,4096]{2,1,0:T(8,128)(2,1)S(1)}, u32[]{:S(2)}, u32[]{:S(2)}) collective-permute-start(bf16[4,16,4096]{2,1,0:T(8,128)(2,1)S(1)} %copy-done.16), channel_id=1, source_target_pairs={{0,1},{1,0},{2,3},{3,2},{4,5},{5,4},{6,7},{7,6},{8,9},{9,8},{10,11... | collective-permute-start | bytes 1572872 | tf_op jit(solution)/shard_map/ppermute | solution.py:648
  75.4 10.0 %all-to-all-start.1 = ((f32[16,4,256]{2,1,0:T(4,128)}), f32[16,4,256]{2,1,0:T(4,128)S(1)}, u32[]{:S(2)}, u32[]{:S(2)}) async-start(f32[16,4,256]{2,1,0:T(4,128)} %owner_stats.1), calls=%async_computation.1 | async-start | bytes 131072 | tf_op jit(solution)/shard_map/all_to_all | solution.py:645
  85.4 11.4 %copy-start.17 = (bf16[4,16,4096]{2,1,0:T(8,128)(2,1)}, bf16[4,16,4096]{2,1,0:T(8,128)(2,1)S(1)}, u32[]{:S(2)}) copy-start(bf16[4,16,4096]{2,1,0:T(8,128)(2,1)S(1)} %collective-permute-done.1) | copy-start | bytes 1572868
  86.8 10.0 %all-to-all-start.2 = ((f32[16,4,256]{2,1,0:T(4,128)}), f32[16,4,256]{2,1,0:T(4,128)S(1)}, u32[]{:S(2)}, u32[]{:S(2)}) async-start(f32[16,4,256]{2,1,0:T(4,128)} %get-tuple-element.72), calls=%async_computation.2 | async-start | bytes 131072 | tf_op jit(solution)/shard_map/all_to_all | solution.py:645
  92.1 0.7 copy-start.4
  96.7 0.6 copy-start.15
  114.3 11.3 %collective-permute-start.2 = (bf16[512,256]{1,0:T(8,128)(2,1)}, bf16[512,256]{1,0:T(8,128)(2,1)S(1)}, u32[]{:S(2)}, u32[]{:S(2)}) collective-permute-start(bf16[512,256]{1,0:T(8,128)(2,1)} %bitcast.39), channel_id=1, source_target_pairs={{0,2},{2,4},{4,6},{6,8},{8,10},{10,12},{12,14},{14,0},{1,3},{3,5},... | collective-permute-start | bytes 786440 | tf_op jit(solution)/shard_map/ppermute | solution.py:589
  116.1 9.6 %collective-permute-start.3 = (bf16[512,256]{1,0:T(8,128)(2,1)}, bf16[512,256]{1,0:T(8,128)(2,1)}, u32[]{:S(2)}, u32[]{:S(2)}) collective-permute-start(bf16[512,256]{1,0:T(8,128)(2,1)} %bitcast.38), channel_id=1, source_target_pairs={{0,14},{2,0},{4,2},{6,4},{8,6},{10,8},{12,10},{14,12},{1,15},{3,1}... | collective-permute-start | bytes 786440 | tf_op jit(solution)/shard_map/ppermute | solution.py:589
  120.0 5.6 %copy-start.2 = (bf16[512,512]{1,0:T(8,128)(2,1)S(1)}, bf16[512,512]{1,0:T(8,128)(2,1)}, u32[]{:S(2)}) copy-start(bf16[512,512]{1,0:T(8,128)(2,1)} %get-tuple-element.88.refs_2_) | copy-start | bytes 1572868
  120.0 43.0 %all-to-all-start.3 = ((bf16[16,32,2048]{2,1,0:T(8,128)(2,1)}), bf16[16,32,2048]{2,1,0:T(8,128)(2,1)S(1)}, u32[]{:S(2)}, u32[]{:S(2)}) async-start(bf16[16,32,2048]{2,1,0:T(8,128)(2,1)} %get-tuple-element.102), calls=%async_computation.3 | async-start | bytes 4194304 | tf_op jit(solution)/shard_map/all_to_all | solution.py:645
  123.9 6.6 %collective-permute-start.6 = (bf16[512,256]{1,0:T(8,128)(2,1)}, bf16[512,256]{1,0:T(8,128)(2,1)S(1)}, u32[]{:S(2)}, u32[]{:S(2)}) collective-permute-start(bf16[512,256]{1,0:T(8,128)(2,1)} %bitcast.37), channel_id=1, source_target_pairs={{0,14},{2,0},{4,2},{6,4},{8,6},{10,8},{12,10},{14,12},{1,15},{3,1}... | collective-permute-start | bytes 786440 | tf_op jit(solution)/shard_map/ppermute | solution.py:589
  125.5 6.9 %collective-permute-start.7 = (bf16[512,256]{1,0:T(8,128)(2,1)}, bf16[512,256]{1,0:T(8,128)(2,1)S(1)}, u32[]{:S(2)}, u32[]{:S(2)}) collective-permute-start(bf16[512,256]{1,0:T(8,128)(2,1)} %bitcast.36), channel_id=1, source_target_pairs={{0,2},{2,4},{4,6},{6,8},{8,10},{10,12},{12,14},{14,0},{1,3},{3,5},... | collective-permute-start | bytes 786440 | tf_op jit(solution)/shard_map/ppermute | solution.py:589
  125.6 1.0 copy-start.8
  126.7 5.8 %copy-start.11 = (bf16[2,512,256]{2,1,0:T(8,128)(2,1)S(1)}, bf16[2,512,256]{2,1,0:T(8,128)(2,1)}, u32[]{:S(2)}) copy-start(bf16[2,512,256]{2,1,0:T(8,128)(2,1)} %get-tuple-element.91.blocks_ref) | copy-start | bytes 1572868
  127.8 8.4 %collective-permute-start.5 = (bf16[512,256]{1,0:T(8,128)(2,1)S(1)}, bf16[512,256]{1,0:T(8,128)(2,1)S(1)}, u32[]{:S(2)}, u32[]{:S(2)}) collective-permute-start(bf16[512,256]{1,0:T(8,128)(2,1)S(1)} %get-tuple-element.90), channel_id=1, source_target_pairs={{0,14},{2,0},{4,2},{6,4},{8,6},{10,8},{12,10},{14,12},{1,15},{3,1}... | collective-permute-start | bytes 786440 | tf_op jit(solution)/shard_map/ppermute | solution.py:589
  130.5 9.1 %collective-permute-start.4 = (bf16[512,256]{1,0:T(8,128)(2,1)S(1)}, bf16[512,256]{1,0:T(8,128)(2,1)S(1)}, u32[]{:S(2)}, u32[]{:S(2)}) collective-permute-start(bf16[512,256]{1,0:T(8,128)(2,1)S(1)} %get-tuple-element.89.refs_2_), channel_id=1, source_target_pairs={{0,2},{2,4},{4,6},{6,8},{8,10},{10,12},{12,14},{14,0},{1,3},{3,5},... | collective-permute-start | bytes 786440 | tf_op jit(solution)/shard_map/ppermute | solution.py:589
  132.5 7.1 %copy-start.10 = (bf16[2,512,256]{2,1,0:T(8,128)(2,1)S(1)}, bf16[2,512,256]{2,1,0:T(8,128)(2,1)}, u32[]{:S(2)}) copy-start(bf16[2,512,256]{2,1,0:T(8,128)(2,1)} %get-tuple-element.84.blocks_ref) | copy-start | bytes 1572868
  132.6 12.6 %collective-permute-start.10 = (bf16[512,256]{1,0:T(8,128)(2,1)S(1)}, bf16[512,256]{1,0:T(8,128)(2,1)S(1)}, u32[]{:S(2)}, u32[]{:S(2)}) collective-permute-start(bf16[512,256]{1,0:T(8,128)(2,1)S(1)} %get-tuple-element.97), channel_id=1, source_target_pairs={{0,2},{2,4},{4,6},{6,8},{8,10},{10,12},{12,14},{14,0},{1,3},{3,5},... | collective-permute-start | bytes 786440 | tf_op jit(solution)/shard_map/ppermute | solution.py:589
  132.7 12.5 %collective-permute-start.9 = (bf16[512,256]{1,0:T(8,128)(2,1)S(1)}, bf16[512,256]{1,0:T(8,128)(2,1)S(1)}, u32[]{:S(2)}, u32[]{:S(2)}) collective-permute-start(bf16[512,256]{1,0:T(8,128)(2,1)S(1)} %get-tuple-element.94.refs_2_), channel_id=1, source_target_pairs={{0,14},{2,0},{4,2},{6,4},{8,6},{10,8},{12,10},{14,12},{1,15},{3,1}... | collective-permute-start | bytes 786440 | tf_op jit(solution)/shard_map/ppermute | solution.py:589
  139.6 5.6 %copy-start.9 = (bf16[2,512,256]{2,1,0:T(8,128)(2,1)S(1)}, bf16[2,512,256]{2,1,0:T(8,128)(2,1)}, u32[]{:S(2)}) copy-start(bf16[2,512,256]{2,1,0:T(8,128)(2,1)} %get-tuple-element.96.blocks_ref) | copy-start | bytes 1572868
  139.7 16.1 %collective-permute-start.12 = (bf16[512,256]{1,0:T(8,128)(2,1)S(1)}, bf16[512,256]{1,0:T(8,128)(2,1)S(1)}, u32[]{:S(2)}, u32[]{:S(2)}) collective-permute-start(bf16[512,256]{1,0:T(8,128)(2,1)S(1)} %get-tuple-element.99), channel_id=1, source_target_pairs={{0,14},{2,0},{4,2},{6,4},{8,6},{10,8},{12,10},{14,12},{1,15},{3,1}... | collective-permute-start | bytes 786440 | tf_op jit(solution)/shard_map/ppermute | solution.py:589
  139.8 11.0 %collective-permute-start.8 = (bf16[512,256]{1,0:T(8,128)(2,1)S(1)}, bf16[512,256]{1,0:T(8,128)(2,1)S(1)}, u32[]{:S(2)}, u32[]{:S(2)}) collective-permute-start(bf16[512,256]{1,0:T(8,128)(2,1)S(1)} %get-tuple-element.95.refs_2_), channel_id=1, source_target_pairs={{0,2},{2,4},{4,6},{6,8},{8,10},{10,12},{12,14},{14,0},{1,3},{3,5},... | collective-permute-start | bytes 786440 | tf_op jit(solution)/shard_map/ppermute | solution.py:589
  145.2 5.6 %copy-start.13 = (bf16[1,512,256]{2,1,0:T(8,128)(2,1)S(1)}, bf16[1,512,256]{2,1,0:T(8,128)(2,1)}, u32[]{:S(2)}) copy-start(bf16[1,512,256]{2,1,0:T(8,128)(2,1)} %get-tuple-element.83.blocks_ref) | copy-start | bytes 786436
  145.3 11.1 %collective-permute-start.15 = (bf16[512,256]{1,0:T(8,128)(2,1)S(1)}, bf16[512,256]{1,0:T(8,128)(2,1)S(1)}, u32[]{:S(2)}, u32[]{:S(2)}) collective-permute-start(bf16[512,256]{1,0:T(8,128)(2,1)S(1)} %get-tuple-element.101), channel_id=1, source_target_pairs={{0,2},{2,4},{4,6},{6,8},{8,10},{10,12},{12,14},{14,0},{1,3},{3,5},... | collective-permute-start | bytes 786440 | tf_op jit(solution)/shard_map/ppermute | solution.py:589
  145.4 8.2 %collective-permute-start.13 = (bf16[512,256]{1,0:T(8,128)(2,1)S(1)}, bf16[512,256]{1,0:T(8,128)(2,1)S(1)}, u32[]{:S(2)}, u32[]{:S(2)}) collective-permute-start(bf16[512,256]{1,0:T(8,128)(2,1)S(1)} %get-tuple-element.98.refs_1_), channel_id=1, source_target_pairs={{0,14},{2,0},{4,2},{6,4},{8,6},{10,8},{12,10},{14,12},{1,15},{3,1}... | collective-permute-start | bytes 786440 | tf_op jit(solution)/shard_map/ppermute | solution.py:589
  150.8 2.8 %copy-start.12 = (bf16[1,512,256]{2,1,0:T(8,128)(2,1)S(1)}, bf16[1,512,256]{2,1,0:T(8,128)(2,1)}, u32[]{:S(2)}) copy-start(bf16[1,512,256]{2,1,0:T(8,128)(2,1)} %get-tuple-element.100.blocks_ref) | copy-start | bytes 786436
  150.9 11.2 %collective-permute-start.11 = (bf16[512,256]{1,0:T(8,128)(2,1)S(1)}, bf16[512,256]{1,0:T(8,128)(2,1)S(1)}, u32[]{:S(2)}, u32[]{:S(2)}) collective-permute-start(bf16[512,256]{1,0:T(8,128)(2,1)S(1)} %add_0_1.1.refs_1_), channel_id=1, source_target_pairs={{0,2},{2,4},{4,6},{6,8},{8,10},{10,12},{12,14},{14,0},{1,3},{3,5},... | collective-permute-start | bytes 786440 | tf_op jit(solution)/shard_map/ppermute | solution.py:589
  153.6 8.4 %copy-start.3 = (bf16[2,512,256]{2,1,0:T(8,128)(2,1)S(1)}, bf16[2,512,256]{2,1,0:T(8,128)(2,1)}, u32[]{:S(2)}) copy-start(bf16[2,512,256]{2,1,0:T(8,128)(2,1)} %get-tuple-element.82.blocks_ref) | copy-start | bytes 1572868
  153.6 21.4 %copy-start.5 = (bf16[128,512]{1,0:T(8,128)(2,1)S(1)}, bf16[128,512]{1,0:T(8,128)(2,1)}, u32[]{:S(2)}) copy-start(bf16[128,512]{1,0:T(8,128)(2,1)} %copy-done.4) | copy-start | bytes 393220
  153.7 8.4 %collective-permute-start.14 = (bf16[512,256]{1,0:T(8,128)(2,1)S(1)}, bf16[512,256]{1,0:T(8,128)(2,1)S(1)}, u32[]{:S(2)}, u32[]{:S(2)}) collective-permute-start(bf16[512,256]{1,0:T(8,128)(2,1)S(1)} %add_1_1.1), channel_id=1, source_target_pairs={{0,14},{2,0},{4,2},{6,4},{8,6},{10,8},{12,10},{14,12},{1,15},{3,1}... | collective-permute-start | bytes 786440 | tf_op jit(solution)/shard_map/ppermute | solution.py:589
  162.0 15.6 %copy-start.7 = (s32[34]{0:T(128)S(1)}, s32[34]{0:T(128)}, u32[]{:S(2)}) copy-start(s32[34]{0:T(128)} %get-tuple-element.57.table.owners) | copy-start | bytes 412
  163.0 23.5 %all-to-all-start.4 = ((bf16[32,16,512]{2,1,0:T(8,128)(2,1)}), bf16[32,16,512]{2,1,0:T(8,128)(2,1)S(1)}, u32[]{:S(2)}, u32[]{:S(2)}) async-start(bf16[32,16,512]{2,1,0:T(8,128)(2,1)} %bitcast.17), calls=%async_computation.4 | async-start | bytes 1048576 | tf_op jit(solution)/shard_map/all_to_all | solution.py:732

commit v8 on v7

--- a/solution.py
+++ b/solution.py
@@ -52,11 +52,13 @@
     )
 
 
-def pack_kernel(slots, refs, blocks, q_ref, g_ref, out_ref, table, held, load_sems, sems):
+def pack_kernel(slots, refs, blocks, q_ref, g_ref, raw_ref, out_ref, table, kv_ref, *scratch):
+    held, raw_held, raw_sem, load_sems, sems = scratch
     peers = out_ref.shape[0]
     samples, rows, _ = q_ref.shape
     per = peers // samples
     me = lax.axis_index("dp")
+    raw_load = pltpu.make_async_copy(raw_ref, raw_held, raw_sem)
     loads = []
     for sample in range(samples):
         pair = []
@@ -70,6 +72,7 @@
             )
             pair[-1].start()
         loads.append(pair)
+    raw_load.start()
     copies = []
     for j in range(peers):
         sample = j // per
@@ -81,8 +84,11 @@
         copy = pltpu.make_async_copy(held.at[sample], out_ref.at[dest], sems.at[j])
         copy.start()
         copies.append(copy)
+    raw_load.wait()
     for slot in range(slots):
-        table[peers + slot] = blocks[me, slot]
+        table[peers + slot] = blocks[slot]
+        for part in range(2):
+            kv_ref[part, slot] = raw_held[slot, :, part, :]
 
     @pl.loop(0, peers)
     def _(reader):
@@ -97,27 +103,30 @@
         copy.wait()
 
 
-def pack_queries(refs, blocks, question_q, question_grad):
+def pack_queries(refs, blocks, question_q, question_grad, passage_kv):
     samples, rows, width = question_q.shape
     peers = refs.shape[0]
-    slots = blocks.shape[1]
+    slots, slot_len, _, channels = passage_kv.shape
     return pl.pallas_call(
         functools.partial(pack_kernel, slots),
         out_shape=(
             jax.ShapeDtypeStruct((peers, 2 * rows, width), BF16),
             jax.ShapeDtypeStruct((2 * peers + slots,), jnp.int32),
+            jax.ShapeDtypeStruct((2, slots, slot_len, channels), BF16),
         ),
-        in_specs=[smem(), smem(), in_hbm(), in_hbm()],
-        out_specs=(in_hbm(), smem()),
+        in_specs=[smem(), smem(), in_hbm(), in_hbm(), in_hbm()],
+        out_specs=(in_hbm(), smem(), whole()),
         scratch_shapes=[
             pltpu.VMEM((samples, 2 * rows, width), BF16),
+            pltpu.VMEM(passage_kv.shape, BF16),
+            pltpu.SemaphoreType.DMA,
             pltpu.SemaphoreType.DMA((samples, 2)),
             pltpu.SemaphoreType.DMA((peers,)),
         ],
         compiler_params=params(VMEM_MOST),
         cost_estimate=cost(0, 6 * 2**20),
         name="pack_queries",
-    )(refs, blocks, question_q, question_grad)
+    )(refs, blocks, question_q, question_grad, passage_kv)
 
 
 def scores_t(keys, queries, valid):
@@ -647,9 +656,9 @@
     def from_partner(x):
         return lax.ppermute(x, "tensor", [(i, cores - 1 - i) for i in range(cores)])
 
-    kv = jnp.transpose(passage_kv, (2, 0, 1, 3))
-    blocks = passage_blocks.reshape(peers, slots)
-    packed, table = pack_queries(refs, blocks, question_q, question_grad)
+    me = lax.axis_index("dp")
+    blocks = lax.dynamic_index_in_dim(passage_blocks, me, 0, keepdims=False).reshape(slots)
+    packed, table, kv = pack_queries(refs, blocks, question_q, question_grad, passage_kv)
     packed, table, kv = lax.optimization_barrier((packed, table, kv))
     got = exchange(packed)
     got, passage_hidden, question_hidden, question_kv, question_q, question_grad = (

time: 188 us -> 187 us (level)
  local copies, waits for them, and re-layouts: 8.32 us -> 6.43 us
    unnamed x37 -> x38, local copies, waits for them, and re-layouts: 4.29 us -> 3.06 us
where the time goes in v8:
time: 187 us; the launch traced here: 186 us
  blocking collectives  57.7 us (31%)
  starting transfers between devices  44.6 us (24%)
  Pallas kernels  38.7 us (21%)
  waiting for transfers between devices  38.1 us (20%)
  local copies, waits for them, and re-layouts  6.43 us (3%)
    all_to_all x1, blocking collectives, exchange(): return lax.all_to_all(x, 'dp', split_axis=0, concat_axis=0, tiled=True)  57.7 us
    ppermute x14, waiting for transfers between devices, travel(): lax.ppermute(block, 'pass', [(i, (i + way) % count) for i in range(count)])  21.5 us
    ppermute x14, starting transfers between devices, travel(): lax.ppermute(block, 'pass', [(i, (i + way) % count) for i in range(count)])  19.3 us
    pallas_call x1, Pallas kernels, owner_grads(): pl.pallas_call(functools.partial(owner_grads_kernel, 2 * columns // both,...  17 us
    all_to_all x1, starting transfers between devices, local(): lax.all_to_all(summed.reshape(peers * cores, share, -1), ('dp', 'tensor')...  12.2 us
    all_to_all x3, starting transfers between devices, exchange(): return lax.all_to_all(x, 'dp', split_axis=0, concat_axis=0, tiled=True)  10.9 us
    all_to_all x3, waiting for transfers between devices, exchange(): return lax.all_to_all(x, 'dp', split_axis=0, concat_axis=0, tiled=True)  9.86 us
    pallas_call x1, Pallas kernels, owner_stats(): pl.pallas_call(functools.partial(owner_stats_kernel, group), out_shape=ja...  7.05 us
  transfers between devices with their start and end apart: 20, of which 11 were waited for; matrix products, arithmetic and copies ran while one was open for 1% of the time, Pallas kernels for 4%

profile of v8, /device:TPU:1, one launch (start us, length us, event | category | flops | bytes accessed | tf_op | source)
XLA Modules:
  0.0 186.5 jit_solution(10796559337821860179)
XLA Ops:
  0.6 0.7 copy-done
  1.3 0.7 dynamic-slice_reduce_fusion.blocks
  2.0 5.4 %pack_queries.1 = (bf16[16,64,2048]{2,1,0:T(8,128)(2,1)}, s32[34]{0:T(128)}, bf16[2,2,256,256]{3,2,1,0:T(8,128)(2,1)}) custom-call(s32[16,16]{1,0:T(8,128)} %bitcast.22, s32[2]{0:T(128)} %dynamic-slice_reduce_fusion.blocks, bf16[4,32,2048]{2,1,0:T(8,128)(2,1)} %q_ref.3, bf16[4,32,2048]{2,1,0:T(8,128)(2,1)} %g_ref.3, bf16[2,256,2,256]{3,2,1,0:T(2,128)(2,1)} %raw_ref.1), custom_call_target="tpu_custom_call" | custom-call | bytes 6291456 | tf_op jit(solution)/shard_map/pack_queries/pallas_call | solution.py:110
  7.4 57.7 %all_to_all.25.got_hbm = bf16[16,64,2048]{2,1,0:T(8,128)(2,1)} all-to-all(bf16[16,64,2048]{2,1,0:T(8,128)(2,1)} %get-tuple-element.54), channel_id=1, replica_groups=mesh['dp'=16,'pass'=8,'tensor'=2] {'dp'}, dimensions={0} | all-to-all | bytes 8388608 | tf_op jit(solution)/shard_map/all_to_all | solution.py:654
  65.2 7.0 %owner_stats.1 = f32[16,4,256]{2,1,0:T(4,128)} custom-call(s32[34]{0:T(128)} %get-tuple-element.53.table.owners, bf16[16,64,2048]{2,1,0:T(8,128)(2,1)} %all_to_all.25.got_hbm, bf16[2,2,256,256]{3,2,1,0:T(8,128)(2,1)} %get-tuple-element.56.kv_ref), custom_call_target="tpu_custom_call" | custom-call | flops 2000000000 | bytes 6291456 | tf_op jit(solution)/shard_map/owner_stats/pallas_call | solution.py:204
  72.3 2.1 %collective-permute-start = (bf16[2,128,4096]{2,1,0:T(8,128)(2,1)}, bf16[2,128,4096]{2,1,0:T(8,128)(2,1)}, u32[]{:S(2)}, u32[]{:S(2)}) collective-permute-start(bf16[2,128,4096]{2,1,0:T(8,128)(2,1)} %param.13), channel_id=1, source_target_pairs={{0,1},{1,0},{2,3},{3,2},{4,5},{5,4},{6,7},{7,6},{8,9},{9,8},{10,11... | collective-permute-start | bytes 6291464 | tf_op jit(solution)/shard_map/ppermute | solution.py:657
  74.3 0.1 collective-permute-start.1
  74.4 3.5 %all-to-all-start.1 = ((f32[16,4,256]{2,1,0:T(4,128)}), f32[16,4,256]{2,1,0:T(4,128)S(1)}, u32[]{:S(2)}, u32[]{:S(2)}) async-start(f32[16,4,256]{2,1,0:T(4,128)} %owner_stats.1), calls=%async_computation.1 | async-start | bytes 131072 | tf_op jit(solution)/shard_map/all_to_all | solution.py:654
  78.0 0.5 own_stats.1.own_ref
  78.5 5.9 %all-to-all-done.1.st_ref = f32[16,4,256]{2,1,0:T(4,128)S(1)} async-done(((f32[16,4,256]{2,1,0:T(4,128)}), f32[16,4,256]{2,1,0:T(4,128)S(1)}, u32[]{:S(2)}, u32[]{:S(2)}) %all-to-all-start.1) | async-done | bytes 65568 | tf_op jit(solution)/shard_map/all_to_all | solution.py:654
  84.4 1.4 merge_stats.1
  85.8 3.5 %all-to-all-start.2 = ((f32[16,4,256]{2,1,0:T(4,128)}), f32[16,4,256]{2,1,0:T(4,128)S(1)}, u32[]{:S(2)}, u32[]{:S(2)}) async-start(f32[16,4,256]{2,1,0:T(4,128)} %get-tuple-element.68), calls=%async_computation.2 | async-start | bytes 131072 | tf_op jit(solution)/shard_map/all_to_all | solution.py:654
  89.3 1.9 own_grads.1
  91.2 0.6 copy-done.5
  91.8 3.9 %all-to-all-done.2.joint_ref = f32[16,4,256]{2,1,0:T(4,128)S(1)} async-done(((f32[16,4,256]{2,1,0:T(4,128)}), f32[16,4,256]{2,1,0:T(4,128)S(1)}, u32[]{:S(2)}, u32[]{:S(2)}) %all-to-all-start.2) | async-done | bytes 65568 | tf_op jit(solution)/shard_map/all_to_all | solution.py:654
  95.8 0.6 copy-done.16
  96.4 17.0 %owner_grads.1 = (bf16[512,512]{1,0:T(8,128)(2,1)}, bf16[16,32,2048]{2,1,0:T(8,128)(2,1)}, bf16[1,512,256]{2,1,0:T(8,128)(2,1)}, bf16[1,512,256]{2,1,0:T(8,128)(...) custom-call(s32[34]{0:T(128)} %get-tuple-element.53.table.owners, ...), custom_call_target="tpu_custom_call" | custom-call | flops 16000000000 | bytes 25165824 | tf_op jit(solution)/shard_map/owner_grads/pallas_call | solution.py:435
  113.4 1.7 collective-permute-start.2
  115.1 4.2 %collective-permute-start.3 = (bf16[512,256]{1,0:T(8,128)(2,1)}, bf16[512,256]{1,0:T(8,128)(2,1)}, u32[]{:S(2)}, u32[]{:S(2)}) collective-permute-start(bf16[512,256]{1,0:T(8,128)(2,1)} %bitcast.31), channel_id=1, source_target_pairs={{0,14},{2,0},{4,2},{6,4},{8,6},{10,8},{12,10},{14,12},{1,15},{3,1}... | collective-permute-start | bytes 786440 | tf_op jit(solution)/shard_map/ppermute | solution.py:598
  119.4 3.8 %all-to-all-start.3 = ((bf16[16,32,2048]{2,1,0:T(8,128)(2,1)}), bf16[16,32,2048]{2,1,0:T(8,128)(2,1)S(1)}, u32[]{:S(2)}, u32[]{:S(2)}) async-start(bf16[16,32,2048]{2,1,0:T(8,128)(2,1)} %get-tuple-element.98), calls=%async_computation.3 | async-start | bytes 4194304 | tf_op jit(solution)/shard_map/all_to_all | solution.py:654
  123.2 1.3 collective-permute-start.6
  124.5 0.3 collective-permute-start.7
  124.8 1.0 copy-done.9
  125.8 1.2 add_0_3.1
  127.0 2.5 %collective-permute-start.5 = (bf16[512,256]{1,0:T(8,128)(2,1)S(1)}, bf16[512,256]{1,0:T(8,128)(2,1)S(1)}, u32[]{:S(2)}, u32[]{:S(2)}) collective-permute-start(bf16[512,256]{1,0:T(8,128)(2,1)S(1)} %get-tuple-element.86), channel_id=1, source_target_pairs={{0,14},{2,0},{4,2},{6,4},{8,6},{10,8},{12,10},{14,12},{1,15},{3,1}... | collective-permute-start | bytes 786440 | tf_op jit(solution)/shard_map/ppermute | solution.py:598
  129.5 2.0 %collective-permute-done.7.refs_1_ = bf16[512,256]{1,0:T(8,128)(2,1)S(1)} collective-permute-done((bf16[512,256]{1,0:T(8,128)(2,1)}, bf16[512,256]{1,0:T(8,128)(2,1)S(1)}, u32[]{:S(2)}, u32[]{:S(2)}) %collective-permute-start.7) | collective-permute-done | bytes 262176 | tf_op jit(solution)/shard_map/ppermute | solution.py:598
  131.4 0.1 add_1_3.1
  131.6 0.1 collective-permute-start.10
  131.7 2.7 %collective-permute-start.9 = (bf16[512,256]{1,0:T(8,128)(2,1)S(1)}, bf16[512,256]{1,0:T(8,128)(2,1)S(1)}, u32[]{:S(2)}, u32[]{:S(2)}) collective-permute-start(bf16[512,256]{1,0:T(8,128)(2,1)S(1)} %get-tuple-element.90.refs_2_), channel_id=1, source_target_pairs={{0,14},{2,0},{4,2},{6,4},{8,6},{10,8},{12,10},{14,12},{1,15},{3,1}... | collective-permute-start | bytes 786440 | tf_op jit(solution)/shard_map/ppermute | solution.py:598
  134.3 1.1 collective-permute-done.5.refs_1_
  135.4 3.1 %collective-permute-done.4.refs_0_ = bf16[512,256]{1,0:T(8,128)(2,1)S(1)} collective-permute-done((bf16[512,256]{1,0:T(8,128)(2,1)S(1)}, bf16[512,256]{1,0:T(8,128)(2,1)S(1)}, u32[]{:S(2)}, u32[]{:S(2)}) %collective-permute-start.4) | collective-permute-done | bytes 262176 | tf_op jit(solution)/shard_map/ppermute | solution.py:598
  138.5 0.1 add_0_2.1
  138.7 1.5 collective-permute-start.8
  140.1 3.9 %collective-permute-done.10.refs_1_ = bf16[512,256]{1,0:T(8,128)(2,1)S(1)} collective-permute-done((bf16[512,256]{1,0:T(8,128)(2,1)S(1)}, bf16[512,256]{1,0:T(8,128)(2,1)S(1)}, u32[]{:S(2)}, u32[]{:S(2)}) %collective-permute-start.10) | collective-permute-done | bytes 262176 | tf_op jit(solution)/shard_map/ppermute | solution.py:598
  144.1 0.1 add_1_2.1
  144.3 2.7 %collective-permute-start.13 = (bf16[512,256]{1,0:T(8,128)(2,1)S(1)}, bf16[512,256]{1,0:T(8,128)(2,1)S(1)}, u32[]{:S(2)}, u32[]{:S(2)}) collective-permute-start(bf16[512,256]{1,0:T(8,128)(2,1)S(1)} %get-tuple-element.94.refs_1_), channel_id=1, source_target_pairs={{0,14},{2,0},{4,2},{6,4},{8,6},{10,8},{12,10},{14,12},{1,15},{3,1}... | collective-permute-start | bytes 786440 | tf_op jit(solution)/shard_map/ppermute | solution.py:598
  147.0 2.7 %collective-permute-done.8.refs_0_ = bf16[512,256]{1,0:T(8,128)(2,1)S(1)} collective-permute-done((bf16[512,256]{1,0:T(8,128)(2,1)S(1)}, bf16[512,256]{1,0:T(8,128)(2,1)S(1)}, u32[]{:S(2)}, u32[]{:S(2)}) %collective-permute-start.8) | collective-permute-done | bytes 262176 | tf_op jit(solution)/shard_map/ppermute | solution.py:598
  149.9 2.6 %collective-permute-done.13.refs_0_ = bf16[512,256]{1,0:T(8,128)(2,1)S(1)} collective-permute-done((bf16[512,256]{1,0:T(8,128)(2,1)S(1)}, bf16[512,256]{1,0:T(8,128)(2,1)S(1)}, u32[]{:S(2)}, u32[]{:S(2)}) %collective-permute-start.13) | collective-permute-done | bytes 262176 | tf_op jit(solution)/shard_map/ppermute | solution.py:598
  152.5 2.3 %collective-permute-start.14 = (bf16[512,256]{1,0:T(8,128)(2,1)S(1)}, bf16[512,256]{1,0:T(8,128)(2,1)S(1)}, u32[]{:S(2)}, u32[]{:S(2)}) collective-permute-start(bf16[512,256]{1,0:T(8,128)(2,1)S(1)} %add_1_1.1), channel_id=1, source_target_pairs={{0,14},{2,0},{4,2},{6,4},{8,6},{10,8},{12,10},{14,12},{1,15},{3,1}... | collective-permute-start | bytes 786440 | tf_op jit(solution)/shard_map/ppermute | solution.py:598
  154.8 0.5 collective-permute-done.15.refs_3_
  155.3 5.6 %collective-permute-done.11.refs_0_ = bf16[512,256]{1,0:T(8,128)(2,1)S(1)} collective-permute-done((bf16[512,256]{1,0:T(8,128)(2,1)S(1)}, bf16[512,256]{1,0:T(8,128)(2,1)S(1)}, u32[]{:S(2)}, u32[]{:S(2)}) %collective-permute-start.11) | collective-permute-done | bytes 262176 | tf_op jit(solution)/shard_map/ppermute | solution.py:598
  160.9 1.0 weights_last.1
  161.9 12.2 %all-to-all-start.4 = ((bf16[32,16,512]{2,1,0:T(8,128)(2,1)}), bf16[32,16,512]{2,1,0:T(8,128)(2,1)S(1)}, u32[]{:S(2)}, u32[]{:S(2)}) async-start(bf16[32,16,512]{2,1,0:T(8,128)(2,1)} %bitcast.15), calls=%async_computation.4 | async-start | bytes 1048576 | tf_op jit(solution)/shard_map/all_to_all | solution.py:741
  174.2 0.7 reshape.51
  174.9 2.0 %reshape.53 = bf16[2,256,2,2,128]{4,3,2,1,0:T(2,128)(2,1)} reshape(bf16[512,512]{1,0:T(8,128)(2,1)} %get-tuple-element.84.refs_2_) | data formatting | bytes 1048576 | tf_op jit(solution)/shard_map/reshape | solution.py:751
  176.8 2.1 %sum_dq.1 = bf16[4,32,2048]{2,1,0:T(8,128)(2,1)} custom-call(s32[34]{0:T(128)S(1)} %copy-done.8, bf16[16,32,2048]{2,1,0:T(8,128)(2,1)S(1)} %all-to-all-done.3.refs_0_.refs_1_.refs_2_.refs_3_, bf16[16,32,2048]{2,1,0:T(8,128)(2,1)S(1)} %all-to-all-done.3.refs_0_.refs_1_.refs_2_.refs_3_, ...), custom_call_target="tpu_custom_call" | custom-call | flops 2000000 | bytes 4194304 | tf_op jit(solution)/shard_map/sum_dq/pallas_call | solution.py:536
  179.0 6.7 %all-to-all-done.4 = bf16[32,16,512]{2,1,0:T(8,128)(2,1)S(1)} async-done(((bf16[32,16,512]{2,1,0:T(8,128)(2,1)}), bf16[32,16,512]{2,1,0:T(8,128)(2,1)S(1)}, u32[]{:S(2)}, u32[]{:S(2)}) %all-to-all-start.4) | async-done | bytes 524320 | tf_op jit(solution)/shard_map/all_to_all | solution.py:741
  185.7 0.7 finish_weights.1
  (51 shorter events, 0.5 us)
Async XLA Ops:
  0.6 0.7 copy-start
  7.4 57.7 %copy-start.15 = (bf16[4,32,2,256]{3,2,1,0:T(2,128)(2,1)S(1)}, bf16[4,32,2,256]{3,2,1,0:T(2,128)(2,1)}, u32[]{:S(2)}) copy-start(bf16[4,32,2,256]{3,2,1,0:T(2,128)(2,1)} %param.10) | copy-start | bytes 393220
  65.2 9.2 %copy-start.17 = (bf16[4,16,4096]{2,1,0:T(8,128)(2,1)S(1)}, bf16[4,16,4096]{2,1,0:T(8,128)(2,1)}, u32[]{:S(2)}) copy-start(bf16[4,16,4096]{2,1,0:T(8,128)(2,1)} %param.12) | copy-start | bytes 1572868
  65.2 12.8 %copy-start.1 = (bf16[4,32,2048]{2,1,0:T(8,128)(2,1)S(1)}, bf16[4,32,2048]{2,1,0:T(8,128)(2,1)}, u32[]{:S(2)}) copy-start(bf16[4,32,2048]{2,1,0:T(8,128)(2,1)} %q_ref.3) | copy-start | bytes 1572868
  65.2 12.8 %copy-start.2 = (bf16[4,32,2048]{2,1,0:T(8,128)(2,1)S(1)}, bf16[4,32,2048]{2,1,0:T(8,128)(2,1)}, u32[]{:S(2)}) copy-start(bf16[4,32,2048]{2,1,0:T(8,128)(2,1)} %g_ref.3) | copy-start | bytes 1572868
  65.2 19.2 %copy-start.7 = (s32[16,1,16]{2,1,0:T(1,128)S(1)}, s32[16,1,16]{2,1,0:T(1,128)}, u32[]{:S(2)}) copy-start(s32[16,1,16]{2,1,0:T(1,128)} %param.14) | copy-start | bytes 3076
  72.3 12.2 %collective-permute-start = (bf16[2,128,4096]{2,1,0:T(8,128)(2,1)}, bf16[2,128,4096]{2,1,0:T(8,128)(2,1)}, u32[]{:S(2)}, u32[]{:S(2)}) collective-permute-start(bf16[2,128,4096]{2,1,0:T(8,128)(2,1)} %param.13), channel_id=1, source_target_pairs={{0,1},{1,0},{2,3},{3,2},{4,5},{5,4},{6,7},{7,6},{8,9},{9,8},{10,11... | collective-permute-start | bytes 6291464 | tf_op jit(solution)/shard_map/ppermute | solution.py:657
  74.3 10.1 %collective-permute-start.1 = (bf16[4,16,4096]{2,1,0:T(8,128)(2,1)S(1)}, bf16[4,16,4096]{2,1,0:T(8,128)(2,1)S(1)}, u32[]{:S(2)}, u32[]{:S(2)}) collective-permute-start(bf16[4,16,4096]{2,1,0:T(8,128)(2,1)S(1)} %copy-done.17), channel_id=1, source_target_pairs={{0,1},{1,0},{2,3},{3,2},{4,5},{5,4},{6,7},{7,6},{8,9},{9,8},{10,11... | collective-permute-start | bytes 1572872 | tf_op jit(solution)/shard_map/ppermute | solution.py:657
  74.4 10.0 %all-to-all-start.1 = ((f32[16,4,256]{2,1,0:T(4,128)}), f32[16,4,256]{2,1,0:T(4,128)S(1)}, u32[]{:S(2)}, u32[]{:S(2)}) async-start(f32[16,4,256]{2,1,0:T(4,128)} %owner_stats.1), calls=%async_computation.1 | async-start | bytes 131072 | tf_op jit(solution)/shard_map/all_to_all | solution.py:654
  84.4 11.4 %copy-start.18 = (bf16[4,16,4096]{2,1,0:T(8,128)(2,1)}, bf16[4,16,4096]{2,1,0:T(8,128)(2,1)S(1)}, u32[]{:S(2)}) copy-start(bf16[4,16,4096]{2,1,0:T(8,128)(2,1)S(1)} %collective-permute-done.1) | copy-start | bytes 1572868
  85.8 10.0 %all-to-all-start.2 = ((f32[16,4,256]{2,1,0:T(4,128)}), f32[16,4,256]{2,1,0:T(4,128)S(1)}, u32[]{:S(2)}, u32[]{:S(2)}) async-start(f32[16,4,256]{2,1,0:T(4,128)} %get-tuple-element.68), calls=%async_computation.2 | async-start | bytes 131072 | tf_op jit(solution)/shard_map/all_to_all | solution.py:654
  91.2 0.7 copy-start.5
  95.8 0.6 copy-start.16
  113.4 11.3 %collective-permute-start.2 = (bf16[512,256]{1,0:T(8,128)(2,1)}, bf16[512,256]{1,0:T(8,128)(2,1)S(1)}, u32[]{:S(2)}, u32[]{:S(2)}) collective-permute-start(bf16[512,256]{1,0:T(8,128)(2,1)} %bitcast.32), channel_id=1, source_target_pairs={{0,2},{2,4},{4,6},{6,8},{8,10},{10,12},{12,14},{14,0},{1,3},{3,5},... | collective-permute-start | bytes 786440 | tf_op jit(solution)/shard_map/ppermute | solution.py:598
  115.1 9.6 %collective-permute-start.3 = (bf16[512,256]{1,0:T(8,128)(2,1)}, bf16[512,256]{1,0:T(8,128)(2,1)}, u32[]{:S(2)}, u32[]{:S(2)}) collective-permute-start(bf16[512,256]{1,0:T(8,128)(2,1)} %bitcast.31), channel_id=1, source_target_pairs={{0,14},{2,0},{4,2},{6,4},{8,6},{10,8},{12,10},{14,12},{1,15},{3,1}... | collective-permute-start | bytes 786440 | tf_op jit(solution)/shard_map/ppermute | solution.py:598
  119.4 5.4 %copy-start.3 = (bf16[512,512]{1,0:T(8,128)(2,1)S(1)}, bf16[512,512]{1,0:T(8,128)(2,1)}, u32[]{:S(2)}) copy-start(bf16[512,512]{1,0:T(8,128)(2,1)} %get-tuple-element.84.refs_2_) | copy-start | bytes 1572868
  119.4 42.6 %all-to-all-start.3 = ((bf16[16,32,2048]{2,1,0:T(8,128)(2,1)}), bf16[16,32,2048]{2,1,0:T(8,128)(2,1)S(1)}, u32[]{:S(2)}, u32[]{:S(2)}) async-start(bf16[16,32,2048]{2,1,0:T(8,128)(2,1)} %get-tuple-element.98), calls=%async_computation.3 | async-start | bytes 4194304 | tf_op jit(solution)/shard_map/all_to_all | solution.py:654
  123.2 6.2 %collective-permute-start.6 = (bf16[512,256]{1,0:T(8,128)(2,1)}, bf16[512,256]{1,0:T(8,128)(2,1)S(1)}, u32[]{:S(2)}, u32[]{:S(2)}) collective-permute-start(bf16[512,256]{1,0:T(8,128)(2,1)} %bitcast.30), channel_id=1, source_target_pairs={{0,14},{2,0},{4,2},{6,4},{8,6},{10,8},{12,10},{14,12},{1,15},{3,1}... | collective-permute-start | bytes 786440 | tf_op jit(solution)/shard_map/ppermute | solution.py:598
  124.5 6.9 %collective-permute-start.7 = (bf16[512,256]{1,0:T(8,128)(2,1)}, bf16[512,256]{1,0:T(8,128)(2,1)S(1)}, u32[]{:S(2)}, u32[]{:S(2)}) collective-permute-start(bf16[512,256]{1,0:T(8,128)(2,1)} %bitcast.29), channel_id=1, source_target_pairs={{0,2},{2,4},{4,6},{6,8},{8,10},{10,12},{12,14},{14,0},{1,3},{3,5},... | collective-permute-start | bytes 786440 | tf_op jit(solution)/shard_map/ppermute | solution.py:598
  124.8 1.0 copy-start.9
  125.8 5.6 %copy-start.12 = (bf16[2,512,256]{2,1,0:T(8,128)(2,1)S(1)}, bf16[2,512,256]{2,1,0:T(8,128)(2,1)}, u32[]{:S(2)}) copy-start(bf16[2,512,256]{2,1,0:T(8,128)(2,1)} %get-tuple-element.87.blocks_ref) | copy-start | bytes 1572868
  127.0 8.4 %collective-permute-start.5 = (bf16[512,256]{1,0:T(8,128)(2,1)S(1)}, bf16[512,256]{1,0:T(8,128)(2,1)S(1)}, u32[]{:S(2)}, u32[]{:S(2)}) collective-permute-start(bf16[512,256]{1,0:T(8,128)(2,1)S(1)} %get-tuple-element.86), channel_id=1, source_target_pairs={{0,14},{2,0},{4,2},{6,4},{8,6},{10,8},{12,10},{14,12},{1,15},{3,1}... | collective-permute-start | bytes 786440 | tf_op jit(solution)/shard_map/ppermute | solution.py:598
  129.5 9.0 %collective-permute-start.4 = (bf16[512,256]{1,0:T(8,128)(2,1)S(1)}, bf16[512,256]{1,0:T(8,128)(2,1)S(1)}, u32[]{:S(2)}, u32[]{:S(2)}) collective-permute-start(bf16[512,256]{1,0:T(8,128)(2,1)S(1)} %get-tuple-element.85.refs_2_), channel_id=1, source_target_pairs={{0,2},{2,4},{4,6},{6,8},{8,10},{10,12},{12,14},{14,0},{1,3},{3,5},... | collective-permute-start | bytes 786440 | tf_op jit(solution)/shard_map/ppermute | solution.py:598
  131.4 7.0 %copy-start.11 = (bf16[2,512,256]{2,1,0:T(8,128)(2,1)S(1)}, bf16[2,512,256]{2,1,0:T(8,128)(2,1)}, u32[]{:S(2)}) copy-start(bf16[2,512,256]{2,1,0:T(8,128)(2,1)} %get-tuple-element.80.blocks_ref) | copy-start | bytes 1572868
  131.6 12.5 %collective-permute-start.10 = (bf16[512,256]{1,0:T(8,128)(2,1)S(1)}, bf16[512,256]{1,0:T(8,128)(2,1)S(1)}, u32[]{:S(2)}, u32[]{:S(2)}) collective-permute-start(bf16[512,256]{1,0:T(8,128)(2,1)S(1)} %get-tuple-element.93), channel_id=1, source_target_pairs={{0,2},{2,4},{4,6},{6,8},{8,10},{10,12},{12,14},{14,0},{1,3},{3,5},... | collective-permute-start | bytes 786440 | tf_op jit(solution)/shard_map/ppermute | solution.py:598
  131.7 12.4 %collective-permute-start.9 = (bf16[512,256]{1,0:T(8,128)(2,1)S(1)}, bf16[512,256]{1,0:T(8,128)(2,1)S(1)}, u32[]{:S(2)}, u32[]{:S(2)}) collective-permute-start(bf16[512,256]{1,0:T(8,128)(2,1)S(1)} %get-tuple-element.90.refs_2_), channel_id=1, source_target_pairs={{0,14},{2,0},{4,2},{6,4},{8,6},{10,8},{12,10},{14,12},{1,15},{3,1}... | collective-permute-start | bytes 786440 | tf_op jit(solution)/shard_map/ppermute | solution.py:598
  138.5 5.6 %copy-start.10 = (bf16[2,512,256]{2,1,0:T(8,128)(2,1)S(1)}, bf16[2,512,256]{2,1,0:T(8,128)(2,1)}, u32[]{:S(2)}) copy-start(bf16[2,512,256]{2,1,0:T(8,128)(2,1)} %get-tuple-element.92.blocks_ref) | copy-start | bytes 1572868
  138.6 16.2 %collective-permute-start.12 = (bf16[512,256]{1,0:T(8,128)(2,1)S(1)}, bf16[512,256]{1,0:T(8,128)(2,1)S(1)}, u32[]{:S(2)}, u32[]{:S(2)}) collective-permute-start(bf16[512,256]{1,0:T(8,128)(2,1)S(1)} %get-tuple-element.95), channel_id=1, source_target_pairs={{0,14},{2,0},{4,2},{6,4},{8,6},{10,8},{12,10},{14,12},{1,15},{3,1}... | collective-permute-start | bytes 786440 | tf_op jit(solution)/shard_map/ppermute | solution.py:598
  138.7 11.0 %collective-permute-start.8 = (bf16[512,256]{1,0:T(8,128)(2,1)S(1)}, bf16[512,256]{1,0:T(8,128)(2,1)S(1)}, u32[]{:S(2)}, u32[]{:S(2)}) collective-permute-start(bf16[512,256]{1,0:T(8,128)(2,1)S(1)} %get-tuple-element.91.refs_2_), channel_id=1, source_target_pairs={{0,2},{2,4},{4,6},{6,8},{8,10},{10,12},{12,14},{14,0},{1,3},{3,5},... | collective-permute-start | bytes 786440 | tf_op jit(solution)/shard_map/ppermute | solution.py:598
  144.1 5.6 %copy-start.14 = (bf16[1,512,256]{2,1,0:T(8,128)(2,1)S(1)}, bf16[1,512,256]{2,1,0:T(8,128)(2,1)}, u32[]{:S(2)}) copy-start(bf16[1,512,256]{2,1,0:T(8,128)(2,1)} %get-tuple-element.79.blocks_ref) | copy-start | bytes 786436
  144.2 11.1 %collective-permute-start.15 = (bf16[512,256]{1,0:T(8,128)(2,1)S(1)}, bf16[512,256]{1,0:T(8,128)(2,1)S(1)}, u32[]{:S(2)}, u32[]{:S(2)}) collective-permute-start(bf16[512,256]{1,0:T(8,128)(2,1)S(1)} %get-tuple-element.97), channel_id=1, source_target_pairs={{0,2},{2,4},{4,6},{6,8},{8,10},{10,12},{12,14},{14,0},{1,3},{3,5},... | collective-permute-start | bytes 786440 | tf_op jit(solution)/shard_map/ppermute | solution.py:598
  144.3 8.1 %collective-permute-start.13 = (bf16[512,256]{1,0:T(8,128)(2,1)S(1)}, bf16[512,256]{1,0:T(8,128)(2,1)S(1)}, u32[]{:S(2)}, u32[]{:S(2)}) collective-permute-start(bf16[512,256]{1,0:T(8,128)(2,1)S(1)} %get-tuple-element.94.refs_1_), channel_id=1, source_target_pairs={{0,14},{2,0},{4,2},{6,4},{8,6},{10,8},{12,10},{14,12},{1,15},{3,1}... | collective-permute-start | bytes 786440 | tf_op jit(solution)/shard_map/ppermute | solution.py:598
  149.7 2.7 %copy-start.13 = (bf16[1,512,256]{2,1,0:T(8,128)(2,1)S(1)}, bf16[1,512,256]{2,1,0:T(8,128)(2,1)}, u32[]{:S(2)}) copy-start(bf16[1,512,256]{2,1,0:T(8,128)(2,1)} %get-tuple-element.96.blocks_ref) | copy-start | bytes 786436
  149.8 11.2 %collective-permute-start.11 = (bf16[512,256]{1,0:T(8,128)(2,1)S(1)}, bf16[512,256]{1,0:T(8,128)(2,1)S(1)}, u32[]{:S(2)}, u32[]{:S(2)}) collective-permute-start(bf16[512,256]{1,0:T(8,128)(2,1)S(1)} %add_0_1.1.refs_1_), channel_id=1, source_target_pairs={{0,2},{2,4},{4,6},{6,8},{8,10},{10,12},{12,14},{14,0},{1,3},{3,5},... | collective-permute-start | bytes 786440 | tf_op jit(solution)/shard_map/ppermute | solution.py:598
  152.4 8.5 %copy-start.4 = (bf16[2,512,256]{2,1,0:T(8,128)(2,1)S(1)}, bf16[2,512,256]{2,1,0:T(8,128)(2,1)}, u32[]{:S(2)}) copy-start(bf16[2,512,256]{2,1,0:T(8,128)(2,1)} %get-tuple-element.78.blocks_ref) | copy-start | bytes 1572868
  152.5 21.7 %copy-start.6 = (bf16[128,512]{1,0:T(8,128)(2,1)S(1)}, bf16[128,512]{1,0:T(8,128)(2,1)}, u32[]{:S(2)}) copy-start(bf16[128,512]{1,0:T(8,128)(2,1)} %copy-done.5) | copy-start | bytes 393220
  152.5 8.4 %collective-permute-start.14 = (bf16[512,256]{1,0:T(8,128)(2,1)S(1)}, bf16[512,256]{1,0:T(8,128)(2,1)S(1)}, u32[]{:S(2)}, u32[]{:S(2)}) collective-permute-start(bf16[512,256]{1,0:T(8,128)(2,1)S(1)} %add_1_1.1), channel_id=1, source_target_pairs={{0,14},{2,0},{4,2},{6,4},{8,6},{10,8},{12,10},{14,12},{1,15},{3,1}... | collective-permute-start | bytes 786440 | tf_op jit(solution)/shard_map/ppermute | solution.py:598
  160.9 15.9 %copy-start.8 = (s32[34]{0:T(128)S(1)}, s32[34]{0:T(128)}, u32[]{:S(2)}) copy-start(s32[34]{0:T(128)} %get-tuple-element.53.table.owners) | copy-start | bytes 412
  161.9 23.8 %all-to-all-start.4 = ((bf16[32,16,512]{2,1,0:T(8,128)(2,1)}), bf16[32,16,512]{2,1,0:T(8,128)(2,1)S(1)}, u32[]{:S(2)}, u32[]{:S(2)}) async-start(bf16[32,16,512]{2,1,0:T(8,128)(2,1)} %bitcast.15), calls=%async_computation.4 | async-start | bytes 1048576 | tf_op jit(solution)/shard_map/all_to_all | solution.py:741

commit v9 on v8

--- a/solution.py
+++ b/solution.py
@@ -206,7 +206,7 @@
         out_shape=jax.ShapeDtypeStruct((peers, 2 * heads, columns), F32),
         in_specs=[smem(), in_hbm(), whole()],
         out_specs=whole(),
-        scratch_shapes=[pltpu.VMEM(got.shape, BF16), pltpu.SemaphoreType.DMA((4,))],
+        scratch_shapes=[pltpu.VMEM(got.shape, BF16), pltpu.SemaphoreType.DMA((8,))],
         compiler_params=params(VMEM_MOST),
         cost_estimate=cost(2 * 10**9, 6 * 2**20, 2 * 10**6),
         name="owner_stats",

time: 187 us -> 188 us (level)
  no operation moved by 1% of the time
where the time goes in v9:
time: 188 us; the launch traced here: 187 us
  blocking collectives  57.7 us (31%)
  starting transfers between devices  44.6 us (24%)
  Pallas kernels  39.2 us (21%)
  waiting for transfers between devices  38.1 us (20%)
  local copies, waits for them, and re-layouts  6.43 us (3%)
    all_to_all x1, blocking collectives, exchange(): return lax.all_to_all(x, 'dp', split_axis=0, concat_axis=0, tiled=True)  57.7 us
    ppermute x14, waiting for transfers between devices, travel(): lax.ppermute(block, 'pass', [(i, (i + way) % count) for i in range(count)])  21.5 us
    ppermute x14, starting transfers between devices, travel(): lax.ppermute(block, 'pass', [(i, (i + way) % count) for i in range(count)])  19.3 us
    pallas_call x1, Pallas kernels, owner_grads(): pl.pallas_call(functools.partial(owner_grads_kernel, 2 * columns // both,...  17 us
    all_to_all x1, starting transfers between devices, local(): lax.all_to_all(summed.reshape(peers * cores, share, -1), ('dp', 'tensor')...  12.2 us
    all_to_all x3, starting transfers between devices, exchange(): return lax.all_to_all(x, 'dp', split_axis=0, concat_axis=0, tiled=True)  10.9 us
    all_to_all x3, waiting for transfers between devices, exchange(): return lax.all_to_all(x, 'dp', split_axis=0, concat_axis=0, tiled=True)  9.86 us
    pallas_call x1, Pallas kernels, owner_stats(): pl.pallas_call(functools.partial(owner_stats_kernel, group), out_shape=ja...  7.53 us
  transfers between devices with their start and end apart: 20, of which 11 were waited for; matrix products, arithmetic and copies ran while one was open for 1% of the time, Pallas kernels for 4%

profile of v9, /device:TPU:1, one launch (start us, length us, event | category | flops | bytes accessed | tf_op | source)
XLA Modules:
  0.0 186.9 jit_solution(10551974744648683427)
XLA Ops:
  0.6 0.7 copy-done
  1.3 0.7 dynamic-slice_reduce_fusion.blocks
  2.0 5.4 %pack_queries.1 = (bf16[16,64,2048]{2,1,0:T(8,128)(2,1)}, s32[34]{0:T(128)}, bf16[2,2,256,256]{3,2,1,0:T(8,128)(2,1)}) custom-call(s32[16,16]{1,0:T(8,128)} %bitcast.22, s32[2]{0:T(128)} %dynamic-slice_reduce_fusion.blocks, bf16[4,32,2048]{2,1,0:T(8,128)(2,1)} %q_ref.3, bf16[4,32,2048]{2,1,0:T(8,128)(2,1)} %g_ref.3, bf16[2,256,2,256]{3,2,1,0:T(2,128)(2,1)} %raw_ref.1), custom_call_target="tpu_custom_call" | custom-call | bytes 6291456 | tf_op jit(solution)/shard_map/pack_queries/pallas_call | solution.py:110
  7.4 57.7 %all_to_all.25.got_hbm = bf16[16,64,2048]{2,1,0:T(8,128)(2,1)} all-to-all(bf16[16,64,2048]{2,1,0:T(8,128)(2,1)} %get-tuple-element.54), channel_id=1, replica_groups=mesh['dp'=16,'pass'=8,'tensor'=2] {'dp'}, dimensions={0} | all-to-all | bytes 8388608 | tf_op jit(solution)/shard_map/all_to_all | solution.py:654
  65.2 7.5 %owner_stats.1 = f32[16,4,256]{2,1,0:T(4,128)} custom-call(s32[34]{0:T(128)} %get-tuple-element.53.table.owners, bf16[16,64,2048]{2,1,0:T(8,128)(2,1)} %all_to_all.25.got_hbm, bf16[2,2,256,256]{3,2,1,0:T(8,128)(2,1)} %get-tuple-element.56.kv_ref), custom_call_target="tpu_custom_call" | custom-call | flops 2000000000 | bytes 6291456 | tf_op jit(solution)/shard_map/owner_stats/pallas_call | solution.py:204
  72.7 2.1 %collective-permute-start = (bf16[2,128,4096]{2,1,0:T(8,128)(2,1)}, bf16[2,128,4096]{2,1,0:T(8,128)(2,1)}, u32[]{:S(2)}, u32[]{:S(2)}) collective-permute-start(bf16[2,128,4096]{2,1,0:T(8,128)(2,1)} %param.13), channel_id=1, source_target_pairs={{0,1},{1,0},{2,3},{3,2},{4,5},{5,4},{6,7},{7,6},{8,9},{9,8},{10,11... | collective-permute-start | bytes 6291464 | tf_op jit(solution)/shard_map/ppermute | solution.py:657
  74.8 0.1 collective-permute-start.1
  74.9 3.5 %all-to-all-start.1 = ((f32[16,4,256]{2,1,0:T(4,128)}), f32[16,4,256]{2,1,0:T(4,128)S(1)}, u32[]{:S(2)}, u32[]{:S(2)}) async-start(f32[16,4,256]{2,1,0:T(4,128)} %owner_stats.1), calls=%async_computation.1 | async-start | bytes 131072 | tf_op jit(solution)/shard_map/all_to_all | solution.py:654
  78.4 0.5 own_stats.1.own_ref
  79.0 5.9 %all-to-all-done.1.st_ref = f32[16,4,256]{2,1,0:T(4,128)S(1)} async-done(((f32[16,4,256]{2,1,0:T(4,128)}), f32[16,4,256]{2,1,0:T(4,128)S(1)}, u32[]{:S(2)}, u32[]{:S(2)}) %all-to-all-start.1) | async-done | bytes 65568 | tf_op jit(solution)/shard_map/all_to_all | solution.py:654
  84.9 1.4 merge_stats.1
  86.3 3.5 %all-to-all-start.2 = ((f32[16,4,256]{2,1,0:T(4,128)}), f32[16,4,256]{2,1,0:T(4,128)S(1)}, u32[]{:S(2)}, u32[]{:S(2)}) async-start(f32[16,4,256]{2,1,0:T(4,128)} %get-tuple-element.68), calls=%async_computation.2 | async-start | bytes 131072 | tf_op jit(solution)/shard_map/all_to_all | solution.py:654
  89.8 1.9 own_grads.1
  91.7 0.6 copy-done.5
  92.3 3.9 %all-to-all-done.2.joint_ref = f32[16,4,256]{2,1,0:T(4,128)S(1)} async-done(((f32[16,4,256]{2,1,0:T(4,128)}), f32[16,4,256]{2,1,0:T(4,128)S(1)}, u32[]{:S(2)}, u32[]{:S(2)}) %all-to-all-start.2) | async-done | bytes 65568 | tf_op jit(solution)/shard_map/all_to_all | solution.py:654
  96.3 0.6 copy-done.16
  96.9 17.0 %owner_grads.1 = (bf16[512,512]{1,0:T(8,128)(2,1)}, bf16[16,32,2048]{2,1,0:T(8,128)(2,1)}, bf16[1,512,256]{2,1,0:T(8,128)(2,1)}, bf16[1,512,256]{2,1,0:T(8,128)(...) custom-call(s32[34]{0:T(128)} %get-tuple-element.53.table.owners, ...), custom_call_target="tpu_custom_call" | custom-call | flops 16000000000 | bytes 25165824 | tf_op jit(solution)/shard_map/owner_grads/pallas_call | solution.py:435
  113.9 1.7 collective-permute-start.2
  115.6 4.2 %collective-permute-start.3 = (bf16[512,256]{1,0:T(8,128)(2,1)}, bf16[512,256]{1,0:T(8,128)(2,1)}, u32[]{:S(2)}, u32[]{:S(2)}) collective-permute-start(bf16[512,256]{1,0:T(8,128)(2,1)} %bitcast.31), channel_id=1, source_target_pairs={{0,14},{2,0},{4,2},{6,4},{8,6},{10,8},{12,10},{14,12},{1,15},{3,1}... | collective-permute-start | bytes 786440 | tf_op jit(solution)/shard_map/ppermute | solution.py:598
  119.8 3.8 %all-to-all-start.3 = ((bf16[16,32,2048]{2,1,0:T(8,128)(2,1)}), bf16[16,32,2048]{2,1,0:T(8,128)(2,1)S(1)}, u32[]{:S(2)}, u32[]{:S(2)}) async-start(bf16[16,32,2048]{2,1,0:T(8,128)(2,1)} %get-tuple-element.98), calls=%async_computation.3 | async-start | bytes 4194304 | tf_op jit(solution)/shard_map/all_to_all | solution.py:654
  123.7 1.3 collective-permute-start.6
  125.0 0.3 collective-permute-start.7
  125.3 1.0 copy-done.9
  126.3 1.2 add_0_3.1
  127.5 2.5 %collective-permute-start.5 = (bf16[512,256]{1,0:T(8,128)(2,1)S(1)}, bf16[512,256]{1,0:T(8,128)(2,1)S(1)}, u32[]{:S(2)}, u32[]{:S(2)}) collective-permute-start(bf16[512,256]{1,0:T(8,128)(2,1)S(1)} %get-tuple-element.86), channel_id=1, source_target_pairs={{0,14},{2,0},{4,2},{6,4},{8,6},{10,8},{12,10},{14,12},{1,15},{3,1}... | collective-permute-start | bytes 786440 | tf_op jit(solution)/shard_map/ppermute | solution.py:598
  129.9 2.0 %collective-permute-done.7.refs_1_ = bf16[512,256]{1,0:T(8,128)(2,1)S(1)} collective-permute-done((bf16[512,256]{1,0:T(8,128)(2,1)}, bf16[512,256]{1,0:T(8,128)(2,1)S(1)}, u32[]{:S(2)}, u32[]{:S(2)}) %collective-permute-start.7) | collective-permute-done | bytes 262176 | tf_op jit(solution)/shard_map/ppermute | solution.py:598
  131.9 0.1 add_1_3.1
  132.0 0.1 collective-permute-start.10
  132.1 2.7 %collective-permute-start.9 = (bf16[512,256]{1,0:T(8,128)(2,1)S(1)}, bf16[512,256]{1,0:T(8,128)(2,1)S(1)}, u32[]{:S(2)}, u32[]{:S(2)}) collective-permute-start(bf16[512,256]{1,0:T(8,128)(2,1)S(1)} %get-tuple-element.90.refs_2_), channel_id=1, source_target_pairs={{0,14},{2,0},{4,2},{6,4},{8,6},{10,8},{12,10},{14,12},{1,15},{3,1}... | collective-permute-start | bytes 786440 | tf_op jit(solution)/shard_map/ppermute | solution.py:598
  134.8 1.1 collective-permute-done.5.refs_1_
  135.9 3.1 %collective-permute-done.4.refs_0_ = bf16[512,256]{1,0:T(8,128)(2,1)S(1)} collective-permute-done((bf16[512,256]{1,0:T(8,128)(2,1)S(1)}, bf16[512,256]{1,0:T(8,128)(2,1)S(1)}, u32[]{:S(2)}, u32[]{:S(2)}) %collective-permute-start.4) | collective-permute-done | bytes 262176 | tf_op jit(solution)/shard_map/ppermute | solution.py:598
  138.9 0.1 add_0_2.1
  139.2 1.5 collective-permute-start.8
  140.6 3.9 %collective-permute-done.10.refs_1_ = bf16[512,256]{1,0:T(8,128)(2,1)S(1)} collective-permute-done((bf16[512,256]{1,0:T(8,128)(2,1)S(1)}, bf16[512,256]{1,0:T(8,128)(2,1)S(1)}, u32[]{:S(2)}, u32[]{:S(2)}) %collective-permute-start.10) | collective-permute-done | bytes 262176 | tf_op jit(solution)/shard_map/ppermute | solution.py:598
  144.6 0.1 add_1_2.1
  144.8 2.7 %collective-permute-start.13 = (bf16[512,256]{1,0:T(8,128)(2,1)S(1)}, bf16[512,256]{1,0:T(8,128)(2,1)S(1)}, u32[]{:S(2)}, u32[]{:S(2)}) collective-permute-start(bf16[512,256]{1,0:T(8,128)(2,1)S(1)} %get-tuple-element.94.refs_1_), channel_id=1, source_target_pairs={{0,14},{2,0},{4,2},{6,4},{8,6},{10,8},{12,10},{14,12},{1,15},{3,1}... | collective-permute-start | bytes 786440 | tf_op jit(solution)/shard_map/ppermute | solution.py:598
  147.5 2.7 %collective-permute-done.8.refs_0_ = bf16[512,256]{1,0:T(8,128)(2,1)S(1)} collective-permute-done((bf16[512,256]{1,0:T(8,128)(2,1)S(1)}, bf16[512,256]{1,0:T(8,128)(2,1)S(1)}, u32[]{:S(2)}, u32[]{:S(2)}) %collective-permute-start.8) | collective-permute-done | bytes 262176 | tf_op jit(solution)/shard_map/ppermute | solution.py:598
  150.3 2.6 %collective-permute-done.13.refs_0_ = bf16[512,256]{1,0:T(8,128)(2,1)S(1)} collective-permute-done((bf16[512,256]{1,0:T(8,128)(2,1)S(1)}, bf16[512,256]{1,0:T(8,128)(2,1)S(1)}, u32[]{:S(2)}, u32[]{:S(2)}) %collective-permute-start.13) | collective-permute-done | bytes 262176 | tf_op jit(solution)/shard_map/ppermute | solution.py:598
  153.0 2.3 %collective-permute-start.14 = (bf16[512,256]{1,0:T(8,128)(2,1)S(1)}, bf16[512,256]{1,0:T(8,128)(2,1)S(1)}, u32[]{:S(2)}, u32[]{:S(2)}) collective-permute-start(bf16[512,256]{1,0:T(8,128)(2,1)S(1)} %add_1_1.1), channel_id=1, source_target_pairs={{0,14},{2,0},{4,2},{6,4},{8,6},{10,8},{12,10},{14,12},{1,15},{3,1}... | collective-permute-start | bytes 786440 | tf_op jit(solution)/shard_map/ppermute | solution.py:598
  155.3 0.5 collective-permute-done.15.refs_3_
  155.8 5.6 %collective-permute-done.11.refs_0_ = bf16[512,256]{1,0:T(8,128)(2,1)S(1)} collective-permute-done((bf16[512,256]{1,0:T(8,128)(2,1)S(1)}, bf16[512,256]{1,0:T(8,128)(2,1)S(1)}, u32[]{:S(2)}, u32[]{:S(2)}) %collective-permute-start.11) | collective-permute-done | bytes 262176 | tf_op jit(solution)/shard_map/ppermute | solution.py:598
  161.4 1.0 weights_last.1
  162.4 12.2 %all-to-all-start.4 = ((bf16[32,16,512]{2,1,0:T(8,128)(2,1)}), bf16[32,16,512]{2,1,0:T(8,128)(2,1)S(1)}, u32[]{:S(2)}, u32[]{:S(2)}) async-start(bf16[32,16,512]{2,1,0:T(8,128)(2,1)} %bitcast.15), calls=%async_computation.4 | async-start | bytes 1048576 | tf_op jit(solution)/shard_map/all_to_all | solution.py:741
  174.7 0.7 reshape.51
  175.4 2.0 %reshape.53 = bf16[2,256,2,2,128]{4,3,2,1,0:T(2,128)(2,1)} reshape(bf16[512,512]{1,0:T(8,128)(2,1)} %get-tuple-element.84.refs_2_) | data formatting | bytes 1048576 | tf_op jit(solution)/shard_map/reshape | solution.py:751
  177.3 2.1 %sum_dq.1 = bf16[4,32,2048]{2,1,0:T(8,128)(2,1)} custom-call(s32[34]{0:T(128)S(1)} %copy-done.8, bf16[16,32,2048]{2,1,0:T(8,128)(2,1)S(1)} %all-to-all-done.3.refs_0_.refs_1_.refs_2_.refs_3_, bf16[16,32,2048]{2,1,0:T(8,128)(2,1)S(1)} %all-to-all-done.3.refs_0_.refs_1_.refs_2_.refs_3_, ...), custom_call_target="tpu_custom_call" | custom-call | flops 2000000 | bytes 4194304 | tf_op jit(solution)/shard_map/sum_dq/pallas_call | solution.py:536
  179.5 6.7 %all-to-all-done.4 = bf16[32,16,512]{2,1,0:T(8,128)(2,1)S(1)} async-done(((bf16[32,16,512]{2,1,0:T(8,128)(2,1)}), bf16[32,16,512]{2,1,0:T(8,128)(2,1)S(1)}, u32[]{:S(2)}, u32[]{:S(2)}) %all-to-all-start.4) | async-done | bytes 524320 | tf_op jit(solution)/shard_map/all_to_all | solution.py:741
  186.2 0.7 finish_weights.1
  (51 shorter events, 0.5 us)
Async XLA Ops:
  0.6 0.7 copy-start
  7.4 57.7 %copy-start.15 = (bf16[4,32,2,256]{3,2,1,0:T(2,128)(2,1)S(1)}, bf16[4,32,2,256]{3,2,1,0:T(2,128)(2,1)}, u32[]{:S(2)}) copy-start(bf16[4,32,2,256]{3,2,1,0:T(2,128)(2,1)} %param.10) | copy-start | bytes 393220
  65.2 9.7 %copy-start.17 = (bf16[4,16,4096]{2,1,0:T(8,128)(2,1)S(1)}, bf16[4,16,4096]{2,1,0:T(8,128)(2,1)}, u32[]{:S(2)}) copy-start(bf16[4,16,4096]{2,1,0:T(8,128)(2,1)} %param.12) | copy-start | bytes 1572868
  65.2 13.3 %copy-start.1 = (bf16[4,32,2048]{2,1,0:T(8,128)(2,1)S(1)}, bf16[4,32,2048]{2,1,0:T(8,128)(2,1)}, u32[]{:S(2)}) copy-start(bf16[4,32,2048]{2,1,0:T(8,128)(2,1)} %q_ref.3) | copy-start | bytes 1572868
  65.2 13.3 %copy-start.2 = (bf16[4,32,2048]{2,1,0:T(8,128)(2,1)S(1)}, bf16[4,32,2048]{2,1,0:T(8,128)(2,1)}, u32[]{:S(2)}) copy-start(bf16[4,32,2048]{2,1,0:T(8,128)(2,1)} %g_ref.3) | copy-start | bytes 1572868
  65.2 19.7 %copy-start.7 = (s32[16,1,16]{2,1,0:T(1,128)S(1)}, s32[16,1,16]{2,1,0:T(1,128)}, u32[]{:S(2)}) copy-start(s32[16,1,16]{2,1,0:T(1,128)} %param.14) | copy-start | bytes 3076
  72.7 12.2 %collective-permute-start = (bf16[2,128,4096]{2,1,0:T(8,128)(2,1)}, bf16[2,128,4096]{2,1,0:T(8,128)(2,1)}, u32[]{:S(2)}, u32[]{:S(2)}) collective-permute-start(bf16[2,128,4096]{2,1,0:T(8,128)(2,1)} %param.13), channel_id=1, source_target_pairs={{0,1},{1,0},{2,3},{3,2},{4,5},{5,4},{6,7},{7,6},{8,9},{9,8},{10,11... | collective-permute-start | bytes 6291464 | tf_op jit(solution)/shard_map/ppermute | solution.py:657
  74.8 10.1 %collective-permute-start.1 = (bf16[4,16,4096]{2,1,0:T(8,128)(2,1)S(1)}, bf16[4,16,4096]{2,1,0:T(8,128)(2,1)S(1)}, u32[]{:S(2)}, u32[]{:S(2)}) collective-permute-start(bf16[4,16,4096]{2,1,0:T(8,128)(2,1)S(1)} %copy-done.17), channel_id=1, source_target_pairs={{0,1},{1,0},{2,3},{3,2},{4,5},{5,4},{6,7},{7,6},{8,9},{9,8},{10,11... | collective-permute-start | bytes 1572872 | tf_op jit(solution)/shard_map/ppermute | solution.py:657
  74.9 10.0 %all-to-all-start.1 = ((f32[16,4,256]{2,1,0:T(4,128)}), f32[16,4,256]{2,1,0:T(4,128)S(1)}, u32[]{:S(2)}, u32[]{:S(2)}) async-start(f32[16,4,256]{2,1,0:T(4,128)} %owner_stats.1), calls=%async_computation.1 | async-start | bytes 131072 | tf_op jit(solution)/shard_map/all_to_all | solution.py:654
  84.9 11.4 %copy-start.18 = (bf16[4,16,4096]{2,1,0:T(8,128)(2,1)}, bf16[4,16,4096]{2,1,0:T(8,128)(2,1)S(1)}, u32[]{:S(2)}) copy-start(bf16[4,16,4096]{2,1,0:T(8,128)(2,1)S(1)} %collective-permute-done.1) | copy-start | bytes 1572868
  86.3 10.0 %all-to-all-start.2 = ((f32[16,4,256]{2,1,0:T(4,128)}), f32[16,4,256]{2,1,0:T(4,128)S(1)}, u32[]{:S(2)}, u32[]{:S(2)}) async-start(f32[16,4,256]{2,1,0:T(4,128)} %get-tuple-element.68), calls=%async_computation.2 | async-start | bytes 131072 | tf_op jit(solution)/shard_map/all_to_all | solution.py:654
  91.7 0.7 copy-start.5
  96.3 0.6 copy-start.16
  113.9 11.3 %collective-permute-start.2 = (bf16[512,256]{1,0:T(8,128)(2,1)}, bf16[512,256]{1,0:T(8,128)(2,1)S(1)}, u32[]{:S(2)}, u32[]{:S(2)}) collective-permute-start(bf16[512,256]{1,0:T(8,128)(2,1)} %bitcast.32), channel_id=1, source_target_pairs={{0,2},{2,4},{4,6},{6,8},{8,10},{10,12},{12,14},{14,0},{1,3},{3,5},... | collective-permute-start | bytes 786440 | tf_op jit(solution)/shard_map/ppermute | solution.py:598
  115.6 9.6 %collective-permute-start.3 = (bf16[512,256]{1,0:T(8,128)(2,1)}, bf16[512,256]{1,0:T(8,128)(2,1)}, u32[]{:S(2)}, u32[]{:S(2)}) collective-permute-start(bf16[512,256]{1,0:T(8,128)(2,1)} %bitcast.31), channel_id=1, source_target_pairs={{0,14},{2,0},{4,2},{6,4},{8,6},{10,8},{12,10},{14,12},{1,15},{3,1}... | collective-permute-start | bytes 786440 | tf_op jit(solution)/shard_map/ppermute | solution.py:598
  119.8 5.4 %copy-start.3 = (bf16[512,512]{1,0:T(8,128)(2,1)S(1)}, bf16[512,512]{1,0:T(8,128)(2,1)}, u32[]{:S(2)}) copy-start(bf16[512,512]{1,0:T(8,128)(2,1)} %get-tuple-element.84.refs_2_) | copy-start | bytes 1572868
  119.8 42.6 %all-to-all-start.3 = ((bf16[16,32,2048]{2,1,0:T(8,128)(2,1)}), bf16[16,32,2048]{2,1,0:T(8,128)(2,1)S(1)}, u32[]{:S(2)}, u32[]{:S(2)}) async-start(bf16[16,32,2048]{2,1,0:T(8,128)(2,1)} %get-tuple-element.98), calls=%async_computation.3 | async-start | bytes 4194304 | tf_op jit(solution)/shard_map/all_to_all | solution.py:654
  123.7 6.2 %collective-permute-start.6 = (bf16[512,256]{1,0:T(8,128)(2,1)}, bf16[512,256]{1,0:T(8,128)(2,1)S(1)}, u32[]{:S(2)}, u32[]{:S(2)}) collective-permute-start(bf16[512,256]{1,0:T(8,128)(2,1)} %bitcast.30), channel_id=1, source_target_pairs={{0,14},{2,0},{4,2},{6,4},{8,6},{10,8},{12,10},{14,12},{1,15},{3,1}... | collective-permute-start | bytes 786440 | tf_op jit(solution)/shard_map/ppermute | solution.py:598
  125.0 6.9 %collective-permute-start.7 = (bf16[512,256]{1,0:T(8,128)(2,1)}, bf16[512,256]{1,0:T(8,128)(2,1)S(1)}, u32[]{:S(2)}, u32[]{:S(2)}) collective-permute-start(bf16[512,256]{1,0:T(8,128)(2,1)} %bitcast.29), channel_id=1, source_target_pairs={{0,2},{2,4},{4,6},{6,8},{8,10},{10,12},{12,14},{14,0},{1,3},{3,5},... | collective-permute-start | bytes 786440 | tf_op jit(solution)/shard_map/ppermute | solution.py:598
  125.3 1.0 copy-start.9
  126.3 5.6 %copy-start.12 = (bf16[2,512,256]{2,1,0:T(8,128)(2,1)S(1)}, bf16[2,512,256]{2,1,0:T(8,128)(2,1)}, u32[]{:S(2)}) copy-start(bf16[2,512,256]{2,1,0:T(8,128)(2,1)} %get-tuple-element.87.blocks_ref) | copy-start | bytes 1572868
  127.5 8.4 %collective-permute-start.5 = (bf16[512,256]{1,0:T(8,128)(2,1)S(1)}, bf16[512,256]{1,0:T(8,128)(2,1)S(1)}, u32[]{:S(2)}, u32[]{:S(2)}) collective-permute-start(bf16[512,256]{1,0:T(8,128)(2,1)S(1)} %get-tuple-element.86), channel_id=1, source_target_pairs={{0,14},{2,0},{4,2},{6,4},{8,6},{10,8},{12,10},{14,12},{1,15},{3,1}... | collective-permute-start | bytes 786440 | tf_op jit(solution)/shard_map/ppermute | solution.py:598
  129.9 9.0 %collective-permute-start.4 = (bf16[512,256]{1,0:T(8,128)(2,1)S(1)}, bf16[512,256]{1,0:T(8,128)(2,1)S(1)}, u32[]{:S(2)}, u32[]{:S(2)}) collective-permute-start(bf16[512,256]{1,0:T(8,128)(2,1)S(1)} %get-tuple-element.85.refs_2_), channel_id=1, source_target_pairs={{0,2},{2,4},{4,6},{6,8},{8,10},{10,12},{12,14},{14,0},{1,3},{3,5},... | collective-permute-start | bytes 786440 | tf_op jit(solution)/shard_map/ppermute | solution.py:598
  131.9 7.0 %copy-start.11 = (bf16[2,512,256]{2,1,0:T(8,128)(2,1)S(1)}, bf16[2,512,256]{2,1,0:T(8,128)(2,1)}, u32[]{:S(2)}) copy-start(bf16[2,512,256]{2,1,0:T(8,128)(2,1)} %get-tuple-element.80.blocks_ref) | copy-start | bytes 1572868
  132.0 12.5 %collective-permute-start.10 = (bf16[512,256]{1,0:T(8,128)(2,1)S(1)}, bf16[512,256]{1,0:T(8,128)(2,1)S(1)}, u32[]{:S(2)}, u32[]{:S(2)}) collective-permute-start(bf16[512,256]{1,0:T(8,128)(2,1)S(1)} %get-tuple-element.93), channel_id=1, source_target_pairs={{0,2},{2,4},{4,6},{6,8},{8,10},{10,12},{12,14},{14,0},{1,3},{3,5},... | collective-permute-start | bytes 786440 | tf_op jit(solution)/shard_map/ppermute | solution.py:598
  132.1 12.4 %collective-permute-start.9 = (bf16[512,256]{1,0:T(8,128)(2,1)S(1)}, bf16[512,256]{1,0:T(8,128)(2,1)S(1)}, u32[]{:S(2)}, u32[]{:S(2)}) collective-permute-start(bf16[512,256]{1,0:T(8,128)(2,1)S(1)} %get-tuple-element.90.refs_2_), channel_id=1, source_target_pairs={{0,14},{2,0},{4,2},{6,4},{8,6},{10,8},{12,10},{14,12},{1,15},{3,1}... | collective-permute-start | bytes 786440 | tf_op jit(solution)/shard_map/ppermute | solution.py:598
  138.9 5.6 %copy-start.10 = (bf16[2,512,256]{2,1,0:T(8,128)(2,1)S(1)}, bf16[2,512,256]{2,1,0:T(8,128)(2,1)}, u32[]{:S(2)}) copy-start(bf16[2,512,256]{2,1,0:T(8,128)(2,1)} %get-tuple-element.92.blocks_ref) | copy-start | bytes 1572868
  139.1 16.2 %collective-permute-start.12 = (bf16[512,256]{1,0:T(8,128)(2,1)S(1)}, bf16[512,256]{1,0:T(8,128)(2,1)S(1)}, u32[]{:S(2)}, u32[]{:S(2)}) collective-permute-start(bf16[512,256]{1,0:T(8,128)(2,1)S(1)} %get-tuple-element.95), channel_id=1, source_target_pairs={{0,14},{2,0},{4,2},{6,4},{8,6},{10,8},{12,10},{14,12},{1,15},{3,1}... | collective-permute-start | bytes 786440 | tf_op jit(solution)/shard_map/ppermute | solution.py:598
  139.2 11.0 %collective-permute-start.8 = (bf16[512,256]{1,0:T(8,128)(2,1)S(1)}, bf16[512,256]{1,0:T(8,128)(2,1)S(1)}, u32[]{:S(2)}, u32[]{:S(2)}) collective-permute-start(bf16[512,256]{1,0:T(8,128)(2,1)S(1)} %get-tuple-element.91.refs_2_), channel_id=1, source_target_pairs={{0,2},{2,4},{4,6},{6,8},{8,10},{10,12},{12,14},{14,0},{1,3},{3,5},... | collective-permute-start | bytes 786440 | tf_op jit(solution)/shard_map/ppermute | solution.py:598
  144.6 5.6 %copy-start.14 = (bf16[1,512,256]{2,1,0:T(8,128)(2,1)S(1)}, bf16[1,512,256]{2,1,0:T(8,128)(2,1)}, u32[]{:S(2)}) copy-start(bf16[1,512,256]{2,1,0:T(8,128)(2,1)} %get-tuple-element.79.blocks_ref) | copy-start | bytes 786436
  144.7 11.1 %collective-permute-start.15 = (bf16[512,256]{1,0:T(8,128)(2,1)S(1)}, bf16[512,256]{1,0:T(8,128)(2,1)S(1)}, u32[]{:S(2)}, u32[]{:S(2)}) collective-permute-start(bf16[512,256]{1,0:T(8,128)(2,1)S(1)} %get-tuple-element.97), channel_id=1, source_target_pairs={{0,2},{2,4},{4,6},{6,8},{8,10},{10,12},{12,14},{14,0},{1,3},{3,5},... | collective-permute-start | bytes 786440 | tf_op jit(solution)/shard_map/ppermute | solution.py:598
  144.8 8.1 %collective-permute-start.13 = (bf16[512,256]{1,0:T(8,128)(2,1)S(1)}, bf16[512,256]{1,0:T(8,128)(2,1)S(1)}, u32[]{:S(2)}, u32[]{:S(2)}) collective-permute-start(bf16[512,256]{1,0:T(8,128)(2,1)S(1)} %get-tuple-element.94.refs_1_), channel_id=1, source_target_pairs={{0,14},{2,0},{4,2},{6,4},{8,6},{10,8},{12,10},{14,12},{1,15},{3,1}... | collective-permute-start | bytes 786440 | tf_op jit(solution)/shard_map/ppermute | solution.py:598
  150.2 2.7 %copy-start.13 = (bf16[1,512,256]{2,1,0:T(8,128)(2,1)S(1)}, bf16[1,512,256]{2,1,0:T(8,128)(2,1)}, u32[]{:S(2)}) copy-start(bf16[1,512,256]{2,1,0:T(8,128)(2,1)} %get-tuple-element.96.blocks_ref) | copy-start | bytes 786436
  150.2 11.2 %collective-permute-start.11 = (bf16[512,256]{1,0:T(8,128)(2,1)S(1)}, bf16[512,256]{1,0:T(8,128)(2,1)S(1)}, u32[]{:S(2)}, u32[]{:S(2)}) collective-permute-start(bf16[512,256]{1,0:T(8,128)(2,1)S(1)} %add_0_1.1.refs_1_), channel_id=1, source_target_pairs={{0,2},{2,4},{4,6},{6,8},{8,10},{10,12},{12,14},{14,0},{1,3},{3,5},... | collective-permute-start | bytes 786440 | tf_op jit(solution)/shard_map/ppermute | solution.py:598
  152.9 8.5 %copy-start.4 = (bf16[2,512,256]{2,1,0:T(8,128)(2,1)S(1)}, bf16[2,512,256]{2,1,0:T(8,128)(2,1)}, u32[]{:S(2)}) copy-start(bf16[2,512,256]{2,1,0:T(8,128)(2,1)} %get-tuple-element.78.blocks_ref) | copy-start | bytes 1572868
  153.0 21.7 %copy-start.6 = (bf16[128,512]{1,0:T(8,128)(2,1)S(1)}, bf16[128,512]{1,0:T(8,128)(2,1)}, u32[]{:S(2)}) copy-start(bf16[128,512]{1,0:T(8,128)(2,1)} %copy-done.5) | copy-start | bytes 393220
  153.0 8.4 %collective-permute-start.14 = (bf16[512,256]{1,0:T(8,128)(2,1)S(1)}, bf16[512,256]{1,0:T(8,128)(2,1)S(1)}, u32[]{:S(2)}, u32[]{:S(2)}) collective-permute-start(bf16[512,256]{1,0:T(8,128)(2,1)S(1)} %add_1_1.1), channel_id=1, source_target_pairs={{0,14},{2,0},{4,2},{6,4},{8,6},{10,8},{12,10},{14,12},{1,15},{3,1}... | collective-permute-start | bytes 786440 | tf_op jit(solution)/shard_map/ppermute | solution.py:598
  161.4 15.9 %copy-start.8 = (s32[34]{0:T(128)S(1)}, s32[34]{0:T(128)}, u32[]{:S(2)}) copy-start(s32[34]{0:T(128)} %get-tuple-element.53.table.owners) | copy-start | bytes 412
  162.4 23.8 %all-to-all-start.4 = ((bf16[32,16,512]{2,1,0:T(8,128)(2,1)}), bf16[32,16,512]{2,1,0:T(8,128)(2,1)S(1)}, u32[]{:S(2)}, u32[]{:S(2)}) async-start(bf16[32,16,512]{2,1,0:T(8,128)(2,1)} %bitcast.15), calls=%async_computation.4 | async-start | bytes 1048576 | tf_op jit(solution)/shard_map/all_to_all | solution.py:741
